TPU v7x, 128 devices: a whole 4x4x4 slice. The times are simulated.
128 devices in a mesh: row: 16 (over z, y), col: 8 (over x, core).
Axes of the slice: x: 4, y: 4, z: 4, core: 2. Of those that a mesh axis runs over, the one named last changes fastest.
Arguments:
- factor: float32 [2, 2048, 2048], P(None, 'row', 'col'), may hold values from -0.09375 to 0.09375
- lower_inverse: float32 [2, 512, 2048], P(None, None, 'row'), may hold values from -1 to 2
- upper_inverse: float32 [2, 512, 2048], P(None, None, 'row'), may hold values from -1 to 2
- krylov_block: float32 [2, 16, 2048], P(None, None, 'row'), may hold values from -6 to 6
- basis: float32 [2, 64, 2048], P(None, None, 'row'), may hold values from -0.09375 to 0.09375
Outputs:
- projected: float32 [2, 16, 2048], P(None, None, 'row')
- coefficients: float32 [2, 64, 16], replicated
All inputs are finite; a program needn't handle non-finite values.
Results may differ from a plain program's by a relative error of at most 0.00012.
Values sent between devices are 32-bit elements; how exact they have to be, the bound alone decides.
No kernel may reach another device: no remote copies, remote signals or barrier semaphores. Data moves between devices by JAX's collectives and lax.ppermute only.
A program may use at most 64 MiB of HBM per device.

v0:
```python
import jax
import jax.numpy as jnp
from jax import lax
from jax.sharding import PartitionSpec as P


def real_dot(left, right):
    return jnp.dot(left, right, preferred_element_type=jnp.float32, precision=lax.Precision.HIGHEST)


def apply_tile(matrix, vectors):
    real_part = real_dot(vectors[0], matrix[0].T) - real_dot(vectors[1], matrix[1].T)
    imag_part = real_dot(vectors[0], matrix[1].T) + real_dot(vectors[1], matrix[0].T)
    return jnp.stack([real_part, imag_part])


def herm_dot(basis_part, vectors):
    real_part = real_dot(basis_part[0], vectors[0].T) + real_dot(basis_part[1], vectors[1].T)
    imag_part = real_dot(basis_part[0], vectors[1].T) - real_dot(basis_part[1], vectors[0].T)
    return jnp.stack([real_part, imag_part])


def combine(basis_part, coeffs):
    real_part = real_dot(coeffs[0].T, basis_part[0]) - real_dot(coeffs[1].T, basis_part[1])
    imag_part = real_dot(coeffs[0].T, basis_part[1]) + real_dot(coeffs[1].T, basis_part[0])
    return jnp.stack([real_part, imag_part])


def local(factor, lower_inverse, upper_inverse, krylov_block, basis):
    tile = lower_inverse.shape[1]
    rows_local = factor.shape[1]
    width = factor.shape[2]
    nvec = krylov_block.shape[1]
    share = tile // rows_local
    tiles = lax.axis_size("row") // share
    row_idx = lax.axis_index("row")
    col_idx = lax.axis_index("col")
    own_tile = row_idx // share
    piece_idx = row_idx % share

    def sweep(inverse, pick, backward):
        start = jnp.zeros((2, nvec, tiles * tile), jnp.float32)

        def step(index, current):
            k = tiles - 1 - index if backward else index
            k = jnp.asarray(k).astype(jnp.int32)
            owner = own_tile == k
            cols = lax.dynamic_slice_in_dim(current, col_idx * width, width, 2)
            partial_value = apply_tile(factor, cols)
            given = pick(k)
            summed = lax.psum(partial_value, "col")
            term = apply_tile(inverse, given - summed)
            term = jnp.where(owner, term, jnp.zeros_like(term))
            piece = lax.psum(term, "row")
            return lax.dynamic_update_slice_in_dim(current, piece, k * tile, 2)

        return lax.fori_loop(0, tiles, step, start)

    def pick_forward(k):
        return krylov_block

    solved = sweep(lower_inverse, pick_forward, False)

    def pick_backward(k):
        return lax.dynamic_slice_in_dim(solved, k * tile + piece_idx * rows_local, rows_local, 2)

    solution = sweep(upper_inverse, pick_backward, True)
    own_rows = lax.dynamic_slice_in_dim(solution, row_idx * rows_local, rows_local, 2)
    local_first = herm_dot(basis, own_rows)
    first = lax.psum(local_first, "row")
    middle = own_rows - combine(basis, first)
    second = lax.psum(herm_dot(basis, middle), "row")
    projected = middle - combine(basis, second)
    return (projected, first + second)


def solution(mesh):
    in_specs = (
        P(None, "row", "col"),
        P(None, None, "row"),
        P(None, None, "row"),
        P(None, None, "row"),
        P(None, None, "row"),
    )
    out_specs = (P(None, None, "row"), P())
    return jax.shard_map(local, mesh=mesh, in_specs=in_specs, out_specs=out_specs, check_vma=False)
```

profile of v0, /device:TPU:2, one launch (start us, length us, event | category | flops | bytes accessed | tf_op | source)
XLA Modules:
  0.0 1009.6 jit_solution(2568802836361800633)
XLA Ops:
  7.2 0.9 copy-done
  8.1 427.0 %while.30 = (s32[]{:T(128)}, f32[2,16,2048]{2,1,0:T(8,128)S(1)}, s32[]{:T(128)}, s32[]{:T(128)}, f32[2,128,256]{2,1,0:T(8,128)S(1)}, /*index=5*/f32[2,16,128]{2,...) while((s32[]{:T(128)}, f32[2,16,2048]{2,1,0:T(8,128)S(1)}, ...), condition=%wide.region_3.4_spmd, body=%wide.region_0.3_spmd.sunk | while | flops 75579392 | bytes 4784409 | solution.py:57
  9.0 22.7 %psum.72 = f32[2,16,128]{2,1,0:T(8,128)S(1)} all-reduce(f32[2,16,128]{2,1,0:T(8,128)S(1)} %pad_maximum_fusion.6), channel_id=1, replica_groups=mesh['row'=16,'col'=8] {'col'}, use_global_device_ids=true, to_apply=%region_1.1 | all-reduce | flops 4096 | bytes 32768 | tf_op jit(solution)/shard_map/while/body/eval_jaxpr/psum | solution.py:51
  33.7 84.0 %all-reduce.3.cloned.1.call-done = f32[2,16,512]{2,1,0:T(8,128)} async-done(((f32[2,16,512]{2,1,0:T(8,128)}), f32[2,16,512]{2,1,0:T(8,128)}) %all-reduce.3.cloned.1.call-update) | async-done | bytes 65552 | tf_op jit(solution)/shard_map/while/body/eval_jaxpr/psum | solution.py:54
  117.6 0.8 constant_dynamic-update-slice_fusion.4
  119.4 21.1 %psum.72 = f32[2,16,128]{2,1,0:T(8,128)S(1)} all-reduce(f32[2,16,128]{2,1,0:T(8,128)S(1)} %pad_maximum_fusion.6), channel_id=1, replica_groups=mesh['row'=16,'col'=8] {'col'}, use_global_device_ids=true, to_apply=%region_1.1 | all-reduce | flops 4096 | bytes 32768 | tf_op jit(solution)/shard_map/while/body/eval_jaxpr/psum | solution.py:51
  142.5 80.7 %all-reduce.3.cloned.1.call-done = f32[2,16,512]{2,1,0:T(8,128)} async-done(((f32[2,16,512]{2,1,0:T(8,128)}), f32[2,16,512]{2,1,0:T(8,128)}) %all-reduce.3.cloned.1.call-update) | async-done | bytes 65552 | tf_op jit(solution)/shard_map/while/body/eval_jaxpr/psum | solution.py:54
  223.2 0.8 constant_dynamic-update-slice_fusion.4
  225.0 21.1 %psum.72 = f32[2,16,128]{2,1,0:T(8,128)S(1)} all-reduce(f32[2,16,128]{2,1,0:T(8,128)S(1)} %pad_maximum_fusion.6), channel_id=1, replica_groups=mesh['row'=16,'col'=8] {'col'}, use_global_device_ids=true, to_apply=%region_1.1 | all-reduce | flops 4096 | bytes 32768 | tf_op jit(solution)/shard_map/while/body/eval_jaxpr/psum | solution.py:51
  248.0 80.7 %all-reduce.3.cloned.1.call-done = f32[2,16,512]{2,1,0:T(8,128)} async-done(((f32[2,16,512]{2,1,0:T(8,128)}), f32[2,16,512]{2,1,0:T(8,128)}) %all-reduce.3.cloned.1.call-update) | async-done | bytes 65552 | tf_op jit(solution)/shard_map/while/body/eval_jaxpr/psum | solution.py:54
  328.7 0.8 constant_dynamic-update-slice_fusion.4
  330.5 21.1 %psum.72 = f32[2,16,128]{2,1,0:T(8,128)S(1)} all-reduce(f32[2,16,128]{2,1,0:T(8,128)S(1)} %pad_maximum_fusion.6), channel_id=1, replica_groups=mesh['row'=16,'col'=8] {'col'}, use_global_device_ids=true, to_apply=%region_1.1 | all-reduce | flops 4096 | bytes 32768 | tf_op jit(solution)/shard_map/while/body/eval_jaxpr/psum | solution.py:51
  353.6 80.7 %all-reduce.3.cloned.1.call-done = f32[2,16,512]{2,1,0:T(8,128)} async-done(((f32[2,16,512]{2,1,0:T(8,128)}), f32[2,16,512]{2,1,0:T(8,128)}) %all-reduce.3.cloned.1.call-update) | async-done | bytes 65552 | tf_op jit(solution)/shard_map/while/body/eval_jaxpr/psum | solution.py:54
  435.1 422.2 %while.31 = (s32[]{:T(128)}, f32[2,16,2048]{2,1,0:T(8,128)S(1)}, s32[]{:T(128)}, s32[]{:T(128)}, f32[2,16,2048]{2,1,0:T(8,128)S(1)}, /*index=5*/s32[]{:T(128)}, ...) while((s32[]{:T(128)}, f32[2,16,2048]{2,1,0:T(8,128)S(1)}, ...), condition=%wide.region_7.8_spmd, body=%wide.region_4.7_spmd.sunk | while | flops 75579392 | bytes 4784487 | solution.py:57
  436.1 21.1 %psum.74 = f32[2,16,128]{2,1,0:T(8,128)S(1)} all-reduce(f32[2,16,128]{2,1,0:T(8,128)S(1)} %pad_maximum_fusion.7), channel_id=1, replica_groups=mesh['row'=16,'col'=8] {'col'}, use_global_device_ids=true, to_apply=%region_5.5 | all-reduce | flops 4096 | bytes 32768 | tf_op jit(solution)/shard_map/while/body/eval_jaxpr/psum | solution.py:51
  459.2 80.7 %all-reduce.5.cloned.1.call-done = f32[2,16,512]{2,1,0:T(8,128)} async-done(((f32[2,16,512]{2,1,0:T(8,128)}), f32[2,16,512]{2,1,0:T(8,128)}) %all-reduce.5.cloned.1.call-update) | async-done | bytes 65552 | tf_op jit(solution)/shard_map/while/body/eval_jaxpr/psum | solution.py:54
  541.7 21.1 %psum.74 = f32[2,16,128]{2,1,0:T(8,128)S(1)} all-reduce(f32[2,16,128]{2,1,0:T(8,128)S(1)} %pad_maximum_fusion.7), channel_id=1, replica_groups=mesh['row'=16,'col'=8] {'col'}, use_global_device_ids=true, to_apply=%region_5.5 | all-reduce | flops 4096 | bytes 32768 | tf_op jit(solution)/shard_map/while/body/eval_jaxpr/psum | solution.py:51
  564.7 80.7 %all-reduce.5.cloned.1.call-done = f32[2,16,512]{2,1,0:T(8,128)} async-done(((f32[2,16,512]{2,1,0:T(8,128)}), f32[2,16,512]{2,1,0:T(8,128)}) %all-reduce.5.cloned.1.call-update) | async-done | bytes 65552 | tf_op jit(solution)/shard_map/while/body/eval_jaxpr/psum | solution.py:54
  647.2 21.1 %psum.74 = f32[2,16,128]{2,1,0:T(8,128)S(1)} all-reduce(f32[2,16,128]{2,1,0:T(8,128)S(1)} %pad_maximum_fusion.7), channel_id=1, replica_groups=mesh['row'=16,'col'=8] {'col'}, use_global_device_ids=true, to_apply=%region_5.5 | all-reduce | flops 4096 | bytes 32768 | tf_op jit(solution)/shard_map/while/body/eval_jaxpr/psum | solution.py:51
  670.2 80.7 %all-reduce.5.cloned.1.call-done = f32[2,16,512]{2,1,0:T(8,128)} async-done(((f32[2,16,512]{2,1,0:T(8,128)}), f32[2,16,512]{2,1,0:T(8,128)}) %all-reduce.5.cloned.1.call-update) | async-done | bytes 65552 | tf_op jit(solution)/shard_map/while/body/eval_jaxpr/psum | solution.py:54
  752.7 21.1 %psum.74 = f32[2,16,128]{2,1,0:T(8,128)S(1)} all-reduce(f32[2,16,128]{2,1,0:T(8,128)S(1)} %pad_maximum_fusion.7), channel_id=1, replica_groups=mesh['row'=16,'col'=8] {'col'}, use_global_device_ids=true, to_apply=%region_5.5 | all-reduce | flops 4096 | bytes 32768 | tf_op jit(solution)/shard_map/while/body/eval_jaxpr/psum | solution.py:51
  775.8 80.7 %all-reduce.5.cloned.1.call-done = f32[2,16,512]{2,1,0:T(8,128)} async-done(((f32[2,16,512]{2,1,0:T(8,128)}), f32[2,16,512]{2,1,0:T(8,128)}) %all-reduce.5.cloned.1.call-update) | async-done | bytes 65552 | tf_op jit(solution)/shard_map/while/body/eval_jaxpr/psum | solution.py:54
  858.0 72.1 %psum.66 = f32[2,64,16]{1,2,0:T(8,128)S(1)} all-reduce(f32[2,64,16]{1,2,0:T(8,128)S(1)} %pad_maximum_fusion.2), channel_id=1, replica_groups=mesh['row'=16,'col'=8] {'row'}, use_global_device_ids=true, to_apply=%region_8.9 | all-reduce | flops 2048 | bytes 16384 | tf_op jit(solution)/shard_map/psum | solution.py:70
  931.4 69.5 %psum.67 = f32[2,64,16]{1,2,0:T(8,128)S(1)} all-reduce(f32[2,64,16]{1,2,0:T(8,128)S(1)} %pad_maximum_fusion.3), channel_id=1, replica_groups=mesh['row'=16,'col'=8] {'row'}, use_global_device_ids=true, to_apply=%region_9.10 | all-reduce | flops 2048 | bytes 16384 | tf_op jit(solution)/shard_map/psum | solution.py:72
  (153 shorter events, 30.8 us)
Async XLA Ops:
  7.2 1.0 copy-start
  7.2 0.9 copy-start.4
  8.1 23.6 %copy-start.1 = (f32[2,512,128]{2,1,0:T(8,128)S(1)}, f32[2,512,128]{2,1,0:T(8,128)}, u32[]{:S(2)}) copy-start(f32[2,512,128]{2,1,0:T(8,128)} %get-tuple-element.525) | copy-start | bytes 1572868 | tf_op jit(solution)/shard_map/while
  8.1 109.5 %all-reduce.3.cloned.1.call-start = ((), (), s32[]{:S(2)}) async-start(), calls=%async_computation | async-start | bytes 131072 | tf_op jit(solution)/shard_map/while/body/eval_jaxpr/psum | solution.py:54
  118.5 22.0 %copy-start.1 = (f32[2,512,128]{2,1,0:T(8,128)S(1)}, f32[2,512,128]{2,1,0:T(8,128)}, u32[]{:S(2)}) copy-start(f32[2,512,128]{2,1,0:T(8,128)} %get-tuple-element.525) | copy-start | bytes 1572868 | tf_op jit(solution)/shard_map/while
  118.5 104.7 %all-reduce.3.cloned.1.call-start = ((), (), s32[]{:S(2)}) async-start(), calls=%async_computation | async-start | bytes 131072 | tf_op jit(solution)/shard_map/while/body/eval_jaxpr/psum | solution.py:54
  224.0 22.0 %copy-start.1 = (f32[2,512,128]{2,1,0:T(8,128)S(1)}, f32[2,512,128]{2,1,0:T(8,128)}, u32[]{:S(2)}) copy-start(f32[2,512,128]{2,1,0:T(8,128)} %get-tuple-element.525) | copy-start | bytes 1572868 | tf_op jit(solution)/shard_map/while
  224.0 104.7 %all-reduce.3.cloned.1.call-start = ((), (), s32[]{:S(2)}) async-start(), calls=%async_computation | async-start | bytes 131072 | tf_op jit(solution)/shard_map/while/body/eval_jaxpr/psum | solution.py:54
  329.6 22.0 %copy-start.1 = (f32[2,512,128]{2,1,0:T(8,128)S(1)}, f32[2,512,128]{2,1,0:T(8,128)}, u32[]{:S(2)}) copy-start(f32[2,512,128]{2,1,0:T(8,128)} %get-tuple-element.525) | copy-start | bytes 1572868 | tf_op jit(solution)/shard_map/while
  329.6 104.7 %all-reduce.3.cloned.1.call-start = ((), (), s32[]{:S(2)}) async-start(), calls=%async_computation | async-start | bytes 131072 | tf_op jit(solution)/shard_map/while/body/eval_jaxpr/psum | solution.py:54
  435.1 422.2 %copy-start.3 = (f32[2,64,128]{2,1,0:T(8,128)S(1)}, f32[2,64,128]{2,1,0:T(8,128)}, u32[]{:S(2)}) copy-start(f32[2,64,128]{2,1,0:T(8,128)} %param.13) | copy-start | bytes 196612
  435.1 22.1 %copy-start.2 = (f32[2,512,128]{2,1,0:T(8,128)S(1)}, f32[2,512,128]{2,1,0:T(8,128)}, u32[]{:S(2)}) copy-start(f32[2,512,128]{2,1,0:T(8,128)} %get-tuple-element.566) | copy-start | bytes 1572868 | tf_op jit(solution)/shard_map/while
  435.2 104.7 %all-reduce.5.cloned.1.call-start = ((), (), s32[]{:S(2)}) async-start(), calls=%async_computation.1 | async-start | bytes 131072 | tf_op jit(solution)/shard_map/while/body/eval_jaxpr/psum | solution.py:54
  540.7 22.0 %copy-start.2 = (f32[2,512,128]{2,1,0:T(8,128)S(1)}, f32[2,512,128]{2,1,0:T(8,128)}, u32[]{:S(2)}) copy-start(f32[2,512,128]{2,1,0:T(8,128)} %get-tuple-element.566) | copy-start | bytes 1572868 | tf_op jit(solution)/shard_map/while
  540.7 104.7 %all-reduce.5.cloned.1.call-start = ((), (), s32[]{:S(2)}) async-start(), calls=%async_computation.1 | async-start | bytes 131072 | tf_op jit(solution)/shard_map/while/body/eval_jaxpr/psum | solution.py:54
  646.2 22.0 %copy-start.2 = (f32[2,512,128]{2,1,0:T(8,128)S(1)}, f32[2,512,128]{2,1,0:T(8,128)}, u32[]{:S(2)}) copy-start(f32[2,512,128]{2,1,0:T(8,128)} %get-tuple-element.566) | copy-start | bytes 1572868 | tf_op jit(solution)/shard_map/while
  646.2 104.7 %all-reduce.5.cloned.1.call-start = ((), (), s32[]{:S(2)}) async-start(), calls=%async_computation.1 | async-start | bytes 131072 | tf_op jit(solution)/shard_map/while/body/eval_jaxpr/psum | solution.py:54
  751.8 22.0 %copy-start.2 = (f32[2,512,128]{2,1,0:T(8,128)S(1)}, f32[2,512,128]{2,1,0:T(8,128)}, u32[]{:S(2)}) copy-start(f32[2,512,128]{2,1,0:T(8,128)} %get-tuple-element.566) | copy-start | bytes 1572868 | tf_op jit(solution)/shard_map/while
  751.8 104.7 %all-reduce.5.cloned.1.call-start = ((), (), s32[]{:S(2)}) async-start(), calls=%async_computation.1 | async-start | bytes 131072 | tf_op jit(solution)/shard_map/while/body/eval_jaxpr/psum | solution.py:54
Sparse Core Ops, SparseCore 0:
  33.8 83.8 all-reduce.2
  142.6 80.5 all-reduce.2
  248.1 80.5 all-reduce.2
  353.7 80.5 all-reduce.2
  459.3 80.5 all-reduce.4
  564.8 80.5 all-reduce.4
  670.4 80.5 all-reduce.4
  775.9 80.5 all-reduce.4
where the time goes:
time: 1010 us
  waiting for transfers between devices  649 us (64%)
  blocking collectives  312 us (31%)
  matrix products  19.4 us (2%)
  between operations  14.1 us (1%)
    psum x8, waiting for transfers between devices, step(): piece = lax.psum(term, 'row')  649 us
    psum x8, blocking collectives, step(): summed = lax.psum(partial_value, 'col')  170 us
    psum x1, blocking collectives, local(): first = lax.psum(local_first, 'row')  72.1 us
    psum x1, blocking collectives, local(): second = lax.psum(herm_dot(basis, middle), 'row')  69.5 us
  transfers between devices with their start and end apart: 8, of which 8 were waited for; matrix products, arithmetic and copies ran while one was open for 0% of the time, Pallas kernels for 0%

commit v1 on v0

v1 whole, which is shorter than its diff:
```python
import jax
import jax.numpy as jnp
from jax import lax
from jax.sharding import Mesh, PartitionSpec as P

SIDE = 4
AXES = ("z", "y", "x", "c")
HIGH = lax.Precision.HIGH
HIGHEST = lax.Precision.HIGHEST


def dot_nt(left, right, precision):
    return lax.dot_general(left, right, (((1,), (1,)), ((), ())), precision=precision, preferred_element_type=jnp.float32)


def apply_rows(vectors, matrix, precision=HIGH):
    n = vectors.shape[1]
    both = jnp.concatenate([vectors[0], vectors[1]], 0)
    by_real = dot_nt(both, matrix[0], precision)
    by_imag = dot_nt(both, matrix[1], precision)
    return jnp.stack([by_real[:n] - by_imag[n:], by_real[n:] + by_imag[:n]])


def herm_rows(vectors, matrix, precision=HIGHEST):
    n = vectors.shape[1]
    both = jnp.concatenate([vectors[0], vectors[1]], 0)
    by_real = dot_nt(both, matrix[0], precision)
    by_imag = dot_nt(both, matrix[1], precision)
    return jnp.stack([by_real[:n] + by_imag[n:], by_real[n:] - by_imag[:n]])


def combine_rows(coeffs, matrix, precision=HIGHEST):
    n = coeffs.shape[1]
    both = jnp.concatenate([coeffs[0], coeffs[1]], 0)
    by_real = jnp.dot(both, matrix[0], precision=precision, preferred_element_type=jnp.float32)
    by_imag = jnp.dot(both, matrix[1], precision=precision, preferred_element_type=jnp.float32)
    return jnp.stack([by_real[:n] - by_imag[n:], by_real[n:] + by_imag[:n]])


def index_of(z, y, x, c):
    return ((z * SIDE + y) * SIDE + x) * 2 + c


def move(value, target):
    pairs = []
    for z in range(SIDE):
        for y in range(SIDE):
            for x in range(SIDE):
                for c in range(2):
                    there = target(z, y, x, c)
                    if there is not None:
                        pairs.append((index_of(z, y, x, c), index_of(*there)))
    return lax.ppermute(value, AXES, pairs)


def swap(value):
    return lax.ppermute(value, "c", [(0, 1), (1, 0)])


def along_y(value, planes, offset):
    def target(z, y, x, c):
        return (z, (y - offset) % SIDE, x, c) if z in planes else None

    return move(value, target)


def along_z(value, source, dest):
    def target(z, y, x, c):
        return (dest, y, x, c) if z == source else None

    return move(value, target)


def spread_x(value, role, offset):
    def target(z, y, x, c):
        return (z, y, (x + offset) % SIDE, c) if x == (z - role) % SIDE else None

    return move(value, target)


def local(factor, lower_inverse, upper_inverse, krylov_block, basis):
    z = lax.axis_index("z")
    y = lax.axis_index("y")
    x = lax.axis_index("x")
    c = lax.axis_index("c")
    piece = factor.shape[1]
    half = factor.shape[2]
    tile = 2 * half
    nvec = krylov_block.shape[1]
    mine = nvec // 2
    every = range(SIDE)

    def role_tile(role):
        own = jnp.where(x == (z - role) % SIDE, factor, 0.0)
        for offset in (1, 3, 2):
            own = own + spread_x(factor, role, offset)
        return own

    roles = {s: role_tile(s) for s in (1, 2, 3)}
    others = {s: swap(roles[s]) for s in (1, 2, 3)}

    def forward_product(vectors, s):
        near = lax.dynamic_slice_in_dim(vectors, c * half, half, 2)
        far = lax.dynamic_slice_in_dim(vectors, (1 - c) * half, half, 2)
        return apply_rows(near, roles[s]) + apply_rows(far, others[s])

    def both_cores(value):
        other = swap(value)
        first = jnp.where(c == 0, value, other)
        second = jnp.where(c == 0, other, value)
        return first, second

    def rotated(value):
        return lax.dynamic_slice_in_dim(jnp.concatenate([value, value], 2), y * piece, tile, 2)

    given = lax.dynamic_slice_in_dim(krylov_block, c * mine, mine, 1)
    rest = given
    solved = jnp.zeros((2, mine, tile), jnp.float32)
    for k in every:
        partial_value = apply_rows(rest, lower_inverse)
        full = partial_value
        for offset in (1, 3, 2):
            full = full + along_y(partial_value, (k,), offset)
        solved = jnp.where(z == k, full, solved)
        for dest in range(k + 1, SIDE):
            rest = rest - forward_product(along_z(full, k, dest), dest - k)

    upper_half = lax.dynamic_slice_in_dim(upper_inverse, c * half, half, 1)
    upper_rows = jnp.concatenate([upper_half] + [along_y(upper_half, every, d) for d in (1, 2, 3)], 2)
    planes_of = {3: (0, 1, 2), 2: (0, 1), 1: (0,)}
    tall = {}
    for s in (3, 2, 1):
        tall[s] = jnp.concatenate([roles[s]] + [along_y(roles[s], planes_of[s], d) for d in (1, 2, 3)], 1)

    basis_all = jnp.stack([basis] + [along_y(basis, every, d) for d in (1, 2, 3)])
    low = lax.dynamic_index_in_dim(basis_all, (2 * c - y) % SIDE, 0, False)
    high = lax.dynamic_index_in_dim(basis_all, (2 * c + 1 - y) % SIDE, 0, False)
    basis_half = jnp.concatenate([low, high], 2)
    gram = herm_rows(basis_half, basis_half)
    gram = gram + swap(gram)
    shifts = [[(i, (i + d) % SIDE) for i in every] for d in (1, 3, 2)]
    gram_parts = [lax.ppermute(gram, "z", s) for s in shifts]
    gram = gram + gram_parts[0] + gram_parts[1] + gram_parts[2]
    nb = basis.shape[1]
    twice = jnp.stack([2.0 * jnp.eye(nb, dtype=jnp.float32), jnp.zeros((nb, nb), jnp.float32)])
    keep = twice - gram
    spread = combine_rows(keep, basis)

    start, end = both_cores(solved)
    held = rotated(jnp.concatenate([start, end], 1))
    acc = jnp.zeros((2, nvec, tile), jnp.float32)
    final = jnp.zeros((2, nvec, half), jnp.float32)
    early = None
    for k in (3, 2, 1, 0):
        if k == 3:
            right = held
        else:
            right = held - (acc + swap(acc))
        part = apply_rows(right, upper_rows)
        if k > 0:
            final = jnp.where(z == k, part, final)
            for dest in range(k - 1, -1, -1):
                acc = acc + apply_rows(along_z(part, k, dest), tall[(dest - k) % SIDE])
        if k == 1:
            early = herm_rows(final, basis_half)
            early = early + swap(early)
            parts = [lax.ppermute(early, "z", s) for s in shifts]
            early = early + parts[0] + parts[1] + parts[2]
            before, after = both_cores(final)
            own_early = jnp.where(y % 2 == 0, 0, piece)
            chosen = jnp.where(y < 2, before, after)
            own_rows = lax.dynamic_slice_in_dim(chosen, own_early, piece, 2)
    last = herm_rows(part, basis_half)
    packed = jnp.concatenate([part, last], 2)
    other = swap(packed)
    last = last + other[:, :, half:]
    from_half = jnp.where((y < 2) == (c == 0), part, other[:, :, :half])
    own_last = lax.dynamic_slice_in_dim(from_half, (y % 2) * piece, piece, 2)
    own_rows = jnp.where(z == 0, own_last, own_rows)
    total = jnp.where(z == 0, last, 0.0)
    for dest in (1, 3, 2):
        total = total + along_z(last, 0, dest)
    first = total + early
    projected = own_rows - combine_rows(first, spread)
    coeffs = combine_rows(first, keep)
    return projected, jnp.swapaxes(coeffs, 1, 2)


def solution(mesh):
    split = Mesh(mesh.devices.reshape(SIDE, SIDE, SIDE, 2), AXES)
    row, col = ("z", "y"), ("x", "c")
    in_specs = (P(None, row, col), P(None, None, row), P(None, None, row), P(None, None, row), P(None, None, row))
    out_specs = (P(None, None, row), P())
    return jax.shard_map(local, mesh=split, in_specs=in_specs, out_specs=out_specs, check_vma=False)
```

time: 1010 us -> 268 us (0.27)
  waiting for transfers between devices: 649 us -> 30.7 us
  blocking collectives: 312 us -> 0 us
  starting transfers between devices: 0.27 us -> 212 us
  between operations: 14.1 us -> 2.4 us
    psum x8 -> x0, waiting for transfers between devices: 649 us -> none  [step(): piece = lax.psum(term, 'row')]
    psum x10 -> x0, blocking collectives: 312 us -> none  [the longest x8 170 us: step(): summed = lax.psum(partial_value, 'col')]
    ppermute x0 -> x68, starting transfers between devices: none -> 212 us  [the longest x51 186 us: move(): return lax.ppermute(value, AXES, pairs)]
    ppermute x0 -> x68, waiting for transfers between devices: none -> 30.7 us  [the longest x51 26.5 us: move(): return lax.ppermute(value, AXES, pairs)]
  transfers between devices with their start and end apart: 8 -> 68, of which waited for: 8 -> 15; matrix products, arithmetic and copies ran while one was open for 0% -> 6% of each run, Pallas kernels for 0% -> 0%
where the time goes in v1:
time: 268 us; the launch traced here: 266 us
  starting transfers between devices  212 us (79%)
  waiting for transfers between devices  30.7 us (11%)
  matrix products  17.1 us (6%)
  other arithmetic  2.79 us (1%)
    ppermute x51, starting transfers between devices, move(): return lax.ppermute(value, AXES, pairs)  186 us
    ppermute x51, waiting for transfers between devices, move(): return lax.ppermute(value, AXES, pairs)  26.5 us
    dot_general x58, matrix products, dot_nt(): lax.dot_general(left, right, (((1,), (1,)), ((), ())), precision=precisio...  15.8 us
    ppermute x3, starting transfers between devices, local(): gram_parts = [lax.ppermute(gram, 'z', s) for s in shifts]  12.3 us
    ppermute x11, starting transfers between devices, swap(): return lax.ppermute(value, 'c', [(0, 1), (1, 0)])  10.4 us
  transfers between devices with their start and end apart: 68, of which 15 were waited for; matrix products, arithmetic and copies ran while one was open for 6% of the time, Pallas kernels for 0%

profile of v1, /device:TPU:2, one launch (start us, length us, event | category | flops | bytes accessed | tf_op | source)
XLA Modules:
  0.0 266.4 jit_solution(618154765613730155)
XLA Ops:
  5.2 4.9 %collective-permute-start = (f32[2,8,512]{2,1,0:T(8,128)S(1)}, f32[2,8,512]{2,1,0:T(8,128)S(1)}, u32[]{:S(2)}, u32[]{:S(2)}) collective-permute-start(f32[2,8,512]{2,1,0:T(8,128)S(1)} %pad_maximum_fusion.22), channel_id=1, source_target_pairs={{0,24},{1,25},{2,26},{3,27},{4,28},{5,29},{6,30},{7,31},{8,0},{9,1... | collective-permute-start | bytes 98312 | tf_op jit(solution)/shard_map/ppermute | solution.py:53
  12.0 4.1 %collective-permute-start.2 = (f32[2,8,512]{2,1,0:T(8,128)S(1)}, f32[2,8,512]{2,1,0:T(8,128)S(1)}, u32[]{:S(2)}, u32[]{:S(2)}) collective-permute-start(f32[2,8,512]{2,1,0:T(8,128)S(1)} %pad_maximum_fusion.22), channel_id=1, source_target_pairs={{0,16},{1,17},{2,18},{3,19},{4,20},{5,21},{6,22},{7,23},{8,24},{9,... | collective-permute-start | bytes 98312 | tf_op jit(solution)/shard_map/ppermute | solution.py:53
  21.4 5.2 %collective-permute-start.14 = (f32[2,128,256]{2,1,0:T(8,128)S(1)}, f32[2,128,256]{2,1,0:T(8,128)S(1)}, u32[]{:S(2)}, u32[]{:S(2)}) collective-permute-start(f32[2,128,256]{2,1,0:T(8,128)S(1)} %copy-done.3), channel_id=1, source_target_pairs={{2,4},{3,5},{10,12},{11,13},{18,20},{19,21},{26,28},{27,29},{36,38... | collective-permute-start | bytes 786440 | tf_op jit(solution)/shard_map/ppermute | solution.py:53
  45.9 5.1 %collective-permute-done.6 = f32[2,128,256]{2,1,0:T(8,128)S(1)} collective-permute-done((f32[2,128,256]{2,1,0:T(8,128)S(1)}, f32[2,128,256]{2,1,0:T(8,128)S(1)}, u32[]{:S(2)}, u32[]{:S(2)}) %collective-permute-start.6) | collective-permute-done | bytes 262176 | tf_op jit(solution)/shard_map/ppermute | solution.py:53
  51.2 8.3 %collective-permute-start.17 = (f32[2,128,256]{2,1,0:T(8,128)S(1)}, f32[2,128,256]{2,1,0:T(8,128)S(1)}, u32[]{:S(2)}, u32[]{:S(2)}) collective-permute-start(f32[2,128,256]{2,1,0:T(8,128)S(1)} %get-tuple-element.4), channel_id=1, source_target_pairs={{0,1},{1,0},{2,3},{3,2},{4,5},{5,4},{6,7},{7,6},{8,9},{9,8},{10,11... | collective-permute-start | bytes 786440 | tf_op jit(solution)/shard_map/ppermute | solution.py:57
  73.5 3.7 %collective-permute-start.43 = (f32[2,128,256]{2,1,0:T(8,128)S(1)}, f32[2,128,256]{2,1,0:T(8,128)S(1)}, u32[]{:S(2)}, u32[]{:S(2)}) collective-permute-start(f32[2,128,256]{2,1,0:T(8,128)S(1)} %get-tuple-element.6), channel_id=1, source_target_pairs={{0,24},{1,25},{2,26},{3,27},{4,28},{5,29},{6,30},{7,31},{8,0},{9,1... | collective-permute-start | bytes 786440 | tf_op jit(solution)/shard_map/ppermute | solution.py:53
  77.2 3.7 %collective-permute-start.44 = (f32[2,128,256]{2,1,0:T(8,128)S(1)}, f32[2,128,256]{2,1,0:T(8,128)S(1)}, u32[]{:S(2)}, u32[]{:S(2)}) collective-permute-start(f32[2,128,256]{2,1,0:T(8,128)S(1)} %get-tuple-element.6), channel_id=1, source_target_pairs={{0,16},{1,17},{2,18},{3,19},{4,20},{5,21},{6,22},{7,23},{8,24},{9,... | collective-permute-start | bytes 786440 | tf_op jit(solution)/shard_map/ppermute | solution.py:53
  84.7 29.7 %collective-permute-start.39 = (f32[2,128,256]{2,1,0:T(8,128)S(1)}, f32[2,128,256]{2,1,0:T(8,128)S(1)}, u32[]{:S(2)}, u32[]{:S(2)}) collective-permute-start(f32[2,128,256]{2,1,0:T(8,128)S(1)} %get-tuple-element.5), channel_id=1, source_target_pairs={{0,24},{1,25},{2,26},{3,27},{4,28},{5,29},{6,30},{7,31},{8,0},{9,1... | collective-permute-start | bytes 786440 | tf_op jit(solution)/shard_map/ppermute | solution.py:53
  114.5 8.9 %collective-permute-start.27 = (f32[2,8,512]{2,1,0:T(8,128)S(1)}, f32[2,8,512]{2,1,0:T(8,128)S(1)}, u32[]{:S(2)}, u32[]{:S(2)}) collective-permute-start(f32[2,8,512]{2,1,0:T(8,128)S(1)} %pad_maximum_fusion.25), channel_id=1, source_target_pairs={{96,120},{97,121},{98,122},{99,123},{100,124},{101,125},{102,126},... | collective-permute-start | bytes 98312 | tf_op jit(solution)/shard_map/ppermute | solution.py:53
  123.5 10.8 %collective-permute-start.40 = (f32[2,128,256]{2,1,0:T(8,128)S(1)}, f32[2,128,256]{2,1,0:T(8,128)S(1)}, u32[]{:S(2)}, u32[]{:S(2)}) collective-permute-start(f32[2,128,256]{2,1,0:T(8,128)S(1)} %get-tuple-element.5), channel_id=1, source_target_pairs={{0,16},{1,17},{2,18},{3,19},{4,20},{5,21},{6,22},{7,23},{8,24},{9,... | collective-permute-start | bytes 786440 | tf_op jit(solution)/shard_map/ppermute | solution.py:53
  134.3 9.6 %collective-permute-start.41 = (f32[2,128,256]{2,1,0:T(8,128)S(1)}, f32[2,128,256]{2,1,0:T(8,128)S(1)}, u32[]{:S(2)}, u32[]{:S(2)}) collective-permute-start(f32[2,128,256]{2,1,0:T(8,128)S(1)} %get-tuple-element.5), channel_id=1, source_target_pairs={{0,8},{1,9},{2,10},{3,11},{4,12},{5,13},{6,14},{7,15},{8,16},{9,17... | collective-permute-start | bytes 786440 | tf_op jit(solution)/shard_map/ppermute | solution.py:53
  143.9 8.9 %collective-permute-start.28 = (f32[2,8,512]{2,1,0:T(8,128)S(1)}, f32[2,8,512]{2,1,0:T(8,128)S(1)}, u32[]{:S(2)}, u32[]{:S(2)}) collective-permute-start(f32[2,8,512]{2,1,0:T(8,128)S(1)} %pad_maximum_fusion.25), channel_id=1, source_target_pairs={{96,104},{97,105},{98,106},{99,107},{100,108},{101,109},{102,110},... | collective-permute-start | bytes 98312 | tf_op jit(solution)/shard_map/ppermute | solution.py:53
  152.8 10.2 %collective-permute-start.29 = (f32[2,8,512]{2,1,0:T(8,128)S(1)}, f32[2,8,512]{2,1,0:T(8,128)S(1)}, u32[]{:S(2)}, u32[]{:S(2)}) collective-permute-start(f32[2,8,512]{2,1,0:T(8,128)S(1)} %pad_maximum_fusion.25), channel_id=1, source_target_pairs={{96,112},{97,113},{98,114},{99,115},{100,116},{101,117},{102,118},... | collective-permute-start | bytes 98312 | tf_op jit(solution)/shard_map/ppermute | solution.py:53
  164.7 7.2 %collective-permute-start.66 = (f32[2,64,64]{1,2,0:T(8,128)S(1)}, f32[2,64,64]{1,2,0:T(8,128)S(1)}, u32[]{:S(2)}, u32[]{:S(2)}) collective-permute-start(f32[2,64,64]{1,2,0:T(8,128)S(1)} %fusion.256), channel_id=1, source_target_pairs={{0,96},{32,0},{64,32},{96,64},{1,97},{33,1},{65,33},{97,65},{2,98}... | collective-permute-start | bytes 98312 | tf_op jit(solution)/shard_map/ppermute | solution.py:142
  172.0 5.4 %collective-permute-start.35 = (f32[2,128,256]{2,1,0:T(8,128)S(1)}, f32[2,128,256]{2,1,0:T(8,128)S(1)}, u32[]{:S(2)}, u32[]{:S(2)}) collective-permute-start(f32[2,128,256]{2,1,0:T(8,128)S(1)} %get-tuple-element.4), channel_id=1, source_target_pairs={{0,24},{1,25},{2,26},{3,27},{4,28},{5,29},{6,30},{7,31},{8,0},{9,1... | collective-permute-start | bytes 786440 | tf_op jit(solution)/shard_map/ppermute | solution.py:53
  177.4 10.2 %collective-permute-start.36 = (f32[2,128,256]{2,1,0:T(8,128)S(1)}, f32[2,128,256]{2,1,0:T(8,128)S(1)}, u32[]{:S(2)}, u32[]{:S(2)}) collective-permute-start(f32[2,128,256]{2,1,0:T(8,128)S(1)} %get-tuple-element.4), channel_id=1, source_target_pairs={{0,16},{1,17},{2,18},{3,19},{4,20},{5,21},{6,22},{7,23},{8,24},{9,... | collective-permute-start | bytes 786440 | tf_op jit(solution)/shard_map/ppermute | solution.py:53
  188.9 10.2 %collective-permute-start.37 = (f32[2,128,256]{2,1,0:T(8,128)S(1)}, f32[2,128,256]{2,1,0:T(8,128)S(1)}, u32[]{:S(2)}, u32[]{:S(2)}) collective-permute-start(f32[2,128,256]{2,1,0:T(8,128)S(1)} %get-tuple-element.4), channel_id=1, source_target_pairs={{0,8},{1,9},{2,10},{3,11},{4,12},{5,13},{6,14},{7,15},{8,16},{9,17... | collective-permute-start | bytes 786440 | tf_op jit(solution)/shard_map/ppermute | solution.py:53
  199.9 3.5 %collective-permute-start.67 = (f32[2,64,64]{1,2,0:T(8,128)S(1)}, f32[2,64,64]{1,2,0:T(8,128)S(1)}, u32[]{:S(2)}, u32[]{:S(2)}) collective-permute-start(f32[2,64,64]{1,2,0:T(8,128)S(1)} %fusion.256), channel_id=1, source_target_pairs={{0,64},{32,96},{64,0},{96,32},{1,65},{33,97},{65,1},{97,33},{2,66}... | collective-permute-start | bytes 98312 | tf_op jit(solution)/shard_map/ppermute | solution.py:142
  204.6 3.8 %collective-permute-done.37 = f32[2,128,256]{2,1,0:T(8,128)S(1)} collective-permute-done((f32[2,128,256]{2,1,0:T(8,128)S(1)}, f32[2,128,256]{2,1,0:T(8,128)S(1)}, u32[]{:S(2)}, u32[]{:S(2)}) %collective-permute-start.37) | collective-permute-done | bytes 262176 | tf_op jit(solution)/shard_map/ppermute | solution.py:53
  208.4 7.4 %collective-permute-start.38 = (f32[2,16,256]{2,1,0:T(8,128)S(1)}, f32[2,16,256]{2,1,0:T(8,128)S(1)}, u32[]{:S(2)}, u32[]{:S(2)}) collective-permute-start(f32[2,16,256]{2,1,0:T(8,128)S(1)} %pad_maximum_fusion.26), channel_id=1, source_target_pairs={{96,32},{97,33},{98,34},{99,35},{100,36},{101,37},{102,38},{103,39... | collective-permute-start | bytes 98312 | tf_op jit(solution)/shard_map/ppermute | solution.py:53
  215.8 10.2 %collective-permute-start.34 = (f32[2,16,256]{2,1,0:T(8,128)S(1)}, f32[2,16,256]{2,1,0:T(8,128)S(1)}, u32[]{:S(2)}, u32[]{:S(2)}) collective-permute-start(f32[2,16,256]{2,1,0:T(8,128)S(1)} %pad_maximum_fusion.26), channel_id=1, source_target_pairs={{96,64},{97,65},{98,66},{99,67},{100,68},{101,69},{102,70},{103,71... | collective-permute-start | bytes 98312 | tf_op jit(solution)/shard_map/ppermute | solution.py:53
  232.4 7.0 %collective-permute-done.48 = f32[2,16,256]{2,1,0:T(8,128)S(1)} collective-permute-done((f32[2,16,256]{2,1,0:T(8,128)S(1)}, f32[2,16,256]{2,1,0:T(8,128)S(1)}, u32[]{:S(2)}, u32[]{:S(2)}) %collective-permute-start.48) | collective-permute-done | bytes 32800 | tf_op jit(solution)/shard_map/ppermute | solution.py:53
  244.8 4.5 %collective-permute-done.50 = f32[2,16,256]{2,1,0:T(8,128)S(1)} collective-permute-done((f32[2,16,256]{2,1,0:T(8,128)S(1)}, f32[2,16,256]{2,1,0:T(8,128)S(1)}, u32[]{:S(2)}, u32[]{:S(2)}) %collective-permute-start.50) | collective-permute-done | bytes 32800 | tf_op jit(solution)/shard_map/ppermute | solution.py:53
  252.9 3.2 %collective-permute-start.62 = (f32[2,16,64]{2,1,0:T(8,128)S(1)}, f32[2,16,64]{2,1,0:T(8,128)S(1)}, u32[]{:S(2)}, u32[]{:S(2)}) collective-permute-start(f32[2,16,64]{2,1,0:T(8,128)S(1)} %fusion.255), channel_id=1, source_target_pairs={{0,96},{32,0},{64,32},{96,64},{1,97},{33,1},{65,33},{97,65},{2,98}... | collective-permute-start | bytes 24584 | tf_op jit(solution)/shard_map/ppermute | solution.py:167
  (285 shorter events, 78.6 us)
Async XLA Ops:
  0.7 37.9 %collective-permute-start.10 = (f32[2,128,256]{2,1,0:T(8,128)}, f32[2,128,256]{2,1,0:T(8,128)S(1)}, u32[]{:S(2)}, u32[]{:S(2)}) collective-permute-start(f32[2,128,256]{2,1,0:T(8,128)} %param.5), channel_id=1, source_target_pairs={{4,2},{5,3},{12,10},{13,11},{20,18},{21,19},{28,26},{29,27},{38,36... | collective-permute-start | bytes 786440 | tf_op jit(solution)/shard_map/ppermute | solution.py:53
  2.1 37.2 %collective-permute-start.11 = (f32[2,128,256]{2,1,0:T(8,128)}, f32[2,128,256]{2,1,0:T(8,128)S(1)}, u32[]{:S(2)}, u32[]{:S(2)}) collective-permute-start(f32[2,128,256]{2,1,0:T(8,128)} %param.5), channel_id=1, source_target_pairs={{4,0},{5,1},{12,8},{13,9},{20,16},{21,17},{28,24},{29,25},{38,34},... | collective-permute-start | bytes 786440 | tf_op jit(solution)/shard_map/ppermute | solution.py:53
  21.4 18.6 %collective-permute-start.14 = (f32[2,128,256]{2,1,0:T(8,128)S(1)}, f32[2,128,256]{2,1,0:T(8,128)S(1)}, u32[]{:S(2)}, u32[]{:S(2)}) collective-permute-start(f32[2,128,256]{2,1,0:T(8,128)S(1)} %copy-done.3), channel_id=1, source_target_pairs={{2,4},{3,5},{10,12},{11,13},{18,20},{19,21},{26,28},{27,29},{36,38... | collective-permute-start | bytes 786440 | tf_op jit(solution)/shard_map/ppermute | solution.py:53
  26.6 14.7 %collective-permute-start.15 = (f32[2,128,256]{2,1,0:T(8,128)S(1)}, f32[2,128,256]{2,1,0:T(8,128)S(1)}, u32[]{:S(2)}, u32[]{:S(2)}) collective-permute-start(f32[2,128,256]{2,1,0:T(8,128)S(1)} %copy-done.3), channel_id=1, source_target_pairs={{2,0},{3,1},{10,8},{11,9},{18,16},{19,17},{26,24},{27,25},{36,34},... | collective-permute-start | bytes 786440 | tf_op jit(solution)/shard_map/ppermute | solution.py:53
  42.4 39.7 %collective-permute-start.31 = (f32[2,256,128]{2,1,0:T(8,128)S(1)}, f32[2,256,128]{2,1,0:T(8,128)S(1)}, u32[]{:S(2)}, u32[]{:S(2)}) collective-permute-start(f32[2,256,128]{2,1,0:T(8,128)S(1)} %constant_dynamic-slice_fusion.13), channel_id=1, source_target_pairs={{0,24},{1,25},{2,26},{3,27},{4,28},{5,29},{6,30},{7,31},{8,0},{9,1... | collective-permute-start | bytes 786440 | tf_op jit(solution)/shard_map/ppermute | solution.py:53
  44.7 40.1 %collective-permute-start.32 = (f32[2,256,128]{2,1,0:T(8,128)S(1)}, f32[2,256,128]{2,1,0:T(8,128)S(1)}, u32[]{:S(2)}, u32[]{:S(2)}) collective-permute-start(f32[2,256,128]{2,1,0:T(8,128)S(1)} %constant_dynamic-slice_fusion.13), channel_id=1, source_target_pairs={{0,16},{1,17},{2,18},{3,19},{4,20},{5,21},{6,22},{7,23},{8,24},{9,... | collective-permute-start | bytes 786440 | tf_op jit(solution)/shard_map/ppermute | solution.py:53
  70.7 43.8 %collective-permute-start.33 = (f32[2,256,128]{2,1,0:T(8,128)S(1)}, f32[2,256,128]{2,1,0:T(8,128)S(1)}, u32[]{:S(2)}, u32[]{:S(2)}) collective-permute-start(f32[2,256,128]{2,1,0:T(8,128)S(1)} %constant_dynamic-slice_fusion.13), channel_id=1, source_target_pairs={{0,8},{1,9},{2,10},{3,11},{4,12},{5,13},{6,14},{7,15},{8,16},{9,17... | collective-permute-start | bytes 786440 | tf_op jit(solution)/shard_map/ppermute | solution.py:53
  73.5 50.0 %collective-permute-start.43 = (f32[2,128,256]{2,1,0:T(8,128)S(1)}, f32[2,128,256]{2,1,0:T(8,128)S(1)}, u32[]{:S(2)}, u32[]{:S(2)}) collective-permute-start(f32[2,128,256]{2,1,0:T(8,128)S(1)} %get-tuple-element.6), channel_id=1, source_target_pairs={{0,24},{1,25},{2,26},{3,27},{4,28},{5,29},{6,30},{7,31},{8,0},{9,1... | collective-permute-start | bytes 786440 | tf_op jit(solution)/shard_map/ppermute | solution.py:53
  77.2 57.1 %collective-permute-start.44 = (f32[2,128,256]{2,1,0:T(8,128)S(1)}, f32[2,128,256]{2,1,0:T(8,128)S(1)}, u32[]{:S(2)}, u32[]{:S(2)}) collective-permute-start(f32[2,128,256]{2,1,0:T(8,128)S(1)} %get-tuple-element.6), channel_id=1, source_target_pairs={{0,16},{1,17},{2,18},{3,19},{4,20},{5,21},{6,22},{7,23},{8,24},{9,... | collective-permute-start | bytes 786440 | tf_op jit(solution)/shard_map/ppermute | solution.py:53
  82.2 61.7 %collective-permute-start.45 = (f32[2,128,256]{2,1,0:T(8,128)S(1)}, f32[2,128,256]{2,1,0:T(8,128)S(1)}, u32[]{:S(2)}, u32[]{:S(2)}) collective-permute-start(f32[2,128,256]{2,1,0:T(8,128)S(1)} %get-tuple-element.6), channel_id=1, source_target_pairs={{0,8},{1,9},{2,10},{3,11},{4,12},{5,13},{6,14},{7,15},{8,16},{9,17... | collective-permute-start | bytes 786440 | tf_op jit(solution)/shard_map/ppermute | solution.py:53
  84.7 87.2 %collective-permute-start.39 = (f32[2,128,256]{2,1,0:T(8,128)S(1)}, f32[2,128,256]{2,1,0:T(8,128)S(1)}, u32[]{:S(2)}, u32[]{:S(2)}) collective-permute-start(f32[2,128,256]{2,1,0:T(8,128)S(1)} %get-tuple-element.5), channel_id=1, source_target_pairs={{0,24},{1,25},{2,26},{3,27},{4,28},{5,29},{6,30},{7,31},{8,0},{9,1... | collective-permute-start | bytes 786440 | tf_op jit(solution)/shard_map/ppermute | solution.py:53
  114.5 38.3 %collective-permute-start.27 = (f32[2,8,512]{2,1,0:T(8,128)S(1)}, f32[2,8,512]{2,1,0:T(8,128)S(1)}, u32[]{:S(2)}, u32[]{:S(2)}) collective-permute-start(f32[2,8,512]{2,1,0:T(8,128)S(1)} %pad_maximum_fusion.25), channel_id=1, source_target_pairs={{96,120},{97,121},{98,122},{99,123},{100,124},{101,125},{102,126},... | collective-permute-start | bytes 98312 | tf_op jit(solution)/shard_map/ppermute | solution.py:53
  123.5 53.9 %collective-permute-start.40 = (f32[2,128,256]{2,1,0:T(8,128)S(1)}, f32[2,128,256]{2,1,0:T(8,128)S(1)}, u32[]{:S(2)}, u32[]{:S(2)}) collective-permute-start(f32[2,128,256]{2,1,0:T(8,128)S(1)} %get-tuple-element.5), channel_id=1, source_target_pairs={{0,16},{1,17},{2,18},{3,19},{4,20},{5,21},{6,22},{7,23},{8,24},{9,... | collective-permute-start | bytes 786440 | tf_op jit(solution)/shard_map/ppermute | solution.py:53
  134.3 53.2 %collective-permute-start.41 = (f32[2,128,256]{2,1,0:T(8,128)S(1)}, f32[2,128,256]{2,1,0:T(8,128)S(1)}, u32[]{:S(2)}, u32[]{:S(2)}) collective-permute-start(f32[2,128,256]{2,1,0:T(8,128)S(1)} %get-tuple-element.5), channel_id=1, source_target_pairs={{0,8},{1,9},{2,10},{3,11},{4,12},{5,13},{6,14},{7,15},{8,16},{9,17... | collective-permute-start | bytes 786440 | tf_op jit(solution)/shard_map/ppermute | solution.py:53
  143.9 19.2 %collective-permute-start.28 = (f32[2,8,512]{2,1,0:T(8,128)S(1)}, f32[2,8,512]{2,1,0:T(8,128)S(1)}, u32[]{:S(2)}, u32[]{:S(2)}) collective-permute-start(f32[2,8,512]{2,1,0:T(8,128)S(1)} %pad_maximum_fusion.25), channel_id=1, source_target_pairs={{96,104},{97,105},{98,106},{99,107},{100,108},{101,109},{102,110},... | collective-permute-start | bytes 98312 | tf_op jit(solution)/shard_map/ppermute | solution.py:53
  152.8 11.9 %collective-permute-start.29 = (f32[2,8,512]{2,1,0:T(8,128)S(1)}, f32[2,8,512]{2,1,0:T(8,128)S(1)}, u32[]{:S(2)}, u32[]{:S(2)}) collective-permute-start(f32[2,8,512]{2,1,0:T(8,128)S(1)} %pad_maximum_fusion.25), channel_id=1, source_target_pairs={{96,112},{97,113},{98,114},{99,115},{100,116},{101,117},{102,118},... | collective-permute-start | bytes 98312 | tf_op jit(solution)/shard_map/ppermute | solution.py:53
  163.1 65.4 %collective-permute-start.65 = (f32[2,64,64]{1,2,0:T(8,128)S(1)}, f32[2,64,64]{1,2,0:T(8,128)S(1)}, u32[]{:S(2)}, u32[]{:S(2)}) collective-permute-start(f32[2,64,64]{1,2,0:T(8,128)S(1)} %fusion.256), channel_id=1, source_target_pairs={{0,32},{32,64},{64,96},{96,0},{1,33},{33,65},{65,97},{97,1},{2,34}... | collective-permute-start | bytes 98312 | tf_op jit(solution)/shard_map/ppermute | solution.py:142
  164.7 63.7 %collective-permute-start.66 = (f32[2,64,64]{1,2,0:T(8,128)S(1)}, f32[2,64,64]{1,2,0:T(8,128)S(1)}, u32[]{:S(2)}, u32[]{:S(2)}) collective-permute-start(f32[2,64,64]{1,2,0:T(8,128)S(1)} %fusion.256), channel_id=1, source_target_pairs={{0,96},{32,0},{64,32},{96,64},{1,97},{33,1},{65,33},{97,65},{2,98}... | collective-permute-start | bytes 98312 | tf_op jit(solution)/shard_map/ppermute | solution.py:142
  172.0 27.9 %collective-permute-start.35 = (f32[2,128,256]{2,1,0:T(8,128)S(1)}, f32[2,128,256]{2,1,0:T(8,128)S(1)}, u32[]{:S(2)}, u32[]{:S(2)}) collective-permute-start(f32[2,128,256]{2,1,0:T(8,128)S(1)} %get-tuple-element.4), channel_id=1, source_target_pairs={{0,24},{1,25},{2,26},{3,27},{4,28},{5,29},{6,30},{7,31},{8,0},{9,1... | collective-permute-start | bytes 786440 | tf_op jit(solution)/shard_map/ppermute | solution.py:53
  177.4 25.9 %collective-permute-start.36 = (f32[2,128,256]{2,1,0:T(8,128)S(1)}, f32[2,128,256]{2,1,0:T(8,128)S(1)}, u32[]{:S(2)}, u32[]{:S(2)}) collective-permute-start(f32[2,128,256]{2,1,0:T(8,128)S(1)} %get-tuple-element.4), channel_id=1, source_target_pairs={{0,16},{1,17},{2,18},{3,19},{4,20},{5,21},{6,22},{7,23},{8,24},{9,... | collective-permute-start | bytes 786440 | tf_op jit(solution)/shard_map/ppermute | solution.py:53
  188.9 19.5 %collective-permute-start.37 = (f32[2,128,256]{2,1,0:T(8,128)S(1)}, f32[2,128,256]{2,1,0:T(8,128)S(1)}, u32[]{:S(2)}, u32[]{:S(2)}) collective-permute-start(f32[2,128,256]{2,1,0:T(8,128)S(1)} %get-tuple-element.4), channel_id=1, source_target_pairs={{0,8},{1,9},{2,10},{3,11},{4,12},{5,13},{6,14},{7,15},{8,16},{9,17... | collective-permute-start | bytes 786440 | tf_op jit(solution)/shard_map/ppermute | solution.py:53
  199.9 28.6 %collective-permute-start.67 = (f32[2,64,64]{1,2,0:T(8,128)S(1)}, f32[2,64,64]{1,2,0:T(8,128)S(1)}, u32[]{:S(2)}, u32[]{:S(2)}) collective-permute-start(f32[2,64,64]{1,2,0:T(8,128)S(1)} %fusion.256), channel_id=1, source_target_pairs={{0,64},{32,96},{64,0},{96,32},{1,65},{33,97},{65,1},{97,33},{2,66}... | collective-permute-start | bytes 98312 | tf_op jit(solution)/shard_map/ppermute | solution.py:142
  203.3 12.5 %collective-permute-start.42 = (f32[2,16,256]{2,1,0:T(8,128)S(1)}, f32[2,16,256]{2,1,0:T(8,128)S(1)}, u32[]{:S(2)}, u32[]{:S(2)}) collective-permute-start(f32[2,16,256]{2,1,0:T(8,128)S(1)} %pad_maximum_fusion.26), channel_id=1, source_target_pairs={{96,0},{97,1},{98,2},{99,3},{100,4},{101,5},{102,6},{103,7},{104,8... | collective-permute-start | bytes 98312 | tf_op jit(solution)/shard_map/ppermute | solution.py:53
  208.4 18.3 %collective-permute-start.38 = (f32[2,16,256]{2,1,0:T(8,128)S(1)}, f32[2,16,256]{2,1,0:T(8,128)S(1)}, u32[]{:S(2)}, u32[]{:S(2)}) collective-permute-start(f32[2,16,256]{2,1,0:T(8,128)S(1)} %pad_maximum_fusion.26), channel_id=1, source_target_pairs={{96,32},{97,33},{98,34},{99,35},{100,36},{101,37},{102,38},{103,39... | collective-permute-start | bytes 98312 | tf_op jit(solution)/shard_map/ppermute | solution.py:53
  (51 other events, 253.4 us)

commit v2 on v1

v2 whole, which is shorter than its diff:
```python
import jax
import jax.numpy as jnp
from jax import lax
from jax.sharding import Mesh, PartitionSpec as P

SIDE = 4
AXES = ("z", "y", "x", "c")
HIGH = lax.Precision.HIGH
HIGHEST = lax.Precision.HIGHEST


def dot_nt(left, right, precision):
    return lax.dot_general(left, right, (((1,), (1,)), ((), ())), precision=precision, preferred_element_type=jnp.float32)


def apply_rows(vectors, matrix, precision=HIGH):
    n = vectors.shape[1]
    both = jnp.concatenate([vectors[0], vectors[1]], 0)
    by_real = dot_nt(both, matrix[0], precision)
    by_imag = dot_nt(both, matrix[1], precision)
    return jnp.stack([by_real[:n] - by_imag[n:], by_real[n:] + by_imag[:n]])


def herm_rows(vectors, matrix, precision=HIGHEST):
    n = vectors.shape[1]
    both = jnp.concatenate([vectors[0], vectors[1]], 0)
    by_real = dot_nt(both, matrix[0], precision)
    by_imag = dot_nt(both, matrix[1], precision)
    return jnp.stack([by_real[:n] + by_imag[n:], by_real[n:] - by_imag[:n]])


def combine_rows(coeffs, matrix, precision=HIGHEST):
    n = coeffs.shape[1]
    both = jnp.concatenate([coeffs[0], coeffs[1]], 0)
    by_real = jnp.dot(both, matrix[0], precision=precision, preferred_element_type=jnp.float32)
    by_imag = jnp.dot(both, matrix[1], precision=precision, preferred_element_type=jnp.float32)
    return jnp.stack([by_real[:n] - by_imag[n:], by_real[n:] + by_imag[:n]])


def index_of(z, y, x, c):
    return ((z * SIDE + y) * SIDE + x) * 2 + c


def move(value, target):
    pairs = []
    for z in range(SIDE):
        for y in range(SIDE):
            for x in range(SIDE):
                for c in range(2):
                    there = target(z, y, x, c)
                    if there is not None:
                        pairs.append((index_of(z, y, x, c), index_of(*there)))
    return lax.ppermute(value, AXES, pairs)


def swap(value):
    return lax.ppermute(value, "c", [(0, 1), (1, 0)])


def turn_y(value, offset):
    return move(value, lambda z, y, x, c: (z, (y - offset) % SIDE, x, c))


def hop(value, routes):
    def target(z, y, x, c):
        there = routes.get((z, x))
        return None if there is None else (there[0], y, there[1], c)

    return move(value, target)


def swap_at(value, places):
    return move(value, lambda z, y, x, c: (z, y, x, 1 - c) if (z, x) in places else None)


def local(factor, lower_inverse, upper_inverse, krylov_block, basis):
    z = lax.axis_index("z")
    y = lax.axis_index("y")
    x = lax.axis_index("x")
    c = lax.axis_index("c")
    piece = factor.shape[1]
    half = factor.shape[2]
    tile = 2 * half
    nvec = krylov_block.shape[1]
    nb = basis.shape[1]
    every = range(SIDE)

    def here(*places):
        found = jnp.zeros((), bool)
        for a, b in places:
            found = found | ((z == a) & (x == b))
        return found

    def rotated(value):
        return lax.dynamic_slice_in_dim(jnp.concatenate([value, value], 2), y * piece, tile, 2)

    def in_order(value, other):
        return jnp.concatenate([jnp.where(c == 0, value, other), jnp.where(c == 0, other, value)], 2)

    lower_half = lax.dynamic_slice_in_dim(lower_inverse, c * half, half, 1)
    upper_half = lax.dynamic_slice_in_dim(upper_inverse, c * half, half, 1)

    lead = apply_rows(krylov_block, lower_half)
    gram = herm_rows(basis, basis)
    lead = jnp.concatenate([lead, gram.reshape(2, nvec, half)], 2)
    lead_parts = [turn_y(lead, d) for d in (1, 3, 2)]

    inverse = jnp.where(x == (z + 3) % SIDE, lower_half, upper_half)
    packed = jnp.concatenate([inverse, krylov_block, basis], 1)
    tall = jnp.concatenate([factor] + [turn_y(factor, d) for d in (1, 2, 3)], 1)
    pieces = [packed] + [turn_y(packed, d) for d in (1, 2, 3)]
    rows = jnp.concatenate([p[:, :half] for p in pieces], 2)
    given = jnp.concatenate([p[:, half:half + nvec] for p in pieces], 2)
    basis_all = jnp.stack([p[:, half + nvec:] for p in pieces])
    low = lax.dynamic_index_in_dim(basis_all, (2 * c - y) % SIDE, 0, False)
    high = lax.dynamic_index_in_dim(basis_all, (2 * c + 1 - y) % SIDE, 0, False)
    basis_half = jnp.concatenate([low, high], 2)

    lead = lead + lead_parts[0] + lead_parts[1] + lead_parts[2]
    y0 = lead[:, :, :half]
    gram = lead[:, :, half:].reshape(2, nb, nb)
    shifts = [[(i, (i + d) % SIDE) for i in every] for d in (1, 3, 2)]
    gram_parts = [lax.ppermute(gram, "z", s) for s in shifts]
    gram = gram + gram_parts[0] + gram_parts[1] + gram_parts[2]
    twice = jnp.stack([2.0 * jnp.eye(nb, dtype=jnp.float32), jnp.zeros((nb, nb), jnp.float32)])
    keep = twice - gram
    spread = combine_rows(keep, basis)

    empty = jnp.zeros((2, nvec, half), jnp.float32)
    blank = jnp.zeros((2, nvec, tile), jnp.float32)

    def product(places, vectors, start=None):
        def run(vectors, start, weights):
            out = apply_rows(vectors, weights)
            return out if start is None else start + out

        return lax.cond(here(*places), run, lambda v, s, w: blank, vectors, blank if start is None else start, tall)

    def finish(place, right, acc):
        other = swap_at(acc, (place,))

        def run(right, acc, other, weights):
            return apply_rows(right - (acc + other), weights)

        return lax.cond(here(place), run, lambda r, a, o, w: empty, right, acc, other, rows)

    acc0 = product(((1, 0), (2, 0), (3, 0)), hop(y0, {(0, 0): (1, 0), (0, 1): (2, 0), (0, 3): (3, 0)}))
    y1 = finish((1, 0), given, acc0)
    held0 = hop(acc0, {(2, 0): (2, 1), (3, 0): (3, 2)})
    near1 = hop(y1, {(1, 0): (2, 1)})
    far1 = hop(y1, {(1, 0): (3, 1)})
    y2 = finish((2, 1), given, product(((2, 1),), near1, held0))
    held1 = held0 + hop(product(((3, 1),), far1), {(3, 1): (3, 2)})
    near2 = hop(y2, {(2, 1): (3, 2)})
    y3 = finish((3, 2), given, product(((3, 2),), near2, held1))

    moved = hop(y1 + y2, {(1, 0): (1, 2), (2, 1): (2, 3)})
    back = jnp.where(z == 0, y0, moved)
    solved = rotated(in_order(back, swap_at(back, ((0, 1), (1, 2), (2, 3)))))

    y3 = hop(y3, {(3, 2): (3, 3)})
    y3_other = swap_at(y3, ((3, 3),))

    def last_tile(value, other, weights):
        return apply_rows(rotated(in_order(value, other)), weights)

    x3 = lax.cond(here((3, 3)), last_tile, lambda v, o, w: empty, y3, y3_other, rows)
    near3 = hop(x3, {(3, 3): (2, 3)})
    x2 = finish((2, 3), solved, product(((2, 3),), near3))
    far3 = hop(near3 + x3, {(3, 3): (0, 3), (2, 3): (1, 3)})
    held2 = hop(product(((0, 3), (1, 3)), far3), {(1, 3): (1, 2), (0, 3): (0, 1)})
    near4 = hop(x2, {(2, 3): (1, 2)})
    far4 = hop(x2, {(2, 3): (0, 2)})
    x1 = finish((1, 2), solved, product(((1, 2),), near4, held2))
    held3 = held2 + hop(product(((0, 2),), far4), {(0, 2): (0, 1)})
    near5 = hop(x1, {(1, 2): (0, 1)})
    x0 = finish((0, 1), solved, product(((0, 1),), near5, held3))

    found = x0 + x1 + x2 + x3
    share = herm_rows(found, basis_half)
    both = jnp.concatenate([found, share], 2)
    other = swap(both)
    share = share + other[:, :, half:]
    chosen = jnp.where((y < 2) == (c == 0), found, other[:, :, :half])
    mine = jnp.where(y % 2 == 0, chosen[:, :, :piece], chosen[:, :, piece:])
    message = jnp.concatenate([mine, share], 2)
    spreadout = jnp.broadcast_to(message[None], (SIDE * SIDE,) + message.shape)
    received = lax.all_to_all(spreadout, ("z", "x"), 0, 0)
    first = jnp.sum(received[:, :, :, piece:], 0)
    same = lax.dynamic_slice_in_dim(received[:, :, :, :piece], z * SIDE, SIDE, 0)
    own_rows = jnp.sum(same, 0)
    projected = own_rows - combine_rows(first, spread)
    coeffs = combine_rows(first, keep)
    return projected, jnp.swapaxes(coeffs, 1, 2)


def solution(mesh):
    split = Mesh(mesh.devices.reshape(SIDE, SIDE, SIDE, 2), AXES)
    row, col = ("z", "y"), ("x", "c")
    in_specs = (P(None, row, col), P(None, None, row), P(None, None, row), P(None, None, row), P(None, None, row))
    out_specs = (P(None, None, row), P())
    return jax.shard_map(local, mesh=split, in_specs=in_specs, out_specs=out_specs, check_vma=False)
```

time: 268 us -> 133 us (0.50)
  starting transfers between devices: 212 us -> 48.2 us
  waiting for transfers between devices: 30.7 us -> 66.7 us
  matrix products: 17.1 us -> 3.6 us
  local copies, waits for them, and re-layouts: 1.13 us -> 8.58 us
    ppermute x51 -> x32, starting transfers between devices: 186 us -> 42.4 us  [move(): return lax.ppermute(value, AXES, pairs)]
    ppermute x51 -> x32, waiting for transfers between devices: 26.5 us -> 55.7 us  [move(): return lax.ppermute(value, AXES, pairs)]
    dot_general x58 -> x10, matrix products: 15.8 us -> 2.63 us  [dot_nt(): lax.dot_general(left, right, (((1,), (1,)), ((), ())), precision=precisio...]
    ppermute x3, starting transfers between devices: 12.3 us -> 2.12 us  [local(): gram_parts = [lax.ppermute(gram, 'z', s) for s in shifts]]
    ppermute x11 -> x1, starting transfers between devices: 10.4 us -> 0.24 us  [swap(): return lax.ppermute(value, 'c', [(0, 1), (1, 0)])]
    all_to_all x0 -> x1, waiting for transfers between devices: none -> 9.93 us  [local(): received = lax.all_to_all(spreadout, ('z', 'x'), 0, 0)]
    all_to_all x0 -> x1, starting transfers between devices: none -> 3.47 us  [local(): received = lax.all_to_all(spreadout, ('z', 'x'), 0, 0)]
    ppermute x3 -> x0, starting transfers between devices: 3.3 us -> none  [local(): parts = [lax.ppermute(early, 'z', s) for s in shifts]]
  transfers between devices with their start and end apart: 68 -> 37, of which waited for: 15 -> 7; matrix products, arithmetic and copies ran while one was open for 6% -> 2% of each run, Pallas kernels for 0% -> 0%
where the time goes in v2:
time: 133 us; the launch traced here: 131 us
  waiting for transfers between devices  66.7 us (50%)
  starting transfers between devices  48.2 us (36%)
  local copies, waits for them, and re-layouts  8.58 us (6%)
  matrix products  3.6 us (3%)
  between operations  1.75 us (1%)
  other arithmetic  1.74 us (1%)
    ppermute x32, waiting for transfers between devices, move(): return lax.ppermute(value, AXES, pairs)  55.7 us
    ppermute x32, starting transfers between devices, move(): return lax.ppermute(value, AXES, pairs)  42.4 us
    all_to_all x1, waiting for transfers between devices, local(): received = lax.all_to_all(spreadout, ('z', 'x'), 0, 0)  9.93 us
    unnamed x21, local copies, waits for them, and re-layouts  3.97 us
    all_to_all x1, starting transfers between devices, local(): received = lax.all_to_all(spreadout, ('z', 'x'), 0, 0)  3.47 us
  transfers between devices with their start and end apart: 37, of which 7 were waited for; matrix products, arithmetic and copies ran while one was open for 2% of the time, Pallas kernels for 0%

profile of v2, /device:TPU:2, one launch (start us, length us, event | category | flops | bytes accessed | tf_op | source)
XLA Modules:
  0.0 130.9 jit_solution(3297733167339813023)
XLA Ops:
  3.5 3.3 %collective-permute-start.2 = (f32[2,16,512]{2,1,0:T(8,128)S(1)}, f32[2,16,512]{2,1,0:T(8,128)S(1)}, u32[]{:S(2)}, u32[]{:S(2)}) collective-permute-start(f32[2,16,512]{2,1,0:T(8,128)S(1)} %maximum_maximum_fusion), channel_id=1, source_target_pairs={{0,16},{1,17},{2,18},{3,19},{4,20},{5,21},{6,22},{7,23},{8,24},{9,... | collective-permute-start | bytes 196616 | tf_op jit(solution)/shard_map/ppermute | solution.py:53
  7.4 2.6 %collective-permute-start = (f32[2,16,512]{2,1,0:T(8,128)S(1)}, f32[2,16,512]{2,1,0:T(8,128)S(1)}, u32[]{:S(2)}, u32[]{:S(2)}) collective-permute-start(f32[2,16,512]{2,1,0:T(8,128)S(1)} %maximum_maximum_fusion), channel_id=1, source_target_pairs={{0,24},{1,25},{2,26},{3,27},{4,28},{5,29},{6,30},{7,31},{8,0},{9,1... | collective-permute-start | bytes 196616 | tf_op jit(solution)/shard_map/ppermute | solution.py:53
  11.0 0.8 copy-done.6
  11.8 2.4 %collective-permute-start.4 = (f32[2,128,256]{2,1,0:T(8,128)S(1)}, f32[2,128,256]{2,1,0:T(8,128)S(1)}, u32[]{:S(2)}, u32[]{:S(2)}) collective-permute-start(f32[2,128,256]{2,1,0:T(8,128)S(1)} %copy-done.6), channel_id=1, source_target_pairs={{0,24},{1,25},{2,26},{3,27},{4,28},{5,29},{6,30},{7,31},{8,0},{9,1... | collective-permute-start | bytes 786440 | tf_op jit(solution)/shard_map/ppermute | solution.py:53
  14.3 3.5 %collective-permute-start.5 = (f32[2,128,256]{2,1,0:T(8,128)S(1)}, f32[2,128,256]{2,1,0:T(8,128)S(1)}, u32[]{:S(2)}, u32[]{:S(2)}) collective-permute-start(f32[2,128,256]{2,1,0:T(8,128)S(1)} %copy-done.6), channel_id=1, source_target_pairs={{0,16},{1,17},{2,18},{3,19},{4,20},{5,21},{6,22},{7,23},{8,24},{9,... | collective-permute-start | bytes 786440 | tf_op jit(solution)/shard_map/ppermute | solution.py:53
  17.9 12.7 %collective-permute-done.4 = f32[2,128,256]{2,1,0:T(8,128)S(1)} collective-permute-done((f32[2,128,256]{2,1,0:T(8,128)S(1)}, f32[2,128,256]{2,1,0:T(8,128)S(1)}, u32[]{:S(2)}, u32[]{:S(2)}) %collective-permute-start.4) | collective-permute-done | bytes 262176 | tf_op jit(solution)/shard_map/ppermute | solution.py:53
  30.6 4.2 %collective-permute-start.9 = (f32[2,336,128]{2,1,0:T(8,128)S(1)}, f32[2,336,128]{2,1,0:T(8,128)S(1)}, u32[]{:S(2)}, u32[]{:S(2)}) collective-permute-start(f32[2,336,128]{2,1,0:T(8,128)S(1)} %pad_maximum_fusion.61), channel_id=1, source_target_pairs={{0,24},{1,25},{2,26},{3,27},{4,28},{5,29},{6,30},{7,31},{8,0},{9,1... | collective-permute-start | bytes 1032200 | tf_op jit(solution)/shard_map/ppermute | solution.py:53
  34.8 5.8 %collective-permute-start.3 = (f32[2,16,256]{2,1,0:T(8,128)S(1)}, f32[2,16,256]{2,1,0:T(8,128)S(1)}, u32[]{:S(2)}, u32[]{:S(2)}) collective-permute-start(f32[2,16,256]{2,1,0:T(8,128)S(1)} %slice.698), channel_id=1, source_target_pairs={{0,32},{1,33},{2,64},{3,65},{6,96},{7,97},{8,40},{9,41},{10,72},{1... | collective-permute-start | bytes 98312 | tf_op jit(solution)/shard_map/ppermute | solution.py:53
  40.7 1.5 %collective-permute-done.3 = f32[2,16,256]{2,1,0:T(8,128)S(1)} collective-permute-done((f32[2,16,256]{2,1,0:T(8,128)S(1)}, f32[2,16,256]{2,1,0:T(8,128)S(1)}, u32[]{:S(2)}, u32[]{:S(2)}) %collective-permute-start.3) | collective-permute-done | bytes 32800 | tf_op jit(solution)/shard_map/ppermute | solution.py:53
  42.8 1.3 collective-permute-start.7
  46.3 0.9 slice-done
  54.4 1.9 %collective-permute-start.25 = (f32[2,16,256]{2,1,0:T(8,128)S(1)}, f32[2,16,256]{2,1,0:T(8,128)S(1)}, u32[]{:S(2)}, u32[]{:S(2)}) collective-permute-start(f32[2,16,256]{2,1,0:T(8,128)S(1)} %get-tuple-element.282), channel_id=1, source_target_pairs={{2,3},{3,2},{10,11},{11,10},{18,19},{19,18},{26,27},{27,26},{36,37... | collective-permute-start | bytes 98312 | tf_op jit(solution)/shard_map/ppermute | solution.py:53
  59.2 1.3 collective-permute-start.22
  61.9 31.7 %collective-permute-done.22 = f32[2,16,512]{2,1,0:T(8,128)S(1)} collective-permute-done((f32[2,16,512]{2,1,0:T(8,128)S(1)}, f32[2,16,512]{2,1,0:T(8,128)S(1)}, u32[]{:S(2)}, u32[]{:S(2)}) %collective-permute-start.22) | collective-permute-done | bytes 65568 | tf_op jit(solution)/shard_map/ppermute | solution.py:53
  94.5 2.0 %collective-permute-start.33 = (f32[2,64,64]{2,1,0:T(8,128)S(1)}, f32[2,64,64]{2,1,0:T(8,128)S(1)}, u32[]{:S(2)}, u32[]{:S(2)}) collective-permute-start(f32[2,64,64]{2,1,0:T(8,128)S(1)} %reshape.27), channel_id=1, source_target_pairs={{0,32},{32,64},{64,96},{96,0},{1,33},{33,65},{65,97},{97,1},{2,34}... | collective-permute-start | bytes 98312 | tf_op jit(solution)/shard_map/ppermute | solution.py:123
  96.6 1.3 collective-permute-start.27
  97.9 1.3 collective-permute-start.30
  99.2 8.6 %collective-permute-done.27 = f32[2,16,512]{2,1,0:T(8,128)S(1)} collective-permute-done((f32[2,16,512]{2,1,0:T(8,128)S(1)}, f32[2,16,512]{2,1,0:T(8,128)S(1)}, u32[]{:S(2)}, u32[]{:S(2)}) %collective-permute-start.27) | collective-permute-done | bytes 65568 | tf_op jit(solution)/shard_map/ppermute | solution.py:53
  108.6 1.9 %collective-permute-start.31 = (f32[2,16,512]{2,1,0:T(8,128)S(1)}, f32[2,16,512]{2,1,0:T(8,128)S(1)}, u32[]{:S(2)}, u32[]{:S(2)}) collective-permute-start(f32[2,16,512]{2,1,0:T(8,128)S(1)} %get-tuple-element.317), channel_id=1, source_target_pairs={{2,3},{3,2},{10,11},{11,10},{18,19},{19,18},{26,27},{27,26}} | collective-permute-start | bytes 196616 | tf_op jit(solution)/shard_map/ppermute | solution.py:53
  110.6 1.2 collective-permute-done.31
  113.2 1.1 collective-permute-done.32
  114.3 0.9 broadcast_in_dim.54
  115.2 3.5 %all-to-all-start = ((f32[16,2,16,192]{3,2,1,0:T(8,128)}), f32[16,2,16,192]{3,2,1,0:T(8,128)S(1)}, u32[]{:S(2)}, u32[]{:S(2)}) async-start(f32[16,2,16,192]{3,2,1,0:T(8,128)} %broadcast_in_dim.54), calls=%async_computation | async-start | bytes 1048576 | tf_op jit(solution)/shard_map/all_to_all | solution.py:188
  119.0 9.9 %all-to-all-done = f32[16,2,16,192]{3,2,1,0:T(8,128)S(1)} async-done(((f32[16,2,16,192]{3,2,1,0:T(8,128)}), f32[16,2,16,192]{3,2,1,0:T(8,128)S(1)}, u32[]{:S(2)}, u32[]{:S(2)}) %all-to-all-start) | async-done | bytes 393248 | tf_op jit(solution)/shard_map/all_to_all | solution.py:188
  (181 shorter events, 25.9 us)
Async XLA Ops:
  3.5 10.7 %collective-permute-start.2 = (f32[2,16,512]{2,1,0:T(8,128)S(1)}, f32[2,16,512]{2,1,0:T(8,128)S(1)}, u32[]{:S(2)}, u32[]{:S(2)}) collective-permute-start(f32[2,16,512]{2,1,0:T(8,128)S(1)} %maximum_maximum_fusion), channel_id=1, source_target_pairs={{0,16},{1,17},{2,18},{3,19},{4,20},{5,21},{6,22},{7,23},{8,24},{9,... | collective-permute-start | bytes 196616 | tf_op jit(solution)/shard_map/ppermute | solution.py:53
  6.8 7.6 %collective-permute-start.1 = (f32[2,16,512]{2,1,0:T(8,128)S(1)}, f32[2,16,512]{2,1,0:T(8,128)S(1)}, u32[]{:S(2)}, u32[]{:S(2)}) collective-permute-start(f32[2,16,512]{2,1,0:T(8,128)S(1)} %maximum_maximum_fusion), channel_id=1, source_target_pairs={{0,8},{1,9},{2,10},{3,11},{4,12},{5,13},{6,14},{7,15},{8,16},{9,17... | collective-permute-start | bytes 196616 | tf_op jit(solution)/shard_map/ppermute | solution.py:53
  7.4 10.4 %collective-permute-start = (f32[2,16,512]{2,1,0:T(8,128)S(1)}, f32[2,16,512]{2,1,0:T(8,128)S(1)}, u32[]{:S(2)}, u32[]{:S(2)}) collective-permute-start(f32[2,16,512]{2,1,0:T(8,128)S(1)} %maximum_maximum_fusion), channel_id=1, source_target_pairs={{0,24},{1,25},{2,26},{3,27},{4,28},{5,29},{6,30},{7,31},{8,0},{9,1... | collective-permute-start | bytes 196616 | tf_op jit(solution)/shard_map/ppermute | solution.py:53
  10.9 33.9 %collective-permute-start.11 = (f32[2,336,128]{2,1,0:T(8,128)S(1)}, f32[2,336,128]{2,1,0:T(8,128)S(1)}, u32[]{:S(2)}, u32[]{:S(2)}) collective-permute-start(f32[2,336,128]{2,1,0:T(8,128)S(1)} %pad_maximum_fusion.61), channel_id=1, source_target_pairs={{0,8},{1,9},{2,10},{3,11},{4,12},{5,13},{6,14},{7,15},{8,16},{9,17... | collective-permute-start | bytes 1032200 | tf_op jit(solution)/shard_map/ppermute | solution.py:53
  11.8 18.8 %collective-permute-start.4 = (f32[2,128,256]{2,1,0:T(8,128)S(1)}, f32[2,128,256]{2,1,0:T(8,128)S(1)}, u32[]{:S(2)}, u32[]{:S(2)}) collective-permute-start(f32[2,128,256]{2,1,0:T(8,128)S(1)} %copy-done.6), channel_id=1, source_target_pairs={{0,24},{1,25},{2,26},{3,27},{4,28},{5,29},{6,30},{7,31},{8,0},{9,1... | collective-permute-start | bytes 786440 | tf_op jit(solution)/shard_map/ppermute | solution.py:53
  14.2 31.2 %collective-permute-start.10 = (f32[2,336,128]{2,1,0:T(8,128)S(1)}, f32[2,336,128]{2,1,0:T(8,128)S(1)}, u32[]{:S(2)}, u32[]{:S(2)}) collective-permute-start(f32[2,336,128]{2,1,0:T(8,128)S(1)} %pad_maximum_fusion.61), channel_id=1, source_target_pairs={{0,16},{1,17},{2,18},{3,19},{4,20},{5,21},{6,22},{7,23},{8,24},{9,... | collective-permute-start | bytes 1032200 | tf_op jit(solution)/shard_map/ppermute | solution.py:53
  14.3 20.5 %collective-permute-start.5 = (f32[2,128,256]{2,1,0:T(8,128)S(1)}, f32[2,128,256]{2,1,0:T(8,128)S(1)}, u32[]{:S(2)}, u32[]{:S(2)}) collective-permute-start(f32[2,128,256]{2,1,0:T(8,128)S(1)} %copy-done.6), channel_id=1, source_target_pairs={{0,16},{1,17},{2,18},{3,19},{4,20},{5,21},{6,22},{7,23},{8,24},{9,... | collective-permute-start | bytes 786440 | tf_op jit(solution)/shard_map/ppermute | solution.py:53
  17.9 22.8 %collective-permute-start.6 = (f32[2,128,256]{2,1,0:T(8,128)S(1)}, f32[2,128,256]{2,1,0:T(8,128)S(1)}, u32[]{:S(2)}, u32[]{:S(2)}) collective-permute-start(f32[2,128,256]{2,1,0:T(8,128)S(1)} %copy-done.6), channel_id=1, source_target_pairs={{0,8},{1,9},{2,10},{3,11},{4,12},{5,13},{6,14},{7,15},{8,16},{9,17... | collective-permute-start | bytes 786440 | tf_op jit(solution)/shard_map/ppermute | solution.py:53
  30.6 15.6 %collective-permute-start.9 = (f32[2,336,128]{2,1,0:T(8,128)S(1)}, f32[2,336,128]{2,1,0:T(8,128)S(1)}, u32[]{:S(2)}, u32[]{:S(2)}) collective-permute-start(f32[2,336,128]{2,1,0:T(8,128)S(1)} %pad_maximum_fusion.61), channel_id=1, source_target_pairs={{0,24},{1,25},{2,26},{3,27},{4,28},{5,29},{6,30},{7,31},{8,0},{9,1... | collective-permute-start | bytes 1032200 | tf_op jit(solution)/shard_map/ppermute | solution.py:53
  34.8 7.3 %collective-permute-start.3 = (f32[2,16,256]{2,1,0:T(8,128)S(1)}, f32[2,16,256]{2,1,0:T(8,128)S(1)}, u32[]{:S(2)}, u32[]{:S(2)}) collective-permute-start(f32[2,16,256]{2,1,0:T(8,128)S(1)} %slice.698), channel_id=1, source_target_pairs={{0,32},{1,33},{2,64},{3,65},{6,96},{7,97},{8,40},{9,41},{10,72},{1... | collective-permute-start | bytes 98312 | tf_op jit(solution)/shard_map/ppermute | solution.py:53
  42.8 6.0 %collective-permute-start.7 = (f32[2,16,512]{2,1,0:T(8,128)}, f32[2,16,512]{2,1,0:T(8,128)}, u32[]{:S(2)}, u32[]{:S(2)}) collective-permute-start(f32[2,16,512]{2,1,0:T(8,128)} %get-tuple-element.303), channel_id=1, source_target_pairs={{64,66},{65,67},{72,74},{73,75},{80,82},{81,83},{88,90},{89,91},{9... | collective-permute-start | bytes 196616 | tf_op jit(solution)/shard_map/ppermute | solution.py:53
  44.1 4.0 %collective-permute-start.8 = (f32[2,16,512]{2,1,0:T(8,128)}, f32[2,16,512]{2,1,0:T(8,128)S(1)}, u32[]{:S(2)}, u32[]{:S(2)}) collective-permute-start(f32[2,16,512]{2,1,0:T(8,128)} %get-tuple-element.303), channel_id=1, source_target_pairs={{32,33},{33,32},{40,41},{41,40},{48,49},{49,48},{56,57},{57,56}} | collective-permute-start | bytes 196616 | tf_op jit(solution)/shard_map/ppermute | solution.py:53
  54.4 3.4 %collective-permute-start.25 = (f32[2,16,256]{2,1,0:T(8,128)S(1)}, f32[2,16,256]{2,1,0:T(8,128)S(1)}, u32[]{:S(2)}, u32[]{:S(2)}) collective-permute-start(f32[2,16,256]{2,1,0:T(8,128)S(1)} %get-tuple-element.282), channel_id=1, source_target_pairs={{2,3},{3,2},{10,11},{11,10},{18,19},{19,18},{26,27},{27,26},{36,37... | collective-permute-start | bytes 98312 | tf_op jit(solution)/shard_map/ppermute | solution.py:53
  59.2 34.4 %collective-permute-start.22 = (f32[2,16,512]{2,1,0:T(8,128)S(1)}, f32[2,16,512]{2,1,0:T(8,128)S(1)}, u32[]{:S(2)}, u32[]{:S(2)}) collective-permute-start(f32[2,16,512]{2,1,0:T(8,128)S(1)} %get-tuple-element.311), channel_id=1, source_target_pairs={{6,2},{7,3},{14,10},{15,11},{22,18},{23,19},{30,26},{31,27},{38,36... | collective-permute-start | bytes 196616 | tf_op jit(solution)/shard_map/ppermute | solution.py:53
  60.6 33.0 %collective-permute-start.28 = (f32[2,16,256]{2,1,0:T(8,128)S(1)}, f32[2,16,256]{2,1,0:T(8,128)S(1)}, u32[]{:S(2)}, u32[]{:S(2)}) collective-permute-start(f32[2,16,256]{2,1,0:T(8,128)S(1)} %get-tuple-element.313), channel_id=1, source_target_pairs={{70,36},{71,37},{78,44},{79,45},{86,52},{87,53},{94,60},{95,61}} | collective-permute-start | bytes 98312 | tf_op jit(solution)/shard_map/ppermute | solution.py:53
  61.3 35.3 %collective-permute-start.26 = (f32[2,16,256]{2,1,0:T(8,128)S(1)}, f32[2,16,256]{2,1,0:T(8,128)S(1)}, u32[]{:S(2)}, u32[]{:S(2)}) collective-permute-start(f32[2,16,256]{2,1,0:T(8,128)S(1)} %get-tuple-element.313), channel_id=1, source_target_pairs={{70,4},{71,5},{78,12},{79,13},{86,20},{87,21},{94,28},{95,29}} | collective-permute-start | bytes 98312 | tf_op jit(solution)/shard_map/ppermute | solution.py:53
  93.6 4.2 %collective-permute-start.29 = (f32[2,16,512]{2,1,0:T(8,128)S(1)}, f32[2,16,512]{2,1,0:T(8,128)S(1)}, u32[]{:S(2)}, u32[]{:S(2)}) collective-permute-start(f32[2,16,512]{2,1,0:T(8,128)S(1)} %get-tuple-element.315), channel_id=1, source_target_pairs={{36,37},{37,36},{44,45},{45,44},{52,53},{53,52},{60,61},{61,60}} | collective-permute-start | bytes 196616 | tf_op jit(solution)/shard_map/ppermute | solution.py:53
  94.4 16.1 %collective-permute-start.35 = (f32[2,64,64]{2,1,0:T(8,128)S(1)}, f32[2,64,64]{2,1,0:T(8,128)S(1)}, u32[]{:S(2)}, u32[]{:S(2)}) collective-permute-start(f32[2,64,64]{2,1,0:T(8,128)S(1)} %reshape.27), channel_id=1, source_target_pairs={{0,64},{32,96},{64,0},{96,32},{1,65},{33,97},{65,1},{97,33},{2,66}... | collective-permute-start | bytes 98312 | tf_op jit(solution)/shard_map/ppermute | solution.py:123
  94.4 16.1 %collective-permute-start.34 = (f32[2,64,64]{2,1,0:T(8,128)S(1)}, f32[2,64,64]{2,1,0:T(8,128)S(1)}, u32[]{:S(2)}, u32[]{:S(2)}) collective-permute-start(f32[2,64,64]{2,1,0:T(8,128)S(1)} %reshape.27), channel_id=1, source_target_pairs={{0,96},{32,0},{64,32},{96,64},{1,97},{33,1},{65,33},{97,65},{2,98}... | collective-permute-start | bytes 98312 | tf_op jit(solution)/shard_map/ppermute | solution.py:123
  94.5 16.0 %collective-permute-start.33 = (f32[2,64,64]{2,1,0:T(8,128)S(1)}, f32[2,64,64]{2,1,0:T(8,128)S(1)}, u32[]{:S(2)}, u32[]{:S(2)}) collective-permute-start(f32[2,64,64]{2,1,0:T(8,128)S(1)} %reshape.27), channel_id=1, source_target_pairs={{0,32},{32,64},{64,96},{96,0},{1,33},{33,65},{65,97},{97,1},{2,34}... | collective-permute-start | bytes 98312 | tf_op jit(solution)/shard_map/ppermute | solution.py:123
  96.6 11.3 %collective-permute-start.27 = (f32[2,16,512]{2,1,0:T(8,128)S(1)}, f32[2,16,512]{2,1,0:T(8,128)S(1)}, u32[]{:S(2)}, u32[]{:S(2)}) collective-permute-start(f32[2,16,512]{2,1,0:T(8,128)S(1)} %get-tuple-element.314), channel_id=1, source_target_pairs={{4,2},{5,3},{12,10},{13,11},{20,18},{21,19},{28,26},{29,27}} | collective-permute-start | bytes 196616 | tf_op jit(solution)/shard_map/ppermute | solution.py:53
  97.9 9.9 %collective-permute-start.30 = (f32[2,16,256]{2,1,0:T(8,128)S(1)}, f32[2,16,256]{2,1,0:T(8,128)S(1)}, u32[]{:S(2)}, u32[]{:S(2)}) collective-permute-start(f32[2,16,256]{2,1,0:T(8,128)S(1)} %get-tuple-element.316), channel_id=1, source_target_pairs={{36,2},{37,3},{44,10},{45,11},{52,18},{53,19},{60,26},{61,27}} | collective-permute-start | bytes 98312 | tf_op jit(solution)/shard_map/ppermute | solution.py:53
  108.6 3.1 %collective-permute-start.31 = (f32[2,16,512]{2,1,0:T(8,128)S(1)}, f32[2,16,512]{2,1,0:T(8,128)S(1)}, u32[]{:S(2)}, u32[]{:S(2)}) collective-permute-start(f32[2,16,512]{2,1,0:T(8,128)S(1)} %get-tuple-element.317), channel_id=1, source_target_pairs={{2,3},{3,2},{10,11},{11,10},{18,19},{19,18},{26,27},{27,26}} | collective-permute-start | bytes 196616 | tf_op jit(solution)/shard_map/ppermute | solution.py:53
  115.2 13.8 %all-to-all-start = ((f32[16,2,16,192]{3,2,1,0:T(8,128)}), f32[16,2,16,192]{3,2,1,0:T(8,128)S(1)}, u32[]{:S(2)}, u32[]{:S(2)}) async-start(f32[16,2,16,192]{3,2,1,0:T(8,128)} %broadcast_in_dim.54), calls=%async_computation | async-start | bytes 1048576 | tf_op jit(solution)/shard_map/all_to_all | solution.py:188
  (26 other events, 41.6 us)

commit v3 on v2

--- a/solution.py
+++ b/solution.py
@@ -62,15 +62,14 @@
 
 
 def hop(value, routes):
+    paired = dict(routes)
+    paired.update({there: start for start, there in routes.items()})
+
     def target(z, y, x, c):
-        there = routes.get((z, x))
-        return None if there is None else (there[0], y, there[1], c)
+        there = paired.get((z, x))
+        return (z, y, x, 1 - c) if there is None else (there[0], y, there[1], c)
 
     return move(value, target)
-
-
-def swap_at(value, places):
-    return move(value, lambda z, y, x, c: (z, y, x, 1 - c) if (z, x) in places else None)
 
 
 def local(factor, lower_inverse, upper_inverse, krylov_block, basis):
@@ -106,12 +105,15 @@
     lead_parts = [turn_y(lead, d) for d in (1, 3, 2)]
 
     inverse = jnp.where(x == (z + 3) % SIDE, lower_half, upper_half)
-    packed = jnp.concatenate([inverse, krylov_block, basis], 1)
-    tall = jnp.concatenate([factor] + [turn_y(factor, d) for d in (1, 2, 3)], 1)
-    pieces = [packed] + [turn_y(packed, d) for d in (1, 2, 3)]
-    rows = jnp.concatenate([p[:, :half] for p in pieces], 2)
-    given = jnp.concatenate([p[:, half:half + nvec] for p in pieces], 2)
-    basis_all = jnp.stack([p[:, half + nvec:] for p in pieces])
+    left, right = factor[:, :, :piece], factor[:, :, piece:]
+    packed = jnp.concatenate([left, right, inverse, krylov_block, basis], 1)
+    pieces = [packed] + [turn_y(packed, d) for d in (1, 3, 2)]
+    pieces = [pieces[0], pieces[1], pieces[3], pieces[2]]
+    tall = jnp.concatenate([jnp.concatenate([p[:, :piece], p[:, piece:half]], 2) for p in pieces], 1)
+    top = half + half
+    rows = jnp.concatenate([p[:, half:top] for p in pieces], 2)
+    given = jnp.concatenate([p[:, top:top + nvec] for p in pieces], 2)
+    basis_all = jnp.stack([p[:, top + nvec:] for p in pieces])
     low = lax.dynamic_index_in_dim(basis_all, (2 * c - y) % SIDE, 0, False)
     high = lax.dynamic_index_in_dim(basis_all, (2 * c + 1 - y) % SIDE, 0, False)
     basis_half = jnp.concatenate([low, high], 2)
@@ -125,56 +127,49 @@
     twice = jnp.stack([2.0 * jnp.eye(nb, dtype=jnp.float32), jnp.zeros((nb, nb), jnp.float32)])
     keep = twice - gram
     spread = combine_rows(keep, basis)
+    y0, spread, keep = lax.optimization_barrier((y0, spread, keep))
 
     empty = jnp.zeros((2, nvec, half), jnp.float32)
     blank = jnp.zeros((2, nvec, tile), jnp.float32)
 
-    def product(places, vectors, start=None):
-        def run(vectors, start, weights):
-            out = apply_rows(vectors, weights)
-            return out if start is None else start + out
-
-        return lax.cond(here(*places), run, lambda v, s, w: blank, vectors, blank if start is None else start, tall)
+    def product(places, vectors):
+        return lax.cond(here(*places), apply_rows, lambda v, w: blank, vectors, tall)
 
     def finish(place, right, acc):
-        other = swap_at(acc, (place,))
+        other = swap(acc)
 
         def run(right, acc, other, weights):
             return apply_rows(right - (acc + other), weights)
 
         return lax.cond(here(place), run, lambda r, a, o, w: empty, right, acc, other, rows)
 
+    def widen(value):
+        return jnp.concatenate([value, value], 2)
+
     acc0 = product(((1, 0), (2, 0), (3, 0)), hop(y0, {(0, 0): (1, 0), (0, 1): (2, 0), (0, 3): (3, 0)}))
     y1 = finish((1, 0), given, acc0)
-    held0 = hop(acc0, {(2, 0): (2, 1), (3, 0): (3, 2)})
     near1 = hop(y1, {(1, 0): (2, 1)})
-    far1 = hop(y1, {(1, 0): (3, 1)})
-    y2 = finish((2, 1), given, product(((2, 1),), near1, held0))
-    held1 = held0 + hop(product(((3, 1),), far1), {(3, 1): (3, 2)})
+    mixed1 = hop(jnp.where(z == 1, widen(y1), acc0), {(1, 0): (3, 1), (2, 0): (2, 1), (3, 0): (3, 2)})
+    y2 = finish((2, 1), given, mixed1 + product(((2, 1),), near1))
     near2 = hop(y2, {(2, 1): (3, 2)})
-    y3 = finish((3, 2), given, product(((3, 2),), near2, held1))
+    held1 = mixed1 + hop(product(((3, 1),), mixed1[:, :, :half]), {(3, 1): (3, 2)})
+    y3 = finish((3, 2), given, held1 + product(((3, 2),), near2))
 
-    moved = hop(y1 + y2, {(1, 0): (1, 2), (2, 1): (2, 3)})
+    moved = hop(y1 + y2 + y3, {(1, 0): (1, 2), (2, 1): (2, 3), (3, 2): (3, 3)})
     back = jnp.where(z == 0, y0, moved)
-    solved = rotated(in_order(back, swap_at(back, ((0, 1), (1, 2), (2, 3)))))
+    solved = rotated(in_order(back, swap(back)))
 
-    y3 = hop(y3, {(3, 2): (3, 3)})
-    y3_other = swap_at(y3, ((3, 3),))
-
-    def last_tile(value, other, weights):
-        return apply_rows(rotated(in_order(value, other)), weights)
-
-    x3 = lax.cond(here((3, 3)), last_tile, lambda v, o, w: empty, y3, y3_other, rows)
+    x3 = lax.cond(here((3, 3)), apply_rows, lambda v, w: empty, solved, rows)
     near3 = hop(x3, {(3, 3): (2, 3)})
     x2 = finish((2, 3), solved, product(((2, 3),), near3))
-    far3 = hop(near3 + x3, {(3, 3): (0, 3), (2, 3): (1, 3)})
-    held2 = hop(product(((0, 3), (1, 3)), far3), {(1, 3): (1, 2), (0, 3): (0, 1)})
+    far3 = hop(jnp.where(z == 3, x3, near3), {(3, 3): (0, 3), (2, 3): (1, 3)})
     near4 = hop(x2, {(2, 3): (1, 2)})
-    far4 = hop(x2, {(2, 3): (0, 2)})
-    x1 = finish((1, 2), solved, product(((1, 2),), near4, held2))
-    held3 = held2 + hop(product(((0, 2),), far4), {(0, 2): (0, 1)})
+    side = product(((0, 3), (1, 3)), far3)
+    mixed3 = hop(jnp.where(z == 2, widen(x2), side), {(2, 3): (0, 2), (1, 3): (1, 2), (0, 3): (0, 1)})
+    x1 = finish((1, 2), solved, mixed3 + product(((1, 2),), near4))
     near5 = hop(x1, {(1, 2): (0, 1)})
-    x0 = finish((0, 1), solved, product(((0, 1),), near5, held3))
+    held3 = mixed3 + hop(product(((0, 2),), mixed3[:, :, :half]), {(0, 2): (0, 1)})
+    x0 = finish((0, 1), solved, held3 + product(((0, 1),), near5))
 
     found = x0 + x1 + x2 + x3
     share = herm_rows(found, basis_half)

time: 133 us -> 113 us (0.85)
  waiting for transfers between devices: 66.7 us -> 40.7 us
  starting transfers between devices: 48.2 us -> 54.8 us
  local copies, waits for them, and re-layouts: 8.58 us -> 6.94 us
    ppermute x32 -> x18, waiting for transfers between devices: 55.7 us -> 23.3 us  [move(): return lax.ppermute(value, AXES, pairs)]
    ppermute x1 -> x8, waiting for transfers between devices: 1.07 us -> 5.58 us  [swap(): return lax.ppermute(value, 'c', [(0, 1), (1, 0)])]
    ppermute x3, starting transfers between devices: 2.12 us -> 5.93 us  [local(): gram_parts = [lax.ppermute(gram, 'z', s) for s in shifts]]
    unnamed x21 -> x27, local copies, waits for them, and re-layouts: 3.97 us -> 2.11 us
    ppermute x3, waiting for transfers between devices: 0.01 us -> 1.4 us  [local(): gram_parts = [lax.ppermute(gram, 'z', s) for s in shifts]]
    ppermute x1 -> x8, starting transfers between devices: 0.24 us -> 1.57 us  [swap(): return lax.ppermute(value, 'c', [(0, 1), (1, 0)])]
    ppermute x32 -> x18, starting transfers between devices: 42.4 us -> 42.6 us  [move(): return lax.ppermute(value, AXES, pairs)]
  transfers between devices with their start and end apart: 37 -> 30, of which waited for: 7 -> 18; matrix products, arithmetic and copies ran while one was open for 2% -> 2% of each run, Pallas kernels for 0% -> 0%
where the time goes in v3:
time: 113 us; the launch traced here: 111 us
  starting transfers between devices  54.8 us (48%)
  waiting for transfers between devices  40.7 us (36%)
  local copies, waits for them, and re-layouts  6.94 us (6%)
  matrix products  4.49 us (4%)
  other arithmetic  2.49 us (2%)
  between operations  1.32 us (1%)
    ppermute x18, starting transfers between devices, move(): return lax.ppermute(value, AXES, pairs)  42.6 us
    ppermute x18, waiting for transfers between devices, move(): return lax.ppermute(value, AXES, pairs)  23.3 us
    all_to_all x1, waiting for transfers between devices, local(): received = lax.all_to_all(spreadout, ('z', 'x'), 0, 0)  10.5 us
    ppermute x3, starting transfers between devices, local(): gram_parts = [lax.ppermute(gram, 'z', s) for s in shifts]  5.93 us
    ppermute x8, waiting for transfers between devices, swap(): return lax.ppermute(value, 'c', [(0, 1), (1, 0)])  5.58 us
    all_to_all x1, starting transfers between devices, local(): received = lax.all_to_all(spreadout, ('z', 'x'), 0, 0)  4.76 us
    dot_general x10, matrix products, dot_nt(): lax.dot_general(left, right, (((1,), (1,)), ((), ())), precision=precisio...  3.53 us
  transfers between devices with their start and end apart: 30, of which 18 were waited for; matrix products, arithmetic and copies ran while one was open for 2% of the time, Pallas kernels for 0%

profile of v3, /device:TPU:2, one launch (start us, length us, event | category | flops | bytes accessed | tf_op | source)
XLA Modules:
  0.0 111.2 jit_solution(7552709845933183570)
XLA Ops:
  2.7 1.1 fusion.161
  4.5 1.6 %collective-permute-start.1 = (f32[2,16,512]{2,1,0:T(8,128)S(1)}, f32[2,16,512]{2,1,0:T(8,128)S(1)}, u32[]{:S(2)}, u32[]{:S(2)}) collective-permute-start(f32[2,16,512]{2,1,0:T(8,128)S(1)} %maximum_maximum_fusion.1), channel_id=1, source_target_pairs={{0,8},{1,9},{2,10},{3,11},{4,12},{5,13},{6,14},{7,15},{8,16},{9,17... | collective-permute-start | bytes 196616 | tf_op jit(solution)/shard_map/ppermute | solution.py:53
  6.1 2.9 %collective-permute-start.2 = (f32[2,16,512]{2,1,0:T(8,128)S(1)}, f32[2,16,512]{2,1,0:T(8,128)S(1)}, u32[]{:S(2)}, u32[]{:S(2)}) collective-permute-start(f32[2,16,512]{2,1,0:T(8,128)S(1)} %maximum_maximum_fusion.1), channel_id=1, source_target_pairs={{0,16},{1,17},{2,18},{3,19},{4,20},{5,21},{6,22},{7,23},{8,24},{9,... | collective-permute-start | bytes 196616 | tf_op jit(solution)/shard_map/ppermute | solution.py:53
  9.0 1.3 %collective-permute-start = (f32[2,16,512]{2,1,0:T(8,128)S(1)}, f32[2,16,512]{2,1,0:T(8,128)S(1)}, u32[]{:S(2)}, u32[]{:S(2)}) collective-permute-start(f32[2,16,512]{2,1,0:T(8,128)S(1)} %maximum_maximum_fusion.1), channel_id=1, source_target_pairs={{0,24},{1,25},{2,26},{3,27},{4,28},{5,29},{6,30},{7,31},{8,0},{9,1... | collective-permute-start | bytes 196616 | tf_op jit(solution)/shard_map/ppermute | solution.py:53
  13.4 3.9 %collective-permute-start.5 = (f32[2,64,64]{2,1,0:T(8,128)S(1)}, f32[2,64,64]{2,1,0:T(8,128)S(1)}, u32[]{:S(2)}, u32[]{:S(2)}) collective-permute-start(f32[2,64,64]{2,1,0:T(8,128)S(1)} %reshape.27), channel_id=1, source_target_pairs={{0,64},{32,96},{64,0},{96,32},{1,65},{33,97},{65,1},{97,33},{2,66}... | collective-permute-start | bytes 98312 | tf_op jit(solution)/shard_map/ppermute | solution.py:125
  18.0 1.3 %collective-permute-start.3 = (f32[2,64,64]{2,1,0:T(8,128)S(1)}, f32[2,64,64]{2,1,0:T(8,128)S(1)}, u32[]{:S(2)}, u32[]{:S(2)}) collective-permute-start(f32[2,64,64]{2,1,0:T(8,128)S(1)} %reshape.27), channel_id=1, source_target_pairs={{0,32},{32,64},{64,96},{96,0},{1,33},{33,65},{65,97},{97,1},{2,34}... | collective-permute-start | bytes 98312 | tf_op jit(solution)/shard_map/ppermute | solution.py:125
  20.0 2.8 %collective-permute-start.7 = (f32[2,592,128]{2,1,0:T(8,128)S(1)}, f32[2,592,128]{2,1,0:T(8,128)S(1)}, u32[]{:S(2)}, u32[]{:S(2)}) collective-permute-start(f32[2,592,128]{2,1,0:T(8,128)S(1)} %constant_dynamic-update-slice_fusion), channel_id=1, source_target_pairs={{0,24},{1,25},{2,26},{3,27},{4,28},{5,29},{6,30},{7,31},{8,0},{9,1... | collective-permute-start | bytes 1818632 | tf_op jit(solution)/shard_map/ppermute | solution.py:53
  24.6 2.1 %collective-permute-start.6 = (f32[2,16,256]{2,1,0:T(8,128)S(1)}, f32[2,16,256]{2,1,0:T(8,128)S(1)}, u32[]{:S(2)}, u32[]{:S(2)}) collective-permute-start(f32[2,16,256]{2,1,0:T(8,128)S(1)} %get-tuple-element.187), channel_id=1, source_target_pairs={{0,32},{1,33},{2,64},{3,65},{4,5},{5,4},{6,96},{7,97},{8,40},{9,41... | collective-permute-start | bytes 98312 | tf_op jit(solution)/shard_map/ppermute | solution.py:53
  26.7 13.4 %collective-permute-done.9 = f32[2,592,128]{2,1,0:T(8,128)S(1)} collective-permute-done((f32[2,592,128]{2,1,0:T(8,128)S(1)}, f32[2,592,128]{2,1,0:T(8,128)S(1)}, u32[]{:S(2)}, u32[]{:S(2)}) %collective-permute-start.9) | collective-permute-done | bytes 606240 | tf_op jit(solution)/shard_map/ppermute | solution.py:53
  44.4 1.1 %collective-permute-done.12 = f32[2,16,256]{2,1,0:T(8,128)S(1)} collective-permute-done((f32[2,16,256]{2,1,0:T(8,128)S(1)}, f32[2,16,256]{2,1,0:T(8,128)S(1)}, u32[]{:S(2)}, u32[]{:S(2)}) %collective-permute-start.12) | collective-permute-done | bytes 32800 | tf_op jit(solution)/shard_map/ppermute | solution.py:53
  47.1 1.0 collective-permute-done.15
  48.4 1.1 collective-permute-done.16
  49.7 1.0 collective-permute-done.17
  51.0 1.0 collective-permute-done.18
  52.3 1.0 collective-permute-done.19
  55.5 22.8 %collective-permute-start.22 = (f32[2,16,512]{2,1,0:T(8,128)S(1)}, f32[2,16,512]{2,1,0:T(8,128)S(1)}, u32[]{:S(2)}, u32[]{:S(2)}) collective-permute-start(f32[2,16,512]{2,1,0:T(8,128)S(1)} %maximum_select_fusion.1), channel_id=1, source_target_pairs={{0,1},{1,0},{2,6},{3,7},{4,70},{5,71},{6,2},{7,3},{8,9},{9,8},{10,... | collective-permute-start | bytes 196616 | tf_op jit(solution)/shard_map/ppermute | solution.py:53
  78.4 2.7 %collective-permute-done.22 = f32[2,16,512]{2,1,0:T(8,128)S(1)} collective-permute-done((f32[2,16,512]{2,1,0:T(8,128)S(1)}, f32[2,16,512]{2,1,0:T(8,128)S(1)}, u32[]{:S(2)}, u32[]{:S(2)}) %collective-permute-start.22) | collective-permute-done | bytes 65568 | tf_op jit(solution)/shard_map/ppermute | solution.py:53
  81.2 2.1 %collective-permute-start.23 = (f32[2,16,512]{2,1,0:T(8,128)S(1)}, f32[2,16,512]{2,1,0:T(8,128)S(1)}, u32[]{:S(2)}, u32[]{:S(2)}) collective-permute-start(f32[2,16,512]{2,1,0:T(8,128)S(1)} %get-tuple-element.301), channel_id=1, source_target_pairs={{0,1},{1,0},{2,4},{3,5},{4,2},{5,3},{6,7},{7,6},{8,9},{9,8},{10,12... | collective-permute-start | bytes 196616 | tf_op jit(solution)/shard_map/ppermute | solution.py:53
  83.3 3.3 %collective-permute-start.26 = (f32[2,16,256]{2,1,0:T(8,128)S(1)}, f32[2,16,256]{2,1,0:T(8,128)S(1)}, u32[]{:S(2)}, u32[]{:S(2)}) collective-permute-start(f32[2,16,256]{2,1,0:T(8,128)S(1)} %get-tuple-element.303), channel_id=1, source_target_pairs={{0,1},{1,0},{2,36},{3,37},{4,5},{5,4},{6,7},{7,6},{8,9},{9,8},{10,... | collective-permute-start | bytes 98312 | tf_op jit(solution)/shard_map/ppermute | solution.py:53
  86.6 1.9 %collective-permute-done.26 = f32[2,16,256]{2,1,0:T(8,128)S(1)} collective-permute-done((f32[2,16,256]{2,1,0:T(8,128)S(1)}, f32[2,16,256]{2,1,0:T(8,128)S(1)}, u32[]{:S(2)}, u32[]{:S(2)}) %collective-permute-start.26) | collective-permute-done | bytes 32800 | tf_op jit(solution)/shard_map/ppermute | solution.py:53
  89.4 1.2 %collective-permute-done.27 = f32[2,16,512]{2,1,0:T(8,128)S(1)} collective-permute-done((f32[2,16,512]{2,1,0:T(8,128)S(1)}, f32[2,16,512]{2,1,0:T(8,128)S(1)}, u32[]{:S(2)}, u32[]{:S(2)}) %collective-permute-start.27) | collective-permute-done | bytes 65568 | tf_op jit(solution)/shard_map/ppermute | solution.py:57
  92.0 1.1 collective-permute-done.28
  94.0 4.8 %all-to-all-start = ((f32[16,2,16,192]{3,2,1,0:T(8,128)}), f32[16,2,16,192]{3,2,1,0:T(8,128)S(1)}, u32[]{:S(2)}, u32[]{:S(2)}) async-start(f32[16,2,16,192]{3,2,1,0:T(8,128)} %broadcast_in_dim.54), calls=%async_computation | async-start | bytes 1048576 | tf_op jit(solution)/shard_map/all_to_all | solution.py:183
  98.8 10.5 %all-to-all-done = f32[16,2,16,192]{3,2,1,0:T(8,128)S(1)} async-done(((f32[16,2,16,192]{3,2,1,0:T(8,128)}), f32[16,2,16,192]{3,2,1,0:T(8,128)S(1)}, u32[]{:S(2)}, u32[]{:S(2)}) %all-to-all-start) | async-done | bytes 393248 | tf_op jit(solution)/shard_map/all_to_all | solution.py:183
  (186 shorter events, 24.3 us)
Async XLA Ops:
  4.5 8.3 %collective-permute-start.1 = (f32[2,16,512]{2,1,0:T(8,128)S(1)}, f32[2,16,512]{2,1,0:T(8,128)S(1)}, u32[]{:S(2)}, u32[]{:S(2)}) collective-permute-start(f32[2,16,512]{2,1,0:T(8,128)S(1)} %maximum_maximum_fusion.1), channel_id=1, source_target_pairs={{0,8},{1,9},{2,10},{3,11},{4,12},{5,13},{6,14},{7,15},{8,16},{9,17... | collective-permute-start | bytes 196616 | tf_op jit(solution)/shard_map/ppermute | solution.py:53
  6.1 6.6 %collective-permute-start.2 = (f32[2,16,512]{2,1,0:T(8,128)S(1)}, f32[2,16,512]{2,1,0:T(8,128)S(1)}, u32[]{:S(2)}, u32[]{:S(2)}) collective-permute-start(f32[2,16,512]{2,1,0:T(8,128)S(1)} %maximum_maximum_fusion.1), channel_id=1, source_target_pairs={{0,16},{1,17},{2,18},{3,19},{4,20},{5,21},{6,22},{7,23},{8,24},{9,... | collective-permute-start | bytes 196616 | tf_op jit(solution)/shard_map/ppermute | solution.py:53
  9.0 4.3 %collective-permute-start = (f32[2,16,512]{2,1,0:T(8,128)S(1)}, f32[2,16,512]{2,1,0:T(8,128)S(1)}, u32[]{:S(2)}, u32[]{:S(2)}) collective-permute-start(f32[2,16,512]{2,1,0:T(8,128)S(1)} %maximum_maximum_fusion.1), channel_id=1, source_target_pairs={{0,24},{1,25},{2,26},{3,27},{4,28},{5,29},{6,30},{7,31},{8,0},{9,1... | collective-permute-start | bytes 196616 | tf_op jit(solution)/shard_map/ppermute | solution.py:53
  11.3 28.8 %collective-permute-start.9 = (f32[2,592,128]{2,1,0:T(8,128)S(1)}, f32[2,592,128]{2,1,0:T(8,128)S(1)}, u32[]{:S(2)}, u32[]{:S(2)}) collective-permute-start(f32[2,592,128]{2,1,0:T(8,128)S(1)} %constant_dynamic-update-slice_fusion), channel_id=1, source_target_pairs={{0,8},{1,9},{2,10},{3,11},{4,12},{5,13},{6,14},{7,15},{8,16},{9,17... | collective-permute-start | bytes 1818632 | tf_op jit(solution)/shard_map/ppermute | solution.py:53
  12.0 28.1 %collective-permute-start.8 = (f32[2,592,128]{2,1,0:T(8,128)S(1)}, f32[2,592,128]{2,1,0:T(8,128)S(1)}, u32[]{:S(2)}, u32[]{:S(2)}) collective-permute-start(f32[2,592,128]{2,1,0:T(8,128)S(1)} %constant_dynamic-update-slice_fusion), channel_id=1, source_target_pairs={{0,16},{1,17},{2,18},{3,19},{4,20},{5,21},{6,22},{7,23},{8,24},{9,... | collective-permute-start | bytes 1818632 | tf_op jit(solution)/shard_map/ppermute | solution.py:53
  13.4 6.6 %collective-permute-start.5 = (f32[2,64,64]{2,1,0:T(8,128)S(1)}, f32[2,64,64]{2,1,0:T(8,128)S(1)}, u32[]{:S(2)}, u32[]{:S(2)}) collective-permute-start(f32[2,64,64]{2,1,0:T(8,128)S(1)} %reshape.27), channel_id=1, source_target_pairs={{0,64},{32,96},{64,0},{96,32},{1,65},{33,97},{65,1},{97,33},{2,66}... | collective-permute-start | bytes 98312 | tf_op jit(solution)/shard_map/ppermute | solution.py:125
  17.3 5.4 %collective-permute-start.4 = (f32[2,64,64]{2,1,0:T(8,128)S(1)}, f32[2,64,64]{2,1,0:T(8,128)S(1)}, u32[]{:S(2)}, u32[]{:S(2)}) collective-permute-start(f32[2,64,64]{2,1,0:T(8,128)S(1)} %reshape.27), channel_id=1, source_target_pairs={{0,96},{32,0},{64,32},{96,64},{1,97},{33,1},{65,33},{97,65},{2,98}... | collective-permute-start | bytes 98312 | tf_op jit(solution)/shard_map/ppermute | solution.py:125
  18.0 5.5 %collective-permute-start.3 = (f32[2,64,64]{2,1,0:T(8,128)S(1)}, f32[2,64,64]{2,1,0:T(8,128)S(1)}, u32[]{:S(2)}, u32[]{:S(2)}) collective-permute-start(f32[2,64,64]{2,1,0:T(8,128)S(1)} %reshape.27), channel_id=1, source_target_pairs={{0,32},{32,64},{64,96},{96,0},{1,33},{33,65},{65,97},{97,1},{2,34}... | collective-permute-start | bytes 98312 | tf_op jit(solution)/shard_map/ppermute | solution.py:125
  20.0 20.7 %collective-permute-start.7 = (f32[2,592,128]{2,1,0:T(8,128)S(1)}, f32[2,592,128]{2,1,0:T(8,128)S(1)}, u32[]{:S(2)}, u32[]{:S(2)}) collective-permute-start(f32[2,592,128]{2,1,0:T(8,128)S(1)} %constant_dynamic-update-slice_fusion), channel_id=1, source_target_pairs={{0,24},{1,25},{2,26},{3,27},{4,28},{5,29},{6,30},{7,31},{8,0},{9,1... | collective-permute-start | bytes 1818632 | tf_op jit(solution)/shard_map/ppermute | solution.py:53
  24.6 17.0 %collective-permute-start.6 = (f32[2,16,256]{2,1,0:T(8,128)S(1)}, f32[2,16,256]{2,1,0:T(8,128)S(1)}, u32[]{:S(2)}, u32[]{:S(2)}) collective-permute-start(f32[2,16,256]{2,1,0:T(8,128)S(1)} %get-tuple-element.187), channel_id=1, source_target_pairs={{0,32},{1,33},{2,64},{3,65},{4,5},{5,4},{6,96},{7,97},{8,40},{9,41... | collective-permute-start | bytes 98312 | tf_op jit(solution)/shard_map/ppermute | solution.py:53
  41.7 2.0 %collective-permute-start.10 = (f32[2,16,512]{2,1,0:T(8,128)S(1)}, f32[2,16,512]{2,1,0:T(8,128)S(1)}, u32[]{:S(2)}, u32[]{:S(2)}) collective-permute-start(f32[2,16,512]{2,1,0:T(8,128)S(1)} %get-tuple-element.290), channel_id=1, source_target_pairs={{0,1},{1,0},{2,3},{3,2},{4,5},{5,4},{6,7},{7,6},{8,9},{9,8},{10,11... | collective-permute-start | bytes 196616 | tf_op jit(solution)/shard_map/ppermute | solution.py:57
  43.8 1.8 %collective-permute-start.11 = (f32[2,16,512]{2,1,0:T(8,128)S(1)}, f32[2,16,512]{2,1,0:T(8,128)S(1)}, u32[]{:S(2)}, u32[]{:S(2)}) collective-permute-start(f32[2,16,512]{2,1,0:T(8,128)S(1)} %maximum_select_fusion), channel_id=1, source_target_pairs={{0,1},{1,0},{2,3},{3,2},{4,5},{5,4},{6,7},{7,6},{8,9},{9,8},{10,11... | collective-permute-start | bytes 196616 | tf_op jit(solution)/shard_map/ppermute | solution.py:53
  45.6 1.3 %collective-permute-start.13 = (f32[2,16,512]{2,1,0:T(8,128)S(1)}, f32[2,16,512]{2,1,0:T(8,128)S(1)}, u32[]{:S(2)}, u32[]{:S(2)}) collective-permute-start(f32[2,16,512]{2,1,0:T(8,128)S(1)} %add.189), channel_id=1, source_target_pairs={{0,1},{1,0},{2,3},{3,2},{4,5},{5,4},{6,7},{7,6},{8,9},{9,8},{10,11... | collective-permute-start | bytes 196616 | tf_op jit(solution)/shard_map/ppermute | solution.py:57
  45.8 2.3 %collective-permute-start.14 = (f32[2,16,512]{2,1,0:T(8,128)S(1)}, f32[2,16,512]{2,1,0:T(8,128)S(1)}, u32[]{:S(2)}, u32[]{:S(2)}) collective-permute-start(f32[2,16,512]{2,1,0:T(8,128)S(1)} %get-tuple-element.294), channel_id=1, source_target_pairs={{0,1},{1,0},{2,3},{3,2},{4,5},{5,4},{6,7},{7,6},{8,9},{9,8},{10,11... | collective-permute-start | bytes 196616 | tf_op jit(solution)/shard_map/ppermute | solution.py:53
  48.2 1.3 %collective-permute-start.16 = (f32[2,16,512]{2,1,0:T(8,128)S(1)}, f32[2,16,512]{2,1,0:T(8,128)S(1)}, u32[]{:S(2)}, u32[]{:S(2)}) collective-permute-start(f32[2,16,512]{2,1,0:T(8,128)S(1)} %add_add_fusion.1), channel_id=1, source_target_pairs={{0,1},{1,0},{2,3},{3,2},{4,5},{5,4},{6,7},{7,6},{8,9},{9,8},{10,11... | collective-permute-start | bytes 196616 | tf_op jit(solution)/shard_map/ppermute | solution.py:57
  53.8 1.3 %collective-permute-start.20 = (f32[2,16,512]{2,1,0:T(8,128)S(1)}, f32[2,16,512]{2,1,0:T(8,128)S(1)}, u32[]{:S(2)}, u32[]{:S(2)}) collective-permute-start(f32[2,16,512]{2,1,0:T(8,128)S(1)} %get-tuple-element.298), channel_id=1, source_target_pairs={{0,1},{1,0},{2,3},{3,2},{4,5},{5,4},{6,7},{7,6},{8,9},{9,8},{10,11... | collective-permute-start | bytes 196616 | tf_op jit(solution)/shard_map/ppermute | solution.py:57
  55.1 23.2 %collective-permute-start.24 = (f32[2,16,256]{2,1,0:T(8,128)S(1)}, f32[2,16,256]{2,1,0:T(8,128)S(1)}, u32[]{:S(2)}, u32[]{:S(2)}) collective-permute-start(f32[2,16,256]{2,1,0:T(8,128)S(1)} %get-tuple-element.299), channel_id=1, source_target_pairs={{0,1},{1,0},{2,3},{3,2},{4,5},{5,4},{6,7},{7,6},{8,9},{9,8},{10,11... | collective-permute-start | bytes 98312 | tf_op jit(solution)/shard_map/ppermute | solution.py:53
  55.5 25.6 %collective-permute-start.22 = (f32[2,16,512]{2,1,0:T(8,128)S(1)}, f32[2,16,512]{2,1,0:T(8,128)S(1)}, u32[]{:S(2)}, u32[]{:S(2)}) collective-permute-start(f32[2,16,512]{2,1,0:T(8,128)S(1)} %maximum_select_fusion.1), channel_id=1, source_target_pairs={{0,1},{1,0},{2,6},{3,7},{4,70},{5,71},{6,2},{7,3},{8,9},{9,8},{10,... | collective-permute-start | bytes 196616 | tf_op jit(solution)/shard_map/ppermute | solution.py:53
  81.0 2.2 %collective-permute-start.25 = (f32[2,16,512]{2,1,0:T(8,128)S(1)}, f32[2,16,512]{2,1,0:T(8,128)}, u32[]{:S(2)}, u32[]{:S(2)}) collective-permute-start(f32[2,16,512]{2,1,0:T(8,128)S(1)} %add.196), channel_id=1, source_target_pairs={{0,1},{1,0},{2,3},{3,2},{4,5},{5,4},{6,7},{7,6},{8,9},{9,8},{10,11... | collective-permute-start | bytes 196616 | tf_op jit(solution)/shard_map/ppermute | solution.py:57
  81.2 8.0 %collective-permute-start.23 = (f32[2,16,512]{2,1,0:T(8,128)S(1)}, f32[2,16,512]{2,1,0:T(8,128)S(1)}, u32[]{:S(2)}, u32[]{:S(2)}) collective-permute-start(f32[2,16,512]{2,1,0:T(8,128)S(1)} %get-tuple-element.301), channel_id=1, source_target_pairs={{0,1},{1,0},{2,4},{3,5},{4,2},{5,3},{6,7},{7,6},{8,9},{9,8},{10,12... | collective-permute-start | bytes 196616 | tf_op jit(solution)/shard_map/ppermute | solution.py:53
  83.3 5.2 %collective-permute-start.26 = (f32[2,16,256]{2,1,0:T(8,128)S(1)}, f32[2,16,256]{2,1,0:T(8,128)S(1)}, u32[]{:S(2)}, u32[]{:S(2)}) collective-permute-start(f32[2,16,256]{2,1,0:T(8,128)S(1)} %get-tuple-element.303), channel_id=1, source_target_pairs={{0,1},{1,0},{2,36},{3,37},{4,5},{5,4},{6,7},{7,6},{8,9},{9,8},{10,... | collective-permute-start | bytes 98312 | tf_op jit(solution)/shard_map/ppermute | solution.py:53
  89.3 1.3 %collective-permute-start.27 = (f32[2,16,512]{2,1,0:T(8,128)S(1)}, f32[2,16,512]{2,1,0:T(8,128)S(1)}, u32[]{:S(2)}, u32[]{:S(2)}) collective-permute-start(f32[2,16,512]{2,1,0:T(8,128)S(1)} %add_add_fusion), channel_id=1, source_target_pairs={{0,1},{1,0},{2,3},{3,2},{4,5},{5,4},{6,7},{7,6},{8,9},{9,8},{10,11... | collective-permute-start | bytes 196616 | tf_op jit(solution)/shard_map/ppermute | solution.py:57
  91.8 1.3 %collective-permute-start.28 = (f32[2,16,320]{2,1,0:T(8,128)S(1)}, f32[2,16,320]{2,1,0:T(8,128)S(1)}, u32[]{:S(2)}, u32[]{:S(2)}) collective-permute-start(f32[2,16,320]{2,1,0:T(8,128)S(1)} %maximum_maximum_fusion.2), channel_id=1, source_target_pairs={{0,1},{1,0},{2,3},{3,2},{4,5},{5,4},{6,7},{7,6},{8,9},{9,8},{10,11... | collective-permute-start | bytes 122888 | tf_op jit(solution)/shard_map/ppermute | solution.py:57
  94.0 15.3 %all-to-all-start = ((f32[16,2,16,192]{3,2,1,0:T(8,128)}), f32[16,2,16,192]{3,2,1,0:T(8,128)S(1)}, u32[]{:S(2)}, u32[]{:S(2)}) async-start(f32[16,2,16,192]{3,2,1,0:T(8,128)} %broadcast_in_dim.54), calls=%async_computation | async-start | bytes 1048576 | tf_op jit(solution)/shard_map/all_to_all | solution.py:183
  (24 other events, 71.8 us)

commit v4 on v3

--- a/solution.py
+++ b/solution.py
@@ -99,14 +99,11 @@
     lower_half = lax.dynamic_slice_in_dim(lower_inverse, c * half, half, 1)
     upper_half = lax.dynamic_slice_in_dim(upper_inverse, c * half, half, 1)
 
-    lead = apply_rows(krylov_block, lower_half)
-    gram = herm_rows(basis, basis)
-    lead = jnp.concatenate([lead, gram.reshape(2, nvec, half)], 2)
-    lead_parts = [turn_y(lead, d) for d in (1, 3, 2)]
-
     inverse = jnp.where(x == (z + 3) % SIDE, lower_half, upper_half)
     left, right = factor[:, :, :piece], factor[:, :, piece:]
     packed = jnp.concatenate([left, right, inverse, krylov_block, basis], 1)
+    packed, krylov_block, lower_half = lax.optimization_barrier((packed, krylov_block, lower_half))
+    lead = apply_rows(krylov_block, lower_half)
     pieces = [packed] + [turn_y(packed, d) for d in (1, 3, 2)]
     pieces = [pieces[0], pieces[1], pieces[3], pieces[2]]
     tall = jnp.concatenate([jnp.concatenate([p[:, :piece], p[:, piece:half]], 2) for p in pieces], 1)
@@ -118,16 +115,10 @@
     high = lax.dynamic_index_in_dim(basis_all, (2 * c + 1 - y) % SIDE, 0, False)
     basis_half = jnp.concatenate([low, high], 2)
 
-    lead = lead + lead_parts[0] + lead_parts[1] + lead_parts[2]
-    y0 = lead[:, :, :half]
-    gram = lead[:, :, half:].reshape(2, nb, nb)
-    shifts = [[(i, (i + d) % SIDE) for i in every] for d in (1, 3, 2)]
-    gram_parts = [lax.ppermute(gram, "z", s) for s in shifts]
-    gram = gram + gram_parts[0] + gram_parts[1] + gram_parts[2]
-    twice = jnp.stack([2.0 * jnp.eye(nb, dtype=jnp.float32), jnp.zeros((nb, nb), jnp.float32)])
-    keep = twice - gram
-    spread = combine_rows(keep, basis)
-    y0, spread, keep = lax.optimization_barrier((y0, spread, keep))
+    lead_parts = [turn_y(lead, d) for d in (1, 3, 2)]
+    y0 = lead + lead_parts[0] + lead_parts[1] + lead_parts[2]
+    plane = jnp.concatenate([basis_all[d] for d in every], 2)
+    gram = herm_rows(plane, plane)
 
     empty = jnp.zeros((2, nvec, half), jnp.float32)
     blank = jnp.zeros((2, nvec, tile), jnp.float32)
@@ -149,10 +140,11 @@
     acc0 = product(((1, 0), (2, 0), (3, 0)), hop(y0, {(0, 0): (1, 0), (0, 1): (2, 0), (0, 3): (3, 0)}))
     y1 = finish((1, 0), given, acc0)
     near1 = hop(y1, {(1, 0): (2, 1)})
-    mixed1 = hop(jnp.where(z == 1, widen(y1), acc0), {(1, 0): (3, 1), (2, 0): (2, 1), (3, 0): (3, 2)})
-    y2 = finish((2, 1), given, mixed1 + product(((2, 1),), near1))
+    early1 = hop(acc0, {(2, 0): (2, 1), (3, 0): (3, 2)})
+    far1 = hop(y1, {(1, 0): (3, 1)})
+    y2 = finish((2, 1), given, early1 + product(((2, 1),), near1))
     near2 = hop(y2, {(2, 1): (3, 2)})
-    held1 = mixed1 + hop(product(((3, 1),), mixed1[:, :, :half]), {(3, 1): (3, 2)})
+    held1 = early1 + hop(product(((3, 1),), far1), {(3, 1): (3, 2)})
     y3 = finish((3, 2), given, held1 + product(((3, 2),), near2))
 
     moved = hop(y1 + y2 + y3, {(1, 0): (1, 2), (2, 1): (2, 3), (3, 2): (3, 3)})
@@ -162,13 +154,14 @@
     x3 = lax.cond(here((3, 3)), apply_rows, lambda v, w: empty, solved, rows)
     near3 = hop(x3, {(3, 3): (2, 3)})
     x2 = finish((2, 3), solved, product(((2, 3),), near3))
-    far3 = hop(jnp.where(z == 3, x3, near3), {(3, 3): (0, 3), (2, 3): (1, 3)})
-    near4 = hop(x2, {(2, 3): (1, 2)})
-    side = product(((0, 3), (1, 3)), far3)
-    mixed3 = hop(jnp.where(z == 2, widen(x2), side), {(2, 3): (0, 2), (1, 3): (1, 2), (0, 3): (0, 1)})
-    x1 = finish((1, 2), solved, mixed3 + product(((1, 2),), near4))
+    far3 = hop(x3, {(3, 3): (1, 3)})
+    side1 = hop(product(((1, 3),), far3), {(1, 3): (1, 2)})
+    near4 = hop(x2 + x3, {(2, 3): (1, 2), (3, 3): (0, 3)})
+    far4 = hop(x2, {(2, 3): (0, 2)})
+    side0 = hop(product(((0, 3),), near4), {(0, 3): (0, 1)})
+    x1 = finish((1, 2), solved, side1 + product(((1, 2),), near4))
     near5 = hop(x1, {(1, 2): (0, 1)})
-    held3 = mixed3 + hop(product(((0, 2),), mixed3[:, :, :half]), {(0, 2): (0, 1)})
+    held3 = side0 + hop(product(((0, 2),), far4), {(0, 2): (0, 1)})
     x0 = finish((0, 1), solved, held3 + product(((0, 1),), near5))
 
     found = x0 + x1 + x2 + x3
@@ -179,13 +172,16 @@
     chosen = jnp.where((y < 2) == (c == 0), found, other[:, :, :half])
     mine = jnp.where(y % 2 == 0, chosen[:, :, :piece], chosen[:, :, piece:])
     message = jnp.concatenate([mine, share], 2)
-    spreadout = jnp.broadcast_to(message[None], (SIDE * SIDE,) + message.shape)
-    received = lax.all_to_all(spreadout, ("z", "x"), 0, 0)
-    first = jnp.sum(received[:, :, :, piece:], 0)
-    same = lax.dynamic_slice_in_dim(received[:, :, :, :piece], z * SIDE, SIDE, 0)
-    own_rows = jnp.sum(same, 0)
-    projected = own_rows - combine_rows(first, spread)
-    coeffs = combine_rows(first, keep)
+    shifts = [[(i, (i + d) % SIDE) for i in every] for d in (1, 3, 2)]
+    across = [lax.ppermute(message, "x", s) for s in shifts]
+    message = message + across[0] + across[1] + across[2]
+    own_rows = message[:, :, :piece]
+    sums = jnp.concatenate([message[:, :, piece:], gram], 1)
+    planes = [lax.ppermute(sums, "z", s) for s in shifts]
+    sums = sums + planes[0] + planes[1] + planes[2]
+    first, gram = sums[:, :nvec], sums[:, nvec:]
+    coeffs = 2.0 * first - combine_rows(first, gram)
+    projected = own_rows - combine_rows(coeffs, basis)
     return projected, jnp.swapaxes(coeffs, 1, 2)
 
 

time: 113 us -> 119 us (1.053)
  the two profiles are of different devices: /device:TPU:2 before, /device:TPU:16 now
where the time goes in v4:
time: 119 us
  starting transfers between devices  55.2 us (46%)
  waiting for transfers between devices  45.8 us (38%)
  local copies, waits for them, and re-layouts  10.5 us (9%)
  other arithmetic  3.28 us (3%)
  matrix products  2.69 us (2%)
  between operations  1.34 us (1%)
    ppermute x3, starting transfers between devices, local(): across = [lax.ppermute(message, 'x', s) for s in shifts]  36.6 us
    ppermute x21, waiting for transfers between devices, move(): return lax.ppermute(value, AXES, pairs)  34 us
    ppermute x21, starting transfers between devices, move(): return lax.ppermute(value, AXES, pairs)  13.9 us
    ppermute x3, waiting for transfers between devices, local(): across = [lax.ppermute(message, 'x', s) for s in shifts]  5.03 us
    ppermute x3, waiting for transfers between devices, local(): planes = [lax.ppermute(sums, 'z', s) for s in shifts]  4.91 us
    unnamed x42, local copies, waits for them, and re-layouts  4.88 us
    slice x4, local copies, waits for them, and re-layouts, local(): basis_all = jnp.stack([p[:, top + nvec:] for p in pieces])  2.82 us
    ppermute x8, starting transfers between devices, swap(): return lax.ppermute(value, 'c', [(0, 1), (1, 0)])  2.61 us
  transfers between devices with their start and end apart: 35, of which 17 were waited for; matrix products, arithmetic and copies ran while one was open for 4% of the time, Pallas kernels for 0%

profile of v4, /device:TPU:16, one launch (start us, length us, event | category | flops | bytes accessed | tf_op | source)
XLA Modules:
  0.0 119.0 jit_solution(305163075025662449)
XLA Ops:
  0.7 1.0 slice_dynamic-update-slice_fusion.1
  1.7 1.1 constant_dynamic-slice_fusion
  2.9 1.4 %collective-permute-start.6 = (f32[2,592,128]{2,1,0:T(8,128)S(1)}, f32[2,592,128]{2,1,0:T(8,128)S(1)}, u32[]{:S(2)}, u32[]{:S(2)}) collective-permute-start(f32[2,592,128]{2,1,0:T(8,128)S(1)} %constant_dynamic-update-slice_fusion), channel_id=1, source_target_pairs={{0,8},{1,9},{2,10},{3,11},{4,12},{5,13},{6,14},{7,15},{8,16},{9,17... | collective-permute-start | bytes 1818632 | tf_op jit(solution)/shard_map/ppermute | solution.py:53
  4.9 2.1 %collective-permute-start.2 = (f32[2,16,256]{2,1,0:T(8,128)S(1)}, f32[2,16,256]{2,1,0:T(8,128)S(1)}, u32[]{:S(2)}, u32[]{:S(2)}) collective-permute-start(f32[2,16,256]{2,1,0:T(8,128)S(1)} %pad_maximum_fusion.76), channel_id=1, source_target_pairs={{0,16},{1,17},{2,18},{3,19},{4,20},{5,21},{6,22},{7,23},{8,24},{9,... | collective-permute-start | bytes 98312 | tf_op jit(solution)/shard_map/ppermute | solution.py:53
  6.9 1.1 collective-permute-start
  8.0 2.9 %collective-permute-start.5 = (f32[2,592,128]{2,1,0:T(8,128)S(1)}, f32[2,592,128]{2,1,0:T(8,128)S(1)}, u32[]{:S(2)}, u32[]{:S(2)}) collective-permute-start(f32[2,592,128]{2,1,0:T(8,128)S(1)} %constant_dynamic-update-slice_fusion), channel_id=1, source_target_pairs={{0,16},{1,17},{2,18},{3,19},{4,20},{5,21},{6,22},{7,23},{8,24},{9,... | collective-permute-start | bytes 1818632 | tf_op jit(solution)/shard_map/ppermute | solution.py:53
  11.0 21.8 %collective-permute-done.1 = f32[2,16,256]{2,1,0:T(8,128)S(1)} collective-permute-done((f32[2,16,256]{2,1,0:T(8,128)S(1)}, f32[2,16,256]{2,1,0:T(8,128)S(1)}, u32[]{:S(2)}, u32[]{:S(2)}) %collective-permute-start.1) | collective-permute-done | bytes 32800 | tf_op jit(solution)/shard_map/ppermute | solution.py:53
  32.8 2.0 %collective-permute-start.3 = (f32[2,16,256]{2,1,0:T(8,128)S(1)}, f32[2,16,256]{2,1,0:T(8,128)S(1)}, u32[]{:S(2)}, u32[]{:S(2)}) collective-permute-start(f32[2,16,256]{2,1,0:T(8,128)S(1)} %add_add_fusion.6), channel_id=1, source_target_pairs={{0,32},{1,33},{2,64},{3,65},{4,5},{5,4},{6,96},{7,97},{8,40},{9,41... | collective-permute-start | bytes 98312 | tf_op jit(solution)/shard_map/ppermute | solution.py:53
  34.9 7.9 %collective-permute-done.4 = f32[2,592,128]{2,1,0:T(8,128)S(1)} collective-permute-done((f32[2,592,128]{2,1,0:T(8,128)S(1)}, f32[2,592,128]{2,1,0:T(8,128)S(1)}, u32[]{:S(2)}, u32[]{:S(2)}) %collective-permute-start.4) | collective-permute-done | bytes 606240 | tf_op jit(solution)/shard_map/ppermute | solution.py:53
  44.9 0.9 slice-done.4
  47.0 1.2 collective-permute-done.9
  48.8 0.9 collective-permute-done.11
  50.3 1.0 collective-permute-done.13
  51.6 1.5 %fusion.218 = (f32[2,64,128]{2,1,0:T(8,128)}, f32[1,2,64,128]{3,2,1,0:T(8,128)S(1)}) fusion(f32[2,592,128]{2,1,0:T(8,128)} %copy-done.6), kind=kLoop, calls=%fused_computation.395 | loop fusion | bytes 196608 | tf_op jit(solution)/shard_map/slice | solution.py:113
  53.7 0.9 add_add_fusion.5
  64.6 1.0 collective-permute-done.27
  67.3 31.7 %collective-permute-start.30 = (f32[2,16,192]{2,1,0:T(8,128)S(1)}, f32[2,16,192]{2,1,0:T(8,128)S(1)}, u32[]{:S(2)}, u32[]{:S(2)}) collective-permute-start(f32[2,16,192]{2,1,0:T(8,128)S(1)} %pad_maximum_fusion.78), channel_id=1, source_target_pairs={{0,6},{2,0},{4,2},{6,4},{1,7},{3,1},{5,3},{7,5},{8,14},{10,8},{12,... | collective-permute-start | bytes 73736 | tf_op jit(solution)/shard_map/ppermute | solution.py:176
  99.0 4.8 %collective-permute-start.31 = (f32[2,16,192]{2,1,0:T(8,128)S(1)}, f32[2,16,192]{2,1,0:T(8,128)S(1)}, u32[]{:S(2)}, u32[]{:S(2)}) collective-permute-start(f32[2,16,192]{2,1,0:T(8,128)S(1)} %pad_maximum_fusion.78), channel_id=1, source_target_pairs={{0,4},{2,6},{4,0},{6,2},{1,5},{3,7},{5,1},{7,3},{8,12},{10,14},{12... | collective-permute-start | bytes 73736 | tf_op jit(solution)/shard_map/ppermute | solution.py:176
  104.0 1.8 %collective-permute-done.31 = f32[2,16,192]{2,1,0:T(8,128)S(1)} collective-permute-done((f32[2,16,192]{2,1,0:T(8,128)S(1)}, f32[2,16,192]{2,1,0:T(8,128)S(1)}, u32[]{:S(2)}, u32[]{:S(2)}) %collective-permute-start.31) | collective-permute-done | bytes 24608 | tf_op jit(solution)/shard_map/ppermute | solution.py:176
  105.8 3.2 %collective-permute-done.29 = f32[2,16,192]{2,1,0:T(8,128)S(1)} collective-permute-done((f32[2,16,192]{2,1,0:T(8,128)S(1)}, f32[2,16,192]{2,1,0:T(8,128)S(1)}, u32[]{:S(2)}, u32[]{:S(2)}) %collective-permute-start.29) | collective-permute-done | bytes 24608 | tf_op jit(solution)/shard_map/ppermute | solution.py:176
  109.6 1.7 %collective-permute-start.32 = (f32[2,80,64]{1,2,0:T(8,128)S(1)}, f32[2,80,64]{1,2,0:T(8,128)S(1)}, u32[]{:S(2)}, u32[]{:S(2)}) collective-permute-start(f32[2,80,64]{1,2,0:T(8,128)S(1)} %maximum_maximum_fusion.1), channel_id=1, source_target_pairs={{0,32},{32,64},{64,96},{96,0},{1,33},{33,65},{65,97},{97,1},{2,34}... | collective-permute-start | bytes 122888 | tf_op jit(solution)/shard_map/ppermute | solution.py:180
  111.3 2.2 %collective-permute-done.33 = f32[2,80,64]{1,2,0:T(8,128)S(1)} collective-permute-done((f32[2,80,64]{1,2,0:T(8,128)S(1)}, f32[2,80,64]{1,2,0:T(8,128)S(1)}, u32[]{:S(2)}, u32[]{:S(2)}) %collective-permute-start.33) | collective-permute-done | bytes 40992 | tf_op jit(solution)/shard_map/ppermute | solution.py:180
  113.6 1.8 %collective-permute-done.34 = f32[2,80,64]{1,2,0:T(8,128)S(1)} collective-permute-done((f32[2,80,64]{1,2,0:T(8,128)S(1)}, f32[2,80,64]{1,2,0:T(8,128)S(1)}, u32[]{:S(2)}, u32[]{:S(2)}) %collective-permute-start.34) | collective-permute-done | bytes 40992 | tf_op jit(solution)/shard_map/ppermute | solution.py:180
  115.3 0.9 collective-permute-done.32
  (198 shorter events, 21.6 us)
Async XLA Ops:
  2.9 31.9 %collective-permute-start.6 = (f32[2,592,128]{2,1,0:T(8,128)S(1)}, f32[2,592,128]{2,1,0:T(8,128)S(1)}, u32[]{:S(2)}, u32[]{:S(2)}) collective-permute-start(f32[2,592,128]{2,1,0:T(8,128)S(1)} %constant_dynamic-update-slice_fusion), channel_id=1, source_target_pairs={{0,8},{1,9},{2,10},{3,11},{4,12},{5,13},{6,14},{7,15},{8,16},{9,17... | collective-permute-start | bytes 1818632 | tf_op jit(solution)/shard_map/ppermute | solution.py:53
  4.7 28.1 %collective-permute-start.1 = (f32[2,16,256]{2,1,0:T(8,128)S(1)}, f32[2,16,256]{2,1,0:T(8,128)S(1)}, u32[]{:S(2)}, u32[]{:S(2)}) collective-permute-start(f32[2,16,256]{2,1,0:T(8,128)S(1)} %pad_maximum_fusion.76), channel_id=1, source_target_pairs={{0,8},{1,9},{2,10},{3,11},{4,12},{5,13},{6,14},{7,15},{8,16},{9,17... | collective-permute-start | bytes 98312 | tf_op jit(solution)/shard_map/ppermute | solution.py:53
  4.9 27.9 %collective-permute-start.2 = (f32[2,16,256]{2,1,0:T(8,128)S(1)}, f32[2,16,256]{2,1,0:T(8,128)S(1)}, u32[]{:S(2)}, u32[]{:S(2)}) collective-permute-start(f32[2,16,256]{2,1,0:T(8,128)S(1)} %pad_maximum_fusion.76), channel_id=1, source_target_pairs={{0,16},{1,17},{2,18},{3,19},{4,20},{5,21},{6,22},{7,23},{8,24},{9,... | collective-permute-start | bytes 98312 | tf_op jit(solution)/shard_map/ppermute | solution.py:53
  6.9 25.8 %collective-permute-start = (f32[2,16,256]{2,1,0:T(8,128)S(1)}, f32[2,16,256]{2,1,0:T(8,128)S(1)}, u32[]{:S(2)}, u32[]{:S(2)}) collective-permute-start(f32[2,16,256]{2,1,0:T(8,128)S(1)} %pad_maximum_fusion.76), channel_id=1, source_target_pairs={{0,24},{1,25},{2,26},{3,27},{4,28},{5,29},{6,30},{7,31},{8,0},{9,1... | collective-permute-start | bytes 98312 | tf_op jit(solution)/shard_map/ppermute | solution.py:53
  8.0 26.8 %collective-permute-start.5 = (f32[2,592,128]{2,1,0:T(8,128)S(1)}, f32[2,592,128]{2,1,0:T(8,128)S(1)}, u32[]{:S(2)}, u32[]{:S(2)}) collective-permute-start(f32[2,592,128]{2,1,0:T(8,128)S(1)} %constant_dynamic-update-slice_fusion), channel_id=1, source_target_pairs={{0,16},{1,17},{2,18},{3,19},{4,20},{5,21},{6,22},{7,23},{8,24},{9,... | collective-permute-start | bytes 1818632 | tf_op jit(solution)/shard_map/ppermute | solution.py:53
  32.7 10.1 %collective-permute-start.4 = (f32[2,592,128]{2,1,0:T(8,128)S(1)}, f32[2,592,128]{2,1,0:T(8,128)S(1)}, u32[]{:S(2)}, u32[]{:S(2)}) collective-permute-start(f32[2,592,128]{2,1,0:T(8,128)S(1)} %constant_dynamic-update-slice_fusion), channel_id=1, source_target_pairs={{0,24},{1,25},{2,26},{3,27},{4,28},{5,29},{6,30},{7,31},{8,0},{9,1... | collective-permute-start | bytes 1818632 | tf_op jit(solution)/shard_map/ppermute | solution.py:53
  32.8 10.9 %collective-permute-start.3 = (f32[2,16,256]{2,1,0:T(8,128)S(1)}, f32[2,16,256]{2,1,0:T(8,128)S(1)}, u32[]{:S(2)}, u32[]{:S(2)}) collective-permute-start(f32[2,16,256]{2,1,0:T(8,128)S(1)} %add_add_fusion.6), channel_id=1, source_target_pairs={{0,32},{1,33},{2,64},{3,65},{4,5},{5,4},{6,96},{7,97},{8,40},{9,41... | collective-permute-start | bytes 98312 | tf_op jit(solution)/shard_map/ppermute | solution.py:53
  44.4 3.8 %collective-permute-start.8 = (f32[2,16,512]{2,1,0:T(8,128)}, f32[2,16,512]{2,1,0:T(8,128)S(1)}, u32[]{:S(2)}, u32[]{:S(2)}) collective-permute-start(f32[2,16,512]{2,1,0:T(8,128)} %get-tuple-element.311), channel_id=1, source_target_pairs={{0,1},{1,0},{2,3},{3,2},{4,5},{5,4},{6,7},{7,6},{8,9},{9,8},{10,11... | collective-permute-start | bytes 196616 | tf_op jit(solution)/shard_map/ppermute | solution.py:53
  44.4 2.4 %collective-permute-start.7 = (f32[2,16,512]{2,1,0:T(8,128)}, f32[2,16,512]{2,1,0:T(8,128)S(1)}, u32[]{:S(2)}, u32[]{:S(2)}) collective-permute-start(f32[2,16,512]{2,1,0:T(8,128)} %get-tuple-element.311), channel_id=1, source_target_pairs={{0,1},{1,0},{2,3},{3,2},{4,5},{5,4},{6,7},{7,6},{8,9},{9,8},{10,11... | collective-permute-start | bytes 196616 | tf_op jit(solution)/shard_map/ppermute | solution.py:57
  48.2 1.8 %collective-permute-start.10 = (f32[2,16,512]{2,1,0:T(8,128)S(1)}, f32[2,16,512]{2,1,0:T(8,128)S(1)}, u32[]{:S(2)}, u32[]{:S(2)}) collective-permute-start(f32[2,16,512]{2,1,0:T(8,128)S(1)} %add.191), channel_id=1, source_target_pairs={{0,1},{1,0},{2,3},{3,2},{4,5},{5,4},{6,7},{7,6},{8,9},{9,8},{10,11... | collective-permute-start | bytes 196616 | tf_op jit(solution)/shard_map/ppermute | solution.py:57
  49.7 1.7 %collective-permute-start.12 = (f32[2,16,512]{2,1,0:T(8,128)S(1)}, f32[2,16,512]{2,1,0:T(8,128)S(1)}, u32[]{:S(2)}, u32[]{:S(2)}) collective-permute-start(f32[2,16,512]{2,1,0:T(8,128)S(1)} %get-tuple-element.315), channel_id=1, source_target_pairs={{0,1},{1,0},{2,3},{3,2},{4,5},{5,4},{6,7},{7,6},{8,9},{9,8},{10,11... | collective-permute-start | bytes 196616 | tf_op jit(solution)/shard_map/ppermute | solution.py:53
  51.4 1.7 %collective-permute-start.14 = (f32[2,16,512]{2,1,0:T(8,128)S(1)}, f32[2,16,512]{2,1,0:T(8,128)S(1)}, u32[]{:S(2)}, u32[]{:S(2)}) collective-permute-start(f32[2,16,512]{2,1,0:T(8,128)S(1)} %add_add_fusion.2), channel_id=1, source_target_pairs={{0,1},{1,0},{2,3},{3,2},{4,5},{5,4},{6,7},{7,6},{8,9},{9,8},{10,11... | collective-permute-start | bytes 196616 | tf_op jit(solution)/shard_map/ppermute | solution.py:57
  57.2 1.5 %collective-permute-start.17 = (f32[2,16,256]{2,1,0:T(8,128)S(1)}, f32[2,16,256]{2,1,0:T(8,128)S(1)}, u32[]{:S(2)}, u32[]{:S(2)}) collective-permute-start(f32[2,16,256]{2,1,0:T(8,128)S(1)} %get-tuple-element.318), channel_id=1, source_target_pairs={{0,1},{1,0},{2,3},{3,2},{4,5},{5,4},{6,7},{7,6},{8,9},{9,8},{10,11... | collective-permute-start | bytes 98312 | tf_op jit(solution)/shard_map/ppermute | solution.py:53
  59.6 1.7 %collective-permute-start.24 = (f32[2,16,512]{2,1,0:T(8,128)S(1)}, f32[2,16,512]{2,1,0:T(8,128)S(1)}, u32[]{:S(2)}, u32[]{:S(2)}) collective-permute-start(f32[2,16,512]{2,1,0:T(8,128)S(1)} %get-tuple-element.323), channel_id=1, source_target_pairs={{0,1},{1,0},{2,3},{3,2},{4,5},{5,4},{6,7},{7,6},{8,9},{9,8},{10,11... | collective-permute-start | bytes 196616 | tf_op jit(solution)/shard_map/ppermute | solution.py:53
  60.4 2.1 %collective-permute-start.21 = (f32[2,16,256]{2,1,0:T(8,128)S(1)}, f32[2,16,256]{2,1,0:T(8,128)S(1)}, u32[]{:S(2)}, u32[]{:S(2)}) collective-permute-start(f32[2,16,256]{2,1,0:T(8,128)S(1)} %get-tuple-element.320), channel_id=1, source_target_pairs={{0,1},{1,0},{2,3},{3,2},{4,70},{5,71},{6,7},{7,6},{8,9},{9,8},{10,... | collective-permute-start | bytes 98312 | tf_op jit(solution)/shard_map/ppermute | solution.py:53
  61.4 1.4 %collective-permute-start.25 = (f32[2,16,512]{2,1,0:T(8,128)S(1)}, f32[2,16,512]{2,1,0:T(8,128)S(1)}, u32[]{:S(2)}, u32[]{:S(2)}) collective-permute-start(f32[2,16,512]{2,1,0:T(8,128)S(1)} %add.199), channel_id=1, source_target_pairs={{0,1},{1,0},{2,3},{3,2},{4,5},{5,4},{6,7},{7,6},{8,9},{9,8},{10,11... | collective-permute-start | bytes 196616 | tf_op jit(solution)/shard_map/ppermute | solution.py:57
  62.1 2.0 %collective-permute-start.20 = (f32[2,16,512]{2,1,0:T(8,128)S(1)}, f32[2,16,512]{2,1,0:T(8,128)S(1)}, u32[]{:S(2)}, u32[]{:S(2)}) collective-permute-start(f32[2,16,512]{2,1,0:T(8,128)S(1)} %get-tuple-element.321), channel_id=1, source_target_pairs={{0,1},{1,0},{2,6},{3,7},{4,5},{5,4},{6,2},{7,3},{8,9},{9,8},{10,14... | collective-permute-start | bytes 196616 | tf_op jit(solution)/shard_map/ppermute | solution.py:53
  62.5 1.6 %collective-permute-start.22 = (f32[2,16,512]{2,1,0:T(8,128)S(1)}, f32[2,16,512]{2,1,0:T(8,128)S(1)}, u32[]{:S(2)}, u32[]{:S(2)}) collective-permute-start(f32[2,16,512]{2,1,0:T(8,128)S(1)} %get-tuple-element.322), channel_id=1, source_target_pairs={{0,1},{1,0},{2,4},{3,5},{4,2},{5,3},{6,7},{7,6},{8,9},{9,8},{10,12... | collective-permute-start | bytes 196616 | tf_op jit(solution)/shard_map/ppermute | solution.py:53
  67.3 36.7 %collective-permute-start.30 = (f32[2,16,192]{2,1,0:T(8,128)S(1)}, f32[2,16,192]{2,1,0:T(8,128)S(1)}, u32[]{:S(2)}, u32[]{:S(2)}) collective-permute-start(f32[2,16,192]{2,1,0:T(8,128)S(1)} %pad_maximum_fusion.78), channel_id=1, source_target_pairs={{0,6},{2,0},{4,2},{6,4},{1,7},{3,1},{5,3},{7,5},{8,14},{10,8},{12,... | collective-permute-start | bytes 73736 | tf_op jit(solution)/shard_map/ppermute | solution.py:176
  99.0 6.7 %collective-permute-start.31 = (f32[2,16,192]{2,1,0:T(8,128)S(1)}, f32[2,16,192]{2,1,0:T(8,128)S(1)}, u32[]{:S(2)}, u32[]{:S(2)}) collective-permute-start(f32[2,16,192]{2,1,0:T(8,128)S(1)} %pad_maximum_fusion.78), channel_id=1, source_target_pairs={{0,4},{2,6},{4,0},{6,2},{1,5},{3,7},{5,1},{7,3},{8,12},{10,14},{12... | collective-permute-start | bytes 73736 | tf_op jit(solution)/shard_map/ppermute | solution.py:176
  103.9 5.1 %collective-permute-start.29 = (f32[2,16,192]{2,1,0:T(8,128)S(1)}, f32[2,16,192]{2,1,0:T(8,128)S(1)}, u32[]{:S(2)}, u32[]{:S(2)}) collective-permute-start(f32[2,16,192]{2,1,0:T(8,128)S(1)} %pad_maximum_fusion.78), channel_id=1, source_target_pairs={{0,2},{2,4},{4,6},{6,0},{1,3},{3,5},{5,7},{7,1},{8,10},{10,12},{12... | collective-permute-start | bytes 73736 | tf_op jit(solution)/shard_map/ppermute | solution.py:176
  109.2 4.3 %collective-permute-start.33 = (f32[2,80,64]{1,2,0:T(8,128)S(1)}, f32[2,80,64]{1,2,0:T(8,128)S(1)}, u32[]{:S(2)}, u32[]{:S(2)}) collective-permute-start(f32[2,80,64]{1,2,0:T(8,128)S(1)} %maximum_maximum_fusion.1), channel_id=1, source_target_pairs={{0,96},{32,0},{64,32},{96,64},{1,97},{33,1},{65,33},{97,65},{2,98}... | collective-permute-start | bytes 122888 | tf_op jit(solution)/shard_map/ppermute | solution.py:180
  109.3 6.0 %collective-permute-start.34 = (f32[2,80,64]{1,2,0:T(8,128)S(1)}, f32[2,80,64]{1,2,0:T(8,128)S(1)}, u32[]{:S(2)}, u32[]{:S(2)}) collective-permute-start(f32[2,80,64]{1,2,0:T(8,128)S(1)} %maximum_maximum_fusion.1), channel_id=1, source_target_pairs={{0,64},{32,96},{64,0},{96,32},{1,65},{33,97},{65,1},{97,33},{2,66}... | collective-permute-start | bytes 122888 | tf_op jit(solution)/shard_map/ppermute | solution.py:180
  109.6 6.7 %collective-permute-start.32 = (f32[2,80,64]{1,2,0:T(8,128)S(1)}, f32[2,80,64]{1,2,0:T(8,128)S(1)}, u32[]{:S(2)}, u32[]{:S(2)}) collective-permute-start(f32[2,80,64]{1,2,0:T(8,128)S(1)} %maximum_maximum_fusion.1), channel_id=1, source_target_pairs={{0,32},{32,64},{64,96},{96,0},{1,33},{33,65},{65,97},{97,1},{2,34}... | collective-permute-start | bytes 122888 | tf_op jit(solution)/shard_map/ppermute | solution.py:180
  (36 other events, 88.1 us)

commit v5 on v4

--- a/solution.py
+++ b/solution.py
@@ -99,11 +99,9 @@
     lower_half = lax.dynamic_slice_in_dim(lower_inverse, c * half, half, 1)
     upper_half = lax.dynamic_slice_in_dim(upper_inverse, c * half, half, 1)
 
-    inverse = jnp.where(x == (z + 3) % SIDE, lower_half, upper_half)
+    inverse = jnp.where(jnp.where(z == 0, x != 1, x == z - 1), lower_half, upper_half)
     left, right = factor[:, :, :piece], factor[:, :, piece:]
     packed = jnp.concatenate([left, right, inverse, krylov_block, basis], 1)
-    packed, krylov_block, lower_half = lax.optimization_barrier((packed, krylov_block, lower_half))
-    lead = apply_rows(krylov_block, lower_half)
     pieces = [packed] + [turn_y(packed, d) for d in (1, 3, 2)]
     pieces = [pieces[0], pieces[1], pieces[3], pieces[2]]
     tall = jnp.concatenate([jnp.concatenate([p[:, :piece], p[:, piece:half]], 2) for p in pieces], 1)
@@ -115,12 +113,11 @@
     high = lax.dynamic_index_in_dim(basis_all, (2 * c + 1 - y) % SIDE, 0, False)
     basis_half = jnp.concatenate([low, high], 2)
 
-    lead_parts = [turn_y(lead, d) for d in (1, 3, 2)]
-    y0 = lead + lead_parts[0] + lead_parts[1] + lead_parts[2]
     plane = jnp.concatenate([basis_all[d] for d in every], 2)
     gram = herm_rows(plane, plane)
 
     empty = jnp.zeros((2, nvec, half), jnp.float32)
+    small = jnp.zeros((2, nvec, nb), jnp.float32)
     blank = jnp.zeros((2, nvec, tile), jnp.float32)
 
     def product(places, vectors):
@@ -134,10 +131,15 @@
 
         return lax.cond(here(place), run, lambda r, a, o, w: empty, right, acc, other, rows)
 
-    def widen(value):
-        return jnp.concatenate([value, value], 2)
-
-    acc0 = product(((1, 0), (2, 0), (3, 0)), hop(y0, {(0, 0): (1, 0), (0, 1): (2, 0), (0, 3): (3, 0)}))
+    def share(value, place):
+        part = lax.cond(here(place), herm_rows, lambda v, w: small, value, basis_half)
+        return jnp.concatenate([part, gram], 1)
+
+    starts = ((0, 0), (0, 2), (0, 3))
+    y0 = lax.cond(here(*starts), apply_rows, lambda v, w: empty, given, rows)
+    arrived = hop(y0, {(0, 0): (1, 0), (0, 2): (2, 0), (0, 3): (3, 0)})
+    arrived, gram = lax.optimization_barrier((arrived, gram))
+    acc0 = product(((1, 0), (2, 0), (3, 0)), arrived)
     y1 = finish((1, 0), given, acc0)
     near1 = hop(y1, {(1, 0): (2, 1)})
     early1 = hop(acc0, {(2, 0): (2, 1), (3, 0): (3, 2)})
@@ -147,42 +149,50 @@
     held1 = early1 + hop(product(((3, 1),), far1), {(3, 1): (3, 2)})
     y3 = finish((3, 2), given, held1 + product(((3, 2),), near2))
 
-    moved = hop(y1 + y2 + y3, {(1, 0): (1, 2), (2, 1): (2, 3), (3, 2): (3, 3)})
-    back = jnp.where(z == 0, y0, moved)
+    back = hop(y0 + y1 + y2 + y3, {(0, 0): (0, 1), (1, 0): (1, 2), (2, 1): (2, 3), (3, 2): (3, 3)})
     solved = rotated(in_order(back, swap(back)))
 
     x3 = lax.cond(here((3, 3)), apply_rows, lambda v, w: empty, solved, rows)
     near3 = hop(x3, {(3, 3): (2, 3)})
+    sent3 = hop(share(x3, (3, 3)), {(3, 3): (0, 1)})
     x2 = finish((2, 3), solved, product(((2, 3),), near3))
     far3 = hop(x3, {(3, 3): (1, 3)})
     side1 = hop(product(((1, 3),), far3), {(1, 3): (1, 2)})
     near4 = hop(x2 + x3, {(2, 3): (1, 2), (3, 3): (0, 3)})
     far4 = hop(x2, {(2, 3): (0, 2)})
+    sent2 = hop(share(x2, (2, 3)), {(2, 3): (0, 1)})
     side0 = hop(product(((0, 3),), near4), {(0, 3): (0, 1)})
     x1 = finish((1, 2), solved, side1 + product(((1, 2),), near4))
     near5 = hop(x1, {(1, 2): (0, 1)})
+    sent1 = hop(share(x1, (1, 2)), {(1, 2): (0, 1)})
     held3 = side0 + hop(product(((0, 2),), far4), {(0, 2): (0, 1)})
     x0 = finish((0, 1), solved, held3 + product(((0, 1),), near5))
 
     found = x0 + x1 + x2 + x3
-    share = herm_rows(found, basis_half)
-    both = jnp.concatenate([found, share], 2)
+    sums = share(x0, (0, 1)) + (sent1 + sent2 + sent3)
+    both = jnp.concatenate([found, sums[:, :nvec]], 2)
     other = swap(both)
-    share = share + other[:, :, half:]
+    first = sums[:, :nvec] + other[:, :, half:]
+    coeffs = 2.0 * first - combine_rows(first, sums[:, nvec:])
     chosen = jnp.where((y < 2) == (c == 0), found, other[:, :, :half])
     mine = jnp.where(y % 2 == 0, chosen[:, :, :piece], chosen[:, :, piece:])
-    message = jnp.concatenate([mine, share], 2)
-    shifts = [[(i, (i + d) % SIDE) for i in every] for d in (1, 3, 2)]
-    across = [lax.ppermute(message, "x", s) for s in shifts]
-    message = message + across[0] + across[1] + across[2]
-    own_rows = message[:, :, :piece]
-    sums = jnp.concatenate([message[:, :, piece:], gram], 1)
-    planes = [lax.ppermute(sums, "z", s) for s in shifts]
-    sums = sums + planes[0] + planes[1] + planes[2]
-    first, gram = sums[:, :nvec], sums[:, nvec:]
-    coeffs = 2.0 * first - combine_rows(first, gram)
-    projected = own_rows - combine_rows(coeffs, basis)
-    return projected, jnp.swapaxes(coeffs, 1, 2)
+    message = jnp.concatenate([mine, coeffs], 2)
+    columns = (1, 2, 3, 3)
+    column = jnp.where(z == 0, 1, jnp.where(z == 1, 2, 3))
+    for d in (1, 3, 2):
+        landed = hop(message, {(a, columns[a]): (a, (columns[a] + d) % SIDE) for a in every})
+        if d == 1:
+            chain = jnp.where(x == column, message, landed)
+        else:
+            chain = jnp.where(x == (column + d) % SIDE, landed, chain)
+    own_rows = chain[:, :, :piece]
+    coeffs = chain[:, :, piece:]
+    total = coeffs
+    for a in (1, 3, 2):
+        landed = hop(coeffs, {(0, b): (a, b) for b in every})
+        total = jnp.where(z == a, landed, total)
+    projected = own_rows - combine_rows(total, basis)
+    return projected, jnp.swapaxes(total, 1, 2)
 
 
 def solution(mesh):

time: 119 us -> 121 us (1.017)
  the two profiles are of different devices: /device:TPU:16 before, /device:TPU:2 now
where the time goes in v5:
time: 121 us
  waiting for transfers between devices  59.4 us (49%)
  starting transfers between devices  48.2 us (40%)
  local copies, waits for them, and re-layouts  6.26 us (5%)
  matrix products  3.04 us (3%)
  other arithmetic  2.24 us (2%)
  between operations  1.39 us (1%)
    ppermute x27, waiting for transfers between devices, move(): return lax.ppermute(value, AXES, pairs)  54.6 us
    ppermute x27, starting transfers between devices, move(): return lax.ppermute(value, AXES, pairs)  47.1 us
    ppermute x8, waiting for transfers between devices, swap(): return lax.ppermute(value, 'c', [(0, 1), (1, 0)])  4.74 us
    unnamed x21, local copies, waits for them, and re-layouts  2.7 us
    dot_general x8, matrix products, dot_nt(): lax.dot_general(left, right, (((1,), (1,)), ((), ())), precision=precisio...  2.47 us
  transfers between devices with their start and end apart: 35, of which 22 were waited for; matrix products, arithmetic and copies ran while one was open for 3% of the time, Pallas kernels for 0%

profile of v5, /device:TPU:2, one launch (start us, length us, event | category | flops | bytes accessed | tf_op | source)
XLA Modules:
  0.0 120.8 jit_solution(1638300569322217626)
XLA Ops:
  1.7 1.1 constant_dynamic-update-slice_fusion.2
  2.8 1.6 %collective-permute-start.2 = (f32[2,592,128]{2,1,0:T(8,128)S(1)}, f32[2,592,128]{2,1,0:T(8,128)S(1)}, u32[]{:S(2)}, u32[]{:S(2)}) collective-permute-start(f32[2,592,128]{2,1,0:T(8,128)S(1)} %constant_dynamic-update-slice_fusion), channel_id=1, source_target_pairs={{0,8},{1,9},{2,10},{3,11},{4,12},{5,13},{6,14},{7,15},{8,16},{9,17... | collective-permute-start | bytes 1818632 | tf_op jit(solution)/shard_map/ppermute | solution.py:53
  4.5 2.9 %collective-permute-start.1 = (f32[2,592,128]{2,1,0:T(8,128)S(1)}, f32[2,592,128]{2,1,0:T(8,128)S(1)}, u32[]{:S(2)}, u32[]{:S(2)}) collective-permute-start(f32[2,592,128]{2,1,0:T(8,128)S(1)} %constant_dynamic-update-slice_fusion), channel_id=1, source_target_pairs={{0,16},{1,17},{2,18},{3,19},{4,20},{5,21},{6,22},{7,23},{8,24},{9,... | collective-permute-start | bytes 1818632 | tf_op jit(solution)/shard_map/ppermute | solution.py:53
  7.4 1.3 %collective-permute-start = (f32[2,592,128]{2,1,0:T(8,128)S(1)}, f32[2,592,128]{2,1,0:T(8,128)S(1)}, u32[]{:S(2)}, u32[]{:S(2)}) collective-permute-start(f32[2,592,128]{2,1,0:T(8,128)S(1)} %constant_dynamic-update-slice_fusion), channel_id=1, source_target_pairs={{0,24},{1,25},{2,26},{3,27},{4,28},{5,29},{6,30},{7,31},{8,0},{9,1... | collective-permute-start | bytes 1818632 | tf_op jit(solution)/shard_map/ppermute | solution.py:53
  8.7 10.9 %collective-permute-done.2 = f32[2,592,128]{2,1,0:T(8,128)S(1)} collective-permute-done((f32[2,592,128]{2,1,0:T(8,128)S(1)}, f32[2,592,128]{2,1,0:T(8,128)S(1)}, u32[]{:S(2)}, u32[]{:S(2)}) %collective-permute-start.2) | collective-permute-done | bytes 606240 | tf_op jit(solution)/shard_map/ppermute | solution.py:53
  19.6 14.2 %collective-permute-done.1 = f32[2,592,128]{2,1,0:T(8,128)S(1)} collective-permute-done((f32[2,592,128]{2,1,0:T(8,128)S(1)}, f32[2,592,128]{2,1,0:T(8,128)S(1)}, u32[]{:S(2)}, u32[]{:S(2)}) %collective-permute-start.1) | collective-permute-done | bytes 606240 | tf_op jit(solution)/shard_map/ppermute | solution.py:53
  37.8 1.0 fusion.246
  41.2 1.0 collective-permute-done.6
  44.3 1.0 collective-permute-done.10
  45.6 1.1 collective-permute-done.11
  46.7 3.0 %collective-permute-start.12 = (f32[2,16,256]{2,1,0:T(8,128)S(1)}, f32[2,16,256]{2,1,0:T(8,128)S(1)}, u32[]{:S(2)}, u32[]{:S(2)}) collective-permute-start(f32[2,16,256]{2,1,0:T(8,128)S(1)} %add_add_fusion.3), channel_id=1, source_target_pairs={{0,2},{1,3},{2,0},{3,1},{4,5},{5,4},{6,7},{7,6},{8,10},{9,11},{10,... | collective-permute-start | bytes 98312 | tf_op jit(solution)/shard_map/ppermute | solution.py:53
  49.7 1.9 %collective-permute-done.12 = f32[2,16,256]{2,1,0:T(8,128)S(1)} collective-permute-done((f32[2,16,256]{2,1,0:T(8,128)S(1)}, f32[2,16,256]{2,1,0:T(8,128)S(1)}, u32[]{:S(2)}, u32[]{:S(2)}) %collective-permute-start.12) | collective-permute-done | bytes 32800 | tf_op jit(solution)/shard_map/ppermute | solution.py:53
  51.6 1.2 collective-permute-done.13
  53.2 1.1 collective-permute-done.14
  57.7 30.6 %collective-permute-start.17 = (f32[2,16,512]{2,1,0:T(8,128)S(1)}, f32[2,16,512]{2,1,0:T(8,128)S(1)}, u32[]{:S(2)}, u32[]{:S(2)}) collective-permute-start(f32[2,16,512]{2,1,0:T(8,128)S(1)} %get-tuple-element.374), channel_id=1, source_target_pairs={{0,1},{1,0},{2,6},{3,7},{4,5},{5,4},{6,2},{7,3},{8,9},{9,8},{10,14... | collective-permute-start | bytes 196616 | tf_op jit(solution)/shard_map/ppermute | solution.py:53
  88.3 1.7 %collective-permute-start.19 = (f32[2,16,512]{2,1,0:T(8,128)S(1)}, f32[2,16,512]{2,1,0:T(8,128)S(1)}, u32[]{:S(2)}, u32[]{:S(2)}) collective-permute-start(f32[2,16,512]{2,1,0:T(8,128)S(1)} %get-tuple-element.375), channel_id=1, source_target_pairs={{0,1},{1,0},{2,4},{3,5},{4,2},{5,3},{6,7},{7,6},{8,9},{9,8},{10,12... | collective-permute-start | bytes 196616 | tf_op jit(solution)/shard_map/ppermute | solution.py:53
  90.0 1.2 collective-permute-start.23
  91.3 3.6 %collective-permute-done.23 = f32[2,16,256]{2,1,0:T(8,128)S(1)} collective-permute-done((f32[2,16,256]{2,1,0:T(8,128)S(1)}, f32[2,16,256]{2,1,0:T(8,128)S(1)}, u32[]{:S(2)}, u32[]{:S(2)}) %collective-permute-start.23) | collective-permute-done | bytes 32800 | tf_op jit(solution)/shard_map/ppermute | solution.py:53
  98.3 8.0 %collective-permute-done.26 = f32[2,80,64]{2,1,0:T(8,128)S(1)} collective-permute-done((f32[2,80,64]{2,1,0:T(8,128)S(1)}, f32[2,80,64]{2,1,0:T(8,128)S(1)}, u32[]{:S(2)}, u32[]{:S(2)}) %collective-permute-start.26) | collective-permute-done | bytes 40992 | tf_op jit(solution)/shard_map/ppermute | solution.py:53
  106.5 1.2 collective-permute-done.28
  108.4 3.7 %collective-permute-done.31 = f32[2,16,192]{2,1,0:T(8,128)S(1)} collective-permute-done((f32[2,16,192]{2,1,0:T(8,128)S(1)}, f32[2,16,192]{2,1,0:T(8,128)S(1)}, u32[]{:S(2)}, u32[]{:S(2)}) %collective-permute-start.31) | collective-permute-done | bytes 24608 | tf_op jit(solution)/shard_map/ppermute | solution.py:53
  112.2 1.6 %collective-permute-done.29 = f32[2,16,192]{2,1,0:T(8,128)S(1)} collective-permute-done((f32[2,16,192]{2,1,0:T(8,128)S(1)}, f32[2,16,192]{2,1,0:T(8,128)S(1)}, u32[]{:S(2)}, u32[]{:S(2)}) %collective-permute-start.29) | collective-permute-done | bytes 24608 | tf_op jit(solution)/shard_map/ppermute | solution.py:53
  114.1 3.5 %collective-permute-done.34 = f32[2,16,64]{2,1,0:T(8,128)S(1)} collective-permute-done((f32[2,16,64]{2,1,0:T(8,128)S(1)}, f32[2,16,64]{2,1,0:T(8,128)S(1)}, u32[]{:S(2)}, u32[]{:S(2)}) %collective-permute-start.34) | collective-permute-done | bytes 8224 | tf_op jit(solution)/shard_map/ppermute | solution.py:53
  117.6 1.3 %collective-permute-done.33 = f32[2,16,64]{2,1,0:T(8,128)S(1)} collective-permute-done((f32[2,16,64]{2,1,0:T(8,128)S(1)}, f32[2,16,64]{2,1,0:T(8,128)S(1)}, u32[]{:S(2)}, u32[]{:S(2)}) %collective-permute-start.33) | collective-permute-done | bytes 8224 | tf_op jit(solution)/shard_map/ppermute | solution.py:53
  (184 shorter events, 22.2 us)
Async XLA Ops:
  2.8 16.8 %collective-permute-start.2 = (f32[2,592,128]{2,1,0:T(8,128)S(1)}, f32[2,592,128]{2,1,0:T(8,128)S(1)}, u32[]{:S(2)}, u32[]{:S(2)}) collective-permute-start(f32[2,592,128]{2,1,0:T(8,128)S(1)} %constant_dynamic-update-slice_fusion), channel_id=1, source_target_pairs={{0,8},{1,9},{2,10},{3,11},{4,12},{5,13},{6,14},{7,15},{8,16},{9,17... | collective-permute-start | bytes 1818632 | tf_op jit(solution)/shard_map/ppermute | solution.py:53
  4.5 29.3 %collective-permute-start.1 = (f32[2,592,128]{2,1,0:T(8,128)S(1)}, f32[2,592,128]{2,1,0:T(8,128)S(1)}, u32[]{:S(2)}, u32[]{:S(2)}) collective-permute-start(f32[2,592,128]{2,1,0:T(8,128)S(1)} %constant_dynamic-update-slice_fusion), channel_id=1, source_target_pairs={{0,16},{1,17},{2,18},{3,19},{4,20},{5,21},{6,22},{7,23},{8,24},{9,... | collective-permute-start | bytes 1818632 | tf_op jit(solution)/shard_map/ppermute | solution.py:53
  7.4 26.4 %collective-permute-start = (f32[2,592,128]{2,1,0:T(8,128)S(1)}, f32[2,592,128]{2,1,0:T(8,128)S(1)}, u32[]{:S(2)}, u32[]{:S(2)}) collective-permute-start(f32[2,592,128]{2,1,0:T(8,128)S(1)} %constant_dynamic-update-slice_fusion), channel_id=1, source_target_pairs={{0,24},{1,25},{2,26},{3,27},{4,28},{5,29},{6,30},{7,31},{8,0},{9,1... | collective-permute-start | bytes 1818632 | tf_op jit(solution)/shard_map/ppermute | solution.py:53
  36.5 2.3 %collective-permute-start.3 = (f32[2,16,256]{2,1,0:T(8,128)S(1)}, f32[2,16,256]{2,1,0:T(8,128)S(1)}, u32[]{:S(2)}, u32[]{:S(2)}) collective-permute-start(f32[2,16,256]{2,1,0:T(8,128)S(1)} %get-tuple-element.363), channel_id=1, source_target_pairs={{0,32},{1,33},{2,3},{3,2},{4,64},{5,65},{6,96},{7,97},{8,40},{9,41... | collective-permute-start | bytes 98312 | tf_op jit(solution)/shard_map/ppermute | solution.py:53
  39.5 2.7 %collective-permute-start.5 = (f32[2,16,512]{2,1,0:T(8,128)}, f32[2,16,512]{2,1,0:T(8,128)S(1)}, u32[]{:S(2)}, u32[]{:S(2)}) collective-permute-start(f32[2,16,512]{2,1,0:T(8,128)} %get-tuple-element.364), channel_id=1, source_target_pairs={{0,1},{1,0},{2,3},{3,2},{4,5},{5,4},{6,7},{7,6},{8,9},{9,8},{10,11... | collective-permute-start | bytes 196616 | tf_op jit(solution)/shard_map/ppermute | solution.py:53
  42.2 1.8 %collective-permute-start.7 = (f32[2,16,512]{2,1,0:T(8,128)S(1)}, f32[2,16,512]{2,1,0:T(8,128)S(1)}, u32[]{:S(2)}, u32[]{:S(2)}) collective-permute-start(f32[2,16,512]{2,1,0:T(8,128)S(1)} %add.191), channel_id=1, source_target_pairs={{0,1},{1,0},{2,3},{3,2},{4,5},{5,4},{6,7},{7,6},{8,9},{9,8},{10,11... | collective-permute-start | bytes 196616 | tf_op jit(solution)/shard_map/ppermute | solution.py:57
  43.7 1.6 %collective-permute-start.9 = (f32[2,16,512]{2,1,0:T(8,128)S(1)}, f32[2,16,512]{2,1,0:T(8,128)S(1)}, u32[]{:S(2)}, u32[]{:S(2)}) collective-permute-start(f32[2,16,512]{2,1,0:T(8,128)S(1)} %get-tuple-element.368), channel_id=1, source_target_pairs={{0,1},{1,0},{2,3},{3,2},{4,5},{5,4},{6,7},{7,6},{8,9},{9,8},{10,11... | collective-permute-start | bytes 196616 | tf_op jit(solution)/shard_map/ppermute | solution.py:53
  46.7 4.9 %collective-permute-start.12 = (f32[2,16,256]{2,1,0:T(8,128)S(1)}, f32[2,16,256]{2,1,0:T(8,128)S(1)}, u32[]{:S(2)}, u32[]{:S(2)}) collective-permute-start(f32[2,16,256]{2,1,0:T(8,128)S(1)} %add_add_fusion.3), channel_id=1, source_target_pairs={{0,2},{1,3},{2,0},{3,1},{4,5},{5,4},{6,7},{7,6},{8,10},{9,11},{10,... | collective-permute-start | bytes 98312 | tf_op jit(solution)/shard_map/ppermute | solution.py:53
  54.2 1.7 %collective-permute-start.15 = (f32[2,16,512]{2,1,0:T(8,128)S(1)}, f32[2,16,512]{2,1,0:T(8,128)S(1)}, u32[]{:S(2)}, u32[]{:S(2)}) collective-permute-start(f32[2,16,512]{2,1,0:T(8,128)S(1)} %get-tuple-element.372), channel_id=1, source_target_pairs={{0,1},{1,0},{2,3},{3,2},{4,5},{5,4},{6,7},{7,6},{8,9},{9,8},{10,11... | collective-permute-start | bytes 196616 | tf_op jit(solution)/shard_map/ppermute | solution.py:57
  55.6 1.7 %collective-permute-start.21 = (f32[2,16,512]{2,1,0:T(8,128)S(1)}, f32[2,16,512]{2,1,0:T(8,128)S(1)}, u32[]{:S(2)}, u32[]{:S(2)}) collective-permute-start(f32[2,16,512]{2,1,0:T(8,128)S(1)} %get-tuple-element.376), channel_id=1, source_target_pairs={{0,1},{1,0},{2,3},{3,2},{4,5},{5,4},{6,7},{7,6},{8,9},{9,8},{10,11... | collective-permute-start | bytes 196616 | tf_op jit(solution)/shard_map/ppermute | solution.py:53
  56.4 32.0 %collective-permute-start.18 = (f32[2,16,256]{2,1,0:T(8,128)S(1)}, f32[2,16,256]{2,1,0:T(8,128)S(1)}, u32[]{:S(2)}, u32[]{:S(2)}) collective-permute-start(f32[2,16,256]{2,1,0:T(8,128)S(1)} %get-tuple-element.373), channel_id=1, source_target_pairs={{0,1},{1,0},{2,3},{3,2},{4,70},{5,71},{6,7},{7,6},{8,9},{9,8},{10,... | collective-permute-start | bytes 98312 | tf_op jit(solution)/shard_map/ppermute | solution.py:53
  57.3 32.7 %collective-permute-start.22 = (f32[2,16,512]{2,1,0:T(8,128)S(1)}, f32[2,16,512]{2,1,0:T(8,128)S(1)}, u32[]{:S(2)}, u32[]{:S(2)}) collective-permute-start(f32[2,16,512]{2,1,0:T(8,128)S(1)} %add.199), channel_id=1, source_target_pairs={{0,1},{1,0},{2,3},{3,2},{4,5},{5,4},{6,7},{7,6},{8,9},{9,8},{10,11... | collective-permute-start | bytes 196616 | tf_op jit(solution)/shard_map/ppermute | solution.py:57
  57.7 38.0 %collective-permute-start.17 = (f32[2,16,512]{2,1,0:T(8,128)S(1)}, f32[2,16,512]{2,1,0:T(8,128)S(1)}, u32[]{:S(2)}, u32[]{:S(2)}) collective-permute-start(f32[2,16,512]{2,1,0:T(8,128)S(1)} %get-tuple-element.374), channel_id=1, source_target_pairs={{0,1},{1,0},{2,6},{3,7},{4,5},{5,4},{6,2},{7,3},{8,9},{9,8},{10,14... | collective-permute-start | bytes 196616 | tf_op jit(solution)/shard_map/ppermute | solution.py:53
  88.3 7.3 %collective-permute-start.19 = (f32[2,16,512]{2,1,0:T(8,128)S(1)}, f32[2,16,512]{2,1,0:T(8,128)S(1)}, u32[]{:S(2)}, u32[]{:S(2)}) collective-permute-start(f32[2,16,512]{2,1,0:T(8,128)S(1)} %get-tuple-element.375), channel_id=1, source_target_pairs={{0,1},{1,0},{2,4},{3,5},{4,2},{5,3},{6,7},{7,6},{8,9},{9,8},{10,12... | collective-permute-start | bytes 196616 | tf_op jit(solution)/shard_map/ppermute | solution.py:53
  90.0 4.9 %collective-permute-start.23 = (f32[2,16,256]{2,1,0:T(8,128)S(1)}, f32[2,16,256]{2,1,0:T(8,128)S(1)}, u32[]{:S(2)}, u32[]{:S(2)}) collective-permute-start(f32[2,16,256]{2,1,0:T(8,128)S(1)} %get-tuple-element.378), channel_id=1, source_target_pairs={{0,1},{1,0},{2,36},{3,37},{4,5},{5,4},{6,7},{7,6},{8,9},{9,8},{10,... | collective-permute-start | bytes 98312 | tf_op jit(solution)/shard_map/ppermute | solution.py:53
  95.8 10.5 %collective-permute-start.26 = (f32[2,80,64]{2,1,0:T(8,128)S(1)}, f32[2,80,64]{2,1,0:T(8,128)S(1)}, u32[]{:S(2)}, u32[]{:S(2)}) collective-permute-start(f32[2,80,64]{2,1,0:T(8,128)S(1)} %get-tuple-element.350), channel_id=1, source_target_pairs={{0,1},{1,0},{2,70},{3,71},{4,5},{5,4},{6,7},{7,6},{8,9},{9,8},{10,... | collective-permute-start | bytes 122888 | tf_op jit(solution)/shard_map/ppermute | solution.py:53
  95.9 10.4 %collective-permute-start.25 = (f32[2,80,64]{2,1,0:T(8,128)S(1)}, f32[2,80,64]{2,1,0:T(8,128)S(1)}, u32[]{:S(2)}, u32[]{:S(2)}) collective-permute-start(f32[2,80,64]{2,1,0:T(8,128)S(1)} %get-tuple-element.351), channel_id=1, source_target_pairs={{0,1},{1,0},{2,36},{3,37},{4,5},{5,4},{6,7},{7,6},{8,9},{9,8},{10,... | collective-permute-start | bytes 122888 | tf_op jit(solution)/shard_map/ppermute | solution.py:53
  96.8 9.6 %collective-permute-start.27 = (f32[2,80,64]{2,1,0:T(8,128)S(1)}, f32[2,80,64]{2,1,0:T(8,128)S(1)}, u32[]{:S(2)}, u32[]{:S(2)}) collective-permute-start(f32[2,80,64]{2,1,0:T(8,128)S(1)} %get-tuple-element.352), channel_id=1, source_target_pairs={{0,1},{1,0},{2,102},{3,103},{4,5},{5,4},{6,7},{7,6},{8,9},{9,8},{1... | collective-permute-start | bytes 122888 | tf_op jit(solution)/shard_map/ppermute | solution.py:53
  108.1 4.0 %collective-permute-start.31 = (f32[2,16,192]{2,1,0:T(8,128)S(1)}, f32[2,16,192]{2,1,0:T(8,128)S(1)}, u32[]{:S(2)}, u32[]{:S(2)}) collective-permute-start(f32[2,16,192]{2,1,0:T(8,128)S(1)} %pad_maximum_fusion.102), channel_id=1, source_target_pairs={{0,1},{1,0},{2,4},{3,5},{4,2},{5,3},{6,7},{7,6},{8,9},{9,8},{10,12... | collective-permute-start | bytes 73736 | tf_op jit(solution)/shard_map/ppermute | solution.py:53
  108.2 4.0 %collective-permute-start.30 = (f32[2,16,192]{2,1,0:T(8,128)S(1)}, f32[2,16,192]{2,1,0:T(8,128)S(1)}, u32[]{:S(2)}, u32[]{:S(2)}) collective-permute-start(f32[2,16,192]{2,1,0:T(8,128)S(1)} %pad_maximum_fusion.102), channel_id=1, source_target_pairs={{0,2},{1,3},{2,0},{3,1},{4,5},{5,4},{6,7},{7,6},{8,10},{9,11},{10,... | collective-permute-start | bytes 73736 | tf_op jit(solution)/shard_map/ppermute | solution.py:53
  108.3 5.5 %collective-permute-start.29 = (f32[2,16,192]{2,1,0:T(8,128)S(1)}, f32[2,16,192]{2,1,0:T(8,128)S(1)}, u32[]{:S(2)}, u32[]{:S(2)}) collective-permute-start(f32[2,16,192]{2,1,0:T(8,128)S(1)} %pad_maximum_fusion.102), channel_id=1, source_target_pairs={{0,1},{1,0},{2,6},{3,7},{4,5},{5,4},{6,2},{7,3},{8,9},{9,8},{10,14... | collective-permute-start | bytes 73736 | tf_op jit(solution)/shard_map/ppermute | solution.py:53
  113.8 3.8 %collective-permute-start.34 = (f32[2,16,64]{2,1,0:T(8,128)S(1)}, f32[2,16,64]{2,1,0:T(8,128)S(1)}, u32[]{:S(2)}, u32[]{:S(2)}) collective-permute-start(f32[2,16,64]{2,1,0:T(8,128)S(1)} %slice.854), channel_id=1, source_target_pairs={{0,32},{1,33},{2,34},{3,35},{4,36},{5,37},{6,38},{7,39},{8,40},{9,... | collective-permute-start | bytes 24584 | tf_op jit(solution)/shard_map/ppermute | solution.py:53
  113.9 5.0 %collective-permute-start.33 = (f32[2,16,64]{2,1,0:T(8,128)S(1)}, f32[2,16,64]{2,1,0:T(8,128)S(1)}, u32[]{:S(2)}, u32[]{:S(2)}) collective-permute-start(f32[2,16,64]{2,1,0:T(8,128)S(1)} %slice.854), channel_id=1, source_target_pairs={{0,96},{1,97},{2,98},{3,99},{4,100},{5,101},{6,102},{7,103},{8,104... | collective-permute-start | bytes 24584 | tf_op jit(solution)/shard_map/ppermute | solution.py:53
  114.0 5.3 %collective-permute-start.32 = (f32[2,16,64]{2,1,0:T(8,128)S(1)}, f32[2,16,64]{2,1,0:T(8,128)S(1)}, u32[]{:S(2)}, u32[]{:S(2)}) collective-permute-start(f32[2,16,64]{2,1,0:T(8,128)S(1)} %slice.854), channel_id=1, source_target_pairs={{0,64},{1,65},{2,66},{3,67},{4,68},{5,69},{6,70},{7,71},{8,72},{9,... | collective-permute-start | bytes 24584 | tf_op jit(solution)/shard_map/ppermute | solution.py:53
  (24 other events, 41.2 us)

commit v6 on v5

--- a/solution.py
+++ b/solution.py
@@ -61,9 +61,15 @@
     return move(value, lambda z, y, x, c: (z, (y - offset) % SIDE, x, c))
 
 
-def hop(value, routes):
+def hop(value, routes, idle=()):
     paired = dict(routes)
-    paired.update({there: start for start, there in routes.items()})
+    spare = dict(zip(routes.values(), idle))
+    for start, there in routes.items():
+        if there in spare:
+            paired[there] = spare[there]
+            paired[spare[there]] = start
+        else:
+            paired[there] = start
 
     def target(z, y, x, c):
         there = paired.get((z, x))
@@ -131,6 +137,9 @@
 
         return lax.cond(here(place), run, lambda r, a, o, w: empty, right, acc, other, rows)
 
+    def after(value, other):
+        return lax.optimization_barrier((value, other))[0]
+
     def share(value, place):
         part = lax.cond(here(place), herm_rows, lambda v, w: small, value, basis_half)
         return jnp.concatenate([part, gram], 1)
@@ -139,37 +148,44 @@
     y0 = lax.cond(here(*starts), apply_rows, lambda v, w: empty, given, rows)
     arrived = hop(y0, {(0, 0): (1, 0), (0, 2): (2, 0), (0, 3): (3, 0)})
     arrived, gram = lax.optimization_barrier((arrived, gram))
-    acc0 = product(((1, 0), (2, 0), (3, 0)), arrived)
+    acc0 = product(((1, 0),), arrived)
     y1 = finish((1, 0), given, acc0)
     near1 = hop(y1, {(1, 0): (2, 1)})
-    early1 = hop(acc0, {(2, 0): (2, 1), (3, 0): (3, 2)})
     far1 = hop(y1, {(1, 0): (3, 1)})
+    near1, far1 = lax.optimization_barrier((near1, far1))
+    early1 = hop(product(((2, 0), (3, 0)), after(arrived, y1)), {(2, 0): (2, 1), (3, 0): (3, 2)}, ((2, 2), (1, 1)))
     y2 = finish((2, 1), given, early1 + product(((2, 1),), near1))
     near2 = hop(y2, {(2, 1): (3, 2)})
-    held1 = early1 + hop(product(((3, 1),), far1), {(3, 1): (3, 2)})
+    held1 = early1 + hop(product(((3, 1),), after(far1, y2)), {(3, 1): (3, 2)}, ((2, 2),))
     y3 = finish((3, 2), given, held1 + product(((3, 2),), near2))
 
+    sent1 = hop(after(gram, y1), {(1, 2): (0, 1)})
+    y3, sent1 = lax.optimization_barrier((y3, sent1))
     back = hop(y0 + y1 + y2 + y3, {(0, 0): (0, 1), (1, 0): (1, 2), (2, 1): (2, 3), (3, 2): (3, 3)})
     solved = rotated(in_order(back, swap(back)))
 
     x3 = lax.cond(here((3, 3)), apply_rows, lambda v, w: empty, solved, rows)
     near3 = hop(x3, {(3, 3): (2, 3)})
-    sent3 = hop(share(x3, (3, 3)), {(3, 3): (0, 1)})
+    far3 = hop(x3, {(3, 3): (1, 3)})
     x2 = finish((2, 3), solved, product(((2, 3),), near3))
-    far3 = hop(x3, {(3, 3): (1, 3)})
-    side1 = hop(product(((1, 3),), far3), {(1, 3): (1, 2)})
     near4 = hop(x2 + x3, {(2, 3): (1, 2), (3, 3): (0, 3)})
+    side1 = hop(product(((1, 3),), after(far3, x2)), {(1, 3): (1, 2)}, ((1, 1),))
     far4 = hop(x2, {(2, 3): (0, 2)})
-    sent2 = hop(share(x2, (2, 3)), {(2, 3): (0, 1)})
-    side0 = hop(product(((0, 3),), near4), {(0, 3): (0, 1)})
+    sent3 = hop(after(share(x3, (3, 3)), x2), {(3, 3): (0, 1)}, ((0, 0),))
+    sent2 = hop(share(x2, (2, 3)), {(2, 3): (0, 1)}, ((1, 1),))
     x1 = finish((1, 2), solved, side1 + product(((1, 2),), near4))
-    near5 = hop(x1, {(1, 2): (0, 1)})
-    sent1 = hop(share(x1, (1, 2)), {(1, 2): (0, 1)})
-    held3 = side0 + hop(product(((0, 2),), far4), {(0, 2): (0, 1)})
+    x1, sent2, sent3 = lax.optimization_barrier((x1, sent2, sent3))
+    part1 = lax.cond(here((1, 2)), herm_rows, lambda v, w: small, x1, basis_half)
+    near5 = hop(jnp.concatenate([x1, part1], 2), {(1, 2): (0, 1)})
+    part1 = near5[:, :, half:]
+    side0 = hop(after(product(((0, 3),), near4), x1), {(0, 3): (0, 1)}, ((0, 0),))
+    held3 = side0 + hop(after(product(((0, 2),), far4), x1), {(0, 2): (0, 1)}, ((1, 1),))
+    sent = jnp.concatenate([part1 + sent2[:, :nvec] + sent3[:, :nvec], sent1 + sent2[:, nvec:] + sent3[:, nvec:]], 1)
+    near5 = near5[:, :, :half]
     x0 = finish((0, 1), solved, held3 + product(((0, 1),), near5))
 
     found = x0 + x1 + x2 + x3
-    sums = share(x0, (0, 1)) + (sent1 + sent2 + sent3)
+    sums = share(x0, (0, 1)) + sent
     both = jnp.concatenate([found, sums[:, :nvec]], 2)
     other = swap(both)
     first = sums[:, :nvec] + other[:, :, half:]

time: 121 us -> 108 us (0.89)
  starting transfers between devices: 48.2 us -> 32.5 us
  waiting for transfers between devices: 59.4 us -> 62.8 us
    ppermute x27, starting transfers between devices: 47.1 us -> 30.9 us  [move(): return lax.ppermute(value, AXES, pairs)]
    ppermute x8, waiting for transfers between devices: 4.74 us -> 6.9 us  [swap(): return lax.ppermute(value, 'c', [(0, 1), (1, 0)])]
    ppermute x27, waiting for transfers between devices: 54.6 us -> 55.9 us  [move(): return lax.ppermute(value, AXES, pairs)]
  transfers between devices with their start and end apart: 35 -> 35, of which waited for: 22 -> 27; matrix products, arithmetic and copies ran while one was open for 3% -> 2% of each run, Pallas kernels for 0% -> 0%
where the time goes in v6:
time: 108 us
  waiting for transfers between devices  62.8 us (58%)
  starting transfers between devices  32.5 us (30%)
  local copies, waits for them, and re-layouts  5.63 us (5%)
  matrix products  3.04 us (3%)
  other arithmetic  2.26 us (2%)
  between operations  1.41 us (1%)
    ppermute x27, waiting for transfers between devices, move(): return lax.ppermute(value, AXES, pairs)  55.9 us
    ppermute x27, starting transfers between devices, move(): return lax.ppermute(value, AXES, pairs)  30.9 us
    ppermute x8, waiting for transfers between devices, swap(): return lax.ppermute(value, 'c', [(0, 1), (1, 0)])  6.9 us
    unnamed x21, local copies, waits for them, and re-layouts  2.7 us
    dot_general x8, matrix products, dot_nt(): lax.dot_general(left, right, (((1,), (1,)), ((), ())), precision=precisio...  2.47 us
  transfers between devices with their start and end apart: 35, of which 27 were waited for; matrix products, arithmetic and copies ran while one was open for 2% of the time, Pallas kernels for 0%

profile of v6, /device:TPU:2, one launch (start us, length us, event | category | flops | bytes accessed | tf_op | source)
XLA Modules:
  0.0 107.9 jit_solution(9379196187159117864)
XLA Ops:
  1.7 1.1 %constant_dynamic-update-slice_fusion.2 = (f32[2,592,128]{2,1,0:T(8,128)S(1)}, f32[2,256,128]{2,1,0:T(8,128)S(1)}) fusion(f32[2,592,128]{2,1,0:T(8,128)S(1)} %slice_dynamic-update-slice_fusion, f32[2,512,128]{2,1,0:T(8,128)} %param.53, s32[]{:T(128)S(6)} %select_n.136, f32[2,512,128]{2,1,0:T(8,128)} %param.52, pred[]{:T(512)S(6)} %select_n.134), kind=kLoop, calls=%fused_computation.439 | loop fusion | flops 65536 | bytes 1048581
  2.8 1.6 %collective-permute-start.2 = (f32[2,592,128]{2,1,0:T(8,128)S(1)}, f32[2,592,128]{2,1,0:T(8,128)S(1)}, u32[]{:S(2)}, u32[]{:S(2)}) collective-permute-start(f32[2,592,128]{2,1,0:T(8,128)S(1)} %constant_dynamic-update-slice_fusion), channel_id=1, source_target_pairs={{0,8},{1,9},{2,10},{3,11},{4,12},{5,13},{6,14},{7,15},{8,16},{9,17... | collective-permute-start | bytes 1818632 | tf_op jit(solution)/shard_map/ppermute | solution.py:53
  4.5 2.9 %collective-permute-start.1 = (f32[2,592,128]{2,1,0:T(8,128)S(1)}, f32[2,592,128]{2,1,0:T(8,128)S(1)}, u32[]{:S(2)}, u32[]{:S(2)}) collective-permute-start(f32[2,592,128]{2,1,0:T(8,128)S(1)} %constant_dynamic-update-slice_fusion), channel_id=1, source_target_pairs={{0,16},{1,17},{2,18},{3,19},{4,20},{5,21},{6,22},{7,23},{8,24},{9,... | collective-permute-start | bytes 1818632 | tf_op jit(solution)/shard_map/ppermute | solution.py:53
  7.4 1.3 %collective-permute-start = (f32[2,592,128]{2,1,0:T(8,128)S(1)}, f32[2,592,128]{2,1,0:T(8,128)S(1)}, u32[]{:S(2)}, u32[]{:S(2)}) collective-permute-start(f32[2,592,128]{2,1,0:T(8,128)S(1)} %constant_dynamic-update-slice_fusion), channel_id=1, source_target_pairs={{0,24},{1,25},{2,26},{3,27},{4,28},{5,29},{6,30},{7,31},{8,0},{9,1... | collective-permute-start | bytes 1818632 | tf_op jit(solution)/shard_map/ppermute | solution.py:53
  8.7 10.9 %collective-permute-done.2 = f32[2,592,128]{2,1,0:T(8,128)S(1)} collective-permute-done((f32[2,592,128]{2,1,0:T(8,128)S(1)}, f32[2,592,128]{2,1,0:T(8,128)S(1)}, u32[]{:S(2)}, u32[]{:S(2)}) %collective-permute-start.2) | collective-permute-done | bytes 606240 | tf_op jit(solution)/shard_map/ppermute | solution.py:53
  19.6 14.2 %collective-permute-done.1 = f32[2,592,128]{2,1,0:T(8,128)S(1)} collective-permute-done((f32[2,592,128]{2,1,0:T(8,128)S(1)}, f32[2,592,128]{2,1,0:T(8,128)S(1)}, u32[]{:S(2)}, u32[]{:S(2)}) %collective-permute-start.1) | collective-permute-done | bytes 606240 | tf_op jit(solution)/shard_map/ppermute | solution.py:53
  37.8 1.0 fusion.257
  39.0 1.2 %collective-permute-done.4 = f32[2,16,512]{2,1,0:T(8,128)S(1)} collective-permute-done((f32[2,16,512]{2,1,0:T(8,128)S(1)}, f32[2,16,512]{2,1,0:T(8,128)S(1)}, u32[]{:S(2)}, u32[]{:S(2)}) %collective-permute-start.4) | collective-permute-done | bytes 65568 | tf_op jit(solution)/shard_map/ppermute | solution.py:57
  42.3 1.1 %collective-permute-done.8 = f32[2,16,512]{2,1,0:T(8,128)S(1)} collective-permute-done((f32[2,16,512]{2,1,0:T(8,128)S(1)}, f32[2,16,512]{2,1,0:T(8,128)S(1)}, u32[]{:S(2)}, u32[]{:S(2)}) %collective-permute-start.8) | collective-permute-done | bytes 65568 | tf_op jit(solution)/shard_map/ppermute | solution.py:57
  45.4 2.8 %collective-permute-start.12 = (f32[2,64,64]{2,1,0:T(8,128)S(1)}, f32[2,64,64]{2,1,0:T(8,128)S(1)}, u32[]{:S(2)}, u32[]{:S(2)}) collective-permute-start(f32[2,64,64]{2,1,0:T(8,128)S(1)} %pad_maximum_fusion.103), channel_id=1, source_target_pairs={{0,1},{1,0},{2,36},{3,37},{4,5},{5,4},{6,7},{7,6},{8,9},{9,8},{10,... | collective-permute-start | bytes 98312 | tf_op jit(solution)/shard_map/ppermute | solution.py:53
  48.2 2.4 %collective-permute-done.12 = f32[2,64,64]{2,1,0:T(8,128)S(1)} collective-permute-done((f32[2,64,64]{2,1,0:T(8,128)S(1)}, f32[2,64,64]{2,1,0:T(8,128)S(1)}, u32[]{:S(2)}, u32[]{:S(2)}) %collective-permute-start.12) | collective-permute-done | bytes 32800 | tf_op jit(solution)/shard_map/ppermute | solution.py:53
  50.7 3.9 %collective-permute-done.13 = f32[2,16,256]{2,1,0:T(8,128)S(1)} collective-permute-done((f32[2,16,256]{2,1,0:T(8,128)S(1)}, f32[2,16,256]{2,1,0:T(8,128)S(1)}, u32[]{:S(2)}, u32[]{:S(2)}) %collective-permute-start.13) | collective-permute-done | bytes 32800 | tf_op jit(solution)/shard_map/ppermute | solution.py:53
  54.6 1.2 %collective-permute-done.14 = f32[2,16,256]{2,1,0:T(8,128)S(1)} collective-permute-done((f32[2,16,256]{2,1,0:T(8,128)S(1)}, f32[2,16,256]{2,1,0:T(8,128)S(1)}, u32[]{:S(2)}, u32[]{:S(2)}) %collective-permute-start.14) | collective-permute-done | bytes 32800 | tf_op jit(solution)/shard_map/ppermute | solution.py:57
  57.4 1.1 collective-permute-done.16
  60.6 18.5 %collective-permute-start.21 = (f32[2,80,64]{2,1,0:T(8,128)S(1)}, f32[2,80,64]{2,1,0:T(8,128)S(1)}, u32[]{:S(2)}, u32[]{:S(2)}) collective-permute-start(f32[2,80,64]{2,1,0:T(8,128)S(1)} %get-tuple-element.399), channel_id=1, source_target_pairs={{0,1},{1,0},{2,34},{3,35},{4,5},{5,4},{6,7},{7,6},{8,9},{9,8},{10,... | collective-permute-start | bytes 122888 | tf_op jit(solution)/shard_map/ppermute | solution.py:53
  79.1 1.2 %collective-permute-done.24 = f32[2,16,256]{2,1,0:T(8,128)S(1)} collective-permute-done((f32[2,16,256]{2,1,0:T(8,128)S(1)}, f32[2,16,256]{2,1,0:T(8,128)S(1)}, u32[]{:S(2)}, u32[]{:S(2)}) %collective-permute-start.24) | collective-permute-done | bytes 32800 | tf_op jit(solution)/shard_map/ppermute | solution.py:53
  80.4 3.8 %collective-permute-done.22 = f32[2,80,64]{2,1,0:T(8,128)S(1)} collective-permute-done((f32[2,80,64]{2,1,0:T(8,128)S(1)}, f32[2,80,64]{2,1,0:T(8,128)S(1)}, u32[]{:S(2)}, u32[]{:S(2)}) %collective-permute-start.22) | collective-permute-done | bytes 40992 | tf_op jit(solution)/shard_map/ppermute | solution.py:53
  85.2 4.8 %collective-permute-done.26 = f32[2,16,320]{2,1,0:T(8,128)S(1)} collective-permute-done((f32[2,16,320]{2,1,0:T(8,128)S(1)}, f32[2,16,320]{2,1,0:T(8,128)S(1)}, u32[]{:S(2)}, u32[]{:S(2)}) %collective-permute-start.26) | collective-permute-done | bytes 40992 | tf_op jit(solution)/shard_map/ppermute | solution.py:53
  91.0 1.2 %collective-permute-done.27 = f32[2,16,512]{2,1,0:T(8,128)S(1)} collective-permute-done((f32[2,16,512]{2,1,0:T(8,128)S(1)}, f32[2,16,512]{2,1,0:T(8,128)S(1)}, u32[]{:S(2)}, u32[]{:S(2)}) %collective-permute-start.27) | collective-permute-done | bytes 65568 | tf_op jit(solution)/shard_map/ppermute | solution.py:57
  93.7 1.1 collective-permute-done.28
  95.5 3.7 %collective-permute-done.31 = f32[2,16,192]{2,1,0:T(8,128)S(1)} collective-permute-done((f32[2,16,192]{2,1,0:T(8,128)S(1)}, f32[2,16,192]{2,1,0:T(8,128)S(1)}, u32[]{:S(2)}, u32[]{:S(2)}) %collective-permute-start.31) | collective-permute-done | bytes 24608 | tf_op jit(solution)/shard_map/ppermute | solution.py:53
  99.2 1.6 %collective-permute-done.29 = f32[2,16,192]{2,1,0:T(8,128)S(1)} collective-permute-done((f32[2,16,192]{2,1,0:T(8,128)S(1)}, f32[2,16,192]{2,1,0:T(8,128)S(1)}, u32[]{:S(2)}, u32[]{:S(2)}) %collective-permute-start.29) | collective-permute-done | bytes 24608 | tf_op jit(solution)/shard_map/ppermute | solution.py:53
  101.2 3.5 %collective-permute-done.34 = f32[2,16,64]{2,1,0:T(8,128)S(1)} collective-permute-done((f32[2,16,64]{2,1,0:T(8,128)S(1)}, f32[2,16,64]{2,1,0:T(8,128)S(1)}, u32[]{:S(2)}, u32[]{:S(2)}) %collective-permute-start.34) | collective-permute-done | bytes 8224 | tf_op jit(solution)/shard_map/ppermute | solution.py:53
  104.7 1.3 %collective-permute-done.33 = f32[2,16,64]{2,1,0:T(8,128)S(1)} collective-permute-done((f32[2,16,64]{2,1,0:T(8,128)S(1)}, f32[2,16,64]{2,1,0:T(8,128)S(1)}, u32[]{:S(2)}, u32[]{:S(2)}) %collective-permute-start.33) | collective-permute-done | bytes 8224 | tf_op jit(solution)/shard_map/ppermute | solution.py:53
  (189 shorter events, 20.9 us)
Async XLA Ops:
  2.8 16.8 %collective-permute-start.2 = (f32[2,592,128]{2,1,0:T(8,128)S(1)}, f32[2,592,128]{2,1,0:T(8,128)S(1)}, u32[]{:S(2)}, u32[]{:S(2)}) collective-permute-start(f32[2,592,128]{2,1,0:T(8,128)S(1)} %constant_dynamic-update-slice_fusion), channel_id=1, source_target_pairs={{0,8},{1,9},{2,10},{3,11},{4,12},{5,13},{6,14},{7,15},{8,16},{9,17... | collective-permute-start | bytes 1818632 | tf_op jit(solution)/shard_map/ppermute | solution.py:53
  4.5 29.3 %collective-permute-start.1 = (f32[2,592,128]{2,1,0:T(8,128)S(1)}, f32[2,592,128]{2,1,0:T(8,128)S(1)}, u32[]{:S(2)}, u32[]{:S(2)}) collective-permute-start(f32[2,592,128]{2,1,0:T(8,128)S(1)} %constant_dynamic-update-slice_fusion), channel_id=1, source_target_pairs={{0,16},{1,17},{2,18},{3,19},{4,20},{5,21},{6,22},{7,23},{8,24},{9,... | collective-permute-start | bytes 1818632 | tf_op jit(solution)/shard_map/ppermute | solution.py:53
  7.4 26.4 %collective-permute-start = (f32[2,592,128]{2,1,0:T(8,128)S(1)}, f32[2,592,128]{2,1,0:T(8,128)S(1)}, u32[]{:S(2)}, u32[]{:S(2)}) collective-permute-start(f32[2,592,128]{2,1,0:T(8,128)S(1)} %constant_dynamic-update-slice_fusion), channel_id=1, source_target_pairs={{0,24},{1,25},{2,26},{3,27},{4,28},{5,29},{6,30},{7,31},{8,0},{9,1... | collective-permute-start | bytes 1818632 | tf_op jit(solution)/shard_map/ppermute | solution.py:53
  36.5 2.3 %collective-permute-start.3 = (f32[2,16,256]{2,1,0:T(8,128)S(1)}, f32[2,16,256]{2,1,0:T(8,128)S(1)}, u32[]{:S(2)}, u32[]{:S(2)}) collective-permute-start(f32[2,16,256]{2,1,0:T(8,128)S(1)} %get-tuple-element.410), channel_id=1, source_target_pairs={{0,32},{1,33},{2,3},{3,2},{4,64},{5,65},{6,96},{7,97},{8,40},{9,41... | collective-permute-start | bytes 98312 | tf_op jit(solution)/shard_map/ppermute | solution.py:53
  38.9 1.3 %collective-permute-start.4 = (f32[2,16,512]{2,1,0:T(8,128)S(1)}, f32[2,16,512]{2,1,0:T(8,128)S(1)}, u32[]{:S(2)}, u32[]{:S(2)}) collective-permute-start(f32[2,16,512]{2,1,0:T(8,128)S(1)} %get-tuple-element.411), channel_id=1, source_target_pairs={{0,1},{1,0},{2,3},{3,2},{4,5},{5,4},{6,7},{7,6},{8,9},{9,8},{10,11... | collective-permute-start | bytes 196616 | tf_op jit(solution)/shard_map/ppermute | solution.py:57
  40.3 1.8 %collective-permute-start.5 = (f32[2,16,512]{2,1,0:T(8,128)S(1)}, f32[2,16,512]{2,1,0:T(8,128)S(1)}, u32[]{:S(2)}, u32[]{:S(2)}) collective-permute-start(f32[2,16,512]{2,1,0:T(8,128)S(1)} %get-tuple-element.413), channel_id=1, source_target_pairs={{0,1},{1,0},{2,3},{3,2},{4,5},{5,4},{6,7},{7,6},{8,9},{9,8},{10,11... | collective-permute-start | bytes 196616 | tf_op jit(solution)/shard_map/ppermute | solution.py:53
  42.1 1.3 %collective-permute-start.8 = (f32[2,16,512]{2,1,0:T(8,128)S(1)}, f32[2,16,512]{2,1,0:T(8,128)S(1)}, u32[]{:S(2)}, u32[]{:S(2)}) collective-permute-start(f32[2,16,512]{2,1,0:T(8,128)S(1)} %add.200), channel_id=1, source_target_pairs={{0,1},{1,0},{2,3},{3,2},{4,5},{5,4},{6,7},{7,6},{8,9},{9,8},{10,11... | collective-permute-start | bytes 196616 | tf_op jit(solution)/shard_map/ppermute | solution.py:57
  43.5 1.5 %collective-permute-start.9 = (f32[2,16,512]{2,1,0:T(8,128)S(1)}, f32[2,16,512]{2,1,0:T(8,128)S(1)}, u32[]{:S(2)}, u32[]{:S(2)}) collective-permute-start(f32[2,16,512]{2,1,0:T(8,128)S(1)} %get-tuple-element.416), channel_id=1, source_target_pairs={{0,1},{1,0},{2,3},{3,2},{4,5},{5,4},{6,7},{7,6},{8,9},{9,8},{10,11... | collective-permute-start | bytes 196616 | tf_op jit(solution)/shard_map/ppermute | solution.py:53
  45.0 3.3 %collective-permute-start.11 = (f32[2,16,512]{2,1,0:T(8,128)S(1)}, f32[2,16,512]{2,1,0:T(8,128)S(1)}, u32[]{:S(2)}, u32[]{:S(2)}) collective-permute-start(f32[2,16,512]{2,1,0:T(8,128)S(1)} %add_add_fusion.1), channel_id=1, source_target_pairs={{0,1},{1,0},{2,3},{3,2},{4,5},{5,4},{6,7},{7,6},{8,9},{9,8},{10,11... | collective-permute-start | bytes 196616 | tf_op jit(solution)/shard_map/ppermute | solution.py:57
  45.4 5.2 %collective-permute-start.12 = (f32[2,64,64]{2,1,0:T(8,128)S(1)}, f32[2,64,64]{2,1,0:T(8,128)S(1)}, u32[]{:S(2)}, u32[]{:S(2)}) collective-permute-start(f32[2,64,64]{2,1,0:T(8,128)S(1)} %pad_maximum_fusion.103), channel_id=1, source_target_pairs={{0,1},{1,0},{2,36},{3,37},{4,5},{5,4},{6,7},{7,6},{8,9},{9,8},{10,... | collective-permute-start | bytes 98312 | tf_op jit(solution)/shard_map/ppermute | solution.py:53
  50.6 4.0 %collective-permute-start.13 = (f32[2,16,256]{2,1,0:T(8,128)S(1)}, f32[2,16,256]{2,1,0:T(8,128)S(1)}, u32[]{:S(2)}, u32[]{:S(2)}) collective-permute-start(f32[2,16,256]{2,1,0:T(8,128)S(1)} %add_add_fusion.3), channel_id=1, source_target_pairs={{0,2},{1,3},{2,0},{3,1},{4,5},{5,4},{6,7},{7,6},{8,10},{9,11},{10,... | collective-permute-start | bytes 98312 | tf_op jit(solution)/shard_map/ppermute | solution.py:53
  56.2 2.3 %collective-permute-start.18 = (f32[2,16,256]{2,1,0:T(8,128)S(1)}, f32[2,16,256]{2,1,0:T(8,128)S(1)}, u32[]{:S(2)}, u32[]{:S(2)}) collective-permute-start(f32[2,16,256]{2,1,0:T(8,128)S(1)} %get-tuple-element.419), channel_id=1, source_target_pairs={{0,1},{1,0},{2,3},{3,2},{4,5},{5,4},{6,7},{7,6},{8,9},{9,8},{10,11... | collective-permute-start | bytes 98312 | tf_op jit(solution)/shard_map/ppermute | solution.py:53
  60.0 20.3 %collective-permute-start.20 = (f32[2,16,512]{2,1,0:T(8,128)S(1)}, f32[2,16,512]{2,1,0:T(8,128)S(1)}, u32[]{:S(2)}, u32[]{:S(2)}) collective-permute-start(f32[2,16,512]{2,1,0:T(8,128)S(1)} %add.207), channel_id=1, source_target_pairs={{0,1},{1,0},{2,3},{3,2},{4,5},{5,4},{6,7},{7,6},{8,9},{9,8},{10,11... | collective-permute-start | bytes 196616 | tf_op jit(solution)/shard_map/ppermute | solution.py:57
  60.5 23.7 %collective-permute-start.22 = (f32[2,80,64]{2,1,0:T(8,128)S(1)}, f32[2,80,64]{2,1,0:T(8,128)S(1)}, u32[]{:S(2)}, u32[]{:S(2)}) collective-permute-start(f32[2,80,64]{2,1,0:T(8,128)S(1)} %get-tuple-element.271), channel_id=1, source_target_pairs={{0,102},{1,103},{2,0},{3,1},{4,5},{5,4},{6,7},{7,6},{8,110},{9,111... | collective-permute-start | bytes 122888 | tf_op jit(solution)/shard_map/ppermute | solution.py:53
  60.6 24.3 %collective-permute-start.21 = (f32[2,80,64]{2,1,0:T(8,128)S(1)}, f32[2,80,64]{2,1,0:T(8,128)S(1)}, u32[]{:S(2)}, u32[]{:S(2)}) collective-permute-start(f32[2,80,64]{2,1,0:T(8,128)S(1)} %get-tuple-element.399), channel_id=1, source_target_pairs={{0,1},{1,0},{2,34},{3,35},{4,5},{5,4},{6,7},{7,6},{8,9},{9,8},{10,... | collective-permute-start | bytes 122888 | tf_op jit(solution)/shard_map/ppermute | solution.py:53
  84.9 5.1 %collective-permute-start.26 = (f32[2,16,320]{2,1,0:T(8,128)S(1)}, f32[2,16,320]{2,1,0:T(8,128)S(1)}, u32[]{:S(2)}, u32[]{:S(2)}) collective-permute-start(f32[2,16,320]{2,1,0:T(8,128)S(1)} %pad_maximum_fusion.104), channel_id=1, source_target_pairs={{0,1},{1,0},{2,36},{3,37},{4,5},{5,4},{6,7},{7,6},{8,9},{9,8},{10,... | collective-permute-start | bytes 122888 | tf_op jit(solution)/shard_map/ppermute | solution.py:53
  85.0 5.8 %collective-permute-start.23 = (f32[2,16,512]{2,1,0:T(8,128)S(1)}, f32[2,16,512]{2,1,0:T(8,128)S(1)}, u32[]{:S(2)}, u32[]{:S(2)}) collective-permute-start(f32[2,16,512]{2,1,0:T(8,128)S(1)} %get-tuple-element.422), channel_id=1, source_target_pairs={{0,6},{1,7},{2,0},{3,1},{4,5},{5,4},{6,2},{7,3},{8,14},{9,15},{10,... | collective-permute-start | bytes 196616 | tf_op jit(solution)/shard_map/ppermute | solution.py:53
  85.1 5.8 %collective-permute-start.25 = (f32[2,16,512]{2,1,0:T(8,128)S(1)}, f32[2,16,512]{2,1,0:T(8,128)S(1)}, u32[]{:S(2)}, u32[]{:S(2)}) collective-permute-start(f32[2,16,512]{2,1,0:T(8,128)S(1)} %get-tuple-element.428), channel_id=1, source_target_pairs={{0,1},{1,0},{2,34},{3,35},{4,2},{5,3},{6,7},{7,6},{8,9},{9,8},{10,... | collective-permute-start | bytes 196616 | tf_op jit(solution)/shard_map/ppermute | solution.py:53
  95.2 4.0 %collective-permute-start.31 = (f32[2,16,192]{2,1,0:T(8,128)S(1)}, f32[2,16,192]{2,1,0:T(8,128)S(1)}, u32[]{:S(2)}, u32[]{:S(2)}) collective-permute-start(f32[2,16,192]{2,1,0:T(8,128)S(1)} %pad_maximum_fusion.106), channel_id=1, source_target_pairs={{0,1},{1,0},{2,4},{3,5},{4,2},{5,3},{6,7},{7,6},{8,9},{9,8},{10,12... | collective-permute-start | bytes 73736 | tf_op jit(solution)/shard_map/ppermute | solution.py:53
  95.3 4.0 %collective-permute-start.30 = (f32[2,16,192]{2,1,0:T(8,128)S(1)}, f32[2,16,192]{2,1,0:T(8,128)S(1)}, u32[]{:S(2)}, u32[]{:S(2)}) collective-permute-start(f32[2,16,192]{2,1,0:T(8,128)S(1)} %pad_maximum_fusion.106), channel_id=1, source_target_pairs={{0,2},{1,3},{2,0},{3,1},{4,5},{5,4},{6,7},{7,6},{8,10},{9,11},{10,... | collective-permute-start | bytes 73736 | tf_op jit(solution)/shard_map/ppermute | solution.py:53
  95.3 5.5 %collective-permute-start.29 = (f32[2,16,192]{2,1,0:T(8,128)S(1)}, f32[2,16,192]{2,1,0:T(8,128)S(1)}, u32[]{:S(2)}, u32[]{:S(2)}) collective-permute-start(f32[2,16,192]{2,1,0:T(8,128)S(1)} %pad_maximum_fusion.106), channel_id=1, source_target_pairs={{0,1},{1,0},{2,6},{3,7},{4,5},{5,4},{6,2},{7,3},{8,9},{9,8},{10,14... | collective-permute-start | bytes 73736 | tf_op jit(solution)/shard_map/ppermute | solution.py:53
  100.9 3.8 %collective-permute-start.34 = (f32[2,16,64]{2,1,0:T(8,128)S(1)}, f32[2,16,64]{2,1,0:T(8,128)S(1)}, u32[]{:S(2)}, u32[]{:S(2)}) collective-permute-start(f32[2,16,64]{2,1,0:T(8,128)S(1)} %slice.907), channel_id=1, source_target_pairs={{0,32},{1,33},{2,34},{3,35},{4,36},{5,37},{6,38},{7,39},{8,40},{9,... | collective-permute-start | bytes 24584 | tf_op jit(solution)/shard_map/ppermute | solution.py:53
  101.0 5.0 %collective-permute-start.33 = (f32[2,16,64]{2,1,0:T(8,128)S(1)}, f32[2,16,64]{2,1,0:T(8,128)S(1)}, u32[]{:S(2)}, u32[]{:S(2)}) collective-permute-start(f32[2,16,64]{2,1,0:T(8,128)S(1)} %slice.907), channel_id=1, source_target_pairs={{0,96},{1,97},{2,98},{3,99},{4,100},{5,101},{6,102},{7,103},{8,104... | collective-permute-start | bytes 24584 | tf_op jit(solution)/shard_map/ppermute | solution.py:53
  101.1 5.3 %collective-permute-start.32 = (f32[2,16,64]{2,1,0:T(8,128)S(1)}, f32[2,16,64]{2,1,0:T(8,128)S(1)}, u32[]{:S(2)}, u32[]{:S(2)}) collective-permute-start(f32[2,16,64]{2,1,0:T(8,128)S(1)} %slice.907), channel_id=1, source_target_pairs={{0,64},{1,65},{2,66},{3,67},{4,68},{5,69},{6,70},{7,71},{8,72},{9,... | collective-permute-start | bytes 24584 | tf_op jit(solution)/shard_map/ppermute | solution.py:53
  (24 other events, 40.9 us)

commit v7 on v6

--- a/solution.py
+++ b/solution.py
@@ -108,6 +108,11 @@
     inverse = jnp.where(jnp.where(z == 0, x != 1, x == z - 1), lower_half, upper_half)
     left, right = factor[:, :, :piece], factor[:, :, piece:]
     packed = jnp.concatenate([left, right, inverse, krylov_block, basis], 1)
+    packed, krylov_block, lower_half = lax.optimization_barrier((packed, krylov_block, lower_half))
+    lead = jnp.concatenate([apply_rows(krylov_block, lower_half), herm_rows(basis, basis).reshape(2, nvec, half)], 2)
+    lead = lead + move(lead, lambda z, y, x, c: (z, y ^ 1, x, c))
+    lead = lead + move(lead, lambda z, y, x, c: (z, 3 - y, x, c))
+    gram = lead[:, :, half:].reshape(2, nb, nb)
     pieces = [packed] + [turn_y(packed, d) for d in (1, 3, 2)]
     pieces = [pieces[0], pieces[1], pieces[3], pieces[2]]
     tall = jnp.concatenate([jnp.concatenate([p[:, :piece], p[:, piece:half]], 2) for p in pieces], 1)
@@ -119,9 +124,6 @@
     high = lax.dynamic_index_in_dim(basis_all, (2 * c + 1 - y) % SIDE, 0, False)
     basis_half = jnp.concatenate([low, high], 2)
 
-    plane = jnp.concatenate([basis_all[d] for d in every], 2)
-    gram = herm_rows(plane, plane)
-
     empty = jnp.zeros((2, nvec, half), jnp.float32)
     small = jnp.zeros((2, nvec, nb), jnp.float32)
     blank = jnp.zeros((2, nvec, tile), jnp.float32)
@@ -145,9 +147,8 @@
         return jnp.concatenate([part, gram], 1)
 
     starts = ((0, 0), (0, 2), (0, 3))
-    y0 = lax.cond(here(*starts), apply_rows, lambda v, w: empty, given, rows)
-    arrived = hop(y0, {(0, 0): (1, 0), (0, 2): (2, 0), (0, 3): (3, 0)})
-    arrived, gram = lax.optimization_barrier((arrived, gram))
+    arrived = hop(lead[:, :, :half], {(0, 0): (1, 0), (0, 2): (2, 0), (0, 3): (3, 0)})
+    y0 = jnp.where(here(*starts), lead[:, :, :half], 0.0)
     acc0 = product(((1, 0),), arrived)
     y1 = finish((1, 0), given, acc0)
     near1 = hop(y1, {(1, 0): (2, 1)})
@@ -171,10 +172,10 @@
     near4 = hop(x2 + x3, {(2, 3): (1, 2), (3, 3): (0, 3)})
     side1 = hop(product(((1, 3),), after(far3, x2)), {(1, 3): (1, 2)}, ((1, 1),))
     far4 = hop(x2, {(2, 3): (0, 2)})
-    sent3 = hop(after(share(x3, (3, 3)), x2), {(3, 3): (0, 1)}, ((0, 0),))
-    sent2 = hop(share(x2, (2, 3)), {(2, 3): (0, 1)}, ((1, 1),))
+    share3, share2 = share(x3, (3, 3)), share(x2, (2, 3))
     x1 = finish((1, 2), solved, side1 + product(((1, 2),), near4))
-    x1, sent2, sent3 = lax.optimization_barrier((x1, sent2, sent3))
+    sent3 = hop(after(share3, x1), {(3, 3): (0, 1)}, ((0, 0),))
+    sent2 = hop(after(share2, x1), {(2, 3): (0, 1)}, ((1, 1),))
     part1 = lax.cond(here((1, 2)), herm_rows, lambda v, w: small, x1, basis_half)
     near5 = hop(jnp.concatenate([x1, part1], 2), {(1, 2): (0, 1)})
     part1 = near5[:, :, half:]
@@ -190,6 +191,7 @@
     other = swap(both)
     first = sums[:, :nvec] + other[:, :, half:]
     coeffs = 2.0 * first - combine_rows(first, sums[:, nvec:])
+    sure = coeffs
     chosen = jnp.where((y < 2) == (c == 0), found, other[:, :, :half])
     mine = jnp.where(y % 2 == 0, chosen[:, :, :piece], chosen[:, :, piece:])
     message = jnp.concatenate([mine, coeffs], 2)
@@ -205,8 +207,12 @@
     coeffs = chain[:, :, piece:]
     total = coeffs
     for a in (1, 3, 2):
-        landed = hop(coeffs, {(0, b): (a, b) for b in every})
-        total = jnp.where(z == a, landed, total)
+        landed = hop(sure, {(0, 1): (a, 1)})
+        total = jnp.where((z == a) & (x == 1), landed, total)
+    relay = total
+    for d in (1, 3, 2):
+        landed = hop(relay, {(a, 1): (a, (1 + d) % SIDE) for a in (1, 2, 3)})
+        total = jnp.where((z > 0) & (x == (1 + d) % SIDE), landed, total)
     projected = own_rows - combine_rows(total, basis)
     return projected, jnp.swapaxes(total, 1, 2)
 

time: 108 us -> 115 us (1.065); the launches traced: 108 us -> 113 us
  waiting for transfers between devices: 62.8 us -> 45.9 us
  local copies, waits for them, and re-layouts: 5.63 us -> 17.3 us
  starting transfers between devices: 32.5 us -> 40.2 us
  other arithmetic: 2.26 us -> 4.56 us
    ppermute x27 -> x32, waiting for transfers between devices: 55.9 us -> 40.1 us  [move(): return lax.ppermute(value, AXES, pairs)]
    ppermute x27 -> x32, starting transfers between devices: 30.9 us -> 38.3 us  [move(): return lax.ppermute(value, AXES, pairs)]
    unnamed x21 -> x43, local copies, waits for them, and re-layouts: 2.7 us -> 6.84 us
    another operation x3 -> x4, local copies, waits for them, and re-layouts: 0.03 us -> 3.34 us  [local(): basis_all = jnp.stack([p[:, top + nvec:] for p in pieces])]
    dynamic_slice x0 -> x1, other arithmetic: none -> 1.72 us  [local(): lower_half = lax.dynamic_slice_in_dim(lower_inverse, c * half, half, 1)]
    dot_general x8 -> x10, matrix products: 2.47 us -> 2.62 us  [dot_nt(): lax.dot_general(left, right, (((1,), (1,)), ((), ())), precision=precisio...]
  transfers between devices with their start and end apart: 35 -> 40, of which waited for: 27 -> 25; matrix products, arithmetic and copies ran while one was open for 2% -> 8% of each run, Pallas kernels for 0% -> 0%
where the time goes in v7:
time: 115 us; the launch traced here: 113 us
  waiting for transfers between devices  45.9 us (40%)
  starting transfers between devices  40.2 us (35%)
  local copies, waits for them, and re-layouts  17.3 us (15%)
  other arithmetic  4.56 us (4%)
  matrix products  3.19 us (3%)
  between operations  1.39 us (1%)
    ppermute x32, waiting for transfers between devices, move(): return lax.ppermute(value, AXES, pairs)  40.1 us
    ppermute x32, starting transfers between devices, move(): return lax.ppermute(value, AXES, pairs)  38.3 us
    unnamed x43, local copies, waits for them, and re-layouts  6.84 us
    ppermute x8, waiting for transfers between devices, swap(): return lax.ppermute(value, 'c', [(0, 1), (1, 0)])  5.86 us
    another operation x4, local copies, waits for them, and re-layouts, local(): basis_all = jnp.stack([p[:, top + nvec:] for p in pieces])  3.34 us
    dot_general x10, matrix products, dot_nt(): lax.dot_general(left, right, (((1,), (1,)), ((), ())), precision=precisio...  2.62 us
  transfers between devices with their start and end apart: 40, of which 25 were waited for; matrix products, arithmetic and copies ran while one was open for 8% of the time, Pallas kernels for 0%

profile of v7, /device:TPU:2, one launch (start us, length us, event | category | flops | bytes accessed | tf_op | source)
XLA Modules:
  0.0 112.9 jit_solution(8022671637097874082)
XLA Ops:
  3.4 1.7 %constant_dynamic-slice_fusion = (f32[2,256,128]{2,1,0:T(8,128)S(1)}, f32[2,592,128]{2,1,0:T(8,128)}) fusion(f32[2,512,128]{2,1,0:T(8,128)S(1)} %copy-done.14, s32[]{:T(128)S(6)} %select_n.163, f32[2,592,128]{2,1,0:T(8,128)} %slice_dynamic-update-slice_fusion, f32[2,512,128]{2,1,0:T(8,128)} %param.51, pred[]{:T(512)S(6)} %select_n.161), kind=kLoop, calls=%fused_computation.449 | loop fusion | flops 65536 | bytes 1048581 | tf_op jit(solution)/shard_map/dynamic_slice | solution.py:105
  7.2 1.7 %collective-permute-start = (f32[2,16,512]{2,1,0:T(8,128)S(1)}, f32[2,16,512]{2,1,0:T(8,128)S(1)}, u32[]{:S(2)}, u32[]{:S(2)}) collective-permute-start(f32[2,16,512]{2,1,0:T(8,128)S(1)} %maximum_maximum_fusion.1), channel_id=1, source_target_pairs={{0,8},{1,9},{2,10},{3,11},{4,12},{5,13},{6,14},{7,15},{8,0},{9,1},... | collective-permute-start | bytes 196616 | tf_op jit(solution)/shard_map/ppermute | solution.py:53
  9.3 3.2 %collective-permute-start.4 = (f32[2,592,128]{2,1,0:T(8,128)}, f32[2,592,128]{2,1,0:T(8,128)S(1)}, u32[]{:S(2)}, u32[]{:S(2)}) collective-permute-start(f32[2,592,128]{2,1,0:T(8,128)} %constant_dynamic-update-slice_fusion), channel_id=1, source_target_pairs={{0,16},{1,17},{2,18},{3,19},{4,20},{5,21},{6,22},{7,23},{8,24},{9,... | collective-permute-start | bytes 1818632 | tf_op jit(solution)/shard_map/ppermute | solution.py:53
  12.5 1.9 %collective-permute-start.3 = (f32[2,592,128]{2,1,0:T(8,128)}, f32[2,592,128]{2,1,0:T(8,128)S(1)}, u32[]{:S(2)}, u32[]{:S(2)}) collective-permute-start(f32[2,592,128]{2,1,0:T(8,128)} %constant_dynamic-update-slice_fusion), channel_id=1, source_target_pairs={{0,24},{1,25},{2,26},{3,27},{4,28},{5,29},{6,30},{7,31},{8,0},{9,1... | collective-permute-start | bytes 1818632 | tf_op jit(solution)/shard_map/ppermute | solution.py:53
  14.4 1.0 collective-permute-start.1
  15.3 1.0 fusion.253
  17.1 1.0 slice.762
  18.1 21.7 %collective-permute-done.1 = f32[2,16,512]{2,1,0:T(8,128)S(1)} collective-permute-done((f32[2,16,512]{2,1,0:T(8,128)S(1)}, f32[2,16,512]{2,1,0:T(8,128)S(1)}, u32[]{:S(2)}, u32[]{:S(2)}) %collective-permute-start.1) | collective-permute-done | bytes 65568 | tf_op jit(solution)/shard_map/ppermute | solution.py:53
  46.3 1.1 collective-permute-done.10
  48.1 1.5 %slice_bitcast_fusion.47 = f32[1,2,64,128]{3,2,1,0:T(8,128)} fusion(f32[2,592,128]{2,1,0:T(8,128)} %constant_dynamic-update-slice_fusion), kind=kLoop, calls=%fused_computation.394 | loop fusion | bytes 131072 | tf_op jit(solution)/shard_map/stack | solution.py:122
  50.4 2.8 %collective-permute-start.14 = (f32[2,64,64]{2,1,0:T(8,128)S(1)}, f32[2,64,64]{2,1,0:T(8,128)}, u32[]{:S(2)}, u32[]{:S(2)}) collective-permute-start(f32[2,64,64]{2,1,0:T(8,128)S(1)} %reshape.12), channel_id=1, source_target_pairs={{0,1},{1,0},{2,36},{3,37},{4,5},{5,4},{6,7},{7,6},{8,9},{9,8},{10,... | collective-permute-start | bytes 98312 | tf_op jit(solution)/shard_map/ppermute | solution.py:53
  57.6 3.1 %collective-permute-done.15 = f32[2,16,256]{2,1,0:T(8,128)S(1)} collective-permute-done((f32[2,16,256]{2,1,0:T(8,128)S(1)}, f32[2,16,256]{2,1,0:T(8,128)S(1)}, u32[]{:S(2)}, u32[]{:S(2)}) %collective-permute-start.15) | collective-permute-done | bytes 32800 | tf_op jit(solution)/shard_map/ppermute | solution.py:53
  63.7 1.0 collective-permute-done.18
  67.8 19.4 %collective-permute-start.28 = (f32[2,80,64]{2,1,0:T(8,128)S(1)}, f32[2,80,64]{2,1,0:T(8,128)S(1)}, u32[]{:S(2)}, u32[]{:S(2)}) collective-permute-start(f32[2,80,64]{2,1,0:T(8,128)S(1)} %get-tuple-element.264), channel_id=1, source_target_pairs={{0,1},{1,0},{2,34},{3,35},{4,5},{5,4},{6,7},{7,6},{8,9},{9,8},{10,... | collective-permute-start | bytes 122888 | tf_op jit(solution)/shard_map/ppermute | solution.py:53
  87.2 3.1 %collective-permute-start.26 = (f32[2,16,320]{2,1,0:T(8,128)S(1)}, f32[2,16,320]{2,1,0:T(8,128)S(1)}, u32[]{:S(2)}, u32[]{:S(2)}) collective-permute-start(f32[2,16,320]{2,1,0:T(8,128)S(1)} %pad_maximum_fusion.98), channel_id=1, source_target_pairs={{0,1},{1,0},{2,36},{3,37},{4,5},{5,4},{6,7},{7,6},{8,9},{9,8},{10,... | collective-permute-start | bytes 122888 | tf_op jit(solution)/shard_map/ppermute | solution.py:53
  90.4 1.0 collective-permute-done.29
  91.4 1.6 %collective-permute-done.28 = f32[2,80,64]{2,1,0:T(8,128)S(1)} collective-permute-done((f32[2,80,64]{2,1,0:T(8,128)S(1)}, f32[2,80,64]{2,1,0:T(8,128)S(1)}, u32[]{:S(2)}, u32[]{:S(2)}) %collective-permute-start.28) | collective-permute-done | bytes 40992 | tf_op jit(solution)/shard_map/ppermute | solution.py:53
  94.7 1.5 %collective-permute-done.23 = f32[2,16,512]{2,1,0:T(8,128)S(1)} collective-permute-done((f32[2,16,512]{2,1,0:T(8,128)S(1)}, f32[2,16,512]{2,1,0:T(8,128)S(1)}, u32[]{:S(2)}, u32[]{:S(2)}) %collective-permute-start.23) | collective-permute-done | bytes 65568 | tf_op jit(solution)/shard_map/ppermute | solution.py:53
  96.2 1.2 %collective-permute-done.27 = f32[2,16,512]{2,1,0:T(8,128)S(1)} collective-permute-done((f32[2,16,512]{2,1,0:T(8,128)S(1)}, f32[2,16,512]{2,1,0:T(8,128)S(1)}, u32[]{:S(2)}, u32[]{:S(2)}) %collective-permute-start.27) | collective-permute-done | bytes 65568 | tf_op jit(solution)/shard_map/ppermute | solution.py:57
  99.0 1.1 collective-permute-done.30
  100.9 1.1 collective-permute-start.35
  101.9 2.5 %collective-permute-done.33 = f32[2,16,192]{2,1,0:T(8,128)S(1)} collective-permute-done((f32[2,16,192]{2,1,0:T(8,128)S(1)}, f32[2,16,192]{2,1,0:T(8,128)S(1)}, u32[]{:S(2)}, u32[]{:S(2)}) %collective-permute-start.33) | collective-permute-done | bytes 24608 | tf_op jit(solution)/shard_map/ppermute | solution.py:53
  104.5 1.6 %collective-permute-done.31 = f32[2,16,192]{2,1,0:T(8,128)S(1)} collective-permute-done((f32[2,16,192]{2,1,0:T(8,128)S(1)}, f32[2,16,192]{2,1,0:T(8,128)S(1)}, u32[]{:S(2)}, u32[]{:S(2)}) %collective-permute-start.31) | collective-permute-done | bytes 24608 | tf_op jit(solution)/shard_map/ppermute | solution.py:53
  106.2 3.5 %collective-permute-done.34 = f32[2,16,64]{2,1,0:T(8,128)S(1)} collective-permute-done((f32[2,16,64]{2,1,0:T(8,128)S(1)}, f32[2,16,64]{2,1,0:T(8,128)S(1)}, u32[]{:S(2)}, u32[]{:S(2)}) %collective-permute-start.34) | collective-permute-done | bytes 8224 | tf_op jit(solution)/shard_map/ppermute | solution.py:53
  (236 shorter events, 33.3 us)
Async XLA Ops:
  7.2 7.2 %collective-permute-start = (f32[2,16,512]{2,1,0:T(8,128)S(1)}, f32[2,16,512]{2,1,0:T(8,128)S(1)}, u32[]{:S(2)}, u32[]{:S(2)}) collective-permute-start(f32[2,16,512]{2,1,0:T(8,128)S(1)} %maximum_maximum_fusion.1), channel_id=1, source_target_pairs={{0,8},{1,9},{2,10},{3,11},{4,12},{5,13},{6,14},{7,15},{8,0},{9,1},... | collective-permute-start | bytes 196616 | tf_op jit(solution)/shard_map/ppermute | solution.py:53
  8.8 31.6 %collective-permute-start.5 = (f32[2,592,128]{2,1,0:T(8,128)}, f32[2,592,128]{2,1,0:T(8,128)S(1)}, u32[]{:S(2)}, u32[]{:S(2)}) collective-permute-start(f32[2,592,128]{2,1,0:T(8,128)} %constant_dynamic-update-slice_fusion), channel_id=1, source_target_pairs={{0,8},{1,9},{2,10},{3,11},{4,12},{5,13},{6,14},{7,15},{8,16},{9,17... | collective-permute-start | bytes 1818632 | tf_op jit(solution)/shard_map/ppermute | solution.py:53
  9.3 31.2 %collective-permute-start.4 = (f32[2,592,128]{2,1,0:T(8,128)}, f32[2,592,128]{2,1,0:T(8,128)S(1)}, u32[]{:S(2)}, u32[]{:S(2)}) collective-permute-start(f32[2,592,128]{2,1,0:T(8,128)} %constant_dynamic-update-slice_fusion), channel_id=1, source_target_pairs={{0,16},{1,17},{2,18},{3,19},{4,20},{5,21},{6,22},{7,23},{8,24},{9,... | collective-permute-start | bytes 1818632 | tf_op jit(solution)/shard_map/ppermute | solution.py:53
  12.5 28.1 %collective-permute-start.3 = (f32[2,592,128]{2,1,0:T(8,128)}, f32[2,592,128]{2,1,0:T(8,128)S(1)}, u32[]{:S(2)}, u32[]{:S(2)}) collective-permute-start(f32[2,592,128]{2,1,0:T(8,128)} %constant_dynamic-update-slice_fusion), channel_id=1, source_target_pairs={{0,24},{1,25},{2,26},{3,27},{4,28},{5,29},{6,30},{7,31},{8,0},{9,1... | collective-permute-start | bytes 1818632 | tf_op jit(solution)/shard_map/ppermute | solution.py:53
  14.4 25.4 %collective-permute-start.1 = (f32[2,16,512]{2,1,0:T(8,128)S(1)}, f32[2,16,512]{2,1,0:T(8,128)S(1)}, u32[]{:S(2)}, u32[]{:S(2)}) collective-permute-start(f32[2,16,512]{2,1,0:T(8,128)S(1)} %fusion.252), channel_id=1, source_target_pairs={{0,24},{1,25},{2,26},{3,27},{4,28},{5,29},{6,30},{7,31},{8,16},{9,... | collective-permute-start | bytes 196616 | tf_op jit(solution)/shard_map/ppermute | solution.py:53
  41.6 2.5 %collective-permute-start.6 = (f32[2,16,512]{2,1,0:T(8,128)S(1)}, f32[2,16,512]{2,1,0:T(8,128)S(1)}, u32[]{:S(2)}, u32[]{:S(2)}) collective-permute-start(f32[2,16,512]{2,1,0:T(8,128)S(1)} %get-tuple-element.389), channel_id=1, source_target_pairs={{0,1},{1,0},{2,3},{3,2},{4,5},{5,4},{6,7},{7,6},{8,9},{9,8},{10,11... | collective-permute-start | bytes 196616 | tf_op jit(solution)/shard_map/ppermute | solution.py:57
  44.2 1.8 %collective-permute-start.7 = (f32[2,16,512]{2,1,0:T(8,128)S(1)}, f32[2,16,512]{2,1,0:T(8,128)S(1)}, u32[]{:S(2)}, u32[]{:S(2)}) collective-permute-start(f32[2,16,512]{2,1,0:T(8,128)S(1)} %get-tuple-element.391), channel_id=1, source_target_pairs={{0,1},{1,0},{2,3},{3,2},{4,5},{5,4},{6,7},{7,6},{8,9},{9,8},{10,11... | collective-permute-start | bytes 196616 | tf_op jit(solution)/shard_map/ppermute | solution.py:53
  47.4 5.9 %collective-permute-start.12 = (f32[2,16,256]{2,1,0:T(8,128)S(1)}, f32[2,16,256]{2,1,0:T(8,128)S(1)}, u32[]{:S(2)}, u32[]{:S(2)}) collective-permute-start(f32[2,16,256]{2,1,0:T(8,128)S(1)} %get-tuple-element.393), channel_id=1, source_target_pairs={{0,1},{1,0},{2,3},{3,2},{4,5},{5,4},{6,7},{7,6},{8,9},{9,8},{10,11... | collective-permute-start | bytes 98312 | tf_op jit(solution)/shard_map/ppermute | solution.py:53
  48.0 5.3 %collective-permute-start.11 = (f32[2,16,512]{2,1,0:T(8,128)S(1)}, f32[2,16,512]{2,1,0:T(8,128)S(1)}, u32[]{:S(2)}, u32[]{:S(2)}) collective-permute-start(f32[2,16,512]{2,1,0:T(8,128)S(1)} %get-tuple-element.394), channel_id=1, source_target_pairs={{0,1},{1,0},{2,3},{3,2},{4,5},{5,4},{6,7},{7,6},{8,9},{9,8},{10,11... | collective-permute-start | bytes 196616 | tf_op jit(solution)/shard_map/ppermute | solution.py:53
  50.4 5.6 %collective-permute-start.14 = (f32[2,64,64]{2,1,0:T(8,128)S(1)}, f32[2,64,64]{2,1,0:T(8,128)}, u32[]{:S(2)}, u32[]{:S(2)}) collective-permute-start(f32[2,64,64]{2,1,0:T(8,128)S(1)} %reshape.12), channel_id=1, source_target_pairs={{0,1},{1,0},{2,36},{3,37},{4,5},{5,4},{6,7},{7,6},{8,9},{9,8},{10,... | collective-permute-start | bytes 98312 | tf_op jit(solution)/shard_map/ppermute | solution.py:53
  53.3 1.7 %collective-permute-start.13 = (f32[2,16,512]{2,1,0:T(8,128)S(1)}, f32[2,16,512]{2,1,0:T(8,128)S(1)}, u32[]{:S(2)}, u32[]{:S(2)}) collective-permute-start(f32[2,16,512]{2,1,0:T(8,128)S(1)} %add_add_fusion.1), channel_id=1, source_target_pairs={{0,1},{1,0},{2,3},{3,2},{4,5},{5,4},{6,7},{7,6},{8,9},{9,8},{10,11... | collective-permute-start | bytes 196616 | tf_op jit(solution)/shard_map/ppermute | solution.py:57
  56.8 4.0 %collective-permute-start.15 = (f32[2,16,256]{2,1,0:T(8,128)S(1)}, f32[2,16,256]{2,1,0:T(8,128)S(1)}, u32[]{:S(2)}, u32[]{:S(2)}) collective-permute-start(f32[2,16,256]{2,1,0:T(8,128)S(1)} %add_add_fusion.3), channel_id=1, source_target_pairs={{0,2},{1,3},{2,0},{3,1},{4,5},{5,4},{6,7},{7,6},{8,10},{9,11},{10,... | collective-permute-start | bytes 98312 | tf_op jit(solution)/shard_map/ppermute | solution.py:53
  63.0 1.7 %collective-permute-start.20 = (f32[2,16,256]{2,1,0:T(8,128)S(1)}, f32[2,16,256]{2,1,0:T(8,128)S(1)}, u32[]{:S(2)}, u32[]{:S(2)}) collective-permute-start(f32[2,16,256]{2,1,0:T(8,128)S(1)} %get-tuple-element.397), channel_id=1, source_target_pairs={{0,1},{1,0},{2,3},{3,2},{4,5},{5,4},{6,7},{7,6},{8,9},{9,8},{10,11... | collective-permute-start | bytes 98312 | tf_op jit(solution)/shard_map/ppermute | solution.py:53
  67.7 23.7 %collective-permute-start.29 = (f32[2,80,64]{2,1,0:T(8,128)S(1)}, f32[2,80,64]{2,1,0:T(8,128)S(1)}, u32[]{:S(2)}, u32[]{:S(2)}) collective-permute-start(f32[2,80,64]{2,1,0:T(8,128)S(1)} %get-tuple-element.265), channel_id=1, source_target_pairs={{0,102},{1,103},{2,0},{3,1},{4,5},{5,4},{6,7},{7,6},{8,110},{9,111... | collective-permute-start | bytes 122888 | tf_op jit(solution)/shard_map/ppermute | solution.py:53
  67.8 25.2 %collective-permute-start.28 = (f32[2,80,64]{2,1,0:T(8,128)S(1)}, f32[2,80,64]{2,1,0:T(8,128)S(1)}, u32[]{:S(2)}, u32[]{:S(2)}) collective-permute-start(f32[2,80,64]{2,1,0:T(8,128)S(1)} %get-tuple-element.264), channel_id=1, source_target_pairs={{0,1},{1,0},{2,34},{3,35},{4,5},{5,4},{6,7},{7,6},{8,9},{9,8},{10,... | collective-permute-start | bytes 122888 | tf_op jit(solution)/shard_map/ppermute | solution.py:53
  87.2 6.7 %collective-permute-start.26 = (f32[2,16,320]{2,1,0:T(8,128)S(1)}, f32[2,16,320]{2,1,0:T(8,128)S(1)}, u32[]{:S(2)}, u32[]{:S(2)}) collective-permute-start(f32[2,16,320]{2,1,0:T(8,128)S(1)} %pad_maximum_fusion.98), channel_id=1, source_target_pairs={{0,1},{1,0},{2,36},{3,37},{4,5},{5,4},{6,7},{7,6},{8,9},{9,8},{10,... | collective-permute-start | bytes 122888 | tf_op jit(solution)/shard_map/ppermute | solution.py:53
  90.3 5.8 %collective-permute-start.23 = (f32[2,16,512]{2,1,0:T(8,128)S(1)}, f32[2,16,512]{2,1,0:T(8,128)S(1)}, u32[]{:S(2)}, u32[]{:S(2)}) collective-permute-start(f32[2,16,512]{2,1,0:T(8,128)S(1)} %get-tuple-element.400), channel_id=1, source_target_pairs={{0,6},{1,7},{2,0},{3,1},{4,5},{5,4},{6,2},{7,3},{8,14},{9,15},{10,... | collective-permute-start | bytes 196616 | tf_op jit(solution)/shard_map/ppermute | solution.py:53
  90.3 5.8 %collective-permute-start.25 = (f32[2,16,512]{2,1,0:T(8,128)S(1)}, f32[2,16,512]{2,1,0:T(8,128)S(1)}, u32[]{:S(2)}, u32[]{:S(2)}) collective-permute-start(f32[2,16,512]{2,1,0:T(8,128)S(1)} %get-tuple-element.404), channel_id=1, source_target_pairs={{0,1},{1,0},{2,34},{3,35},{4,2},{5,3},{6,7},{7,6},{8,9},{9,8},{10,... | collective-permute-start | bytes 196616 | tf_op jit(solution)/shard_map/ppermute | solution.py:53
  100.4 4.0 %collective-permute-start.33 = (f32[2,16,192]{2,1,0:T(8,128)S(1)}, f32[2,16,192]{2,1,0:T(8,128)S(1)}, u32[]{:S(2)}, u32[]{:S(2)}) collective-permute-start(f32[2,16,192]{2,1,0:T(8,128)S(1)} %pad_maximum_fusion.100), channel_id=1, source_target_pairs={{0,1},{1,0},{2,4},{3,5},{4,2},{5,3},{6,7},{7,6},{8,9},{9,8},{10,12... | collective-permute-start | bytes 73736 | tf_op jit(solution)/shard_map/ppermute | solution.py:53
  100.5 4.0 %collective-permute-start.32 = (f32[2,16,192]{2,1,0:T(8,128)S(1)}, f32[2,16,192]{2,1,0:T(8,128)S(1)}, u32[]{:S(2)}, u32[]{:S(2)}) collective-permute-start(f32[2,16,192]{2,1,0:T(8,128)S(1)} %pad_maximum_fusion.100), channel_id=1, source_target_pairs={{0,2},{1,3},{2,0},{3,1},{4,5},{5,4},{6,7},{7,6},{8,10},{9,11},{10,... | collective-permute-start | bytes 73736 | tf_op jit(solution)/shard_map/ppermute | solution.py:53
  100.6 5.5 %collective-permute-start.31 = (f32[2,16,192]{2,1,0:T(8,128)S(1)}, f32[2,16,192]{2,1,0:T(8,128)S(1)}, u32[]{:S(2)}, u32[]{:S(2)}) collective-permute-start(f32[2,16,192]{2,1,0:T(8,128)S(1)} %pad_maximum_fusion.100), channel_id=1, source_target_pairs={{0,1},{1,0},{2,6},{3,7},{4,5},{5,4},{6,2},{7,3},{8,9},{9,8},{10,14... | collective-permute-start | bytes 73736 | tf_op jit(solution)/shard_map/ppermute | solution.py:53
  100.8 5.4 %collective-permute-start.36 = (f32[2,16,64]{2,1,0:T(8,128)S(1)}, f32[2,16,64]{2,1,0:T(8,128)S(1)}, u32[]{:S(2)}, u32[]{:S(2)}) collective-permute-start(f32[2,16,64]{2,1,0:T(8,128)S(1)} %maximum_subtract_fusion), channel_id=1, source_target_pairs={{0,1},{1,0},{2,34},{3,35},{4,5},{5,4},{6,7},{7,6},{8,9},{9,8},{10,... | collective-permute-start | bytes 24584 | tf_op jit(solution)/shard_map/ppermute | solution.py:53
  100.9 5.3 %collective-permute-start.35 = (f32[2,16,64]{2,1,0:T(8,128)S(1)}, f32[2,16,64]{2,1,0:T(8,128)S(1)}, u32[]{:S(2)}, u32[]{:S(2)}) collective-permute-start(f32[2,16,64]{2,1,0:T(8,128)S(1)} %maximum_subtract_fusion), channel_id=1, source_target_pairs={{0,1},{1,0},{2,98},{3,99},{4,5},{5,4},{6,7},{7,6},{8,9},{9,8},{10,... | collective-permute-start | bytes 24584 | tf_op jit(solution)/shard_map/ppermute | solution.py:53
  104.4 5.2 %collective-permute-start.34 = (f32[2,16,64]{2,1,0:T(8,128)S(1)}, f32[2,16,64]{2,1,0:T(8,128)S(1)}, u32[]{:S(2)}, u32[]{:S(2)}) collective-permute-start(f32[2,16,64]{2,1,0:T(8,128)S(1)} %maximum_subtract_fusion), channel_id=1, source_target_pairs={{0,1},{1,0},{2,66},{3,67},{4,5},{5,4},{6,7},{7,6},{8,9},{9,8},{10,... | collective-permute-start | bytes 24584 | tf_op jit(solution)/shard_map/ppermute | solution.py:53
  (42 other events, 54.3 us)

commit v8 on v6

--- a/solution.py
+++ b/solution.py
@@ -141,8 +141,7 @@
         return lax.optimization_barrier((value, other))[0]
 
     def share(value, place):
-        part = lax.cond(here(place), herm_rows, lambda v, w: small, value, basis_half)
-        return jnp.concatenate([part, gram], 1)
+        return lax.cond(here(place), herm_rows, lambda v, w: small, value, basis_half)
 
     starts = ((0, 0), (0, 2), (0, 3))
     y0 = lax.cond(here(*starts), apply_rows, lambda v, w: empty, given, rows)
@@ -159,8 +158,9 @@
     held1 = early1 + hop(product(((3, 1),), after(far1, y2)), {(3, 1): (3, 2)}, ((2, 2),))
     y3 = finish((3, 2), given, held1 + product(((3, 2),), near2))
 
-    sent1 = hop(after(gram, y1), {(1, 2): (0, 1)})
-    y3, sent1 = lax.optimization_barrier((y3, sent1))
+    grams = [hop(after(gram, y1), {place: (0, 1)}) for place in ((1, 1), (2, 2), (3, 3))]
+    y3, grams = lax.optimization_barrier((y3, grams))
+    gram = gram + (grams[0] + grams[1] + grams[2])
     back = hop(y0 + y1 + y2 + y3, {(0, 0): (0, 1), (1, 0): (1, 2), (2, 1): (2, 3), (3, 2): (3, 3)})
     solved = rotated(in_order(back, swap(back)))
 
@@ -169,44 +169,41 @@
     far3 = hop(x3, {(3, 3): (1, 3)})
     x2 = finish((2, 3), solved, product(((2, 3),), near3))
     near4 = hop(x2 + x3, {(2, 3): (1, 2), (3, 3): (0, 3)})
+    sent3 = hop(share(after(x3, x2), (3, 3)), {(3, 3): (0, 1)})
+    sent2 = hop(share(x2, (2, 3)), {(2, 3): (0, 1)})
+    far4 = hop(x2, {(2, 3): (0, 2)})
+    near4, far4, sent2, sent3 = lax.optimization_barrier((near4, far4, sent2, sent3))
     side1 = hop(product(((1, 3),), after(far3, x2)), {(1, 3): (1, 2)}, ((1, 1),))
-    far4 = hop(x2, {(2, 3): (0, 2)})
-    sent3 = hop(after(share(x3, (3, 3)), x2), {(3, 3): (0, 1)}, ((0, 0),))
-    sent2 = hop(share(x2, (2, 3)), {(2, 3): (0, 1)}, ((1, 1),))
     x1 = finish((1, 2), solved, side1 + product(((1, 2),), near4))
-    x1, sent2, sent3 = lax.optimization_barrier((x1, sent2, sent3))
     part1 = lax.cond(here((1, 2)), herm_rows, lambda v, w: small, x1, basis_half)
     near5 = hop(jnp.concatenate([x1, part1], 2), {(1, 2): (0, 1)})
-    part1 = near5[:, :, half:]
-    side0 = hop(after(product(((0, 3),), near4), x1), {(0, 3): (0, 1)}, ((0, 0),))
-    held3 = side0 + hop(after(product(((0, 2),), far4), x1), {(0, 2): (0, 1)}, ((1, 1),))
-    sent = jnp.concatenate([part1 + sent2[:, :nvec] + sent3[:, :nvec], sent1 + sent2[:, nvec:] + sent3[:, nvec:]], 1)
+    moved = hop(after(x1 + x2 + x3, part1), {(1, 2): (1, 1), (2, 3): (2, 1), (3, 3): (3, 1)})
+    carried = near5[:, :, half:]
+    side0 = hop(after(product(((0, 3),), near4), part1), {(0, 3): (0, 1)}, ((0, 0),))
+    held3 = side0 + hop(after(product(((0, 2),), far4), part1), {(0, 2): (0, 1)}, ((2, 2),))
+    sent = carried + sent2 + sent3
     near5 = near5[:, :, :half]
     x0 = finish((0, 1), solved, held3 + product(((0, 1),), near5))
 
-    found = x0 + x1 + x2 + x3
+    found = jnp.where(z == 0, x0, moved)
     sums = share(x0, (0, 1)) + sent
-    both = jnp.concatenate([found, sums[:, :nvec]], 2)
+    both = jnp.concatenate([found, sums], 2)
     other = swap(both)
-    first = sums[:, :nvec] + other[:, :, half:]
-    coeffs = 2.0 * first - combine_rows(first, sums[:, nvec:])
+    first = sums + other[:, :, half:]
+    coeffs = 2.0 * first - combine_rows(first, gram)
+    far = [hop(coeffs, {(0, 1): (a, 1)}) for a in (2, 1, 3)]
+    total = coeffs
+    for a, landed in zip((2, 1, 3), far):
+        total = jnp.where(z == a, landed, total)
     chosen = jnp.where((y < 2) == (c == 0), found, other[:, :, :half])
     mine = jnp.where(y % 2 == 0, chosen[:, :, :piece], chosen[:, :, piece:])
-    message = jnp.concatenate([mine, coeffs], 2)
-    columns = (1, 2, 3, 3)
-    column = jnp.where(z == 0, 1, jnp.where(z == 1, 2, 3))
-    for d in (1, 3, 2):
-        landed = hop(message, {(a, columns[a]): (a, (columns[a] + d) % SIDE) for a in every})
-        if d == 1:
-            chain = jnp.where(x == column, message, landed)
-        else:
-            chain = jnp.where(x == (column + d) % SIDE, landed, chain)
+    message = jnp.concatenate([mine, total], 2)
+    chain = message
+    for d in (2, 1, 3):
+        landed = hop(message, {(a, 1): (a, (1 + d) % SIDE) for a in every})
+        chain = jnp.where(x == (1 + d) % SIDE, landed, chain)
     own_rows = chain[:, :, :piece]
-    coeffs = chain[:, :, piece:]
-    total = coeffs
-    for a in (1, 3, 2):
-        landed = hop(coeffs, {(0, b): (a, b) for b in every})
-        total = jnp.where(z == a, landed, total)
+    total = chain[:, :, piece:]
     projected = own_rows - combine_rows(total, basis)
     return projected, jnp.swapaxes(total, 1, 2)
 

time: 108 us -> 109 us (level)
  waiting for transfers between devices: 62.8 us -> 64.3 us
  starting transfers between devices: 32.5 us -> 31.3 us
    ppermute x27 -> x30, starting transfers between devices: 30.9 us -> 29.9 us  [move(): return lax.ppermute(value, AXES, pairs)]
    ppermute x27 -> x30, waiting for transfers between devices: 55.9 us -> 56.8 us  [move(): return lax.ppermute(value, AXES, pairs)]
    unnamed x21 -> x19, local copies, waits for them, and re-layouts: 2.7 us -> 2.03 us
  transfers between devices with their start and end apart: 35 -> 38, of which waited for: 27 -> 22; matrix products, arithmetic and copies ran while one was open for 2% -> 3% of each run, Pallas kernels for 0% -> 0%
where the time goes in v8:
time: 109 us; the launch traced here: 108 us
  waiting for transfers between devices  64.3 us (59%)
  starting transfers between devices  31.3 us (29%)
  local copies, waits for them, and re-layouts  5.57 us (5%)
  matrix products  3.17 us (3%)
  other arithmetic  2.32 us (2%)
  between operations  1.38 us (1%)
    ppermute x30, waiting for transfers between devices, move(): return lax.ppermute(value, AXES, pairs)  56.8 us
    ppermute x30, starting transfers between devices, move(): return lax.ppermute(value, AXES, pairs)  29.9 us
    ppermute x8, waiting for transfers between devices, swap(): return lax.ppermute(value, 'c', [(0, 1), (1, 0)])  7.49 us
    dot_general x8, matrix products, dot_nt(): lax.dot_general(left, right, (((1,), (1,)), ((), ())), precision=precisio...  2.55 us
  transfers between devices with their start and end apart: 38, of which 22 were waited for; matrix products, arithmetic and copies ran while one was open for 3% of the time, Pallas kernels for 0%

profile of v8, /device:TPU:2, one launch (start us, length us, event | category | flops | bytes accessed | tf_op | source)
XLA Modules:
  0.0 108.3 jit_solution(16165840723921491793)
XLA Ops:
  1.7 1.1 %constant_dynamic-update-slice_fusion.2 = (f32[2,592,128]{2,1,0:T(8,128)S(1)}, f32[2,256,128]{2,1,0:T(8,128)S(1)}) fusion(f32[2,592,128]{2,1,0:T(8,128)S(1)} %slice_dynamic-update-slice_fusion, f32[2,512,128]{2,1,0:T(8,128)} %param.53, s32[]{:T(128)S(6)} %select_n.121, f32[2,512,128]{2,1,0:T(8,128)} %param.52, pred[]{:T(512)S(6)} %select_n.119), kind=kLoop, calls=%fused_computation.438 | loop fusion | flops 65536 | bytes 1048581
  2.8 1.6 %collective-permute-start.2 = (f32[2,592,128]{2,1,0:T(8,128)S(1)}, f32[2,592,128]{2,1,0:T(8,128)S(1)}, u32[]{:S(2)}, u32[]{:S(2)}) collective-permute-start(f32[2,592,128]{2,1,0:T(8,128)S(1)} %constant_dynamic-update-slice_fusion), channel_id=1, source_target_pairs={{0,8},{1,9},{2,10},{3,11},{4,12},{5,13},{6,14},{7,15},{8,16},{9,17... | collective-permute-start | bytes 1818632 | tf_op jit(solution)/shard_map/ppermute | solution.py:53
  4.5 2.9 %collective-permute-start.1 = (f32[2,592,128]{2,1,0:T(8,128)S(1)}, f32[2,592,128]{2,1,0:T(8,128)S(1)}, u32[]{:S(2)}, u32[]{:S(2)}) collective-permute-start(f32[2,592,128]{2,1,0:T(8,128)S(1)} %constant_dynamic-update-slice_fusion), channel_id=1, source_target_pairs={{0,16},{1,17},{2,18},{3,19},{4,20},{5,21},{6,22},{7,23},{8,24},{9,... | collective-permute-start | bytes 1818632 | tf_op jit(solution)/shard_map/ppermute | solution.py:53
  7.4 1.3 %collective-permute-start = (f32[2,592,128]{2,1,0:T(8,128)S(1)}, f32[2,592,128]{2,1,0:T(8,128)S(1)}, u32[]{:S(2)}, u32[]{:S(2)}) collective-permute-start(f32[2,592,128]{2,1,0:T(8,128)S(1)} %constant_dynamic-update-slice_fusion), channel_id=1, source_target_pairs={{0,24},{1,25},{2,26},{3,27},{4,28},{5,29},{6,30},{7,31},{8,0},{9,1... | collective-permute-start | bytes 1818632 | tf_op jit(solution)/shard_map/ppermute | solution.py:53
  8.7 10.9 %collective-permute-done.2 = f32[2,592,128]{2,1,0:T(8,128)S(1)} collective-permute-done((f32[2,592,128]{2,1,0:T(8,128)S(1)}, f32[2,592,128]{2,1,0:T(8,128)S(1)}, u32[]{:S(2)}, u32[]{:S(2)}) %collective-permute-start.2) | collective-permute-done | bytes 606240 | tf_op jit(solution)/shard_map/ppermute | solution.py:53
  19.6 14.2 %collective-permute-done.1 = f32[2,592,128]{2,1,0:T(8,128)S(1)} collective-permute-done((f32[2,592,128]{2,1,0:T(8,128)S(1)}, f32[2,592,128]{2,1,0:T(8,128)S(1)}, u32[]{:S(2)}, u32[]{:S(2)}) %collective-permute-start.1) | collective-permute-done | bytes 606240 | tf_op jit(solution)/shard_map/ppermute | solution.py:53
  39.1 1.2 %collective-permute-done.4 = f32[2,16,512]{2,1,0:T(8,128)S(1)} collective-permute-done((f32[2,16,512]{2,1,0:T(8,128)S(1)}, f32[2,16,512]{2,1,0:T(8,128)S(1)}, u32[]{:S(2)}, u32[]{:S(2)}) %collective-permute-start.4) | collective-permute-done | bytes 65568 | tf_op jit(solution)/shard_map/ppermute | solution.py:57
  42.4 1.1 %collective-permute-done.8 = f32[2,16,512]{2,1,0:T(8,128)S(1)} collective-permute-done((f32[2,16,512]{2,1,0:T(8,128)S(1)}, f32[2,16,512]{2,1,0:T(8,128)S(1)}, u32[]{:S(2)}, u32[]{:S(2)}) %collective-permute-start.8) | collective-permute-done | bytes 65568 | tf_op jit(solution)/shard_map/ppermute | solution.py:57
  45.5 5.6 %collective-permute-start.14 = (f32[2,64,64]{1,2,0:T(8,128)S(1)}, f32[2,64,64]{1,2,0:T(8,128)S(1)}, u32[]{:S(2)}, u32[]{:S(2)}) collective-permute-start(f32[2,64,64]{1,2,0:T(8,128)S(1)} %pad_maximum_fusion.100), channel_id=1, source_target_pairs={{0,1},{1,0},{2,102},{3,103},{4,5},{5,4},{6,7},{7,6},{8,9},{9,8},{1... | collective-permute-start | bytes 98312 | tf_op jit(solution)/shard_map/ppermute | solution.py:53
  51.0 9.2 %collective-permute-start.13 = (f32[2,64,64]{1,2,0:T(8,128)S(1)}, f32[2,64,64]{1,2,0:T(8,128)S(1)}, u32[]{:S(2)}, u32[]{:S(2)}) collective-permute-start(f32[2,64,64]{1,2,0:T(8,128)S(1)} %pad_maximum_fusion.100), channel_id=1, source_target_pairs={{0,1},{1,0},{2,68},{3,69},{4,5},{5,4},{6,7},{7,6},{8,9},{9,8},{10,... | collective-permute-start | bytes 98312 | tf_op jit(solution)/shard_map/ppermute | solution.py:53
  60.3 2.3 %collective-permute-done.13 = f32[2,64,64]{1,2,0:T(8,128)S(1)} collective-permute-done((f32[2,64,64]{1,2,0:T(8,128)S(1)}, f32[2,64,64]{1,2,0:T(8,128)S(1)}, u32[]{:S(2)}, u32[]{:S(2)}) %collective-permute-start.13) | collective-permute-done | bytes 32800 | tf_op jit(solution)/shard_map/ppermute | solution.py:53
  62.6 1.9 %collective-permute-done.12 = f32[2,64,64]{1,2,0:T(8,128)S(1)} collective-permute-done((f32[2,64,64]{1,2,0:T(8,128)S(1)}, f32[2,64,64]{1,2,0:T(8,128)S(1)}, u32[]{:S(2)}, u32[]{:S(2)}) %collective-permute-start.12) | collective-permute-done | bytes 32800 | tf_op jit(solution)/shard_map/ppermute | solution.py:53
  64.6 3.9 %collective-permute-done.15 = f32[2,16,256]{2,1,0:T(8,128)S(1)} collective-permute-done((f32[2,16,256]{2,1,0:T(8,128)S(1)}, f32[2,16,256]{2,1,0:T(8,128)S(1)}, u32[]{:S(2)}, u32[]{:S(2)}) %collective-permute-start.15) | collective-permute-done | bytes 32800 | tf_op jit(solution)/shard_map/ppermute | solution.py:53
  68.5 1.2 %collective-permute-done.16 = f32[2,16,256]{2,1,0:T(8,128)S(1)} collective-permute-done((f32[2,16,256]{2,1,0:T(8,128)S(1)}, f32[2,16,256]{2,1,0:T(8,128)S(1)}, u32[]{:S(2)}, u32[]{:S(2)}) %collective-permute-start.16) | collective-permute-done | bytes 32800 | tf_op jit(solution)/shard_map/ppermute | solution.py:57
  71.4 1.1 %collective-permute-done.18 = f32[2,16,512]{2,1,0:T(8,128)S(1)} collective-permute-done((f32[2,16,512]{2,1,0:T(8,128)S(1)}, f32[2,16,512]{2,1,0:T(8,128)S(1)}, u32[]{:S(2)}, u32[]{:S(2)}) %collective-permute-start.18) | collective-permute-done | bytes 65568 | tf_op jit(solution)/shard_map/ppermute | solution.py:57
  73.3 2.6 %collective-permute-start.22 = (f32[2,16,64]{2,1,0:T(8,128)S(1)}, f32[2,16,64]{2,1,0:T(8,128)S(1)}, u32[]{:S(2)}, u32[]{:S(2)}) collective-permute-start(f32[2,16,64]{2,1,0:T(8,128)S(1)} %get-tuple-element.421), channel_id=1, source_target_pairs={{0,1},{1,0},{2,102},{3,103},{4,5},{5,4},{6,7},{7,6},{8,9},{9,8},{1... | collective-permute-start | bytes 24584 | tf_op jit(solution)/shard_map/ppermute | solution.py:53
  75.9 1.7 %collective-permute-start.21 = (f32[2,16,64]{2,1,0:T(8,128)S(1)}, f32[2,16,64]{2,1,0:T(8,128)S(1)}, u32[]{:S(2)}, u32[]{:S(2)}) collective-permute-start(f32[2,16,64]{2,1,0:T(8,128)S(1)} %get-tuple-element.420), channel_id=1, source_target_pairs={{0,1},{1,0},{2,70},{3,71},{4,5},{5,4},{6,7},{7,6},{8,9},{9,8},{10,... | collective-permute-start | bytes 24584 | tf_op jit(solution)/shard_map/ppermute | solution.py:53
  77.5 3.2 %collective-permute-done.22 = f32[2,16,64]{2,1,0:T(8,128)S(1)} collective-permute-done((f32[2,16,64]{2,1,0:T(8,128)S(1)}, f32[2,16,64]{2,1,0:T(8,128)S(1)}, u32[]{:S(2)}, u32[]{:S(2)}) %collective-permute-start.22) | collective-permute-done | bytes 8224 | tf_op jit(solution)/shard_map/ppermute | solution.py:53
  80.7 2.8 %collective-permute-done.21 = f32[2,16,64]{2,1,0:T(8,128)S(1)} collective-permute-done((f32[2,16,64]{2,1,0:T(8,128)S(1)}, f32[2,16,64]{2,1,0:T(8,128)S(1)}, u32[]{:S(2)}, u32[]{:S(2)}) %collective-permute-start.21) | collective-permute-done | bytes 8224 | tf_op jit(solution)/shard_map/ppermute | solution.py:53
  83.7 1.2 %collective-permute-done.25 = f32[2,16,512]{2,1,0:T(8,128)S(1)} collective-permute-done((f32[2,16,512]{2,1,0:T(8,128)S(1)}, f32[2,16,512]{2,1,0:T(8,128)S(1)}, u32[]{:S(2)}, u32[]{:S(2)}) %collective-permute-start.25) | collective-permute-done | bytes 65568 | tf_op jit(solution)/shard_map/ppermute | solution.py:57
  85.2 5.0 %collective-permute-done.28 = f32[2,16,320]{2,1,0:T(8,128)S(1)} collective-permute-done((f32[2,16,320]{2,1,0:T(8,128)S(1)}, f32[2,16,320]{2,1,0:T(8,128)S(1)}, u32[]{:S(2)}, u32[]{:S(2)}) %collective-permute-start.28) | collective-permute-done | bytes 40992 | tf_op jit(solution)/shard_map/ppermute | solution.py:53
  93.8 1.1 collective-permute-done.31
  96.3 4.3 %collective-permute-done.34 = f32[2,16,64]{2,1,0:T(8,128)S(1)} collective-permute-done((f32[2,16,64]{2,1,0:T(8,128)S(1)}, f32[2,16,64]{2,1,0:T(8,128)S(1)}, u32[]{:S(2)}, u32[]{:S(2)}) %collective-permute-start.34) | collective-permute-done | bytes 8224 | tf_op jit(solution)/shard_map/ppermute | solution.py:53
  101.5 5.2 %collective-permute-done.37 = f32[2,16,192]{2,1,0:T(8,128)S(1)} collective-permute-done((f32[2,16,192]{2,1,0:T(8,128)S(1)}, f32[2,16,192]{2,1,0:T(8,128)S(1)}, u32[]{:S(2)}, u32[]{:S(2)}) %collective-permute-start.37) | collective-permute-done | bytes 24608 | tf_op jit(solution)/shard_map/ppermute | solution.py:53
  (191 shorter events, 22.3 us)
Async XLA Ops:
  2.8 16.8 %collective-permute-start.2 = (f32[2,592,128]{2,1,0:T(8,128)S(1)}, f32[2,592,128]{2,1,0:T(8,128)S(1)}, u32[]{:S(2)}, u32[]{:S(2)}) collective-permute-start(f32[2,592,128]{2,1,0:T(8,128)S(1)} %constant_dynamic-update-slice_fusion), channel_id=1, source_target_pairs={{0,8},{1,9},{2,10},{3,11},{4,12},{5,13},{6,14},{7,15},{8,16},{9,17... | collective-permute-start | bytes 1818632 | tf_op jit(solution)/shard_map/ppermute | solution.py:53
  4.5 29.3 %collective-permute-start.1 = (f32[2,592,128]{2,1,0:T(8,128)S(1)}, f32[2,592,128]{2,1,0:T(8,128)S(1)}, u32[]{:S(2)}, u32[]{:S(2)}) collective-permute-start(f32[2,592,128]{2,1,0:T(8,128)S(1)} %constant_dynamic-update-slice_fusion), channel_id=1, source_target_pairs={{0,16},{1,17},{2,18},{3,19},{4,20},{5,21},{6,22},{7,23},{8,24},{9,... | collective-permute-start | bytes 1818632 | tf_op jit(solution)/shard_map/ppermute | solution.py:53
  7.4 26.4 %collective-permute-start = (f32[2,592,128]{2,1,0:T(8,128)S(1)}, f32[2,592,128]{2,1,0:T(8,128)S(1)}, u32[]{:S(2)}, u32[]{:S(2)}) collective-permute-start(f32[2,592,128]{2,1,0:T(8,128)S(1)} %constant_dynamic-update-slice_fusion), channel_id=1, source_target_pairs={{0,24},{1,25},{2,26},{3,27},{4,28},{5,29},{6,30},{7,31},{8,0},{9,1... | collective-permute-start | bytes 1818632 | tf_op jit(solution)/shard_map/ppermute | solution.py:53
  45.0 15.2 %collective-permute-start.11 = (f32[2,16,512]{2,1,0:T(8,128)S(1)}, f32[2,16,512]{2,1,0:T(8,128)S(1)}, u32[]{:S(2)}, u32[]{:S(2)}) collective-permute-start(f32[2,16,512]{2,1,0:T(8,128)S(1)} %add_add_fusion.2), channel_id=1, source_target_pairs={{0,1},{1,0},{2,3},{3,2},{4,5},{5,4},{6,7},{7,6},{8,9},{9,8},{10,11... | collective-permute-start | bytes 196616 | tf_op jit(solution)/shard_map/ppermute | solution.py:57
  45.5 14.8 %collective-permute-start.14 = (f32[2,64,64]{1,2,0:T(8,128)S(1)}, f32[2,64,64]{1,2,0:T(8,128)S(1)}, u32[]{:S(2)}, u32[]{:S(2)}) collective-permute-start(f32[2,64,64]{1,2,0:T(8,128)S(1)} %pad_maximum_fusion.100), channel_id=1, source_target_pairs={{0,1},{1,0},{2,102},{3,103},{4,5},{5,4},{6,7},{7,6},{8,9},{9,8},{1... | collective-permute-start | bytes 98312 | tf_op jit(solution)/shard_map/ppermute | solution.py:53
  51.0 11.6 %collective-permute-start.13 = (f32[2,64,64]{1,2,0:T(8,128)S(1)}, f32[2,64,64]{1,2,0:T(8,128)S(1)}, u32[]{:S(2)}, u32[]{:S(2)}) collective-permute-start(f32[2,64,64]{1,2,0:T(8,128)S(1)} %pad_maximum_fusion.100), channel_id=1, source_target_pairs={{0,1},{1,0},{2,68},{3,69},{4,5},{5,4},{6,7},{7,6},{8,9},{9,8},{10,... | collective-permute-start | bytes 98312 | tf_op jit(solution)/shard_map/ppermute | solution.py:53
  60.2 4.3 %collective-permute-start.12 = (f32[2,64,64]{1,2,0:T(8,128)S(1)}, f32[2,64,64]{1,2,0:T(8,128)S(1)}, u32[]{:S(2)}, u32[]{:S(2)}) collective-permute-start(f32[2,64,64]{1,2,0:T(8,128)S(1)} %pad_maximum_fusion.100), channel_id=1, source_target_pairs={{0,1},{1,0},{2,34},{3,35},{4,5},{5,4},{6,7},{7,6},{8,9},{9,8},{10,... | collective-permute-start | bytes 98312 | tf_op jit(solution)/shard_map/ppermute | solution.py:53
  64.5 4.0 %collective-permute-start.15 = (f32[2,16,256]{2,1,0:T(8,128)S(1)}, f32[2,16,256]{2,1,0:T(8,128)S(1)}, u32[]{:S(2)}, u32[]{:S(2)}) collective-permute-start(f32[2,16,256]{2,1,0:T(8,128)S(1)} %add_add_fusion.4), channel_id=1, source_target_pairs={{0,2},{1,3},{2,0},{3,1},{4,5},{5,4},{6,7},{7,6},{8,10},{9,11},{10,... | collective-permute-start | bytes 98312 | tf_op jit(solution)/shard_map/ppermute | solution.py:53
  70.1 2.7 %collective-permute-start.23 = (f32[2,16,256]{2,1,0:T(8,128)S(1)}, f32[2,16,256]{2,1,0:T(8,128)S(1)}, u32[]{:S(2)}, u32[]{:S(2)}) collective-permute-start(f32[2,16,256]{2,1,0:T(8,128)S(1)} %get-tuple-element.417), channel_id=1, source_target_pairs={{0,1},{1,0},{2,3},{3,2},{4,5},{5,4},{6,7},{7,6},{8,9},{9,8},{10,11... | collective-permute-start | bytes 98312 | tf_op jit(solution)/shard_map/ppermute | solution.py:53
  72.5 11.0 %collective-permute-start.20 = (f32[2,16,256]{2,1,0:T(8,128)S(1)}, f32[2,16,256]{2,1,0:T(8,128)S(1)}, u32[]{:S(2)}, u32[]{:S(2)}) collective-permute-start(f32[2,16,256]{2,1,0:T(8,128)S(1)} %get-tuple-element.419), channel_id=1, source_target_pairs={{0,1},{1,0},{2,3},{3,2},{4,70},{5,71},{6,7},{7,6},{8,9},{9,8},{10,... | collective-permute-start | bytes 98312 | tf_op jit(solution)/shard_map/ppermute | solution.py:53
  72.7 10.8 %collective-permute-start.19 = (f32[2,16,256]{2,1,0:T(8,128)S(1)}, f32[2,16,256]{2,1,0:T(8,128)S(1)}, u32[]{:S(2)}, u32[]{:S(2)}) collective-permute-start(f32[2,16,256]{2,1,0:T(8,128)S(1)} %add.191), channel_id=1, source_target_pairs={{0,1},{1,0},{2,3},{3,2},{4,5},{5,4},{6,102},{7,103},{8,9},{9,8},{1... | collective-permute-start | bytes 98312 | tf_op jit(solution)/shard_map/ppermute | solution.py:53
  73.1 10.5 %collective-permute-start.24 = (f32[2,16,512]{2,1,0:T(8,128)S(1)}, f32[2,16,512]{2,1,0:T(8,128)S(1)}, u32[]{:S(2)}, u32[]{:S(2)}) collective-permute-start(f32[2,16,512]{2,1,0:T(8,128)S(1)} %get-tuple-element.423), channel_id=1, source_target_pairs={{0,1},{1,0},{2,3},{3,2},{4,5},{5,4},{6,7},{7,6},{8,9},{9,8},{10,11... | collective-permute-start | bytes 196616 | tf_op jit(solution)/shard_map/ppermute | solution.py:53
  73.3 7.4 %collective-permute-start.22 = (f32[2,16,64]{2,1,0:T(8,128)S(1)}, f32[2,16,64]{2,1,0:T(8,128)S(1)}, u32[]{:S(2)}, u32[]{:S(2)}) collective-permute-start(f32[2,16,64]{2,1,0:T(8,128)S(1)} %get-tuple-element.421), channel_id=1, source_target_pairs={{0,1},{1,0},{2,102},{3,103},{4,5},{5,4},{6,7},{7,6},{8,9},{9,8},{1... | collective-permute-start | bytes 24584 | tf_op jit(solution)/shard_map/ppermute | solution.py:53
  75.9 7.6 %collective-permute-start.21 = (f32[2,16,64]{2,1,0:T(8,128)S(1)}, f32[2,16,64]{2,1,0:T(8,128)S(1)}, u32[]{:S(2)}, u32[]{:S(2)}) collective-permute-start(f32[2,16,64]{2,1,0:T(8,128)S(1)} %get-tuple-element.420), channel_id=1, source_target_pairs={{0,1},{1,0},{2,70},{3,71},{4,5},{5,4},{6,7},{7,6},{8,9},{9,8},{10,... | collective-permute-start | bytes 24584 | tf_op jit(solution)/shard_map/ppermute | solution.py:53
  84.9 6.0 %collective-permute-start.26 = (f32[2,16,512]{2,1,0:T(8,128)S(1)}, f32[2,16,512]{2,1,0:T(8,128)S(1)}, u32[]{:S(2)}, u32[]{:S(2)}) collective-permute-start(f32[2,16,512]{2,1,0:T(8,128)S(1)} %get-tuple-element.422), channel_id=1, source_target_pairs={{0,6},{1,7},{2,0},{3,1},{4,5},{5,4},{6,2},{7,3},{8,14},{9,15},{10,... | collective-permute-start | bytes 196616 | tf_op jit(solution)/shard_map/ppermute | solution.py:53
  85.0 5.9 %collective-permute-start.27 = (f32[2,16,512]{2,1,0:T(8,128)S(1)}, f32[2,16,512]{2,1,0:T(8,128)S(1)}, u32[]{:S(2)}, u32[]{:S(2)}) collective-permute-start(f32[2,16,512]{2,1,0:T(8,128)S(1)} %get-tuple-element.427), channel_id=1, source_target_pairs={{0,1},{1,0},{2,68},{3,69},{4,2},{5,3},{6,7},{7,6},{8,9},{9,8},{10,... | collective-permute-start | bytes 196616 | tf_op jit(solution)/shard_map/ppermute | solution.py:53
  85.1 5.1 %collective-permute-start.28 = (f32[2,16,320]{2,1,0:T(8,128)S(1)}, f32[2,16,320]{2,1,0:T(8,128)S(1)}, u32[]{:S(2)}, u32[]{:S(2)}) collective-permute-start(f32[2,16,320]{2,1,0:T(8,128)S(1)} %pad_maximum_fusion.101), channel_id=1, source_target_pairs={{0,1},{1,0},{2,36},{3,37},{4,5},{5,4},{6,7},{7,6},{8,9},{9,8},{10,... | collective-permute-start | bytes 122888 | tf_op jit(solution)/shard_map/ppermute | solution.py:53
  91.1 2.4 %collective-permute-start.30 = (f32[2,16,256]{2,1,0:T(8,128)S(1)}, f32[2,16,256]{2,1,0:T(8,128)S(1)}, u32[]{:S(2)}, u32[]{:S(2)}) collective-permute-start(f32[2,16,256]{2,1,0:T(8,128)S(1)} %add_add_fusion.3), channel_id=1, source_target_pairs={{0,1},{1,0},{2,3},{3,2},{4,5},{5,4},{6,7},{7,6},{8,9},{9,8},{10,11... | collective-permute-start | bytes 98312 | tf_op jit(solution)/shard_map/ppermute | solution.py:53
  95.3 5.3 %collective-permute-start.34 = (f32[2,16,64]{2,1,0:T(8,128)S(1)}, f32[2,16,64]{2,1,0:T(8,128)S(1)}, u32[]{:S(2)}, u32[]{:S(2)}) collective-permute-start(f32[2,16,64]{2,1,0:T(8,128)S(1)} %maximum_subtract_fusion), channel_id=1, source_target_pairs={{0,1},{1,0},{2,66},{3,67},{4,5},{5,4},{6,7},{7,6},{8,9},{9,8},{10,... | collective-permute-start | bytes 24584 | tf_op jit(solution)/shard_map/ppermute | solution.py:53
  95.3 5.2 %collective-permute-start.33 = (f32[2,16,64]{2,1,0:T(8,128)S(1)}, f32[2,16,64]{2,1,0:T(8,128)S(1)}, u32[]{:S(2)}, u32[]{:S(2)}) collective-permute-start(f32[2,16,64]{2,1,0:T(8,128)S(1)} %maximum_subtract_fusion), channel_id=1, source_target_pairs={{0,1},{1,0},{2,34},{3,35},{4,5},{5,4},{6,7},{7,6},{8,9},{9,8},{10,... | collective-permute-start | bytes 24584 | tf_op jit(solution)/shard_map/ppermute | solution.py:53
  96.3 4.9 %collective-permute-start.32 = (f32[2,16,64]{2,1,0:T(8,128)S(1)}, f32[2,16,64]{2,1,0:T(8,128)S(1)}, u32[]{:S(2)}, u32[]{:S(2)}) collective-permute-start(f32[2,16,64]{2,1,0:T(8,128)S(1)} %maximum_subtract_fusion), channel_id=1, source_target_pairs={{0,1},{1,0},{2,98},{3,99},{4,5},{5,4},{6,7},{7,6},{8,9},{9,8},{10,... | collective-permute-start | bytes 24584 | tf_op jit(solution)/shard_map/ppermute | solution.py:53
  101.2 5.5 %collective-permute-start.37 = (f32[2,16,192]{2,1,0:T(8,128)S(1)}, f32[2,16,192]{2,1,0:T(8,128)S(1)}, u32[]{:S(2)}, u32[]{:S(2)}) collective-permute-start(f32[2,16,192]{2,1,0:T(8,128)S(1)} %pad_maximum_fusion.103), channel_id=1, source_target_pairs={{0,1},{1,0},{2,6},{3,7},{4,5},{5,4},{6,2},{7,3},{8,9},{9,8},{10,14... | collective-permute-start | bytes 73736 | tf_op jit(solution)/shard_map/ppermute | solution.py:53
  101.3 5.4 %collective-permute-start.36 = (f32[2,16,192]{2,1,0:T(8,128)S(1)}, f32[2,16,192]{2,1,0:T(8,128)S(1)}, u32[]{:S(2)}, u32[]{:S(2)}) collective-permute-start(f32[2,16,192]{2,1,0:T(8,128)S(1)} %pad_maximum_fusion.103), channel_id=1, source_target_pairs={{0,1},{1,0},{2,4},{3,5},{4,2},{5,3},{6,7},{7,6},{8,9},{9,8},{10,12... | collective-permute-start | bytes 73736 | tf_op jit(solution)/shard_map/ppermute | solution.py:53
  101.4 5.3 %collective-permute-start.35 = (f32[2,16,192]{2,1,0:T(8,128)S(1)}, f32[2,16,192]{2,1,0:T(8,128)S(1)}, u32[]{:S(2)}, u32[]{:S(2)}) collective-permute-start(f32[2,16,192]{2,1,0:T(8,128)S(1)} %pad_maximum_fusion.103), channel_id=1, source_target_pairs={{0,2},{1,3},{2,0},{3,1},{4,5},{5,4},{6,7},{7,6},{8,10},{9,11},{10,... | collective-permute-start | bytes 73736 | tf_op jit(solution)/shard_map/ppermute | solution.py:53
  (26 other events, 46.4 us)

commit v9 on v8

--- a/solution.py
+++ b/solution.py
@@ -155,12 +155,10 @@
     early1 = hop(product(((2, 0), (3, 0)), after(arrived, y1)), {(2, 0): (2, 1), (3, 0): (3, 2)}, ((2, 2), (1, 1)))
     y2 = finish((2, 1), given, early1 + product(((2, 1),), near1))
     near2 = hop(y2, {(2, 1): (3, 2)})
-    held1 = early1 + hop(product(((3, 1),), after(far1, y2)), {(3, 1): (3, 2)}, ((2, 2),))
+    held1 = early1 + hop(product(((3, 1),), after(far1, y2)), {(3, 1): (3, 2)}, ((0, 0),))
     y3 = finish((3, 2), given, held1 + product(((3, 2),), near2))
 
-    grams = [hop(after(gram, y1), {place: (0, 1)}) for place in ((1, 1), (2, 2), (3, 3))]
-    y3, grams = lax.optimization_barrier((y3, grams))
-    gram = gram + (grams[0] + grams[1] + grams[2])
+    sent1 = hop(after(gram, y1), {(1, 1): (0, 1)})
     back = hop(y0 + y1 + y2 + y3, {(0, 0): (0, 1), (1, 0): (1, 2), (2, 1): (2, 3), (3, 2): (3, 3)})
     solved = rotated(in_order(back, swap(back)))
 
@@ -169,19 +167,23 @@
     far3 = hop(x3, {(3, 3): (1, 3)})
     x2 = finish((2, 3), solved, product(((2, 3),), near3))
     near4 = hop(x2 + x3, {(2, 3): (1, 2), (3, 3): (0, 3)})
-    sent3 = hop(share(after(x3, x2), (3, 3)), {(3, 3): (0, 1)})
-    sent2 = hop(share(x2, (2, 3)), {(2, 3): (0, 1)})
     far4 = hop(x2, {(2, 3): (0, 2)})
-    near4, far4, sent2, sent3 = lax.optimization_barrier((near4, far4, sent2, sent3))
+    share3 = jnp.concatenate([share(after(x3, x2), (3, 3)), gram], 1)
+    share2 = jnp.concatenate([share(x2, (2, 3)), gram], 1)
+    near4, far4, sent1, share3, share2 = lax.optimization_barrier((near4, far4, sent1, share3, share2))
     side1 = hop(product(((1, 3),), after(far3, x2)), {(1, 3): (1, 2)}, ((1, 1),))
     x1 = finish((1, 2), solved, side1 + product(((1, 2),), near4))
     part1 = lax.cond(here((1, 2)), herm_rows, lambda v, w: small, x1, basis_half)
     near5 = hop(jnp.concatenate([x1, part1], 2), {(1, 2): (0, 1)})
+    sent3 = hop(after(share3, x1), {(3, 3): (0, 1)})
+    sent2 = hop(after(share2, x1), {(2, 3): (0, 1)})
+    near5, sent2, sent3 = lax.optimization_barrier((near5, sent2, sent3))
     moved = hop(after(x1 + x2 + x3, part1), {(1, 2): (1, 1), (2, 3): (2, 1), (3, 3): (3, 1)})
     carried = near5[:, :, half:]
     side0 = hop(after(product(((0, 3),), near4), part1), {(0, 3): (0, 1)}, ((0, 0),))
     held3 = side0 + hop(after(product(((0, 2),), far4), part1), {(0, 2): (0, 1)}, ((2, 2),))
-    sent = carried + sent2 + sent3
+    sent = carried + sent2[:, :nvec] + sent3[:, :nvec]
+    gram = gram + sent1 + sent2[:, nvec:] + sent3[:, nvec:]
     near5 = near5[:, :, :half]
     x0 = finish((0, 1), solved, held3 + product(((0, 1),), near5))
 

time: 109 us -> 121 us (1.11)
  starting transfers between devices: 31.3 us -> 40.8 us
  waiting for transfers between devices: 64.3 us -> 59.8 us
  local copies, waits for them, and re-layouts: 5.57 us -> 9.62 us
  other arithmetic: 2.32 us -> 4.97 us
    ppermute x30 -> x28, starting transfers between devices: 29.9 us -> 39.4 us  [move(): return lax.ppermute(value, AXES, pairs)]
    ppermute x30 -> x28, waiting for transfers between devices: 56.8 us -> 52.4 us  [move(): return lax.ppermute(value, AXES, pairs)]
    broadcast_in_dim x10, local copies, waits for them, and re-layouts: 0.06 us -> 1.32 us  [local(): blank = jnp.zeros((2, nvec, tile), jnp.float32)]
  transfers between devices with their start and end apart: 38 -> 36, of which waited for: 22 -> 21; matrix products, arithmetic and copies ran while one was open for 3% -> 7% of each run, Pallas kernels for 0% -> 0%
where the time goes in v9:
time: 121 us; the launch traced here: 120 us
  waiting for transfers between devices  59.8 us (49%)
  starting transfers between devices  40.8 us (34%)
  local copies, waits for them, and re-layouts  9.62 us (8%)
  other arithmetic  4.97 us (4%)
  matrix products  3.42 us (3%)
  between operations  1.34 us (1%)
    ppermute x28, waiting for transfers between devices, move(): return lax.ppermute(value, AXES, pairs)  52.4 us
    ppermute x28, starting transfers between devices, move(): return lax.ppermute(value, AXES, pairs)  39.4 us
    ppermute x8, waiting for transfers between devices, swap(): return lax.ppermute(value, 'c', [(0, 1), (1, 0)])  7.38 us
    dot_general x8, matrix products, dot_nt(): lax.dot_general(left, right, (((1,), (1,)), ((), ())), precision=precisio...  2.57 us
  transfers between devices with their start and end apart: 36, of which 21 were waited for; matrix products, arithmetic and copies ran while one was open for 7% of the time, Pallas kernels for 0%

profile of v9, /device:TPU:2, one launch (start us, length us, event | category | flops | bytes accessed | tf_op | source)
XLA Modules:
  0.0 120.2 jit_solution(8270269819094967896)
XLA Ops:
  1.7 1.1 constant_dynamic-update-slice_fusion.2
  2.8 1.6 %collective-permute-start.2 = (f32[2,592,128]{2,1,0:T(8,128)S(1)}, f32[2,592,128]{2,1,0:T(8,128)S(1)}, u32[]{:S(2)}, u32[]{:S(2)}) collective-permute-start(f32[2,592,128]{2,1,0:T(8,128)S(1)} %constant_dynamic-update-slice_fusion), channel_id=1, source_target_pairs={{0,8},{1,9},{2,10},{3,11},{4,12},{5,13},{6,14},{7,15},{8,16},{9,17... | collective-permute-start | bytes 1818632 | tf_op jit(solution)/shard_map/ppermute | solution.py:53
  4.5 2.9 %collective-permute-start.1 = (f32[2,592,128]{2,1,0:T(8,128)S(1)}, f32[2,592,128]{2,1,0:T(8,128)S(1)}, u32[]{:S(2)}, u32[]{:S(2)}) collective-permute-start(f32[2,592,128]{2,1,0:T(8,128)S(1)} %constant_dynamic-update-slice_fusion), channel_id=1, source_target_pairs={{0,16},{1,17},{2,18},{3,19},{4,20},{5,21},{6,22},{7,23},{8,24},{9,... | collective-permute-start | bytes 1818632 | tf_op jit(solution)/shard_map/ppermute | solution.py:53
  7.4 1.3 %collective-permute-start = (f32[2,592,128]{2,1,0:T(8,128)S(1)}, f32[2,592,128]{2,1,0:T(8,128)S(1)}, u32[]{:S(2)}, u32[]{:S(2)}) collective-permute-start(f32[2,592,128]{2,1,0:T(8,128)S(1)} %constant_dynamic-update-slice_fusion), channel_id=1, source_target_pairs={{0,24},{1,25},{2,26},{3,27},{4,28},{5,29},{6,30},{7,31},{8,0},{9,1... | collective-permute-start | bytes 1818632 | tf_op jit(solution)/shard_map/ppermute | solution.py:53
  8.7 10.9 %collective-permute-done.2 = f32[2,592,128]{2,1,0:T(8,128)S(1)} collective-permute-done((f32[2,592,128]{2,1,0:T(8,128)S(1)}, f32[2,592,128]{2,1,0:T(8,128)S(1)}, u32[]{:S(2)}, u32[]{:S(2)}) %collective-permute-start.2) | collective-permute-done | bytes 606240 | tf_op jit(solution)/shard_map/ppermute | solution.py:53
  19.6 14.2 %collective-permute-done.1 = f32[2,592,128]{2,1,0:T(8,128)S(1)} collective-permute-done((f32[2,592,128]{2,1,0:T(8,128)S(1)}, f32[2,592,128]{2,1,0:T(8,128)S(1)}, u32[]{:S(2)}, u32[]{:S(2)}) %collective-permute-start.1) | collective-permute-done | bytes 606240 | tf_op jit(solution)/shard_map/ppermute | solution.py:53
  37.8 1.0 fusion.255
  39.1 1.2 %collective-permute-done.4 = f32[2,16,512]{2,1,0:T(8,128)S(1)} collective-permute-done((f32[2,16,512]{2,1,0:T(8,128)S(1)}, f32[2,16,512]{2,1,0:T(8,128)S(1)}, u32[]{:S(2)}, u32[]{:S(2)}) %collective-permute-start.4) | collective-permute-done | bytes 65568 | tf_op jit(solution)/shard_map/ppermute | solution.py:57
  42.4 1.1 collective-permute-done.8
  46.4 15.3 %collective-permute-start.12 = (f32[2,16,256]{2,1,0:T(8,128)S(1)}, f32[2,16,256]{2,1,0:T(8,128)S(1)}, u32[]{:S(2)}, u32[]{:S(2)}) collective-permute-start(f32[2,16,256]{2,1,0:T(8,128)S(1)} %add_add_fusion.4), channel_id=1, source_target_pairs={{0,2},{1,3},{2,0},{3,1},{4,5},{5,4},{6,7},{7,6},{8,10},{9,11},{10,... | collective-permute-start | bytes 98312 | tf_op jit(solution)/shard_map/ppermute | solution.py:53
  61.6 1.9 %collective-permute-done.12 = f32[2,16,256]{2,1,0:T(8,128)S(1)} collective-permute-done((f32[2,16,256]{2,1,0:T(8,128)S(1)}, f32[2,16,256]{2,1,0:T(8,128)S(1)}, u32[]{:S(2)}, u32[]{:S(2)}) %collective-permute-start.12) | collective-permute-done | bytes 32800 | tf_op jit(solution)/shard_map/ppermute | solution.py:53
  63.5 1.2 collective-permute-done.13
  68.9 1.8 %collective-permute-done.18 = f32[2,64,64]{1,2,0:T(8,128)S(1)} collective-permute-done((f32[2,64,64]{1,2,0:T(8,128)S(1)}, f32[2,64,64]{1,2,0:T(8,128)S(1)}, u32[]{:S(2)}, u32[]{:S(2)}) %collective-permute-start.18) | collective-permute-done | bytes 32800 | tf_op jit(solution)/shard_map/ppermute | solution.py:53
  72.9 11.1 %collective-permute-start.25 = (f32[2,80,64]{1,2,0:T(8,128)}, f32[2,80,64]{1,2,0:T(8,128)S(1)}, u32[]{:S(2)}, u32[]{:S(2)}) collective-permute-start(f32[2,80,64]{1,2,0:T(8,128)} %get-tuple-element.282), channel_id=1, source_target_pairs={{0,1},{1,0},{2,70},{3,71},{4,5},{5,4},{6,7},{7,6},{8,9},{9,8},{10,... | collective-permute-start | bytes 122888 | tf_op jit(solution)/shard_map/ppermute | solution.py:53
  85.3 1.6 %collective-permute-done.25 = f32[2,80,64]{1,2,0:T(8,128)S(1)} collective-permute-done((f32[2,80,64]{1,2,0:T(8,128)}, f32[2,80,64]{1,2,0:T(8,128)S(1)}, u32[]{:S(2)}, u32[]{:S(2)}) %collective-permute-start.25) | collective-permute-done | bytes 40992 | tf_op jit(solution)/shard_map/ppermute | solution.py:53
  86.9 5.0 %collective-permute-done.26 = f32[2,80,64]{1,2,0:T(8,128)S(1)} collective-permute-done((f32[2,80,64]{1,2,0:T(8,128)S(1)}, f32[2,80,64]{1,2,0:T(8,128)S(1)}, u32[]{:S(2)}, u32[]{:S(2)}) %collective-permute-start.26) | collective-permute-done | bytes 40992 | tf_op jit(solution)/shard_map/ppermute | solution.py:53
  91.9 4.0 %collective-permute-done.24 = f32[2,16,320]{1,2,0:T(8,128)} collective-permute-done((f32[2,16,320]{1,2,0:T(8,128)}, f32[2,16,320]{1,2,0:T(8,128)}, u32[]{:S(2)}, u32[]{:S(2)}) %collective-permute-start.24) | collective-permute-done | bytes 40992 | tf_op jit(solution)/shard_map/ppermute | solution.py:53
  95.9 1.9 %conditional.43 = (f32[2,16,512]{2,1,0:T(8,128)S(1)}) conditional(s32[]{:T(128)} %convert_element_type.49, () %tuple.210, (f32[2,16,320]{1,2,0:T(8,128)}, f32[2,512,256]{2,1,0:T(8,128)S(1)}) %tuple.214), branch_computations={%region_40.41_spmd, %region_41.42_spmd} | conditional | flops 50380800 | bytes 1720328 | solution.py:130
  95.9 1.1 copy.45
  102.7 1.4 %collective-permute-done.29 = f32[2,16,320]{1,2,0:T(8,128)S(1)} collective-permute-done((f32[2,16,320]{1,2,0:T(8,128)S(1)}, f32[2,16,320]{1,2,0:T(8,128)S(1)}, u32[]{:S(2)}, u32[]{:S(2)}) %collective-permute-start.29) | collective-permute-done | bytes 40992 | tf_op jit(solution)/shard_map/ppermute | solution.py:57
  104.9 2.7 %collective-permute-start.31 = (f32[2,16,64]{1,2,0:T(8,128)S(1)}, f32[2,16,64]{1,2,0:T(8,128)S(1)}, u32[]{:S(2)}, u32[]{:S(2)}) collective-permute-start(f32[2,16,64]{1,2,0:T(8,128)S(1)} %multiply_subtract_fusion), channel_id=1, source_target_pairs={{0,1},{1,0},{2,34},{3,35},{4,5},{5,4},{6,7},{7,6},{8,9},{9,8},{10,... | collective-permute-start | bytes 24584 | tf_op jit(solution)/shard_map/ppermute | solution.py:53
  107.7 3.0 %collective-permute-done.32 = f32[2,16,64]{1,2,0:T(8,128)S(1)} collective-permute-done((f32[2,16,64]{1,2,0:T(8,128)S(1)}, f32[2,16,64]{1,2,0:T(8,128)S(1)}, u32[]{:S(2)}, u32[]{:S(2)}) %collective-permute-start.32) | collective-permute-done | bytes 8224 | tf_op jit(solution)/shard_map/ppermute | solution.py:53
  110.6 2.4 %collective-permute-done.30 = f32[2,16,64]{1,2,0:T(8,128)S(1)} collective-permute-done((f32[2,16,64]{1,2,0:T(8,128)S(1)}, f32[2,16,64]{1,2,0:T(8,128)S(1)}, u32[]{:S(2)}, u32[]{:S(2)}) %collective-permute-start.30) | collective-permute-done | bytes 8224 | tf_op jit(solution)/shard_map/ppermute | solution.py:53
  113.4 5.2 %collective-permute-done.35 = f32[2,16,192]{2,1,0:T(8,128)S(1)} collective-permute-done((f32[2,16,192]{2,1,0:T(8,128)S(1)}, f32[2,16,192]{2,1,0:T(8,128)S(1)}, u32[]{:S(2)}, u32[]{:S(2)}) %collective-permute-start.35) | collective-permute-done | bytes 24608 | tf_op jit(solution)/shard_map/ppermute | solution.py:53
  (199 shorter events, 28.5 us)
Async XLA Ops:
  2.8 16.8 %collective-permute-start.2 = (f32[2,592,128]{2,1,0:T(8,128)S(1)}, f32[2,592,128]{2,1,0:T(8,128)S(1)}, u32[]{:S(2)}, u32[]{:S(2)}) collective-permute-start(f32[2,592,128]{2,1,0:T(8,128)S(1)} %constant_dynamic-update-slice_fusion), channel_id=1, source_target_pairs={{0,8},{1,9},{2,10},{3,11},{4,12},{5,13},{6,14},{7,15},{8,16},{9,17... | collective-permute-start | bytes 1818632 | tf_op jit(solution)/shard_map/ppermute | solution.py:53
  4.5 29.3 %collective-permute-start.1 = (f32[2,592,128]{2,1,0:T(8,128)S(1)}, f32[2,592,128]{2,1,0:T(8,128)S(1)}, u32[]{:S(2)}, u32[]{:S(2)}) collective-permute-start(f32[2,592,128]{2,1,0:T(8,128)S(1)} %constant_dynamic-update-slice_fusion), channel_id=1, source_target_pairs={{0,16},{1,17},{2,18},{3,19},{4,20},{5,21},{6,22},{7,23},{8,24},{9,... | collective-permute-start | bytes 1818632 | tf_op jit(solution)/shard_map/ppermute | solution.py:53
  7.4 26.4 %collective-permute-start = (f32[2,592,128]{2,1,0:T(8,128)S(1)}, f32[2,592,128]{2,1,0:T(8,128)S(1)}, u32[]{:S(2)}, u32[]{:S(2)}) collective-permute-start(f32[2,592,128]{2,1,0:T(8,128)S(1)} %constant_dynamic-update-slice_fusion), channel_id=1, source_target_pairs={{0,24},{1,25},{2,26},{3,27},{4,28},{5,29},{6,30},{7,31},{8,0},{9,1... | collective-permute-start | bytes 1818632 | tf_op jit(solution)/shard_map/ppermute | solution.py:53
  36.6 2.3 %collective-permute-start.3 = (f32[2,16,256]{2,1,0:T(8,128)S(1)}, f32[2,16,256]{2,1,0:T(8,128)S(1)}, u32[]{:S(2)}, u32[]{:S(2)}) collective-permute-start(f32[2,16,256]{2,1,0:T(8,128)S(1)} %get-tuple-element.431), channel_id=1, source_target_pairs={{0,32},{1,33},{2,3},{3,2},{4,64},{5,65},{6,96},{7,97},{8,40},{9,41... | collective-permute-start | bytes 98312 | tf_op jit(solution)/shard_map/ppermute | solution.py:53
  40.3 1.8 %collective-permute-start.5 = (f32[2,16,512]{2,1,0:T(8,128)S(1)}, f32[2,16,512]{2,1,0:T(8,128)S(1)}, u32[]{:S(2)}, u32[]{:S(2)}) collective-permute-start(f32[2,16,512]{2,1,0:T(8,128)S(1)} %get-tuple-element.434), channel_id=1, source_target_pairs={{0,1},{1,0},{2,3},{3,2},{4,5},{5,4},{6,7},{7,6},{8,9},{9,8},{10,11... | collective-permute-start | bytes 196616 | tf_op jit(solution)/shard_map/ppermute | solution.py:53
  46.4 17.2 %collective-permute-start.12 = (f32[2,16,256]{2,1,0:T(8,128)S(1)}, f32[2,16,256]{2,1,0:T(8,128)S(1)}, u32[]{:S(2)}, u32[]{:S(2)}) collective-permute-start(f32[2,16,256]{2,1,0:T(8,128)S(1)} %add_add_fusion.4), channel_id=1, source_target_pairs={{0,2},{1,3},{2,0},{3,1},{4,5},{5,4},{6,7},{7,6},{8,10},{9,11},{10,... | collective-permute-start | bytes 98312 | tf_op jit(solution)/shard_map/ppermute | solution.py:53
  65.1 2.6 %collective-permute-start.19 = (f32[2,16,256]{2,1,0:T(8,128)S(1)}, f32[2,16,256]{2,1,0:T(8,128)S(1)}, u32[]{:S(2)}, u32[]{:S(2)}) collective-permute-start(f32[2,16,256]{2,1,0:T(8,128)S(1)} %get-tuple-element.440), channel_id=1, source_target_pairs={{0,1},{1,0},{2,3},{3,2},{4,5},{5,4},{6,7},{7,6},{8,9},{9,8},{10,11... | collective-permute-start | bytes 98312 | tf_op jit(solution)/shard_map/ppermute | solution.py:53
  66.3 4.4 %collective-permute-start.18 = (f32[2,64,64]{1,2,0:T(8,128)S(1)}, f32[2,64,64]{1,2,0:T(8,128)S(1)}, u32[]{:S(2)}, u32[]{:S(2)}) collective-permute-start(f32[2,64,64]{1,2,0:T(8,128)S(1)} %pad_maximum_fusion.101), channel_id=1, source_target_pairs={{0,1},{1,0},{2,34},{3,35},{4,5},{5,4},{6,7},{7,6},{8,9},{9,8},{10,... | collective-permute-start | bytes 98312 | tf_op jit(solution)/shard_map/ppermute | solution.py:53
  67.4 3.3 %collective-permute-start.17 = (f32[2,16,256]{2,1,0:T(8,128)S(1)}, f32[2,16,256]{2,1,0:T(8,128)S(1)}, u32[]{:S(2)}, u32[]{:S(2)}) collective-permute-start(f32[2,16,256]{2,1,0:T(8,128)S(1)} %get-tuple-element.442), channel_id=1, source_target_pairs={{0,1},{1,0},{2,3},{3,2},{4,70},{5,71},{6,7},{7,6},{8,9},{9,8},{10,... | collective-permute-start | bytes 98312 | tf_op jit(solution)/shard_map/ppermute | solution.py:53
  67.6 3.1 %collective-permute-start.16 = (f32[2,16,256]{2,1,0:T(8,128)S(1)}, f32[2,16,256]{2,1,0:T(8,128)S(1)}, u32[]{:S(2)}, u32[]{:S(2)}) collective-permute-start(f32[2,16,256]{2,1,0:T(8,128)S(1)} %add.191), channel_id=1, source_target_pairs={{0,1},{1,0},{2,3},{3,2},{4,5},{5,4},{6,102},{7,103},{8,9},{9,8},{1... | collective-permute-start | bytes 98312 | tf_op jit(solution)/shard_map/ppermute | solution.py:53
  68.0 2.8 %collective-permute-start.20 = (f32[2,16,512]{2,1,0:T(8,128)S(1)}, f32[2,16,512]{2,1,0:T(8,128)S(1)}, u32[]{:S(2)}, u32[]{:S(2)}) collective-permute-start(f32[2,16,512]{2,1,0:T(8,128)S(1)} %get-tuple-element.444), channel_id=1, source_target_pairs={{0,1},{1,0},{2,3},{3,2},{4,5},{5,4},{6,7},{7,6},{8,9},{9,8},{10,11... | collective-permute-start | bytes 196616 | tf_op jit(solution)/shard_map/ppermute | solution.py:53
  72.2 25.5 %collective-permute-start.22 = (f32[2,16,512]{2,1,0:T(8,128)}, f32[2,16,512]{2,1,0:T(8,128)}, u32[]{:S(2)}, u32[]{:S(2)}) collective-permute-start(f32[2,16,512]{2,1,0:T(8,128)} %get-tuple-element.443), channel_id=1, source_target_pairs={{0,6},{1,7},{2,0},{3,1},{4,5},{5,4},{6,2},{7,3},{8,14},{9,15},{10,... | collective-permute-start | bytes 196616 | tf_op jit(solution)/shard_map/ppermute | solution.py:53
  72.9 24.8 %collective-permute-start.23 = (f32[2,16,512]{2,1,0:T(8,128)}, f32[2,16,512]{2,1,0:T(8,128)}, u32[]{:S(2)}, u32[]{:S(2)}) collective-permute-start(f32[2,16,512]{2,1,0:T(8,128)} %get-tuple-element.448), channel_id=1, source_target_pairs={{0,1},{1,0},{2,68},{3,69},{4,2},{5,3},{6,7},{7,6},{8,9},{9,8},{10,... | collective-permute-start | bytes 196616 | tf_op jit(solution)/shard_map/ppermute | solution.py:53
  72.9 13.9 %collective-permute-start.25 = (f32[2,80,64]{1,2,0:T(8,128)}, f32[2,80,64]{1,2,0:T(8,128)S(1)}, u32[]{:S(2)}, u32[]{:S(2)}) collective-permute-start(f32[2,80,64]{1,2,0:T(8,128)} %get-tuple-element.282), channel_id=1, source_target_pairs={{0,1},{1,0},{2,70},{3,71},{4,5},{5,4},{6,7},{7,6},{8,9},{9,8},{10,... | collective-permute-start | bytes 122888 | tf_op jit(solution)/shard_map/ppermute | solution.py:53
  84.0 7.9 %collective-permute-start.26 = (f32[2,80,64]{1,2,0:T(8,128)S(1)}, f32[2,80,64]{1,2,0:T(8,128)S(1)}, u32[]{:S(2)}, u32[]{:S(2)}) collective-permute-start(f32[2,80,64]{1,2,0:T(8,128)S(1)} %get-tuple-element.284), channel_id=1, source_target_pairs={{0,1},{1,0},{2,102},{3,103},{4,5},{5,4},{6,7},{7,6},{8,9},{9,8},{1... | collective-permute-start | bytes 122888 | tf_op jit(solution)/shard_map/ppermute | solution.py:53
  84.9 11.0 %collective-permute-start.24 = (f32[2,16,320]{1,2,0:T(8,128)}, f32[2,16,320]{1,2,0:T(8,128)}, u32[]{:S(2)}, u32[]{:S(2)}) collective-permute-start(f32[2,16,320]{1,2,0:T(8,128)} %copy.44), channel_id=1, source_target_pairs={{0,1},{1,0},{2,36},{3,37},{4,5},{5,4},{6,7},{7,6},{8,9},{9,8},{10,... | collective-permute-start | bytes 122888 | tf_op jit(solution)/shard_map/ppermute | solution.py:53
  98.8 3.5 %collective-permute-start.28 = (f32[2,16,256]{1,2,0:T(8,128)S(1)}, f32[2,16,256]{1,2,0:T(8,128)S(1)}, u32[]{:S(2)}, u32[]{:S(2)}) collective-permute-start(f32[2,16,256]{1,2,0:T(8,128)S(1)} %add_add_fusion), channel_id=1, source_target_pairs={{0,1},{1,0},{2,3},{3,2},{4,5},{5,4},{6,7},{7,6},{8,9},{9,8},{10,11... | collective-permute-start | bytes 98312 | tf_op jit(solution)/shard_map/ppermute | solution.py:53
  102.3 1.7 %collective-permute-start.29 = (f32[2,16,320]{1,2,0:T(8,128)S(1)}, f32[2,16,320]{1,2,0:T(8,128)S(1)}, u32[]{:S(2)}, u32[]{:S(2)}) collective-permute-start(f32[2,16,320]{1,2,0:T(8,128)S(1)} %pad_maximum_fusion.93), channel_id=1, source_target_pairs={{0,1},{1,0},{2,3},{3,2},{4,5},{5,4},{6,7},{7,6},{8,9},{9,8},{10,11... | collective-permute-start | bytes 122888 | tf_op jit(solution)/shard_map/ppermute | solution.py:57
  104.8 5.8 %collective-permute-start.32 = (f32[2,16,64]{1,2,0:T(8,128)S(1)}, f32[2,16,64]{1,2,0:T(8,128)S(1)}, u32[]{:S(2)}, u32[]{:S(2)}) collective-permute-start(f32[2,16,64]{1,2,0:T(8,128)S(1)} %multiply_subtract_fusion), channel_id=1, source_target_pairs={{0,1},{1,0},{2,66},{3,67},{4,5},{5,4},{6,7},{7,6},{8,9},{9,8},{10,... | collective-permute-start | bytes 24584 | tf_op jit(solution)/shard_map/ppermute | solution.py:53
  104.9 5.8 %collective-permute-start.31 = (f32[2,16,64]{1,2,0:T(8,128)S(1)}, f32[2,16,64]{1,2,0:T(8,128)S(1)}, u32[]{:S(2)}, u32[]{:S(2)}) collective-permute-start(f32[2,16,64]{1,2,0:T(8,128)S(1)} %multiply_subtract_fusion), channel_id=1, source_target_pairs={{0,1},{1,0},{2,34},{3,35},{4,5},{5,4},{6,7},{7,6},{8,9},{9,8},{10,... | collective-permute-start | bytes 24584 | tf_op jit(solution)/shard_map/ppermute | solution.py:53
  107.6 5.5 %collective-permute-start.30 = (f32[2,16,64]{1,2,0:T(8,128)S(1)}, f32[2,16,64]{1,2,0:T(8,128)S(1)}, u32[]{:S(2)}, u32[]{:S(2)}) collective-permute-start(f32[2,16,64]{1,2,0:T(8,128)S(1)} %multiply_subtract_fusion), channel_id=1, source_target_pairs={{0,1},{1,0},{2,98},{3,99},{4,5},{5,4},{6,7},{7,6},{8,9},{9,8},{10,... | collective-permute-start | bytes 24584 | tf_op jit(solution)/shard_map/ppermute | solution.py:53
  113.1 5.5 %collective-permute-start.35 = (f32[2,16,192]{2,1,0:T(8,128)S(1)}, f32[2,16,192]{2,1,0:T(8,128)S(1)}, u32[]{:S(2)}, u32[]{:S(2)}) collective-permute-start(f32[2,16,192]{2,1,0:T(8,128)S(1)} %pad_maximum_fusion.106), channel_id=1, source_target_pairs={{0,1},{1,0},{2,6},{3,7},{4,5},{5,4},{6,2},{7,3},{8,9},{9,8},{10,14... | collective-permute-start | bytes 73736 | tf_op jit(solution)/shard_map/ppermute | solution.py:53
  113.2 5.4 %collective-permute-start.34 = (f32[2,16,192]{2,1,0:T(8,128)S(1)}, f32[2,16,192]{2,1,0:T(8,128)S(1)}, u32[]{:S(2)}, u32[]{:S(2)}) collective-permute-start(f32[2,16,192]{2,1,0:T(8,128)S(1)} %pad_maximum_fusion.106), channel_id=1, source_target_pairs={{0,1},{1,0},{2,4},{3,5},{4,2},{5,3},{6,7},{7,6},{8,9},{9,8},{10,12... | collective-permute-start | bytes 73736 | tf_op jit(solution)/shard_map/ppermute | solution.py:53
  113.3 5.3 %collective-permute-start.33 = (f32[2,16,192]{2,1,0:T(8,128)S(1)}, f32[2,16,192]{2,1,0:T(8,128)S(1)}, u32[]{:S(2)}, u32[]{:S(2)}) collective-permute-start(f32[2,16,192]{2,1,0:T(8,128)S(1)} %pad_maximum_fusion.106), channel_id=1, source_target_pairs={{0,2},{1,3},{2,0},{3,1},{4,5},{5,4},{6,7},{7,6},{8,10},{9,11},{10,... | collective-permute-start | bytes 73736 | tf_op jit(solution)/shard_map/ppermute | solution.py:53
  (24 other events, 42.2 us)

commit v10 on v8

--- a/solution.py
+++ b/solution.py
@@ -155,7 +155,7 @@
     early1 = hop(product(((2, 0), (3, 0)), after(arrived, y1)), {(2, 0): (2, 1), (3, 0): (3, 2)}, ((2, 2), (1, 1)))
     y2 = finish((2, 1), given, early1 + product(((2, 1),), near1))
     near2 = hop(y2, {(2, 1): (3, 2)})
-    held1 = early1 + hop(product(((3, 1),), after(far1, y2)), {(3, 1): (3, 2)}, ((2, 2),))
+    held1 = early1 + hop(product(((3, 1),), after(far1, y2)), {(3, 1): (3, 2)}, ((0, 0),))
     y3 = finish((3, 2), given, held1 + product(((3, 2),), near2))
 
     grams = [hop(after(gram, y1), {place: (0, 1)}) for place in ((1, 1), (2, 2), (3, 3))]
@@ -169,14 +169,13 @@
     far3 = hop(x3, {(3, 3): (1, 3)})
     x2 = finish((2, 3), solved, product(((2, 3),), near3))
     near4 = hop(x2 + x3, {(2, 3): (1, 2), (3, 3): (0, 3)})
-    sent3 = hop(share(after(x3, x2), (3, 3)), {(3, 3): (0, 1)})
-    sent2 = hop(share(x2, (2, 3)), {(2, 3): (0, 1)})
+    side1 = hop(product(((1, 3),), after(far3, x2)), {(1, 3): (1, 2)}, ((1, 1),))
     far4 = hop(x2, {(2, 3): (0, 2)})
-    near4, far4, sent2, sent3 = lax.optimization_barrier((near4, far4, sent2, sent3))
-    side1 = hop(product(((1, 3),), after(far3, x2)), {(1, 3): (1, 2)}, ((1, 1),))
     x1 = finish((1, 2), solved, side1 + product(((1, 2),), near4))
     part1 = lax.cond(here((1, 2)), herm_rows, lambda v, w: small, x1, basis_half)
     near5 = hop(jnp.concatenate([x1, part1], 2), {(1, 2): (0, 1)})
+    sent3 = hop(share(after(x3, part1), (3, 3)), {(3, 3): (0, 1)})
+    sent2 = hop(share(after(x2, part1), (2, 3)), {(2, 3): (0, 1)})
     moved = hop(after(x1 + x2 + x3, part1), {(1, 2): (1, 1), (2, 3): (2, 1), (3, 3): (3, 1)})
     carried = near5[:, :, half:]
     side0 = hop(after(product(((0, 3),), near4), part1), {(0, 3): (0, 1)}, ((0, 0),))

time: 109 us -> 109 us (level)
  starting transfers between devices: 31.3 us -> 35.1 us
  waiting for transfers between devices: 64.3 us -> 61.3 us
    ppermute x30, starting transfers between devices: 29.9 us -> 33.6 us  [move(): return lax.ppermute(value, AXES, pairs)]
    ppermute x30, waiting for transfers between devices: 56.8 us -> 54.1 us  [move(): return lax.ppermute(value, AXES, pairs)]
  transfers between devices with their start and end apart: 38 -> 38, of which waited for: 22 -> 23; matrix products, arithmetic and copies ran while one was open for 3% -> 3% of each run, Pallas kernels for 0% -> 0%
where the time goes in v10:
time: 109 us
  waiting for transfers between devices  61.3 us (56%)
  starting transfers between devices  35.1 us (32%)
  local copies, waits for them, and re-layouts  5.57 us (5%)
  matrix products  3.16 us (3%)
  other arithmetic  2.32 us (2%)
  between operations  1.35 us (1%)
    ppermute x30, waiting for transfers between devices, move(): return lax.ppermute(value, AXES, pairs)  54.1 us
    ppermute x30, starting transfers between devices, move(): return lax.ppermute(value, AXES, pairs)  33.6 us
    ppermute x8, waiting for transfers between devices, swap(): return lax.ppermute(value, 'c', [(0, 1), (1, 0)])  7.16 us
    dot_general x8, matrix products, dot_nt(): lax.dot_general(left, right, (((1,), (1,)), ((), ())), precision=precisio...  2.55 us
  transfers between devices with their start and end apart: 38, of which 23 were waited for; matrix products, arithmetic and copies ran while one was open for 3% of the time, Pallas kernels for 0%

profile of v10, /device:TPU:2, one launch (start us, length us, event | category | flops | bytes accessed | tf_op | source)
XLA Modules:
  0.0 109.1 jit_solution(4277330513030760374)
XLA Ops:
  0.7 1.0 slice_dynamic-update-slice_fusion.1
  1.7 1.1 %constant_dynamic-update-slice_fusion.2 = (f32[2,592,128]{2,1,0:T(8,128)S(1)}, f32[2,256,128]{2,1,0:T(8,128)S(1)}) fusion(f32[2,592,128]{2,1,0:T(8,128)S(1)} %slice_dynamic-update-slice_fusion, f32[2,512,128]{2,1,0:T(8,128)} %param.53, s32[]{:T(128)S(6)} %select_n.121, f32[2,512,128]{2,1,0:T(8,128)} %param.52, pred[]{:T(512)S(6)} %select_n.119), kind=kLoop, calls=%fused_computation.438 | loop fusion | flops 65536 | bytes 1048581
  2.8 1.6 %collective-permute-start.2 = (f32[2,592,128]{2,1,0:T(8,128)S(1)}, f32[2,592,128]{2,1,0:T(8,128)S(1)}, u32[]{:S(2)}, u32[]{:S(2)}) collective-permute-start(f32[2,592,128]{2,1,0:T(8,128)S(1)} %constant_dynamic-update-slice_fusion), channel_id=1, source_target_pairs={{0,8},{1,9},{2,10},{3,11},{4,12},{5,13},{6,14},{7,15},{8,16},{9,17... | collective-permute-start | bytes 1818632 | tf_op jit(solution)/shard_map/ppermute | solution.py:53
  4.5 2.9 %collective-permute-start.1 = (f32[2,592,128]{2,1,0:T(8,128)S(1)}, f32[2,592,128]{2,1,0:T(8,128)S(1)}, u32[]{:S(2)}, u32[]{:S(2)}) collective-permute-start(f32[2,592,128]{2,1,0:T(8,128)S(1)} %constant_dynamic-update-slice_fusion), channel_id=1, source_target_pairs={{0,16},{1,17},{2,18},{3,19},{4,20},{5,21},{6,22},{7,23},{8,24},{9,... | collective-permute-start | bytes 1818632 | tf_op jit(solution)/shard_map/ppermute | solution.py:53
  7.4 1.3 %collective-permute-start = (f32[2,592,128]{2,1,0:T(8,128)S(1)}, f32[2,592,128]{2,1,0:T(8,128)S(1)}, u32[]{:S(2)}, u32[]{:S(2)}) collective-permute-start(f32[2,592,128]{2,1,0:T(8,128)S(1)} %constant_dynamic-update-slice_fusion), channel_id=1, source_target_pairs={{0,24},{1,25},{2,26},{3,27},{4,28},{5,29},{6,30},{7,31},{8,0},{9,1... | collective-permute-start | bytes 1818632 | tf_op jit(solution)/shard_map/ppermute | solution.py:53
  8.7 10.9 %collective-permute-done.2 = f32[2,592,128]{2,1,0:T(8,128)S(1)} collective-permute-done((f32[2,592,128]{2,1,0:T(8,128)S(1)}, f32[2,592,128]{2,1,0:T(8,128)S(1)}, u32[]{:S(2)}, u32[]{:S(2)}) %collective-permute-start.2) | collective-permute-done | bytes 606240 | tf_op jit(solution)/shard_map/ppermute | solution.py:53
  19.6 14.2 %collective-permute-done.1 = f32[2,592,128]{2,1,0:T(8,128)S(1)} collective-permute-done((f32[2,592,128]{2,1,0:T(8,128)S(1)}, f32[2,592,128]{2,1,0:T(8,128)S(1)}, u32[]{:S(2)}, u32[]{:S(2)}) %collective-permute-start.1) | collective-permute-done | bytes 606240 | tf_op jit(solution)/shard_map/ppermute | solution.py:53
  35.5 0.9 slice-done.1
  37.8 1.0 fusion.257
  39.1 1.2 %collective-permute-done.4 = f32[2,16,512]{2,1,0:T(8,128)S(1)} collective-permute-done((f32[2,16,512]{2,1,0:T(8,128)S(1)}, f32[2,16,512]{2,1,0:T(8,128)S(1)}, u32[]{:S(2)}, u32[]{:S(2)}) %collective-permute-start.4) | collective-permute-done | bytes 65568 | tf_op jit(solution)/shard_map/ppermute | solution.py:57
  42.4 1.1 %collective-permute-done.8 = f32[2,16,512]{2,1,0:T(8,128)S(1)} collective-permute-done((f32[2,16,512]{2,1,0:T(8,128)S(1)}, f32[2,16,512]{2,1,0:T(8,128)S(1)}, u32[]{:S(2)}, u32[]{:S(2)}) %collective-permute-start.8) | collective-permute-done | bytes 65568 | tf_op jit(solution)/shard_map/ppermute | solution.py:57
  45.4 5.6 %collective-permute-start.14 = (f32[2,64,64]{1,2,0:T(8,128)S(1)}, f32[2,64,64]{1,2,0:T(8,128)S(1)}, u32[]{:S(2)}, u32[]{:S(2)}) collective-permute-start(f32[2,64,64]{1,2,0:T(8,128)S(1)} %pad_maximum_fusion.100), channel_id=1, source_target_pairs={{0,1},{1,0},{2,102},{3,103},{4,5},{5,4},{6,7},{7,6},{8,9},{9,8},{1... | collective-permute-start | bytes 98312 | tf_op jit(solution)/shard_map/ppermute | solution.py:53
  51.0 6.4 %collective-permute-start.13 = (f32[2,64,64]{1,2,0:T(8,128)S(1)}, f32[2,64,64]{1,2,0:T(8,128)S(1)}, u32[]{:S(2)}, u32[]{:S(2)}) collective-permute-start(f32[2,64,64]{1,2,0:T(8,128)S(1)} %pad_maximum_fusion.100), channel_id=1, source_target_pairs={{0,1},{1,0},{2,68},{3,69},{4,5},{5,4},{6,7},{7,6},{8,9},{9,8},{10,... | collective-permute-start | bytes 98312 | tf_op jit(solution)/shard_map/ppermute | solution.py:53
  57.4 2.6 %collective-permute-done.13 = f32[2,64,64]{1,2,0:T(8,128)S(1)} collective-permute-done((f32[2,64,64]{1,2,0:T(8,128)S(1)}, f32[2,64,64]{1,2,0:T(8,128)S(1)}, u32[]{:S(2)}, u32[]{:S(2)}) %collective-permute-start.13) | collective-permute-done | bytes 32800 | tf_op jit(solution)/shard_map/ppermute | solution.py:53
  60.0 1.7 %collective-permute-done.12 = f32[2,64,64]{1,2,0:T(8,128)S(1)} collective-permute-done((f32[2,64,64]{1,2,0:T(8,128)S(1)}, f32[2,64,64]{1,2,0:T(8,128)S(1)}, u32[]{:S(2)}, u32[]{:S(2)}) %collective-permute-start.12) | collective-permute-done | bytes 32800 | tf_op jit(solution)/shard_map/ppermute | solution.py:53
  62.3 3.4 %collective-permute-done.15 = f32[2,16,256]{2,1,0:T(8,128)S(1)} collective-permute-done((f32[2,16,256]{2,1,0:T(8,128)S(1)}, f32[2,16,256]{2,1,0:T(8,128)S(1)}, u32[]{:S(2)}, u32[]{:S(2)}) %collective-permute-start.15) | collective-permute-done | bytes 32800 | tf_op jit(solution)/shard_map/ppermute | solution.py:53
  65.7 1.2 %collective-permute-done.16 = f32[2,16,256]{2,1,0:T(8,128)S(1)} collective-permute-done((f32[2,16,256]{2,1,0:T(8,128)S(1)}, f32[2,16,256]{2,1,0:T(8,128)S(1)}, u32[]{:S(2)}, u32[]{:S(2)}) %collective-permute-start.16) | collective-permute-done | bytes 32800 | tf_op jit(solution)/shard_map/ppermute | solution.py:57
  68.5 1.1 collective-permute-done.18
  73.1 10.5 %collective-permute-start.26 = (f32[2,16,320]{2,1,0:T(8,128)S(1)}, f32[2,16,320]{2,1,0:T(8,128)S(1)}, u32[]{:S(2)}, u32[]{:S(2)}) collective-permute-start(f32[2,16,320]{2,1,0:T(8,128)S(1)} %pad_maximum_fusion.101), channel_id=1, source_target_pairs={{0,1},{1,0},{2,36},{3,37},{4,5},{5,4},{6,7},{7,6},{8,9},{9,8},{10,... | collective-permute-start | bytes 122888 | tf_op jit(solution)/shard_map/ppermute | solution.py:53
  83.6 2.1 %collective-permute-done.26 = f32[2,16,320]{2,1,0:T(8,128)S(1)} collective-permute-done((f32[2,16,320]{2,1,0:T(8,128)S(1)}, f32[2,16,320]{2,1,0:T(8,128)S(1)}, u32[]{:S(2)}, u32[]{:S(2)}) %collective-permute-start.26) | collective-permute-done | bytes 40992 | tf_op jit(solution)/shard_map/ppermute | solution.py:53
  89.0 5.5 %collective-permute-done.30 = f32[2,16,64]{2,1,0:T(8,128)S(1)} collective-permute-done((f32[2,16,64]{2,1,0:T(8,128)S(1)}, f32[2,16,64]{2,1,0:T(8,128)S(1)}, u32[]{:S(2)}, u32[]{:S(2)}) %collective-permute-start.30) | collective-permute-done | bytes 8224 | tf_op jit(solution)/shard_map/ppermute | solution.py:53
  95.0 1.2 %collective-permute-done.31 = f32[2,16,320]{2,1,0:T(8,128)S(1)} collective-permute-done((f32[2,16,320]{2,1,0:T(8,128)S(1)}, f32[2,16,320]{2,1,0:T(8,128)S(1)}, u32[]{:S(2)}, u32[]{:S(2)}) %collective-permute-start.31) | collective-permute-done | bytes 40992 | tf_op jit(solution)/shard_map/ppermute | solution.py:57
  96.9 5.0 %collective-permute-done.34 = f32[2,16,64]{2,1,0:T(8,128)S(1)} collective-permute-done((f32[2,16,64]{2,1,0:T(8,128)S(1)}, f32[2,16,64]{2,1,0:T(8,128)S(1)}, u32[]{:S(2)}, u32[]{:S(2)}) %collective-permute-start.34) | collective-permute-done | bytes 8224 | tf_op jit(solution)/shard_map/ppermute | solution.py:53
  102.3 5.2 %collective-permute-done.37 = f32[2,16,192]{2,1,0:T(8,128)S(1)} collective-permute-done((f32[2,16,192]{2,1,0:T(8,128)S(1)}, f32[2,16,192]{2,1,0:T(8,128)S(1)}, u32[]{:S(2)}, u32[]{:S(2)}) %collective-permute-start.37) | collective-permute-done | bytes 24608 | tf_op jit(solution)/shard_map/ppermute | solution.py:53
  (191 shorter events, 21.2 us)
Async XLA Ops:
  2.8 16.8 %collective-permute-start.2 = (f32[2,592,128]{2,1,0:T(8,128)S(1)}, f32[2,592,128]{2,1,0:T(8,128)S(1)}, u32[]{:S(2)}, u32[]{:S(2)}) collective-permute-start(f32[2,592,128]{2,1,0:T(8,128)S(1)} %constant_dynamic-update-slice_fusion), channel_id=1, source_target_pairs={{0,8},{1,9},{2,10},{3,11},{4,12},{5,13},{6,14},{7,15},{8,16},{9,17... | collective-permute-start | bytes 1818632 | tf_op jit(solution)/shard_map/ppermute | solution.py:53
  4.5 29.3 %collective-permute-start.1 = (f32[2,592,128]{2,1,0:T(8,128)S(1)}, f32[2,592,128]{2,1,0:T(8,128)S(1)}, u32[]{:S(2)}, u32[]{:S(2)}) collective-permute-start(f32[2,592,128]{2,1,0:T(8,128)S(1)} %constant_dynamic-update-slice_fusion), channel_id=1, source_target_pairs={{0,16},{1,17},{2,18},{3,19},{4,20},{5,21},{6,22},{7,23},{8,24},{9,... | collective-permute-start | bytes 1818632 | tf_op jit(solution)/shard_map/ppermute | solution.py:53
  7.4 26.4 %collective-permute-start = (f32[2,592,128]{2,1,0:T(8,128)S(1)}, f32[2,592,128]{2,1,0:T(8,128)S(1)}, u32[]{:S(2)}, u32[]{:S(2)}) collective-permute-start(f32[2,592,128]{2,1,0:T(8,128)S(1)} %constant_dynamic-update-slice_fusion), channel_id=1, source_target_pairs={{0,24},{1,25},{2,26},{3,27},{4,28},{5,29},{6,30},{7,31},{8,0},{9,1... | collective-permute-start | bytes 1818632 | tf_op jit(solution)/shard_map/ppermute | solution.py:53
  36.6 2.3 %collective-permute-start.3 = (f32[2,16,256]{2,1,0:T(8,128)S(1)}, f32[2,16,256]{2,1,0:T(8,128)S(1)}, u32[]{:S(2)}, u32[]{:S(2)}) collective-permute-start(f32[2,16,256]{2,1,0:T(8,128)S(1)} %get-tuple-element.402), channel_id=1, source_target_pairs={{0,32},{1,33},{2,3},{3,2},{4,64},{5,65},{6,96},{7,97},{8,40},{9,41... | collective-permute-start | bytes 98312 | tf_op jit(solution)/shard_map/ppermute | solution.py:53
  40.3 1.8 %collective-permute-start.5 = (f32[2,16,512]{2,1,0:T(8,128)S(1)}, f32[2,16,512]{2,1,0:T(8,128)S(1)}, u32[]{:S(2)}, u32[]{:S(2)}) collective-permute-start(f32[2,16,512]{2,1,0:T(8,128)S(1)} %get-tuple-element.405), channel_id=1, source_target_pairs={{0,1},{1,0},{2,3},{3,2},{4,5},{5,4},{6,7},{7,6},{8,9},{9,8},{10,11... | collective-permute-start | bytes 196616 | tf_op jit(solution)/shard_map/ppermute | solution.py:53
  43.5 1.4 %collective-permute-start.9 = (f32[2,16,512]{2,1,0:T(8,128)S(1)}, f32[2,16,512]{2,1,0:T(8,128)S(1)}, u32[]{:S(2)}, u32[]{:S(2)}) collective-permute-start(f32[2,16,512]{2,1,0:T(8,128)S(1)} %get-tuple-element.408), channel_id=1, source_target_pairs={{0,98},{1,99},{2,3},{3,2},{4,5},{5,4},{6,7},{7,6},{8,106},{9,107},... | collective-permute-start | bytes 196616 | tf_op jit(solution)/shard_map/ppermute | solution.py:53
  45.0 12.4 %collective-permute-start.11 = (f32[2,16,512]{2,1,0:T(8,128)S(1)}, f32[2,16,512]{2,1,0:T(8,128)S(1)}, u32[]{:S(2)}, u32[]{:S(2)}) collective-permute-start(f32[2,16,512]{2,1,0:T(8,128)S(1)} %add_add_fusion.2), channel_id=1, source_target_pairs={{0,1},{1,0},{2,3},{3,2},{4,5},{5,4},{6,7},{7,6},{8,9},{9,8},{10,11... | collective-permute-start | bytes 196616 | tf_op jit(solution)/shard_map/ppermute | solution.py:57
  45.4 12.0 %collective-permute-start.14 = (f32[2,64,64]{1,2,0:T(8,128)S(1)}, f32[2,64,64]{1,2,0:T(8,128)S(1)}, u32[]{:S(2)}, u32[]{:S(2)}) collective-permute-start(f32[2,64,64]{1,2,0:T(8,128)S(1)} %pad_maximum_fusion.100), channel_id=1, source_target_pairs={{0,1},{1,0},{2,102},{3,103},{4,5},{5,4},{6,7},{7,6},{8,9},{9,8},{1... | collective-permute-start | bytes 98312 | tf_op jit(solution)/shard_map/ppermute | solution.py:53
  51.0 9.0 %collective-permute-start.13 = (f32[2,64,64]{1,2,0:T(8,128)S(1)}, f32[2,64,64]{1,2,0:T(8,128)S(1)}, u32[]{:S(2)}, u32[]{:S(2)}) collective-permute-start(f32[2,64,64]{1,2,0:T(8,128)S(1)} %pad_maximum_fusion.100), channel_id=1, source_target_pairs={{0,1},{1,0},{2,68},{3,69},{4,5},{5,4},{6,7},{7,6},{8,9},{9,8},{10,... | collective-permute-start | bytes 98312 | tf_op jit(solution)/shard_map/ppermute | solution.py:53
  57.4 4.3 %collective-permute-start.12 = (f32[2,64,64]{1,2,0:T(8,128)S(1)}, f32[2,64,64]{1,2,0:T(8,128)S(1)}, u32[]{:S(2)}, u32[]{:S(2)}) collective-permute-start(f32[2,64,64]{1,2,0:T(8,128)S(1)} %pad_maximum_fusion.100), channel_id=1, source_target_pairs={{0,1},{1,0},{2,34},{3,35},{4,5},{5,4},{6,7},{7,6},{8,9},{9,8},{10,... | collective-permute-start | bytes 98312 | tf_op jit(solution)/shard_map/ppermute | solution.py:53
  61.7 4.0 %collective-permute-start.15 = (f32[2,16,256]{2,1,0:T(8,128)S(1)}, f32[2,16,256]{2,1,0:T(8,128)S(1)}, u32[]{:S(2)}, u32[]{:S(2)}) collective-permute-start(f32[2,16,256]{2,1,0:T(8,128)S(1)} %add_add_fusion.4), channel_id=1, source_target_pairs={{0,2},{1,3},{2,0},{3,1},{4,5},{5,4},{6,7},{7,6},{8,10},{9,11},{10,... | collective-permute-start | bytes 98312 | tf_op jit(solution)/shard_map/ppermute | solution.py:53
  67.2 2.4 %collective-permute-start.20 = (f32[2,16,256]{2,1,0:T(8,128)S(1)}, f32[2,16,256]{2,1,0:T(8,128)S(1)}, u32[]{:S(2)}, u32[]{:S(2)}) collective-permute-start(f32[2,16,256]{2,1,0:T(8,128)S(1)} %get-tuple-element.411), channel_id=1, source_target_pairs={{0,1},{1,0},{2,3},{3,2},{4,5},{5,4},{6,7},{7,6},{8,9},{9,8},{10,11... | collective-permute-start | bytes 98312 | tf_op jit(solution)/shard_map/ppermute | solution.py:53
  72.5 13.9 %collective-permute-start.23 = (f32[2,16,512]{2,1,0:T(8,128)S(1)}, f32[2,16,512]{2,1,0:T(8,128)S(1)}, u32[]{:S(2)}, u32[]{:S(2)}) collective-permute-start(f32[2,16,512]{2,1,0:T(8,128)S(1)} %get-tuple-element.414), channel_id=1, source_target_pairs={{0,6},{1,7},{2,0},{3,1},{4,5},{5,4},{6,2},{7,3},{8,14},{9,15},{10,... | collective-permute-start | bytes 196616 | tf_op jit(solution)/shard_map/ppermute | solution.py:53
  73.1 13.3 %collective-permute-start.25 = (f32[2,16,512]{2,1,0:T(8,128)S(1)}, f32[2,16,512]{2,1,0:T(8,128)S(1)}, u32[]{:S(2)}, u32[]{:S(2)}) collective-permute-start(f32[2,16,512]{2,1,0:T(8,128)S(1)} %get-tuple-element.419), channel_id=1, source_target_pairs={{0,1},{1,0},{2,68},{3,69},{4,2},{5,3},{6,7},{7,6},{8,9},{9,8},{10,... | collective-permute-start | bytes 196616 | tf_op jit(solution)/shard_map/ppermute | solution.py:53
  73.1 12.5 %collective-permute-start.26 = (f32[2,16,320]{2,1,0:T(8,128)S(1)}, f32[2,16,320]{2,1,0:T(8,128)S(1)}, u32[]{:S(2)}, u32[]{:S(2)}) collective-permute-start(f32[2,16,320]{2,1,0:T(8,128)S(1)} %pad_maximum_fusion.101), channel_id=1, source_target_pairs={{0,1},{1,0},{2,36},{3,37},{4,5},{5,4},{6,7},{7,6},{8,9},{9,8},{10,... | collective-permute-start | bytes 122888 | tf_op jit(solution)/shard_map/ppermute | solution.py:53
  86.6 2.0 %collective-permute-start.28 = (f32[2,16,256]{2,1,0:T(8,128)S(1)}, f32[2,16,256]{2,1,0:T(8,128)S(1)}, u32[]{:S(2)}, u32[]{:S(2)}) collective-permute-start(f32[2,16,256]{2,1,0:T(8,128)S(1)} %add_add_fusion.3), channel_id=1, source_target_pairs={{0,1},{1,0},{2,3},{3,2},{4,5},{5,4},{6,7},{7,6},{8,9},{9,8},{10,11... | collective-permute-start | bytes 98312 | tf_op jit(solution)/shard_map/ppermute | solution.py:53
  87.1 7.4 %collective-permute-start.30 = (f32[2,16,64]{2,1,0:T(8,128)S(1)}, f32[2,16,64]{2,1,0:T(8,128)S(1)}, u32[]{:S(2)}, u32[]{:S(2)}) collective-permute-start(f32[2,16,64]{2,1,0:T(8,128)S(1)} %get-tuple-element.424), channel_id=1, source_target_pairs={{0,1},{1,0},{2,102},{3,103},{4,5},{5,4},{6,7},{7,6},{8,9},{9,8},{1... | collective-permute-start | bytes 24584 | tf_op jit(solution)/shard_map/ppermute | solution.py:53
  87.1 7.7 %collective-permute-start.29 = (f32[2,16,64]{2,1,0:T(8,128)S(1)}, f32[2,16,64]{2,1,0:T(8,128)S(1)}, u32[]{:S(2)}, u32[]{:S(2)}) collective-permute-start(f32[2,16,64]{2,1,0:T(8,128)S(1)} %get-tuple-element.423), channel_id=1, source_target_pairs={{0,1},{1,0},{2,70},{3,71},{4,5},{5,4},{6,7},{7,6},{8,9},{9,8},{10,... | collective-permute-start | bytes 24584 | tf_op jit(solution)/shard_map/ppermute | solution.py:53
  96.6 5.3 %collective-permute-start.34 = (f32[2,16,64]{2,1,0:T(8,128)S(1)}, f32[2,16,64]{2,1,0:T(8,128)S(1)}, u32[]{:S(2)}, u32[]{:S(2)}) collective-permute-start(f32[2,16,64]{2,1,0:T(8,128)S(1)} %maximum_subtract_fusion), channel_id=1, source_target_pairs={{0,1},{1,0},{2,66},{3,67},{4,5},{5,4},{6,7},{7,6},{8,9},{9,8},{10,... | collective-permute-start | bytes 24584 | tf_op jit(solution)/shard_map/ppermute | solution.py:53
  96.7 5.3 %collective-permute-start.33 = (f32[2,16,64]{2,1,0:T(8,128)S(1)}, f32[2,16,64]{2,1,0:T(8,128)S(1)}, u32[]{:S(2)}, u32[]{:S(2)}) collective-permute-start(f32[2,16,64]{2,1,0:T(8,128)S(1)} %maximum_subtract_fusion), channel_id=1, source_target_pairs={{0,1},{1,0},{2,34},{3,35},{4,5},{5,4},{6,7},{7,6},{8,9},{9,8},{10,... | collective-permute-start | bytes 24584 | tf_op jit(solution)/shard_map/ppermute | solution.py:53
  96.8 5.2 %collective-permute-start.32 = (f32[2,16,64]{2,1,0:T(8,128)S(1)}, f32[2,16,64]{2,1,0:T(8,128)S(1)}, u32[]{:S(2)}, u32[]{:S(2)}) collective-permute-start(f32[2,16,64]{2,1,0:T(8,128)S(1)} %maximum_subtract_fusion), channel_id=1, source_target_pairs={{0,1},{1,0},{2,98},{3,99},{4,5},{5,4},{6,7},{7,6},{8,9},{9,8},{10,... | collective-permute-start | bytes 24584 | tf_op jit(solution)/shard_map/ppermute | solution.py:53
  102.0 5.5 %collective-permute-start.37 = (f32[2,16,192]{2,1,0:T(8,128)S(1)}, f32[2,16,192]{2,1,0:T(8,128)S(1)}, u32[]{:S(2)}, u32[]{:S(2)}) collective-permute-start(f32[2,16,192]{2,1,0:T(8,128)S(1)} %pad_maximum_fusion.103), channel_id=1, source_target_pairs={{0,1},{1,0},{2,6},{3,7},{4,5},{5,4},{6,2},{7,3},{8,9},{9,8},{10,14... | collective-permute-start | bytes 73736 | tf_op jit(solution)/shard_map/ppermute | solution.py:53
  102.1 5.4 %collective-permute-start.36 = (f32[2,16,192]{2,1,0:T(8,128)S(1)}, f32[2,16,192]{2,1,0:T(8,128)S(1)}, u32[]{:S(2)}, u32[]{:S(2)}) collective-permute-start(f32[2,16,192]{2,1,0:T(8,128)S(1)} %pad_maximum_fusion.103), channel_id=1, source_target_pairs={{0,1},{1,0},{2,4},{3,5},{4,2},{5,3},{6,7},{7,6},{8,9},{9,8},{10,12... | collective-permute-start | bytes 73736 | tf_op jit(solution)/shard_map/ppermute | solution.py:53
  102.2 5.3 %collective-permute-start.35 = (f32[2,16,192]{2,1,0:T(8,128)S(1)}, f32[2,16,192]{2,1,0:T(8,128)S(1)}, u32[]{:S(2)}, u32[]{:S(2)}) collective-permute-start(f32[2,16,192]{2,1,0:T(8,128)S(1)} %pad_maximum_fusion.103), channel_id=1, source_target_pairs={{0,2},{1,3},{2,0},{3,1},{4,5},{5,4},{6,7},{7,6},{8,10},{9,11},{10,... | collective-permute-start | bytes 73736 | tf_op jit(solution)/shard_map/ppermute | solution.py:53
  (26 other events, 44.7 us)

commit v11 on v10

--- a/solution.py
+++ b/solution.py
@@ -173,15 +173,15 @@
     far4 = hop(x2, {(2, 3): (0, 2)})
     x1 = finish((1, 2), solved, side1 + product(((1, 2),), near4))
     part1 = lax.cond(here((1, 2)), herm_rows, lambda v, w: small, x1, basis_half)
-    near5 = hop(jnp.concatenate([x1, part1], 2), {(1, 2): (0, 1)})
-    sent3 = hop(share(after(x3, part1), (3, 3)), {(3, 3): (0, 1)})
-    sent2 = hop(share(after(x2, part1), (2, 3)), {(2, 3): (0, 1)})
+    near5 = hop(jnp.concatenate([x1, part1], 2), {(1, 2): (0, 1)}, ((0, 0),))
+    sent3 = hop(after(share(after(x3, x2), (3, 3)), x1), {(3, 3): (0, 1)})
+    sent2 = hop(after(share(x2, (2, 3)), x1), {(2, 3): (0, 1)})
     moved = hop(after(x1 + x2 + x3, part1), {(1, 2): (1, 1), (2, 3): (2, 1), (3, 3): (3, 1)})
     carried = near5[:, :, half:]
     side0 = hop(after(product(((0, 3),), near4), part1), {(0, 3): (0, 1)}, ((0, 0),))
     held3 = side0 + hop(after(product(((0, 2),), far4), part1), {(0, 2): (0, 1)}, ((2, 2),))
     sent = carried + sent2 + sent3
-    near5 = near5[:, :, :half]
+    near5 = after(near5[:, :, :half], (sent2, sent3))
     x0 = finish((0, 1), solved, held3 + product(((0, 1),), near5))
 
     found = jnp.where(z == 0, x0, moved)

time: 109 us -> 109 us (level)
  no operation moved by 1% of the time
where the time goes in v11:
time: 109 us
  waiting for transfers between devices  60.7 us (56%)
  starting transfers between devices  35.8 us (33%)
  local copies, waits for them, and re-layouts  5.57 us (5%)
  matrix products  3.16 us (3%)
  other arithmetic  2.32 us (2%)
  between operations  1.33 us (1%)
    ppermute x30, waiting for transfers between devices, move(): return lax.ppermute(value, AXES, pairs)  53.5 us
    ppermute x30, starting transfers between devices, move(): return lax.ppermute(value, AXES, pairs)  34.1 us
    ppermute x8, waiting for transfers between devices, swap(): return lax.ppermute(value, 'c', [(0, 1), (1, 0)])  7.13 us
    dot_general x8, matrix products, dot_nt(): lax.dot_general(left, right, (((1,), (1,)), ((), ())), precision=precisio...  2.55 us
  transfers between devices with their start and end apart: 38, of which 23 were waited for; matrix products, arithmetic and copies ran while one was open for 3% of the time, Pallas kernels for 0%

profile of v11, /device:TPU:2, one launch (start us, length us, event | category | flops | bytes accessed | tf_op | source)
XLA Modules:
  0.0 109.1 jit_solution(10982144727255834957)
XLA Ops:
  1.7 1.1 %constant_dynamic-update-slice_fusion.2 = (f32[2,592,128]{2,1,0:T(8,128)S(1)}, f32[2,256,128]{2,1,0:T(8,128)S(1)}) fusion(f32[2,592,128]{2,1,0:T(8,128)S(1)} %slice_dynamic-update-slice_fusion, f32[2,512,128]{2,1,0:T(8,128)} %param.53, s32[]{:T(128)S(6)} %select_n.121, f32[2,512,128]{2,1,0:T(8,128)} %param.52, pred[]{:T(512)S(6)} %select_n.119), kind=kLoop, calls=%fused_computation.438 | loop fusion | flops 65536 | bytes 1048581
  2.8 1.6 %collective-permute-start.2 = (f32[2,592,128]{2,1,0:T(8,128)S(1)}, f32[2,592,128]{2,1,0:T(8,128)S(1)}, u32[]{:S(2)}, u32[]{:S(2)}) collective-permute-start(f32[2,592,128]{2,1,0:T(8,128)S(1)} %constant_dynamic-update-slice_fusion), channel_id=1, source_target_pairs={{0,8},{1,9},{2,10},{3,11},{4,12},{5,13},{6,14},{7,15},{8,16},{9,17... | collective-permute-start | bytes 1818632 | tf_op jit(solution)/shard_map/ppermute | solution.py:53
  4.5 2.9 %collective-permute-start.1 = (f32[2,592,128]{2,1,0:T(8,128)S(1)}, f32[2,592,128]{2,1,0:T(8,128)S(1)}, u32[]{:S(2)}, u32[]{:S(2)}) collective-permute-start(f32[2,592,128]{2,1,0:T(8,128)S(1)} %constant_dynamic-update-slice_fusion), channel_id=1, source_target_pairs={{0,16},{1,17},{2,18},{3,19},{4,20},{5,21},{6,22},{7,23},{8,24},{9,... | collective-permute-start | bytes 1818632 | tf_op jit(solution)/shard_map/ppermute | solution.py:53
  7.4 1.3 %collective-permute-start = (f32[2,592,128]{2,1,0:T(8,128)S(1)}, f32[2,592,128]{2,1,0:T(8,128)S(1)}, u32[]{:S(2)}, u32[]{:S(2)}) collective-permute-start(f32[2,592,128]{2,1,0:T(8,128)S(1)} %constant_dynamic-update-slice_fusion), channel_id=1, source_target_pairs={{0,24},{1,25},{2,26},{3,27},{4,28},{5,29},{6,30},{7,31},{8,0},{9,1... | collective-permute-start | bytes 1818632 | tf_op jit(solution)/shard_map/ppermute | solution.py:53
  8.7 10.9 %collective-permute-done.2 = f32[2,592,128]{2,1,0:T(8,128)S(1)} collective-permute-done((f32[2,592,128]{2,1,0:T(8,128)S(1)}, f32[2,592,128]{2,1,0:T(8,128)S(1)}, u32[]{:S(2)}, u32[]{:S(2)}) %collective-permute-start.2) | collective-permute-done | bytes 606240 | tf_op jit(solution)/shard_map/ppermute | solution.py:53
  19.6 14.2 %collective-permute-done.1 = f32[2,592,128]{2,1,0:T(8,128)S(1)} collective-permute-done((f32[2,592,128]{2,1,0:T(8,128)S(1)}, f32[2,592,128]{2,1,0:T(8,128)S(1)}, u32[]{:S(2)}, u32[]{:S(2)}) %collective-permute-start.1) | collective-permute-done | bytes 606240 | tf_op jit(solution)/shard_map/ppermute | solution.py:53
  37.8 1.0 fusion.257
  39.1 1.2 %collective-permute-done.4 = f32[2,16,512]{2,1,0:T(8,128)S(1)} collective-permute-done((f32[2,16,512]{2,1,0:T(8,128)S(1)}, f32[2,16,512]{2,1,0:T(8,128)S(1)}, u32[]{:S(2)}, u32[]{:S(2)}) %collective-permute-start.4) | collective-permute-done | bytes 65568 | tf_op jit(solution)/shard_map/ppermute | solution.py:57
  42.4 1.1 %collective-permute-done.8 = f32[2,16,512]{2,1,0:T(8,128)S(1)} collective-permute-done((f32[2,16,512]{2,1,0:T(8,128)S(1)}, f32[2,16,512]{2,1,0:T(8,128)S(1)}, u32[]{:S(2)}, u32[]{:S(2)}) %collective-permute-start.8) | collective-permute-done | bytes 65568 | tf_op jit(solution)/shard_map/ppermute | solution.py:57
  45.4 5.6 %collective-permute-start.14 = (f32[2,64,64]{1,2,0:T(8,128)S(1)}, f32[2,64,64]{1,2,0:T(8,128)S(1)}, u32[]{:S(2)}, u32[]{:S(2)}) collective-permute-start(f32[2,64,64]{1,2,0:T(8,128)S(1)} %pad_maximum_fusion.100), channel_id=1, source_target_pairs={{0,1},{1,0},{2,102},{3,103},{4,5},{5,4},{6,7},{7,6},{8,9},{9,8},{1... | collective-permute-start | bytes 98312 | tf_op jit(solution)/shard_map/ppermute | solution.py:53
  51.0 6.4 %collective-permute-start.13 = (f32[2,64,64]{1,2,0:T(8,128)S(1)}, f32[2,64,64]{1,2,0:T(8,128)S(1)}, u32[]{:S(2)}, u32[]{:S(2)}) collective-permute-start(f32[2,64,64]{1,2,0:T(8,128)S(1)} %pad_maximum_fusion.100), channel_id=1, source_target_pairs={{0,1},{1,0},{2,68},{3,69},{4,5},{5,4},{6,7},{7,6},{8,9},{9,8},{10,... | collective-permute-start | bytes 98312 | tf_op jit(solution)/shard_map/ppermute | solution.py:53
  57.4 2.6 %collective-permute-done.13 = f32[2,64,64]{1,2,0:T(8,128)S(1)} collective-permute-done((f32[2,64,64]{1,2,0:T(8,128)S(1)}, f32[2,64,64]{1,2,0:T(8,128)S(1)}, u32[]{:S(2)}, u32[]{:S(2)}) %collective-permute-start.13) | collective-permute-done | bytes 32800 | tf_op jit(solution)/shard_map/ppermute | solution.py:53
  60.0 1.7 %collective-permute-done.12 = f32[2,64,64]{1,2,0:T(8,128)S(1)} collective-permute-done((f32[2,64,64]{1,2,0:T(8,128)S(1)}, f32[2,64,64]{1,2,0:T(8,128)S(1)}, u32[]{:S(2)}, u32[]{:S(2)}) %collective-permute-start.12) | collective-permute-done | bytes 32800 | tf_op jit(solution)/shard_map/ppermute | solution.py:53
  62.3 3.4 %collective-permute-done.15 = f32[2,16,256]{2,1,0:T(8,128)S(1)} collective-permute-done((f32[2,16,256]{2,1,0:T(8,128)S(1)}, f32[2,16,256]{2,1,0:T(8,128)S(1)}, u32[]{:S(2)}, u32[]{:S(2)}) %collective-permute-start.15) | collective-permute-done | bytes 32800 | tf_op jit(solution)/shard_map/ppermute | solution.py:53
  65.7 1.2 %collective-permute-done.16 = f32[2,16,256]{2,1,0:T(8,128)S(1)} collective-permute-done((f32[2,16,256]{2,1,0:T(8,128)S(1)}, f32[2,16,256]{2,1,0:T(8,128)S(1)}, u32[]{:S(2)}, u32[]{:S(2)}) %collective-permute-start.16) | collective-permute-done | bytes 32800 | tf_op jit(solution)/shard_map/ppermute | solution.py:57
  68.5 1.1 collective-permute-done.18
  73.1 7.2 %collective-permute-start.26 = (f32[2,16,320]{2,1,0:T(8,128)S(1)}, f32[2,16,320]{2,1,0:T(8,128)S(1)}, u32[]{:S(2)}, u32[]{:S(2)}) collective-permute-start(f32[2,16,320]{2,1,0:T(8,128)S(1)} %pad_maximum_fusion.101), channel_id=1, source_target_pairs={{0,36},{1,37},{2,0},{3,1},{4,5},{5,4},{6,7},{7,6},{8,44},{9,45},{1... | collective-permute-start | bytes 122888 | tf_op jit(solution)/shard_map/ppermute | solution.py:53
  80.3 3.9 %collective-permute-start.27 = (f32[2,16,64]{2,1,0:T(8,128)S(1)}, f32[2,16,64]{2,1,0:T(8,128)S(1)}, u32[]{:S(2)}, u32[]{:S(2)}) collective-permute-start(f32[2,16,64]{2,1,0:T(8,128)S(1)} %get-tuple-element.423), channel_id=1, source_target_pairs={{0,1},{1,0},{2,70},{3,71},{4,5},{5,4},{6,7},{7,6},{8,9},{9,8},{10,... | collective-permute-start | bytes 24584 | tf_op jit(solution)/shard_map/ppermute | solution.py:53
  84.2 1.5 %collective-permute-done.26 = f32[2,16,320]{2,1,0:T(8,128)S(1)} collective-permute-done((f32[2,16,320]{2,1,0:T(8,128)S(1)}, f32[2,16,320]{2,1,0:T(8,128)S(1)}, u32[]{:S(2)}, u32[]{:S(2)}) %collective-permute-start.26) | collective-permute-done | bytes 40992 | tf_op jit(solution)/shard_map/ppermute | solution.py:53
  85.7 2.3 %collective-permute-done.27 = f32[2,16,64]{2,1,0:T(8,128)S(1)} collective-permute-done((f32[2,16,64]{2,1,0:T(8,128)S(1)}, f32[2,16,64]{2,1,0:T(8,128)S(1)}, u32[]{:S(2)}, u32[]{:S(2)}) %collective-permute-start.27) | collective-permute-done | bytes 8224 | tf_op jit(solution)/shard_map/ppermute | solution.py:53
  87.9 3.6 %collective-permute-done.28 = f32[2,16,64]{2,1,0:T(8,128)S(1)} collective-permute-done((f32[2,16,64]{2,1,0:T(8,128)S(1)}, f32[2,16,64]{2,1,0:T(8,128)S(1)}, u32[]{:S(2)}, u32[]{:S(2)}) %collective-permute-start.28) | collective-permute-done | bytes 8224 | tf_op jit(solution)/shard_map/ppermute | solution.py:53
  95.2 1.1 collective-permute-done.31
  97.0 5.0 %collective-permute-done.34 = f32[2,16,64]{2,1,0:T(8,128)S(1)} collective-permute-done((f32[2,16,64]{2,1,0:T(8,128)S(1)}, f32[2,16,64]{2,1,0:T(8,128)S(1)}, u32[]{:S(2)}, u32[]{:S(2)}) %collective-permute-start.34) | collective-permute-done | bytes 8224 | tf_op jit(solution)/shard_map/ppermute | solution.py:53
  102.3 5.2 %collective-permute-done.37 = f32[2,16,192]{2,1,0:T(8,128)S(1)} collective-permute-done((f32[2,16,192]{2,1,0:T(8,128)S(1)}, f32[2,16,192]{2,1,0:T(8,128)S(1)}, u32[]{:S(2)}, u32[]{:S(2)}) %collective-permute-start.37) | collective-permute-done | bytes 24608 | tf_op jit(solution)/shard_map/ppermute | solution.py:53
  (192 shorter events, 22.8 us)
Async XLA Ops:
  2.8 16.8 %collective-permute-start.2 = (f32[2,592,128]{2,1,0:T(8,128)S(1)}, f32[2,592,128]{2,1,0:T(8,128)S(1)}, u32[]{:S(2)}, u32[]{:S(2)}) collective-permute-start(f32[2,592,128]{2,1,0:T(8,128)S(1)} %constant_dynamic-update-slice_fusion), channel_id=1, source_target_pairs={{0,8},{1,9},{2,10},{3,11},{4,12},{5,13},{6,14},{7,15},{8,16},{9,17... | collective-permute-start | bytes 1818632 | tf_op jit(solution)/shard_map/ppermute | solution.py:53
  4.5 29.3 %collective-permute-start.1 = (f32[2,592,128]{2,1,0:T(8,128)S(1)}, f32[2,592,128]{2,1,0:T(8,128)S(1)}, u32[]{:S(2)}, u32[]{:S(2)}) collective-permute-start(f32[2,592,128]{2,1,0:T(8,128)S(1)} %constant_dynamic-update-slice_fusion), channel_id=1, source_target_pairs={{0,16},{1,17},{2,18},{3,19},{4,20},{5,21},{6,22},{7,23},{8,24},{9,... | collective-permute-start | bytes 1818632 | tf_op jit(solution)/shard_map/ppermute | solution.py:53
  7.4 26.4 %collective-permute-start = (f32[2,592,128]{2,1,0:T(8,128)S(1)}, f32[2,592,128]{2,1,0:T(8,128)S(1)}, u32[]{:S(2)}, u32[]{:S(2)}) collective-permute-start(f32[2,592,128]{2,1,0:T(8,128)S(1)} %constant_dynamic-update-slice_fusion), channel_id=1, source_target_pairs={{0,24},{1,25},{2,26},{3,27},{4,28},{5,29},{6,30},{7,31},{8,0},{9,1... | collective-permute-start | bytes 1818632 | tf_op jit(solution)/shard_map/ppermute | solution.py:53
  36.6 2.3 %collective-permute-start.3 = (f32[2,16,256]{2,1,0:T(8,128)S(1)}, f32[2,16,256]{2,1,0:T(8,128)S(1)}, u32[]{:S(2)}, u32[]{:S(2)}) collective-permute-start(f32[2,16,256]{2,1,0:T(8,128)S(1)} %get-tuple-element.405), channel_id=1, source_target_pairs={{0,32},{1,33},{2,3},{3,2},{4,64},{5,65},{6,96},{7,97},{8,40},{9,41... | collective-permute-start | bytes 98312 | tf_op jit(solution)/shard_map/ppermute | solution.py:53
  40.3 1.8 %collective-permute-start.5 = (f32[2,16,512]{2,1,0:T(8,128)S(1)}, f32[2,16,512]{2,1,0:T(8,128)S(1)}, u32[]{:S(2)}, u32[]{:S(2)}) collective-permute-start(f32[2,16,512]{2,1,0:T(8,128)S(1)} %get-tuple-element.408), channel_id=1, source_target_pairs={{0,1},{1,0},{2,3},{3,2},{4,5},{5,4},{6,7},{7,6},{8,9},{9,8},{10,11... | collective-permute-start | bytes 196616 | tf_op jit(solution)/shard_map/ppermute | solution.py:53
  43.5 1.4 %collective-permute-start.9 = (f32[2,16,512]{2,1,0:T(8,128)S(1)}, f32[2,16,512]{2,1,0:T(8,128)S(1)}, u32[]{:S(2)}, u32[]{:S(2)}) collective-permute-start(f32[2,16,512]{2,1,0:T(8,128)S(1)} %get-tuple-element.411), channel_id=1, source_target_pairs={{0,98},{1,99},{2,3},{3,2},{4,5},{5,4},{6,7},{7,6},{8,106},{9,107},... | collective-permute-start | bytes 196616 | tf_op jit(solution)/shard_map/ppermute | solution.py:53
  45.0 12.4 %collective-permute-start.11 = (f32[2,16,512]{2,1,0:T(8,128)S(1)}, f32[2,16,512]{2,1,0:T(8,128)S(1)}, u32[]{:S(2)}, u32[]{:S(2)}) collective-permute-start(f32[2,16,512]{2,1,0:T(8,128)S(1)} %add_add_fusion.2), channel_id=1, source_target_pairs={{0,1},{1,0},{2,3},{3,2},{4,5},{5,4},{6,7},{7,6},{8,9},{9,8},{10,11... | collective-permute-start | bytes 196616 | tf_op jit(solution)/shard_map/ppermute | solution.py:57
  45.4 12.0 %collective-permute-start.14 = (f32[2,64,64]{1,2,0:T(8,128)S(1)}, f32[2,64,64]{1,2,0:T(8,128)S(1)}, u32[]{:S(2)}, u32[]{:S(2)}) collective-permute-start(f32[2,64,64]{1,2,0:T(8,128)S(1)} %pad_maximum_fusion.100), channel_id=1, source_target_pairs={{0,1},{1,0},{2,102},{3,103},{4,5},{5,4},{6,7},{7,6},{8,9},{9,8},{1... | collective-permute-start | bytes 98312 | tf_op jit(solution)/shard_map/ppermute | solution.py:53
  51.0 9.0 %collective-permute-start.13 = (f32[2,64,64]{1,2,0:T(8,128)S(1)}, f32[2,64,64]{1,2,0:T(8,128)S(1)}, u32[]{:S(2)}, u32[]{:S(2)}) collective-permute-start(f32[2,64,64]{1,2,0:T(8,128)S(1)} %pad_maximum_fusion.100), channel_id=1, source_target_pairs={{0,1},{1,0},{2,68},{3,69},{4,5},{5,4},{6,7},{7,6},{8,9},{9,8},{10,... | collective-permute-start | bytes 98312 | tf_op jit(solution)/shard_map/ppermute | solution.py:53
  57.4 4.3 %collective-permute-start.12 = (f32[2,64,64]{1,2,0:T(8,128)S(1)}, f32[2,64,64]{1,2,0:T(8,128)S(1)}, u32[]{:S(2)}, u32[]{:S(2)}) collective-permute-start(f32[2,64,64]{1,2,0:T(8,128)S(1)} %pad_maximum_fusion.100), channel_id=1, source_target_pairs={{0,1},{1,0},{2,34},{3,35},{4,5},{5,4},{6,7},{7,6},{8,9},{9,8},{10,... | collective-permute-start | bytes 98312 | tf_op jit(solution)/shard_map/ppermute | solution.py:53
  61.7 4.0 %collective-permute-start.15 = (f32[2,16,256]{2,1,0:T(8,128)S(1)}, f32[2,16,256]{2,1,0:T(8,128)S(1)}, u32[]{:S(2)}, u32[]{:S(2)}) collective-permute-start(f32[2,16,256]{2,1,0:T(8,128)S(1)} %add_add_fusion.4), channel_id=1, source_target_pairs={{0,2},{1,3},{2,0},{3,1},{4,5},{5,4},{6,7},{7,6},{8,10},{9,11},{10,... | collective-permute-start | bytes 98312 | tf_op jit(solution)/shard_map/ppermute | solution.py:53
  67.2 2.4 %collective-permute-start.20 = (f32[2,16,256]{2,1,0:T(8,128)S(1)}, f32[2,16,256]{2,1,0:T(8,128)S(1)}, u32[]{:S(2)}, u32[]{:S(2)}) collective-permute-start(f32[2,16,256]{2,1,0:T(8,128)S(1)} %get-tuple-element.414), channel_id=1, source_target_pairs={{0,1},{1,0},{2,3},{3,2},{4,5},{5,4},{6,7},{7,6},{8,9},{9,8},{10,11... | collective-permute-start | bytes 98312 | tf_op jit(solution)/shard_map/ppermute | solution.py:53
  72.5 19.8 %collective-permute-start.23 = (f32[2,16,512]{2,1,0:T(8,128)S(1)}, f32[2,16,512]{2,1,0:T(8,128)S(1)}, u32[]{:S(2)}, u32[]{:S(2)}) collective-permute-start(f32[2,16,512]{2,1,0:T(8,128)S(1)} %get-tuple-element.417), channel_id=1, source_target_pairs={{0,6},{1,7},{2,0},{3,1},{4,5},{5,4},{6,2},{7,3},{8,14},{9,15},{10,... | collective-permute-start | bytes 196616 | tf_op jit(solution)/shard_map/ppermute | solution.py:53
  73.1 19.2 %collective-permute-start.25 = (f32[2,16,512]{2,1,0:T(8,128)S(1)}, f32[2,16,512]{2,1,0:T(8,128)S(1)}, u32[]{:S(2)}, u32[]{:S(2)}) collective-permute-start(f32[2,16,512]{2,1,0:T(8,128)S(1)} %get-tuple-element.422), channel_id=1, source_target_pairs={{0,1},{1,0},{2,68},{3,69},{4,2},{5,3},{6,7},{7,6},{8,9},{9,8},{10,... | collective-permute-start | bytes 196616 | tf_op jit(solution)/shard_map/ppermute | solution.py:53
  73.1 12.5 %collective-permute-start.26 = (f32[2,16,320]{2,1,0:T(8,128)S(1)}, f32[2,16,320]{2,1,0:T(8,128)S(1)}, u32[]{:S(2)}, u32[]{:S(2)}) collective-permute-start(f32[2,16,320]{2,1,0:T(8,128)S(1)} %pad_maximum_fusion.101), channel_id=1, source_target_pairs={{0,36},{1,37},{2,0},{3,1},{4,5},{5,4},{6,7},{7,6},{8,44},{9,45},{1... | collective-permute-start | bytes 122888 | tf_op jit(solution)/shard_map/ppermute | solution.py:53
  80.3 7.6 %collective-permute-start.27 = (f32[2,16,64]{2,1,0:T(8,128)S(1)}, f32[2,16,64]{2,1,0:T(8,128)S(1)}, u32[]{:S(2)}, u32[]{:S(2)}) collective-permute-start(f32[2,16,64]{2,1,0:T(8,128)S(1)} %get-tuple-element.423), channel_id=1, source_target_pairs={{0,1},{1,0},{2,70},{3,71},{4,5},{5,4},{6,7},{7,6},{8,9},{9,8},{10,... | collective-permute-start | bytes 24584 | tf_op jit(solution)/shard_map/ppermute | solution.py:53
  84.2 7.4 %collective-permute-start.28 = (f32[2,16,64]{2,1,0:T(8,128)S(1)}, f32[2,16,64]{2,1,0:T(8,128)S(1)}, u32[]{:S(2)}, u32[]{:S(2)}) collective-permute-start(f32[2,16,64]{2,1,0:T(8,128)S(1)} %get-tuple-element.424), channel_id=1, source_target_pairs={{0,1},{1,0},{2,102},{3,103},{4,5},{5,4},{6,7},{7,6},{8,9},{9,8},{1... | collective-permute-start | bytes 24584 | tf_op jit(solution)/shard_map/ppermute | solution.py:53
  92.4 2.4 %collective-permute-start.30 = (f32[2,16,256]{2,1,0:T(8,128)S(1)}, f32[2,16,256]{2,1,0:T(8,128)S(1)}, u32[]{:S(2)}, u32[]{:S(2)}) collective-permute-start(f32[2,16,256]{2,1,0:T(8,128)S(1)} %add_add_fusion.3), channel_id=1, source_target_pairs={{0,1},{1,0},{2,3},{3,2},{4,5},{5,4},{6,7},{7,6},{8,9},{9,8},{10,11... | collective-permute-start | bytes 98312 | tf_op jit(solution)/shard_map/ppermute | solution.py:53
  96.6 5.3 %collective-permute-start.34 = (f32[2,16,64]{2,1,0:T(8,128)S(1)}, f32[2,16,64]{2,1,0:T(8,128)S(1)}, u32[]{:S(2)}, u32[]{:S(2)}) collective-permute-start(f32[2,16,64]{2,1,0:T(8,128)S(1)} %maximum_subtract_fusion), channel_id=1, source_target_pairs={{0,1},{1,0},{2,66},{3,67},{4,5},{5,4},{6,7},{7,6},{8,9},{9,8},{10,... | collective-permute-start | bytes 24584 | tf_op jit(solution)/shard_map/ppermute | solution.py:53
  96.7 5.3 %collective-permute-start.33 = (f32[2,16,64]{2,1,0:T(8,128)S(1)}, f32[2,16,64]{2,1,0:T(8,128)S(1)}, u32[]{:S(2)}, u32[]{:S(2)}) collective-permute-start(f32[2,16,64]{2,1,0:T(8,128)S(1)} %maximum_subtract_fusion), channel_id=1, source_target_pairs={{0,1},{1,0},{2,34},{3,35},{4,5},{5,4},{6,7},{7,6},{8,9},{9,8},{10,... | collective-permute-start | bytes 24584 | tf_op jit(solution)/shard_map/ppermute | solution.py:53
  96.8 5.2 %collective-permute-start.32 = (f32[2,16,64]{2,1,0:T(8,128)S(1)}, f32[2,16,64]{2,1,0:T(8,128)S(1)}, u32[]{:S(2)}, u32[]{:S(2)}) collective-permute-start(f32[2,16,64]{2,1,0:T(8,128)S(1)} %maximum_subtract_fusion), channel_id=1, source_target_pairs={{0,1},{1,0},{2,98},{3,99},{4,5},{5,4},{6,7},{7,6},{8,9},{9,8},{10,... | collective-permute-start | bytes 24584 | tf_op jit(solution)/shard_map/ppermute | solution.py:53
  102.1 5.5 %collective-permute-start.37 = (f32[2,16,192]{2,1,0:T(8,128)S(1)}, f32[2,16,192]{2,1,0:T(8,128)S(1)}, u32[]{:S(2)}, u32[]{:S(2)}) collective-permute-start(f32[2,16,192]{2,1,0:T(8,128)S(1)} %pad_maximum_fusion.103), channel_id=1, source_target_pairs={{0,1},{1,0},{2,6},{3,7},{4,5},{5,4},{6,2},{7,3},{8,9},{9,8},{10,14... | collective-permute-start | bytes 73736 | tf_op jit(solution)/shard_map/ppermute | solution.py:53
  102.1 5.4 %collective-permute-start.36 = (f32[2,16,192]{2,1,0:T(8,128)S(1)}, f32[2,16,192]{2,1,0:T(8,128)S(1)}, u32[]{:S(2)}, u32[]{:S(2)}) collective-permute-start(f32[2,16,192]{2,1,0:T(8,128)S(1)} %pad_maximum_fusion.103), channel_id=1, source_target_pairs={{0,1},{1,0},{2,4},{3,5},{4,2},{5,3},{6,7},{7,6},{8,9},{9,8},{10,12... | collective-permute-start | bytes 73736 | tf_op jit(solution)/shard_map/ppermute | solution.py:53
  102.2 5.3 %collective-permute-start.35 = (f32[2,16,192]{2,1,0:T(8,128)S(1)}, f32[2,16,192]{2,1,0:T(8,128)S(1)}, u32[]{:S(2)}, u32[]{:S(2)}) collective-permute-start(f32[2,16,192]{2,1,0:T(8,128)S(1)} %pad_maximum_fusion.103), channel_id=1, source_target_pairs={{0,2},{1,3},{2,0},{3,1},{4,5},{5,4},{6,7},{7,6},{8,10},{9,11},{10,... | collective-permute-start | bytes 73736 | tf_op jit(solution)/shard_map/ppermute | solution.py:53
  (26 other events, 44.7 us)

commit v12 on v6

--- a/solution.py
+++ b/solution.py
@@ -171,15 +171,15 @@
     near4 = hop(x2 + x3, {(2, 3): (1, 2), (3, 3): (0, 3)})
     side1 = hop(product(((1, 3),), after(far3, x2)), {(1, 3): (1, 2)}, ((1, 1),))
     far4 = hop(x2, {(2, 3): (0, 2)})
-    sent3 = hop(after(share(x3, (3, 3)), x2), {(3, 3): (0, 1)}, ((0, 0),))
-    sent2 = hop(share(x2, (2, 3)), {(2, 3): (0, 1)}, ((1, 1),))
+    share3, share2 = share(x3, (3, 3)), share(x2, (2, 3))
     x1 = finish((1, 2), solved, side1 + product(((1, 2),), near4))
-    x1, sent2, sent3 = lax.optimization_barrier((x1, sent2, sent3))
+    sent3 = hop(after(share3, x1), {(3, 3): (0, 1)})
+    sent2 = hop(after(share2, x1), {(2, 3): (0, 1)})
     part1 = lax.cond(here((1, 2)), herm_rows, lambda v, w: small, x1, basis_half)
     near5 = hop(jnp.concatenate([x1, part1], 2), {(1, 2): (0, 1)})
     part1 = near5[:, :, half:]
     side0 = hop(after(product(((0, 3),), near4), x1), {(0, 3): (0, 1)}, ((0, 0),))
-    held3 = side0 + hop(after(product(((0, 2),), far4), x1), {(0, 2): (0, 1)}, ((1, 1),))
+    held3 = side0 + hop(after(product(((0, 2),), far4), x1), {(0, 2): (0, 1)}, ((2, 2),))
     sent = jnp.concatenate([part1 + sent2[:, :nvec] + sent3[:, :nvec], sent1 + sent2[:, nvec:] + sent3[:, nvec:]], 1)
     near5 = near5[:, :, :half]
     x0 = finish((0, 1), solved, held3 + product(((0, 1),), near5))

time: 108 us -> 109 us (level)
  waiting for transfers between devices: 62.8 us -> 58.5 us
  starting transfers between devices: 32.5 us -> 35.6 us
    ppermute x27, waiting for transfers between devices: 55.9 us -> 51.5 us  [move(): return lax.ppermute(value, AXES, pairs)]
    ppermute x27, starting transfers between devices: 30.9 us -> 33.9 us  [move(): return lax.ppermute(value, AXES, pairs)]
  transfers between devices with their start and end apart: 35 -> 35, of which waited for: 27 -> 25; matrix products, arithmetic and copies ran while one was open for 2% -> 3% of each run, Pallas kernels for 0% -> 0%
where the time goes in v12:
time: 109 us; the launch traced here: 108 us
  waiting for transfers between devices  58.5 us (54%)
  starting transfers between devices  35.6 us (33%)
  local copies, waits for them, and re-layouts  6.36 us (6%)
  matrix products  3.04 us (3%)
  other arithmetic  2.97 us (3%)
  between operations  1.39 us (1%)
    ppermute x27, waiting for transfers between devices, move(): return lax.ppermute(value, AXES, pairs)  51.5 us
    ppermute x27, starting transfers between devices, move(): return lax.ppermute(value, AXES, pairs)  33.9 us
    ppermute x8, waiting for transfers between devices, swap(): return lax.ppermute(value, 'c', [(0, 1), (1, 0)])  7.01 us
    unnamed x21, local copies, waits for them, and re-layouts  2.7 us
    dot_general x8, matrix products, dot_nt(): lax.dot_general(left, right, (((1,), (1,)), ((), ())), precision=precisio...  2.47 us
  transfers between devices with their start and end apart: 35, of which 25 were waited for; matrix products, arithmetic and copies ran while one was open for 3% of the time, Pallas kernels for 0%

profile of v12, /device:TPU:2, one launch (start us, length us, event | category | flops | bytes accessed | tf_op | source)
XLA Modules:
  0.0 108.2 jit_solution(4149213465762198437)
XLA Ops:
  0.7 1.0 slice_dynamic-update-slice_fusion.1
  1.7 1.1 %constant_dynamic-update-slice_fusion.2 = (f32[2,592,128]{2,1,0:T(8,128)S(1)}, f32[2,256,128]{2,1,0:T(8,128)S(1)}) fusion(f32[2,592,128]{2,1,0:T(8,128)S(1)} %slice_dynamic-update-slice_fusion, f32[2,512,128]{2,1,0:T(8,128)} %param.53, s32[]{:T(128)S(6)} %select_n.136, f32[2,512,128]{2,1,0:T(8,128)} %param.52, pred[]{:T(512)S(6)} %select_n.134), kind=kLoop, calls=%fused_computation.440 | loop fusion | flops 65536 | bytes 1048581
  2.8 1.6 %collective-permute-start.2 = (f32[2,592,128]{2,1,0:T(8,128)S(1)}, f32[2,592,128]{2,1,0:T(8,128)S(1)}, u32[]{:S(2)}, u32[]{:S(2)}) collective-permute-start(f32[2,592,128]{2,1,0:T(8,128)S(1)} %constant_dynamic-update-slice_fusion), channel_id=1, source_target_pairs={{0,8},{1,9},{2,10},{3,11},{4,12},{5,13},{6,14},{7,15},{8,16},{9,17... | collective-permute-start | bytes 1818632 | tf_op jit(solution)/shard_map/ppermute | solution.py:53
  4.5 2.9 %collective-permute-start.1 = (f32[2,592,128]{2,1,0:T(8,128)S(1)}, f32[2,592,128]{2,1,0:T(8,128)S(1)}, u32[]{:S(2)}, u32[]{:S(2)}) collective-permute-start(f32[2,592,128]{2,1,0:T(8,128)S(1)} %constant_dynamic-update-slice_fusion), channel_id=1, source_target_pairs={{0,16},{1,17},{2,18},{3,19},{4,20},{5,21},{6,22},{7,23},{8,24},{9,... | collective-permute-start | bytes 1818632 | tf_op jit(solution)/shard_map/ppermute | solution.py:53
  7.4 1.3 %collective-permute-start = (f32[2,592,128]{2,1,0:T(8,128)S(1)}, f32[2,592,128]{2,1,0:T(8,128)S(1)}, u32[]{:S(2)}, u32[]{:S(2)}) collective-permute-start(f32[2,592,128]{2,1,0:T(8,128)S(1)} %constant_dynamic-update-slice_fusion), channel_id=1, source_target_pairs={{0,24},{1,25},{2,26},{3,27},{4,28},{5,29},{6,30},{7,31},{8,0},{9,1... | collective-permute-start | bytes 1818632 | tf_op jit(solution)/shard_map/ppermute | solution.py:53
  8.7 10.9 %collective-permute-done.2 = f32[2,592,128]{2,1,0:T(8,128)S(1)} collective-permute-done((f32[2,592,128]{2,1,0:T(8,128)S(1)}, f32[2,592,128]{2,1,0:T(8,128)S(1)}, u32[]{:S(2)}, u32[]{:S(2)}) %collective-permute-start.2) | collective-permute-done | bytes 606240 | tf_op jit(solution)/shard_map/ppermute | solution.py:53
  19.6 14.2 %collective-permute-done.1 = f32[2,592,128]{2,1,0:T(8,128)S(1)} collective-permute-done((f32[2,592,128]{2,1,0:T(8,128)S(1)}, f32[2,592,128]{2,1,0:T(8,128)S(1)}, u32[]{:S(2)}, u32[]{:S(2)}) %collective-permute-start.1) | collective-permute-done | bytes 606240 | tf_op jit(solution)/shard_map/ppermute | solution.py:53
  37.8 1.0 fusion.256
  39.0 1.2 %collective-permute-done.4 = f32[2,16,512]{2,1,0:T(8,128)S(1)} collective-permute-done((f32[2,16,512]{2,1,0:T(8,128)S(1)}, f32[2,16,512]{2,1,0:T(8,128)S(1)}, u32[]{:S(2)}, u32[]{:S(2)}) %collective-permute-start.4) | collective-permute-done | bytes 65568 | tf_op jit(solution)/shard_map/ppermute | solution.py:57
  42.3 1.1 %collective-permute-done.8 = f32[2,16,512]{2,1,0:T(8,128)S(1)} collective-permute-done((f32[2,16,512]{2,1,0:T(8,128)S(1)}, f32[2,16,512]{2,1,0:T(8,128)S(1)}, u32[]{:S(2)}, u32[]{:S(2)}) %collective-permute-start.8) | collective-permute-done | bytes 65568 | tf_op jit(solution)/shard_map/ppermute | solution.py:57
  45.4 2.8 %collective-permute-start.12 = (f32[2,64,64]{2,1,0:T(8,128)S(1)}, f32[2,64,64]{2,1,0:T(8,128)S(1)}, u32[]{:S(2)}, u32[]{:S(2)}) collective-permute-start(f32[2,64,64]{2,1,0:T(8,128)S(1)} %pad_maximum_fusion.103), channel_id=1, source_target_pairs={{0,1},{1,0},{2,36},{3,37},{4,5},{5,4},{6,7},{7,6},{8,9},{9,8},{10,... | collective-permute-start | bytes 98312 | tf_op jit(solution)/shard_map/ppermute | solution.py:53
  48.2 2.4 %collective-permute-done.12 = f32[2,64,64]{2,1,0:T(8,128)S(1)} collective-permute-done((f32[2,64,64]{2,1,0:T(8,128)S(1)}, f32[2,64,64]{2,1,0:T(8,128)S(1)}, u32[]{:S(2)}, u32[]{:S(2)}) %collective-permute-start.12) | collective-permute-done | bytes 32800 | tf_op jit(solution)/shard_map/ppermute | solution.py:53
  50.7 3.9 %collective-permute-done.13 = f32[2,16,256]{2,1,0:T(8,128)S(1)} collective-permute-done((f32[2,16,256]{2,1,0:T(8,128)S(1)}, f32[2,16,256]{2,1,0:T(8,128)S(1)}, u32[]{:S(2)}, u32[]{:S(2)}) %collective-permute-start.13) | collective-permute-done | bytes 32800 | tf_op jit(solution)/shard_map/ppermute | solution.py:53
  54.6 1.2 %collective-permute-done.14 = f32[2,16,256]{2,1,0:T(8,128)S(1)} collective-permute-done((f32[2,16,256]{2,1,0:T(8,128)S(1)}, f32[2,16,256]{2,1,0:T(8,128)S(1)}, u32[]{:S(2)}, u32[]{:S(2)}) %collective-permute-start.14) | collective-permute-done | bytes 32800 | tf_op jit(solution)/shard_map/ppermute | solution.py:57
  57.4 1.1 collective-permute-done.16
  61.4 19.8 %collective-permute-start.27 = (f32[2,80,64]{2,1,0:T(8,128)S(1)}, f32[2,80,64]{2,1,0:T(8,128)S(1)}, u32[]{:S(2)}, u32[]{:S(2)}) collective-permute-start(f32[2,80,64]{2,1,0:T(8,128)S(1)} %get-tuple-element.272), channel_id=1, source_target_pairs={{0,1},{1,0},{2,102},{3,103},{4,5},{5,4},{6,7},{7,6},{8,9},{9,8},{1... | collective-permute-start | bytes 122888 | tf_op jit(solution)/shard_map/ppermute | solution.py:53
  81.2 1.4 %collective-permute-start.26 = (f32[2,80,64]{2,1,0:T(8,128)S(1)}, f32[2,80,64]{2,1,0:T(8,128)S(1)}, u32[]{:S(2)}, u32[]{:S(2)}) collective-permute-start(f32[2,80,64]{2,1,0:T(8,128)S(1)} %get-tuple-element.271), channel_id=1, source_target_pairs={{0,1},{1,0},{2,70},{3,71},{4,5},{5,4},{6,7},{7,6},{8,9},{9,8},{10,... | collective-permute-start | bytes 122888 | tf_op jit(solution)/shard_map/ppermute | solution.py:53
  84.0 5.6 %collective-permute-done.26 = f32[2,80,64]{2,1,0:T(8,128)S(1)} collective-permute-done((f32[2,80,64]{2,1,0:T(8,128)S(1)}, f32[2,80,64]{2,1,0:T(8,128)S(1)}, u32[]{:S(2)}, u32[]{:S(2)}) %collective-permute-start.26) | collective-permute-done | bytes 40992 | tf_op jit(solution)/shard_map/ppermute | solution.py:53
  89.6 1.5 %conditional.41 = (f32[2,16,512]{2,1,0:T(8,128)S(1)}) conditional(s32[]{:T(128)} %convert_element_type.49, () %tuple.200, (f32[2,16,320]{2,1,0:T(8,128)}, f32[2,512,256]{2,1,0:T(8,128)S(1)}) %tuple.203), branch_computations={%region_36.37_spmd, %region_37.38_spmd} | conditional | flops 50380800 | bytes 1638408 | solution.py:130
  94.0 1.1 collective-permute-done.28
  95.7 3.7 %collective-permute-done.31 = f32[2,16,192]{2,1,0:T(8,128)S(1)} collective-permute-done((f32[2,16,192]{2,1,0:T(8,128)S(1)}, f32[2,16,192]{2,1,0:T(8,128)S(1)}, u32[]{:S(2)}, u32[]{:S(2)}) %collective-permute-start.31) | collective-permute-done | bytes 24608 | tf_op jit(solution)/shard_map/ppermute | solution.py:53
  99.5 1.6 %collective-permute-done.29 = f32[2,16,192]{2,1,0:T(8,128)S(1)} collective-permute-done((f32[2,16,192]{2,1,0:T(8,128)S(1)}, f32[2,16,192]{2,1,0:T(8,128)S(1)}, u32[]{:S(2)}, u32[]{:S(2)}) %collective-permute-start.29) | collective-permute-done | bytes 24608 | tf_op jit(solution)/shard_map/ppermute | solution.py:53
  101.4 3.5 %collective-permute-done.34 = f32[2,16,64]{2,1,0:T(8,128)S(1)} collective-permute-done((f32[2,16,64]{2,1,0:T(8,128)S(1)}, f32[2,16,64]{2,1,0:T(8,128)S(1)}, u32[]{:S(2)}, u32[]{:S(2)}) %collective-permute-start.34) | collective-permute-done | bytes 8224 | tf_op jit(solution)/shard_map/ppermute | solution.py:53
  105.0 1.3 %collective-permute-done.33 = f32[2,16,64]{2,1,0:T(8,128)S(1)} collective-permute-done((f32[2,16,64]{2,1,0:T(8,128)S(1)}, f32[2,16,64]{2,1,0:T(8,128)S(1)}, u32[]{:S(2)}, u32[]{:S(2)}) %collective-permute-start.33) | collective-permute-done | bytes 8224 | tf_op jit(solution)/shard_map/ppermute | solution.py:53
  (189 shorter events, 22.3 us)
Async XLA Ops:
  2.8 16.8 %collective-permute-start.2 = (f32[2,592,128]{2,1,0:T(8,128)S(1)}, f32[2,592,128]{2,1,0:T(8,128)S(1)}, u32[]{:S(2)}, u32[]{:S(2)}) collective-permute-start(f32[2,592,128]{2,1,0:T(8,128)S(1)} %constant_dynamic-update-slice_fusion), channel_id=1, source_target_pairs={{0,8},{1,9},{2,10},{3,11},{4,12},{5,13},{6,14},{7,15},{8,16},{9,17... | collective-permute-start | bytes 1818632 | tf_op jit(solution)/shard_map/ppermute | solution.py:53
  4.5 29.3 %collective-permute-start.1 = (f32[2,592,128]{2,1,0:T(8,128)S(1)}, f32[2,592,128]{2,1,0:T(8,128)S(1)}, u32[]{:S(2)}, u32[]{:S(2)}) collective-permute-start(f32[2,592,128]{2,1,0:T(8,128)S(1)} %constant_dynamic-update-slice_fusion), channel_id=1, source_target_pairs={{0,16},{1,17},{2,18},{3,19},{4,20},{5,21},{6,22},{7,23},{8,24},{9,... | collective-permute-start | bytes 1818632 | tf_op jit(solution)/shard_map/ppermute | solution.py:53
  7.4 26.4 %collective-permute-start = (f32[2,592,128]{2,1,0:T(8,128)S(1)}, f32[2,592,128]{2,1,0:T(8,128)S(1)}, u32[]{:S(2)}, u32[]{:S(2)}) collective-permute-start(f32[2,592,128]{2,1,0:T(8,128)S(1)} %constant_dynamic-update-slice_fusion), channel_id=1, source_target_pairs={{0,24},{1,25},{2,26},{3,27},{4,28},{5,29},{6,30},{7,31},{8,0},{9,1... | collective-permute-start | bytes 1818632 | tf_op jit(solution)/shard_map/ppermute | solution.py:53
  36.5 2.3 %collective-permute-start.3 = (f32[2,16,256]{2,1,0:T(8,128)S(1)}, f32[2,16,256]{2,1,0:T(8,128)S(1)}, u32[]{:S(2)}, u32[]{:S(2)}) collective-permute-start(f32[2,16,256]{2,1,0:T(8,128)S(1)} %get-tuple-element.406), channel_id=1, source_target_pairs={{0,32},{1,33},{2,3},{3,2},{4,64},{5,65},{6,96},{7,97},{8,40},{9,41... | collective-permute-start | bytes 98312 | tf_op jit(solution)/shard_map/ppermute | solution.py:53
  38.9 1.3 %collective-permute-start.4 = (f32[2,16,512]{2,1,0:T(8,128)S(1)}, f32[2,16,512]{2,1,0:T(8,128)S(1)}, u32[]{:S(2)}, u32[]{:S(2)}) collective-permute-start(f32[2,16,512]{2,1,0:T(8,128)S(1)} %get-tuple-element.407), channel_id=1, source_target_pairs={{0,1},{1,0},{2,3},{3,2},{4,5},{5,4},{6,7},{7,6},{8,9},{9,8},{10,11... | collective-permute-start | bytes 196616 | tf_op jit(solution)/shard_map/ppermute | solution.py:57
  40.3 1.8 %collective-permute-start.5 = (f32[2,16,512]{2,1,0:T(8,128)S(1)}, f32[2,16,512]{2,1,0:T(8,128)S(1)}, u32[]{:S(2)}, u32[]{:S(2)}) collective-permute-start(f32[2,16,512]{2,1,0:T(8,128)S(1)} %get-tuple-element.409), channel_id=1, source_target_pairs={{0,1},{1,0},{2,3},{3,2},{4,5},{5,4},{6,7},{7,6},{8,9},{9,8},{10,11... | collective-permute-start | bytes 196616 | tf_op jit(solution)/shard_map/ppermute | solution.py:53
  42.1 1.3 %collective-permute-start.8 = (f32[2,16,512]{2,1,0:T(8,128)S(1)}, f32[2,16,512]{2,1,0:T(8,128)S(1)}, u32[]{:S(2)}, u32[]{:S(2)}) collective-permute-start(f32[2,16,512]{2,1,0:T(8,128)S(1)} %add.200), channel_id=1, source_target_pairs={{0,1},{1,0},{2,3},{3,2},{4,5},{5,4},{6,7},{7,6},{8,9},{9,8},{10,11... | collective-permute-start | bytes 196616 | tf_op jit(solution)/shard_map/ppermute | solution.py:57
  43.5 1.5 %collective-permute-start.9 = (f32[2,16,512]{2,1,0:T(8,128)S(1)}, f32[2,16,512]{2,1,0:T(8,128)S(1)}, u32[]{:S(2)}, u32[]{:S(2)}) collective-permute-start(f32[2,16,512]{2,1,0:T(8,128)S(1)} %get-tuple-element.412), channel_id=1, source_target_pairs={{0,1},{1,0},{2,3},{3,2},{4,5},{5,4},{6,7},{7,6},{8,9},{9,8},{10,11... | collective-permute-start | bytes 196616 | tf_op jit(solution)/shard_map/ppermute | solution.py:53
  45.0 3.3 %collective-permute-start.11 = (f32[2,16,512]{2,1,0:T(8,128)S(1)}, f32[2,16,512]{2,1,0:T(8,128)S(1)}, u32[]{:S(2)}, u32[]{:S(2)}) collective-permute-start(f32[2,16,512]{2,1,0:T(8,128)S(1)} %add_add_fusion.1), channel_id=1, source_target_pairs={{0,1},{1,0},{2,3},{3,2},{4,5},{5,4},{6,7},{7,6},{8,9},{9,8},{10,11... | collective-permute-start | bytes 196616 | tf_op jit(solution)/shard_map/ppermute | solution.py:57
  45.4 5.2 %collective-permute-start.12 = (f32[2,64,64]{2,1,0:T(8,128)S(1)}, f32[2,64,64]{2,1,0:T(8,128)S(1)}, u32[]{:S(2)}, u32[]{:S(2)}) collective-permute-start(f32[2,64,64]{2,1,0:T(8,128)S(1)} %pad_maximum_fusion.103), channel_id=1, source_target_pairs={{0,1},{1,0},{2,36},{3,37},{4,5},{5,4},{6,7},{7,6},{8,9},{9,8},{10,... | collective-permute-start | bytes 98312 | tf_op jit(solution)/shard_map/ppermute | solution.py:53
  50.6 4.0 %collective-permute-start.13 = (f32[2,16,256]{2,1,0:T(8,128)S(1)}, f32[2,16,256]{2,1,0:T(8,128)S(1)}, u32[]{:S(2)}, u32[]{:S(2)}) collective-permute-start(f32[2,16,256]{2,1,0:T(8,128)S(1)} %add_add_fusion.3), channel_id=1, source_target_pairs={{0,2},{1,3},{2,0},{3,1},{4,5},{5,4},{6,7},{7,6},{8,10},{9,11},{10,... | collective-permute-start | bytes 98312 | tf_op jit(solution)/shard_map/ppermute | solution.py:53
  56.2 2.3 %collective-permute-start.18 = (f32[2,16,256]{2,1,0:T(8,128)S(1)}, f32[2,16,256]{2,1,0:T(8,128)S(1)}, u32[]{:S(2)}, u32[]{:S(2)}) collective-permute-start(f32[2,16,256]{2,1,0:T(8,128)S(1)} %get-tuple-element.415), channel_id=1, source_target_pairs={{0,1},{1,0},{2,3},{3,2},{4,5},{5,4},{6,7},{7,6},{8,9},{9,8},{10,11... | collective-permute-start | bytes 98312 | tf_op jit(solution)/shard_map/ppermute | solution.py:53
  59.2 1.4 %collective-permute-start.22 = (f32[2,16,256]{2,1,0:T(8,128)S(1)}, f32[2,16,256]{2,1,0:T(8,128)S(1)}, u32[]{:S(2)}, u32[]{:S(2)}) collective-permute-start(f32[2,16,256]{2,1,0:T(8,128)S(1)} %get-tuple-element.417), channel_id=1, source_target_pairs={{0,1},{1,0},{2,3},{3,2},{4,70},{5,71},{6,7},{7,6},{8,9},{9,8},{10,... | collective-permute-start | bytes 98312 | tf_op jit(solution)/shard_map/ppermute | solution.py:53
  61.4 22.6 %collective-permute-start.27 = (f32[2,80,64]{2,1,0:T(8,128)S(1)}, f32[2,80,64]{2,1,0:T(8,128)S(1)}, u32[]{:S(2)}, u32[]{:S(2)}) collective-permute-start(f32[2,80,64]{2,1,0:T(8,128)S(1)} %get-tuple-element.272), channel_id=1, source_target_pairs={{0,1},{1,0},{2,102},{3,103},{4,5},{5,4},{6,7},{7,6},{8,9},{9,8},{1... | collective-permute-start | bytes 122888 | tf_op jit(solution)/shard_map/ppermute | solution.py:53
  81.2 8.3 %collective-permute-start.26 = (f32[2,80,64]{2,1,0:T(8,128)S(1)}, f32[2,80,64]{2,1,0:T(8,128)S(1)}, u32[]{:S(2)}, u32[]{:S(2)}) collective-permute-start(f32[2,80,64]{2,1,0:T(8,128)S(1)} %get-tuple-element.271), channel_id=1, source_target_pairs={{0,1},{1,0},{2,70},{3,71},{4,5},{5,4},{6,7},{7,6},{8,9},{9,8},{10,... | collective-permute-start | bytes 122888 | tf_op jit(solution)/shard_map/ppermute | solution.py:53
  82.6 7.0 %collective-permute-start.24 = (f32[2,16,320]{2,1,0:T(8,128)S(1)}, f32[2,16,320]{2,1,0:T(8,128)}, u32[]{:S(2)}, u32[]{:S(2)}) collective-permute-start(f32[2,16,320]{2,1,0:T(8,128)S(1)} %pad_maximum_fusion.104), channel_id=1, source_target_pairs={{0,1},{1,0},{2,36},{3,37},{4,5},{5,4},{6,7},{7,6},{8,9},{9,8},{10,... | collective-permute-start | bytes 122888 | tf_op jit(solution)/shard_map/ppermute | solution.py:53
  83.1 8.0 %collective-permute-start.21 = (f32[2,16,512]{2,1,0:T(8,128)S(1)}, f32[2,16,512]{2,1,0:T(8,128)S(1)}, u32[]{:S(2)}, u32[]{:S(2)}) collective-permute-start(f32[2,16,512]{2,1,0:T(8,128)S(1)} %get-tuple-element.418), channel_id=1, source_target_pairs={{0,6},{1,7},{2,0},{3,1},{4,5},{5,4},{6,2},{7,3},{8,14},{9,15},{10,... | collective-permute-start | bytes 196616 | tf_op jit(solution)/shard_map/ppermute | solution.py:53
  83.1 8.0 %collective-permute-start.23 = (f32[2,16,512]{2,1,0:T(8,128)S(1)}, f32[2,16,512]{2,1,0:T(8,128)S(1)}, u32[]{:S(2)}, u32[]{:S(2)}) collective-permute-start(f32[2,16,512]{2,1,0:T(8,128)S(1)} %get-tuple-element.422), channel_id=1, source_target_pairs={{0,1},{1,0},{2,68},{3,69},{4,2},{5,3},{6,7},{7,6},{8,9},{9,8},{10,... | collective-permute-start | bytes 196616 | tf_op jit(solution)/shard_map/ppermute | solution.py:53
  95.4 4.0 %collective-permute-start.31 = (f32[2,16,192]{2,1,0:T(8,128)S(1)}, f32[2,16,192]{2,1,0:T(8,128)S(1)}, u32[]{:S(2)}, u32[]{:S(2)}) collective-permute-start(f32[2,16,192]{2,1,0:T(8,128)S(1)} %pad_maximum_fusion.106), channel_id=1, source_target_pairs={{0,1},{1,0},{2,4},{3,5},{4,2},{5,3},{6,7},{7,6},{8,9},{9,8},{10,12... | collective-permute-start | bytes 73736 | tf_op jit(solution)/shard_map/ppermute | solution.py:53
  95.5 4.0 %collective-permute-start.30 = (f32[2,16,192]{2,1,0:T(8,128)S(1)}, f32[2,16,192]{2,1,0:T(8,128)S(1)}, u32[]{:S(2)}, u32[]{:S(2)}) collective-permute-start(f32[2,16,192]{2,1,0:T(8,128)S(1)} %pad_maximum_fusion.106), channel_id=1, source_target_pairs={{0,2},{1,3},{2,0},{3,1},{4,5},{5,4},{6,7},{7,6},{8,10},{9,11},{10,... | collective-permute-start | bytes 73736 | tf_op jit(solution)/shard_map/ppermute | solution.py:53
  95.6 5.5 %collective-permute-start.29 = (f32[2,16,192]{2,1,0:T(8,128)S(1)}, f32[2,16,192]{2,1,0:T(8,128)S(1)}, u32[]{:S(2)}, u32[]{:S(2)}) collective-permute-start(f32[2,16,192]{2,1,0:T(8,128)S(1)} %pad_maximum_fusion.106), channel_id=1, source_target_pairs={{0,1},{1,0},{2,6},{3,7},{4,5},{5,4},{6,2},{7,3},{8,9},{9,8},{10,14... | collective-permute-start | bytes 73736 | tf_op jit(solution)/shard_map/ppermute | solution.py:53
  101.1 3.8 %collective-permute-start.34 = (f32[2,16,64]{2,1,0:T(8,128)S(1)}, f32[2,16,64]{2,1,0:T(8,128)S(1)}, u32[]{:S(2)}, u32[]{:S(2)}) collective-permute-start(f32[2,16,64]{2,1,0:T(8,128)S(1)} %slice.911), channel_id=1, source_target_pairs={{0,32},{1,33},{2,34},{3,35},{4,36},{5,37},{6,38},{7,39},{8,40},{9,... | collective-permute-start | bytes 24584 | tf_op jit(solution)/shard_map/ppermute | solution.py:53
  101.2 5.0 %collective-permute-start.33 = (f32[2,16,64]{2,1,0:T(8,128)S(1)}, f32[2,16,64]{2,1,0:T(8,128)S(1)}, u32[]{:S(2)}, u32[]{:S(2)}) collective-permute-start(f32[2,16,64]{2,1,0:T(8,128)S(1)} %slice.911), channel_id=1, source_target_pairs={{0,96},{1,97},{2,98},{3,99},{4,100},{5,101},{6,102},{7,103},{8,104... | collective-permute-start | bytes 24584 | tf_op jit(solution)/shard_map/ppermute | solution.py:53
  101.3 5.3 %collective-permute-start.32 = (f32[2,16,64]{2,1,0:T(8,128)S(1)}, f32[2,16,64]{2,1,0:T(8,128)S(1)}, u32[]{:S(2)}, u32[]{:S(2)}) collective-permute-start(f32[2,16,64]{2,1,0:T(8,128)S(1)} %slice.911), channel_id=1, source_target_pairs={{0,64},{1,65},{2,66},{3,67},{4,68},{5,69},{6,70},{7,71},{8,72},{9,... | collective-permute-start | bytes 24584 | tf_op jit(solution)/shard_map/ppermute | solution.py:53
  (24 other events, 41.0 us)

commit v13 on v6

--- a/solution.py
+++ b/solution.py
@@ -171,10 +171,9 @@
     near4 = hop(x2 + x3, {(2, 3): (1, 2), (3, 3): (0, 3)})
     side1 = hop(product(((1, 3),), after(far3, x2)), {(1, 3): (1, 2)}, ((1, 1),))
     far4 = hop(x2, {(2, 3): (0, 2)})
-    sent3 = hop(after(share(x3, (3, 3)), x2), {(3, 3): (0, 1)}, ((0, 0),))
-    sent2 = hop(share(x2, (2, 3)), {(2, 3): (0, 1)}, ((1, 1),))
-    x1 = finish((1, 2), solved, side1 + product(((1, 2),), near4))
-    x1, sent2, sent3 = lax.optimization_barrier((x1, sent2, sent3))
+    sent3 = hop(after(share(x3, (3, 3)), x2), {(3, 3): (0, 1)})
+    sent2 = hop(share(x2, (2, 3)), {(2, 3): (0, 1)})
+    x1 = finish((1, 2), after(solved, (sent2, sent3)), side1 + product(((1, 2),), near4))
     part1 = lax.cond(here((1, 2)), herm_rows, lambda v, w: small, x1, basis_half)
     near5 = hop(jnp.concatenate([x1, part1], 2), {(1, 2): (0, 1)})
     part1 = near5[:, :, half:]

time: 108 us -> 112 us (1.037)
  starting transfers between devices: 32.5 us -> 34.7 us
  waiting for transfers between devices: 62.8 us -> 64.9 us
    ppermute x27, starting transfers between devices: 30.9 us -> 33 us  [move(): return lax.ppermute(value, AXES, pairs)]
    ppermute x27, waiting for transfers between devices: 55.9 us -> 58 us  [move(): return lax.ppermute(value, AXES, pairs)]
where the time goes in v13:
time: 112 us
  waiting for transfers between devices  64.9 us (58%)
  starting transfers between devices  34.7 us (31%)
  local copies, waits for them, and re-layouts  5.63 us (5%)
  matrix products  3.04 us (3%)
  other arithmetic  2.25 us (2%)
  between operations  1.35 us (1%)
    ppermute x27, waiting for transfers between devices, move(): return lax.ppermute(value, AXES, pairs)  58 us
    ppermute x27, starting transfers between devices, move(): return lax.ppermute(value, AXES, pairs)  33 us
    ppermute x8, waiting for transfers between devices, swap(): return lax.ppermute(value, 'c', [(0, 1), (1, 0)])  6.91 us
    unnamed x21, local copies, waits for them, and re-layouts  2.7 us
    dot_general x8, matrix products, dot_nt(): lax.dot_general(left, right, (((1,), (1,)), ((), ())), precision=precisio...  2.47 us
  transfers between devices with their start and end apart: 35, of which 27 were waited for; matrix products, arithmetic and copies ran while one was open for 2% of the time, Pallas kernels for 0%

profile of v13, /device:TPU:2, one launch (start us, length us, event | category | flops | bytes accessed | tf_op | source)
XLA Modules:
  0.0 112.1 jit_solution(9245600041580277957)
XLA Ops:
  1.7 1.1 constant_dynamic-update-slice_fusion.2
  2.8 1.6 %collective-permute-start.2 = (f32[2,592,128]{2,1,0:T(8,128)S(1)}, f32[2,592,128]{2,1,0:T(8,128)S(1)}, u32[]{:S(2)}, u32[]{:S(2)}) collective-permute-start(f32[2,592,128]{2,1,0:T(8,128)S(1)} %constant_dynamic-update-slice_fusion), channel_id=1, source_target_pairs={{0,8},{1,9},{2,10},{3,11},{4,12},{5,13},{6,14},{7,15},{8,16},{9,17... | collective-permute-start | bytes 1818632 | tf_op jit(solution)/shard_map/ppermute | solution.py:53
  4.5 2.9 %collective-permute-start.1 = (f32[2,592,128]{2,1,0:T(8,128)S(1)}, f32[2,592,128]{2,1,0:T(8,128)S(1)}, u32[]{:S(2)}, u32[]{:S(2)}) collective-permute-start(f32[2,592,128]{2,1,0:T(8,128)S(1)} %constant_dynamic-update-slice_fusion), channel_id=1, source_target_pairs={{0,16},{1,17},{2,18},{3,19},{4,20},{5,21},{6,22},{7,23},{8,24},{9,... | collective-permute-start | bytes 1818632 | tf_op jit(solution)/shard_map/ppermute | solution.py:53
  7.4 1.3 %collective-permute-start = (f32[2,592,128]{2,1,0:T(8,128)S(1)}, f32[2,592,128]{2,1,0:T(8,128)S(1)}, u32[]{:S(2)}, u32[]{:S(2)}) collective-permute-start(f32[2,592,128]{2,1,0:T(8,128)S(1)} %constant_dynamic-update-slice_fusion), channel_id=1, source_target_pairs={{0,24},{1,25},{2,26},{3,27},{4,28},{5,29},{6,30},{7,31},{8,0},{9,1... | collective-permute-start | bytes 1818632 | tf_op jit(solution)/shard_map/ppermute | solution.py:53
  8.7 10.9 %collective-permute-done.2 = f32[2,592,128]{2,1,0:T(8,128)S(1)} collective-permute-done((f32[2,592,128]{2,1,0:T(8,128)S(1)}, f32[2,592,128]{2,1,0:T(8,128)S(1)}, u32[]{:S(2)}, u32[]{:S(2)}) %collective-permute-start.2) | collective-permute-done | bytes 606240 | tf_op jit(solution)/shard_map/ppermute | solution.py:53
  19.6 14.2 %collective-permute-done.1 = f32[2,592,128]{2,1,0:T(8,128)S(1)} collective-permute-done((f32[2,592,128]{2,1,0:T(8,128)S(1)}, f32[2,592,128]{2,1,0:T(8,128)S(1)}, u32[]{:S(2)}, u32[]{:S(2)}) %collective-permute-start.1) | collective-permute-done | bytes 606240 | tf_op jit(solution)/shard_map/ppermute | solution.py:53
  39.0 1.2 %collective-permute-done.4 = f32[2,16,512]{2,1,0:T(8,128)S(1)} collective-permute-done((f32[2,16,512]{2,1,0:T(8,128)S(1)}, f32[2,16,512]{2,1,0:T(8,128)S(1)}, u32[]{:S(2)}, u32[]{:S(2)}) %collective-permute-start.4) | collective-permute-done | bytes 65568 | tf_op jit(solution)/shard_map/ppermute | solution.py:57
  42.3 1.1 collective-permute-done.8
  45.4 2.8 %collective-permute-start.12 = (f32[2,64,64]{2,1,0:T(8,128)S(1)}, f32[2,64,64]{2,1,0:T(8,128)S(1)}, u32[]{:S(2)}, u32[]{:S(2)}) collective-permute-start(f32[2,64,64]{2,1,0:T(8,128)S(1)} %pad_maximum_fusion.103), channel_id=1, source_target_pairs={{0,1},{1,0},{2,36},{3,37},{4,5},{5,4},{6,7},{7,6},{8,9},{9,8},{10,... | collective-permute-start | bytes 98312 | tf_op jit(solution)/shard_map/ppermute | solution.py:53
  48.2 2.4 %collective-permute-done.12 = f32[2,64,64]{2,1,0:T(8,128)S(1)} collective-permute-done((f32[2,64,64]{2,1,0:T(8,128)S(1)}, f32[2,64,64]{2,1,0:T(8,128)S(1)}, u32[]{:S(2)}, u32[]{:S(2)}) %collective-permute-start.12) | collective-permute-done | bytes 32800 | tf_op jit(solution)/shard_map/ppermute | solution.py:53
  50.7 3.9 %collective-permute-done.13 = f32[2,16,256]{2,1,0:T(8,128)S(1)} collective-permute-done((f32[2,16,256]{2,1,0:T(8,128)S(1)}, f32[2,16,256]{2,1,0:T(8,128)S(1)}, u32[]{:S(2)}, u32[]{:S(2)}) %collective-permute-start.13) | collective-permute-done | bytes 32800 | tf_op jit(solution)/shard_map/ppermute | solution.py:53
  54.6 1.2 %collective-permute-done.14 = f32[2,16,256]{2,1,0:T(8,128)S(1)} collective-permute-done((f32[2,16,256]{2,1,0:T(8,128)S(1)}, f32[2,16,256]{2,1,0:T(8,128)S(1)}, u32[]{:S(2)}, u32[]{:S(2)}) %collective-permute-start.14) | collective-permute-done | bytes 32800 | tf_op jit(solution)/shard_map/ppermute | solution.py:57
  57.4 1.1 collective-permute-done.16
  60.5 19.6 %collective-permute-start.22 = (f32[2,80,64]{2,1,0:T(8,128)S(1)}, f32[2,80,64]{2,1,0:T(8,128)S(1)}, u32[]{:S(2)}, u32[]{:S(2)}) collective-permute-start(f32[2,80,64]{2,1,0:T(8,128)S(1)} %get-tuple-element.269), channel_id=1, source_target_pairs={{0,1},{1,0},{2,102},{3,103},{4,5},{5,4},{6,7},{7,6},{8,9},{9,8},{1... | collective-permute-start | bytes 122888 | tf_op jit(solution)/shard_map/ppermute | solution.py:53
  80.0 1.1 collective-permute-start.21
  81.2 1.2 %collective-permute-done.24 = f32[2,16,256]{2,1,0:T(8,128)S(1)} collective-permute-done((f32[2,16,256]{2,1,0:T(8,128)S(1)}, f32[2,16,256]{2,1,0:T(8,128)S(1)}, u32[]{:S(2)}, u32[]{:S(2)}) %collective-permute-start.24) | collective-permute-done | bytes 32800 | tf_op jit(solution)/shard_map/ppermute | solution.py:53
  83.1 5.7 %collective-permute-done.21 = f32[2,80,64]{2,1,0:T(8,128)S(1)} collective-permute-done((f32[2,80,64]{2,1,0:T(8,128)S(1)}, f32[2,80,64]{2,1,0:T(8,128)S(1)}, u32[]{:S(2)}, u32[]{:S(2)}) %collective-permute-start.21) | collective-permute-done | bytes 40992 | tf_op jit(solution)/shard_map/ppermute | solution.py:53
  89.2 4.8 %collective-permute-done.26 = f32[2,16,320]{2,1,0:T(8,128)S(1)} collective-permute-done((f32[2,16,320]{2,1,0:T(8,128)S(1)}, f32[2,16,320]{2,1,0:T(8,128)S(1)}, u32[]{:S(2)}, u32[]{:S(2)}) %collective-permute-start.26) | collective-permute-done | bytes 40992 | tf_op jit(solution)/shard_map/ppermute | solution.py:53
  95.1 1.2 %collective-permute-done.27 = f32[2,16,512]{2,1,0:T(8,128)S(1)} collective-permute-done((f32[2,16,512]{2,1,0:T(8,128)S(1)}, f32[2,16,512]{2,1,0:T(8,128)S(1)}, u32[]{:S(2)}, u32[]{:S(2)}) %collective-permute-start.27) | collective-permute-done | bytes 65568 | tf_op jit(solution)/shard_map/ppermute | solution.py:57
  97.8 1.1 collective-permute-done.28
  99.6 3.7 %collective-permute-done.31 = f32[2,16,192]{2,1,0:T(8,128)S(1)} collective-permute-done((f32[2,16,192]{2,1,0:T(8,128)S(1)}, f32[2,16,192]{2,1,0:T(8,128)S(1)}, u32[]{:S(2)}, u32[]{:S(2)}) %collective-permute-start.31) | collective-permute-done | bytes 24608 | tf_op jit(solution)/shard_map/ppermute | solution.py:53
  103.5 1.5 %collective-permute-done.29 = f32[2,16,192]{2,1,0:T(8,128)S(1)} collective-permute-done((f32[2,16,192]{2,1,0:T(8,128)S(1)}, f32[2,16,192]{2,1,0:T(8,128)S(1)}, u32[]{:S(2)}, u32[]{:S(2)}) %collective-permute-start.29) | collective-permute-done | bytes 24608 | tf_op jit(solution)/shard_map/ppermute | solution.py:53
  105.4 3.5 %collective-permute-done.34 = f32[2,16,64]{2,1,0:T(8,128)S(1)} collective-permute-done((f32[2,16,64]{2,1,0:T(8,128)S(1)}, f32[2,16,64]{2,1,0:T(8,128)S(1)}, u32[]{:S(2)}, u32[]{:S(2)}) %collective-permute-start.34) | collective-permute-done | bytes 8224 | tf_op jit(solution)/shard_map/ppermute | solution.py:53
  108.9 1.3 %collective-permute-done.33 = f32[2,16,64]{2,1,0:T(8,128)S(1)} collective-permute-done((f32[2,16,64]{2,1,0:T(8,128)S(1)}, f32[2,16,64]{2,1,0:T(8,128)S(1)}, u32[]{:S(2)}, u32[]{:S(2)}) %collective-permute-start.33) | collective-permute-done | bytes 8224 | tf_op jit(solution)/shard_map/ppermute | solution.py:53
  (189 shorter events, 22.2 us)
Async XLA Ops:
  2.8 16.8 %collective-permute-start.2 = (f32[2,592,128]{2,1,0:T(8,128)S(1)}, f32[2,592,128]{2,1,0:T(8,128)S(1)}, u32[]{:S(2)}, u32[]{:S(2)}) collective-permute-start(f32[2,592,128]{2,1,0:T(8,128)S(1)} %constant_dynamic-update-slice_fusion), channel_id=1, source_target_pairs={{0,8},{1,9},{2,10},{3,11},{4,12},{5,13},{6,14},{7,15},{8,16},{9,17... | collective-permute-start | bytes 1818632 | tf_op jit(solution)/shard_map/ppermute | solution.py:53
  4.5 29.3 %collective-permute-start.1 = (f32[2,592,128]{2,1,0:T(8,128)S(1)}, f32[2,592,128]{2,1,0:T(8,128)S(1)}, u32[]{:S(2)}, u32[]{:S(2)}) collective-permute-start(f32[2,592,128]{2,1,0:T(8,128)S(1)} %constant_dynamic-update-slice_fusion), channel_id=1, source_target_pairs={{0,16},{1,17},{2,18},{3,19},{4,20},{5,21},{6,22},{7,23},{8,24},{9,... | collective-permute-start | bytes 1818632 | tf_op jit(solution)/shard_map/ppermute | solution.py:53
  7.4 26.4 %collective-permute-start = (f32[2,592,128]{2,1,0:T(8,128)S(1)}, f32[2,592,128]{2,1,0:T(8,128)S(1)}, u32[]{:S(2)}, u32[]{:S(2)}) collective-permute-start(f32[2,592,128]{2,1,0:T(8,128)S(1)} %constant_dynamic-update-slice_fusion), channel_id=1, source_target_pairs={{0,24},{1,25},{2,26},{3,27},{4,28},{5,29},{6,30},{7,31},{8,0},{9,1... | collective-permute-start | bytes 1818632 | tf_op jit(solution)/shard_map/ppermute | solution.py:53
  36.5 2.3 %collective-permute-start.3 = (f32[2,16,256]{2,1,0:T(8,128)S(1)}, f32[2,16,256]{2,1,0:T(8,128)S(1)}, u32[]{:S(2)}, u32[]{:S(2)}) collective-permute-start(f32[2,16,256]{2,1,0:T(8,128)S(1)} %get-tuple-element.406), channel_id=1, source_target_pairs={{0,32},{1,33},{2,3},{3,2},{4,64},{5,65},{6,96},{7,97},{8,40},{9,41... | collective-permute-start | bytes 98312 | tf_op jit(solution)/shard_map/ppermute | solution.py:53
  38.9 1.3 %collective-permute-start.4 = (f32[2,16,512]{2,1,0:T(8,128)S(1)}, f32[2,16,512]{2,1,0:T(8,128)S(1)}, u32[]{:S(2)}, u32[]{:S(2)}) collective-permute-start(f32[2,16,512]{2,1,0:T(8,128)S(1)} %get-tuple-element.407), channel_id=1, source_target_pairs={{0,1},{1,0},{2,3},{3,2},{4,5},{5,4},{6,7},{7,6},{8,9},{9,8},{10,11... | collective-permute-start | bytes 196616 | tf_op jit(solution)/shard_map/ppermute | solution.py:57
  40.3 1.8 %collective-permute-start.5 = (f32[2,16,512]{2,1,0:T(8,128)S(1)}, f32[2,16,512]{2,1,0:T(8,128)S(1)}, u32[]{:S(2)}, u32[]{:S(2)}) collective-permute-start(f32[2,16,512]{2,1,0:T(8,128)S(1)} %get-tuple-element.409), channel_id=1, source_target_pairs={{0,1},{1,0},{2,3},{3,2},{4,5},{5,4},{6,7},{7,6},{8,9},{9,8},{10,11... | collective-permute-start | bytes 196616 | tf_op jit(solution)/shard_map/ppermute | solution.py:53
  43.5 1.5 %collective-permute-start.9 = (f32[2,16,512]{2,1,0:T(8,128)S(1)}, f32[2,16,512]{2,1,0:T(8,128)S(1)}, u32[]{:S(2)}, u32[]{:S(2)}) collective-permute-start(f32[2,16,512]{2,1,0:T(8,128)S(1)} %get-tuple-element.412), channel_id=1, source_target_pairs={{0,1},{1,0},{2,3},{3,2},{4,5},{5,4},{6,7},{7,6},{8,9},{9,8},{10,11... | collective-permute-start | bytes 196616 | tf_op jit(solution)/shard_map/ppermute | solution.py:53
  45.0 3.3 %collective-permute-start.11 = (f32[2,16,512]{2,1,0:T(8,128)S(1)}, f32[2,16,512]{2,1,0:T(8,128)S(1)}, u32[]{:S(2)}, u32[]{:S(2)}) collective-permute-start(f32[2,16,512]{2,1,0:T(8,128)S(1)} %add_add_fusion.1), channel_id=1, source_target_pairs={{0,1},{1,0},{2,3},{3,2},{4,5},{5,4},{6,7},{7,6},{8,9},{9,8},{10,11... | collective-permute-start | bytes 196616 | tf_op jit(solution)/shard_map/ppermute | solution.py:57
  45.4 5.2 %collective-permute-start.12 = (f32[2,64,64]{2,1,0:T(8,128)S(1)}, f32[2,64,64]{2,1,0:T(8,128)S(1)}, u32[]{:S(2)}, u32[]{:S(2)}) collective-permute-start(f32[2,64,64]{2,1,0:T(8,128)S(1)} %pad_maximum_fusion.103), channel_id=1, source_target_pairs={{0,1},{1,0},{2,36},{3,37},{4,5},{5,4},{6,7},{7,6},{8,9},{9,8},{10,... | collective-permute-start | bytes 98312 | tf_op jit(solution)/shard_map/ppermute | solution.py:53
  50.6 4.0 %collective-permute-start.13 = (f32[2,16,256]{2,1,0:T(8,128)S(1)}, f32[2,16,256]{2,1,0:T(8,128)S(1)}, u32[]{:S(2)}, u32[]{:S(2)}) collective-permute-start(f32[2,16,256]{2,1,0:T(8,128)S(1)} %add_add_fusion.3), channel_id=1, source_target_pairs={{0,2},{1,3},{2,0},{3,1},{4,5},{5,4},{6,7},{7,6},{8,10},{9,11},{10,... | collective-permute-start | bytes 98312 | tf_op jit(solution)/shard_map/ppermute | solution.py:53
  56.2 2.3 %collective-permute-start.18 = (f32[2,16,256]{2,1,0:T(8,128)S(1)}, f32[2,16,256]{2,1,0:T(8,128)S(1)}, u32[]{:S(2)}, u32[]{:S(2)}) collective-permute-start(f32[2,16,256]{2,1,0:T(8,128)S(1)} %get-tuple-element.415), channel_id=1, source_target_pairs={{0,1},{1,0},{2,3},{3,2},{4,5},{5,4},{6,7},{7,6},{8,9},{9,8},{10,11... | collective-permute-start | bytes 98312 | tf_op jit(solution)/shard_map/ppermute | solution.py:53
  60.0 28.8 %collective-permute-start.20 = (f32[2,16,512]{2,1,0:T(8,128)S(1)}, f32[2,16,512]{2,1,0:T(8,128)S(1)}, u32[]{:S(2)}, u32[]{:S(2)}) collective-permute-start(f32[2,16,512]{2,1,0:T(8,128)S(1)} %add.207), channel_id=1, source_target_pairs={{0,1},{1,0},{2,3},{3,2},{4,5},{5,4},{6,7},{7,6},{8,9},{9,8},{10,11... | collective-permute-start | bytes 196616 | tf_op jit(solution)/shard_map/ppermute | solution.py:57
  60.5 22.7 %collective-permute-start.22 = (f32[2,80,64]{2,1,0:T(8,128)S(1)}, f32[2,80,64]{2,1,0:T(8,128)S(1)}, u32[]{:S(2)}, u32[]{:S(2)}) collective-permute-start(f32[2,80,64]{2,1,0:T(8,128)S(1)} %get-tuple-element.269), channel_id=1, source_target_pairs={{0,1},{1,0},{2,102},{3,103},{4,5},{5,4},{6,7},{7,6},{8,9},{9,8},{1... | collective-permute-start | bytes 122888 | tf_op jit(solution)/shard_map/ppermute | solution.py:53
  80.0 8.8 %collective-permute-start.21 = (f32[2,80,64]{2,1,0:T(8,128)S(1)}, f32[2,80,64]{2,1,0:T(8,128)S(1)}, u32[]{:S(2)}, u32[]{:S(2)}) collective-permute-start(f32[2,80,64]{2,1,0:T(8,128)S(1)} %get-tuple-element.395), channel_id=1, source_target_pairs={{0,1},{1,0},{2,70},{3,71},{4,5},{5,4},{6,7},{7,6},{8,9},{9,8},{10,... | collective-permute-start | bytes 122888 | tf_op jit(solution)/shard_map/ppermute | solution.py:53
  88.9 5.1 %collective-permute-start.26 = (f32[2,16,320]{2,1,0:T(8,128)S(1)}, f32[2,16,320]{2,1,0:T(8,128)S(1)}, u32[]{:S(2)}, u32[]{:S(2)}) collective-permute-start(f32[2,16,320]{2,1,0:T(8,128)S(1)} %pad_maximum_fusion.104), channel_id=1, source_target_pairs={{0,1},{1,0},{2,36},{3,37},{4,5},{5,4},{6,7},{7,6},{8,9},{9,8},{10,... | collective-permute-start | bytes 122888 | tf_op jit(solution)/shard_map/ppermute | solution.py:53
  89.0 5.9 %collective-permute-start.23 = (f32[2,16,512]{2,1,0:T(8,128)S(1)}, f32[2,16,512]{2,1,0:T(8,128)S(1)}, u32[]{:S(2)}, u32[]{:S(2)}) collective-permute-start(f32[2,16,512]{2,1,0:T(8,128)S(1)} %get-tuple-element.418), channel_id=1, source_target_pairs={{0,6},{1,7},{2,0},{3,1},{4,5},{5,4},{6,2},{7,3},{8,14},{9,15},{10,... | collective-permute-start | bytes 196616 | tf_op jit(solution)/shard_map/ppermute | solution.py:53
  89.1 5.9 %collective-permute-start.25 = (f32[2,16,512]{2,1,0:T(8,128)S(1)}, f32[2,16,512]{2,1,0:T(8,128)S(1)}, u32[]{:S(2)}, u32[]{:S(2)}) collective-permute-start(f32[2,16,512]{2,1,0:T(8,128)S(1)} %get-tuple-element.424), channel_id=1, source_target_pairs={{0,1},{1,0},{2,34},{3,35},{4,2},{5,3},{6,7},{7,6},{8,9},{9,8},{10,... | collective-permute-start | bytes 196616 | tf_op jit(solution)/shard_map/ppermute | solution.py:53
  95.0 1.3 %collective-permute-start.27 = (f32[2,16,512]{2,1,0:T(8,128)S(1)}, f32[2,16,512]{2,1,0:T(8,128)S(1)}, u32[]{:S(2)}, u32[]{:S(2)}) collective-permute-start(f32[2,16,512]{2,1,0:T(8,128)S(1)} %add_add_fusion), channel_id=1, source_target_pairs={{0,1},{1,0},{2,3},{3,2},{4,5},{5,4},{6,7},{7,6},{8,9},{9,8},{10,11... | collective-permute-start | bytes 196616 | tf_op jit(solution)/shard_map/ppermute | solution.py:57
  99.3 4.0 %collective-permute-start.31 = (f32[2,16,192]{2,1,0:T(8,128)S(1)}, f32[2,16,192]{2,1,0:T(8,128)S(1)}, u32[]{:S(2)}, u32[]{:S(2)}) collective-permute-start(f32[2,16,192]{2,1,0:T(8,128)S(1)} %pad_maximum_fusion.106), channel_id=1, source_target_pairs={{0,1},{1,0},{2,4},{3,5},{4,2},{5,3},{6,7},{7,6},{8,9},{9,8},{10,12... | collective-permute-start | bytes 73736 | tf_op jit(solution)/shard_map/ppermute | solution.py:53
  99.6 3.9 %collective-permute-start.30 = (f32[2,16,192]{2,1,0:T(8,128)S(1)}, f32[2,16,192]{2,1,0:T(8,128)S(1)}, u32[]{:S(2)}, u32[]{:S(2)}) collective-permute-start(f32[2,16,192]{2,1,0:T(8,128)S(1)} %pad_maximum_fusion.106), channel_id=1, source_target_pairs={{0,2},{1,3},{2,0},{3,1},{4,5},{5,4},{6,7},{7,6},{8,10},{9,11},{10,... | collective-permute-start | bytes 73736 | tf_op jit(solution)/shard_map/ppermute | solution.py:53
  99.6 5.4 %collective-permute-start.29 = (f32[2,16,192]{2,1,0:T(8,128)S(1)}, f32[2,16,192]{2,1,0:T(8,128)S(1)}, u32[]{:S(2)}, u32[]{:S(2)}) collective-permute-start(f32[2,16,192]{2,1,0:T(8,128)S(1)} %pad_maximum_fusion.106), channel_id=1, source_target_pairs={{0,1},{1,0},{2,6},{3,7},{4,5},{5,4},{6,2},{7,3},{8,9},{9,8},{10,14... | collective-permute-start | bytes 73736 | tf_op jit(solution)/shard_map/ppermute | solution.py:53
  105.1 3.8 %collective-permute-start.34 = (f32[2,16,64]{2,1,0:T(8,128)S(1)}, f32[2,16,64]{2,1,0:T(8,128)S(1)}, u32[]{:S(2)}, u32[]{:S(2)}) collective-permute-start(f32[2,16,64]{2,1,0:T(8,128)S(1)} %slice.911), channel_id=1, source_target_pairs={{0,32},{1,33},{2,34},{3,35},{4,36},{5,37},{6,38},{7,39},{8,40},{9,... | collective-permute-start | bytes 24584 | tf_op jit(solution)/shard_map/ppermute | solution.py:53
  105.2 5.0 %collective-permute-start.33 = (f32[2,16,64]{2,1,0:T(8,128)S(1)}, f32[2,16,64]{2,1,0:T(8,128)S(1)}, u32[]{:S(2)}, u32[]{:S(2)}) collective-permute-start(f32[2,16,64]{2,1,0:T(8,128)S(1)} %slice.911), channel_id=1, source_target_pairs={{0,96},{1,97},{2,98},{3,99},{4,100},{5,101},{6,102},{7,103},{8,104... | collective-permute-start | bytes 24584 | tf_op jit(solution)/shard_map/ppermute | solution.py:53
  105.3 5.3 %collective-permute-start.32 = (f32[2,16,64]{2,1,0:T(8,128)S(1)}, f32[2,16,64]{2,1,0:T(8,128)S(1)}, u32[]{:S(2)}, u32[]{:S(2)}) collective-permute-start(f32[2,16,64]{2,1,0:T(8,128)S(1)} %slice.911), channel_id=1, source_target_pairs={{0,64},{1,65},{2,66},{3,67},{4,68},{5,69},{6,70},{7,71},{8,72},{9,... | collective-permute-start | bytes 24584 | tf_op jit(solution)/shard_map/ppermute | solution.py:53
  (24 other events, 40.9 us)
